TPU v7x, 512 devices: a whole 4x8x8 slice. The times are simulated.
512 devices in a mesh: section: 8 (over x, z_hi), ctx: 64 (over y, z_lo, core).
Axes of the slice: x: 4, y: 8, z: 8 (z_hi: 2, z_lo: 4; z = z_hi * 4 + z_lo), core: 2. Of those that a mesh axis runs over, the one named last changes fastest.
Arguments:
- section_in: bfloat16 [8, 8192, 4096], P('section', 'ctx'), may hold values from -12 to 12
- back_in: bfloat16 [8, 8192, 4096], P('section', 'ctx'), may hold values from -12 to 12
- upstream: bfloat16 [8, 8192, 4096], P('section', 'ctx'), may hold values from -6 to 6
- gains: float32 [8, 4096], P('section'), may hold values from 0.25 to 1.75
- kv_weight: bfloat16 [8, 4096, 1024], P('section', 'ctx')
Outputs:
- next_in: bfloat16 [8, 8192, 4096], P('section', 'ctx')
- next_grad: bfloat16 [8, 8192, 4096], P('section', 'ctx')
- gain_grad: float32 [8, 4096], P('section')
All inputs are finite; a program needn't handle non-finite values.
Results may differ from a plain program's by a relative error of at most 0.012.
Values may be sent and summed in bfloat16 or wider, within the bound.
No kernel may reach another device: no remote copies, remote signals or barrier semaphores. Data moves between devices by JAX's collectives and lax.ppermute only.
A program may use at most 64 MiB of HBM per device.

v0:
```python
import jax
import jax.numpy as jnp
from jax import lax
from jax.sharding import PartitionSpec as P

HD = 128
STEPS = 2


EPSILON = 1e-05


def from_behind(value, axis, by):
    peers = lax.axis_size(axis)
    pairs = [(i, i + by) for i in range(peers) if 0 <= i + by < peers]
    return lax.ppermute(value, axis, pairs)


def shifted(block, axis, distance):
    devices = range(lax.axis_size(axis))
    route = [((i - distance) % len(devices), i) for i in devices]
    return lax.ppermute(block, axis, route)


def norm_forward(section_x, gain_row):
    values = section_x.astype(jnp.float32)
    inv_rms = lax.rsqrt(jnp.mean(values * values, axis=-1, keepdims=True) + EPSILON)
    scaled = values * inv_rms
    return (scaled, inv_rms, (scaled * gain_row).astype(jnp.bfloat16))


def key_mask(row_count, block_id):
    span = (STEPS + 1) * row_count
    tok_pos = lax.broadcasted_iota(jnp.int32, (row_count, span), 0)
    slot_pos = lax.broadcasted_iota(jnp.int32, (row_count, span), 1)
    slot_block = slot_pos // row_count
    earlier = slot_block < STEPS
    present = block_id - STEPS + slot_block >= 0
    causal = slot_pos - slot_block * row_count <= tok_pos
    return present & (earlier | causal)


def fetch_window(key_values):
    gathered = []
    for shift_back in range(STEPS, 0, -1):
        gathered.append(from_behind(key_values, "ctx", shift_back))
    return jnp.concatenate(gathered + [key_values], axis=0)


def fetch_again(key_values):
    gathered = []
    for shift_back in range(STEPS, 0, -1):
        gathered.append(from_behind(key_values, "ctx", shift_back))
    return jnp.concatenate(gathered + [key_values], axis=0)


def head_probs(queries, keys, key_valid):
    score_scale = HD ** (-0.5)
    logits = (
        jnp.einsum("tgd,ld->gtl", queries, keys, preferred_element_type=jnp.float32) * score_scale
    )
    logits = jnp.where(key_valid[None], logits, -1e30)
    row_max = jnp.max(logits, axis=-1, keepdims=True)
    exp_terms = jnp.exp(logits - row_max)
    probs = exp_terms / jnp.sum(exp_terms, axis=-1, keepdims=True)
    return (probs, probs.astype(jnp.bfloat16))


def split_heads(normed, window_kv):
    row_count = normed.shape[0]
    span = window_kv.shape[0]
    kv_width = window_kv.shape[1] // 2
    kv_heads = kv_width // HD
    group = normed.shape[1] // kv_width
    heads_q = jnp.transpose(normed.reshape(row_count, kv_heads, group, HD), (1, 0, 2, 3))
    keys = jnp.transpose(window_kv[:, :kv_width].reshape(span, kv_heads, HD), (1, 0, 2))
    values = jnp.transpose(window_kv[:, kv_width:].reshape(span, kv_heads, HD), (1, 0, 2))
    return (heads_q, keys, values)


def merge_heads(per_head):
    moved = jnp.transpose(per_head, (1, 0, 2, 3))
    return moved.reshape(moved.shape[0], -1)


def body(section_in, back_in, upstream, gains, kv_weight):
    block_id = lax.axis_index("ctx")
    gain_row = gains[0]
    x_fwd = section_in[0]
    x_back = back_in[0]
    upper_in = upstream[0]
    row_count = x_fwd.shape[0]
    w_full = lax.all_gather(kv_weight[0], "ctx", axis=0, tiled=True)
    kv_width = w_full.shape[1] // 2
    key_valid = key_mask(row_count, block_id)

    def project(normed):
        return jnp.dot(normed, w_full, preferred_element_type=jnp.float32).astype(jnp.bfloat16)

    scaled, inv_rms, normed = norm_forward(x_fwd, gain_row)
    window_kv = fetch_window(project(normed))
    heads_q, keys, values = split_heads(normed, window_kv)

    def forward_head(operands):
        query_h, key_h, value_h = operands
        probs, probs_b = head_probs(query_h, key_h, key_valid)
        return jnp.einsum("gtl,ld->tgd", probs_b, value_h, preferred_element_type=jnp.float32)

    attended = merge_heads(lax.map(forward_head, (heads_q, keys, values)))
    layer_out = (x_fwd.astype(jnp.float32) + attended).astype(jnp.bfloat16)
    next_in = shifted(layer_out, "section", 1)
    scaled_b, inv_rms_b, normed_b = norm_forward(x_back, gain_row)
    window_b = fetch_again(project(normed_b))
    heads_qb, keys_b, values_b = split_heads(normed_b, window_b)
    heads_up = jnp.transpose(
        upper_in.reshape(heads_qb.shape[1], heads_qb.shape[0], heads_qb.shape[2], HD), (1, 0, 2, 3)
    )
    score_scale = HD ** (-0.5)

    def backward_head(operands):
        query_h, key_h, value_h, upper_h = operands
        probs, probs_b = head_probs(query_h, key_h, key_valid)
        head_out = jnp.einsum("gtl,ld->tgd", probs_b, value_h, preferred_element_type=jnp.float32)
        grad_probs = jnp.einsum("tgd,ld->gtl", upper_h, value_h, preferred_element_type=jnp.float32)
        row_dot = jnp.transpose(jnp.sum(upper_h.astype(jnp.float32) * head_out, axis=-1), (1, 0))
        dlogits = (probs * (grad_probs - row_dot[..., None]) * score_scale).astype(jnp.bfloat16)
        grad_query = jnp.einsum("gtl,ld->tgd", dlogits, key_h, preferred_element_type=jnp.float32)
        grad_keys = jnp.einsum("gtl,tgd->ld", dlogits, query_h, preferred_element_type=jnp.float32)
        grad_values = jnp.einsum(
            "gtl,tgd->ld", probs_b, upper_h, preferred_element_type=jnp.float32
        )
        return (grad_query, grad_keys, grad_values)

    grad_query, grad_keys, grad_values = lax.map(
        backward_head, (heads_qb, keys_b, values_b, heads_up)
    )
    span = window_b.shape[0]
    grad_keys = jnp.transpose(grad_keys, (1, 0, 2)).reshape(span, kv_width)
    grad_values = jnp.transpose(grad_values, (1, 0, 2)).reshape(span, kv_width)
    grad_window = jnp.concatenate([grad_keys, grad_values], axis=1)
    own_grad = grad_window[STEPS * row_count :]
    for shift_back in range(1, STEPS + 1):
        first_row = (STEPS - shift_back) * row_count
        own_grad = own_grad + from_behind(
            grad_window[first_row : first_row + row_count], "ctx", -shift_back
        )
    grad_kv = own_grad.astype(jnp.bfloat16)
    back_proj = lax.dot_general(
        grad_kv, w_full, (((1,), (1,)), ((), ())), preferred_element_type=jnp.float32
    )
    grad_normed = merge_heads(grad_query) + back_proj
    gain_total = lax.psum(jnp.sum(grad_normed * scaled_b, axis=0), "ctx")
    grad_scaled = grad_normed * gain_row
    inner = jnp.mean(grad_scaled * scaled_b, axis=-1, keepdims=True)
    grad_input = (
        inv_rms_b * (grad_scaled - scaled_b * inner) + upper_in.astype(jnp.float32)
    ).astype(jnp.bfloat16)
    next_grad = shifted(grad_input, "section", -1)
    return (next_in[None], next_grad[None], gain_total[None])


def solution(mesh):
    in_specs = (
        P("section", "ctx", None),
        P("section", "ctx", None),
        P("section", "ctx", None),
        P("section", None),
        P("section", "ctx", None),
    )
    out_specs = (P("section", "ctx", None), P("section", "ctx", None), P("section", None))
    return jax.shard_map(body, mesh=mesh, in_specs=in_specs, out_specs=out_specs, check_vma=False)
```

profile of v0, /device:TPU:1, one launch (start us, length us, event | category | flops | bytes accessed | tf_op | source)
XLA Modules:
  0.0 655.1 jit_solution(12599974904776684757)
XLA Ops:
  7.9 2.3 copy.35
  15.7 6.0 fusion.161
  21.7 120.0 %all-gather.3.cloned.1.call-done = bf16[1,4096,1024]{2,1,0:T(8,128)(2,1)} async-done(((bf16[1,64,1024]{2,1,0:T(8,128)(2,1)}), bf16[1,4096,1024]{2,1,0:T(8,128)(2,1)}) %all-gather.3.cloned.1.call-update) | async-done | bytes 8388624 | tf_op jit(solution)/shard_map/all_gather | solution.py:93
  141.7 4.8 fusion.157
  148.6 3.4 collective-permute-start.3
  153.4 2.4 collective-permute-start.1
  155.9 2.2 collective-permute-start
  159.0 2.8 collective-permute-done.1
  161.8 4.2 collective-permute-done
  169.5 18.3 %while.26 = (s32[]{:T(128)}, f32[4,128,8,128]{1,3,2,0:T(8,128)}, bf16[4,384,128]{1,2,0:T(8,128)(2,1)}, bf16[4,384,128]{2,1,0:T(8,128)(2,1)S(1)}, bf16[4,128,8,12...) while((s32[]{:T(128)}, f32[4,128,8,128]{1,3,2,0:T(8,128)}, ...), condition=%wide.region_4.5_spmd.clone, body=%wide.region_1.4_spmd.clone.sunk | while | flops 305972992 | bytes 1505777 | solution.py:109
  171.3 2.8 fusion.228
  175.9 2.7 fusion.228
  180.5 2.7 fusion.228
  185.1 2.7 fusion.228
  187.8 3.0 copy.47
  192.3 56.2 %while.27 = (s32[]{:T(128)}, f32[4,128,8,128]{1,3,2,0:T(8,128)}, f32[4,384,128]{1,2,0:T(8,128)}, f32[4,384,128]{1,2,0:T(8,128)}, bf16[4,384,128]{2,1,0:T(8,128)(...) while((s32[]{:T(128)}, f32[4,128,8,128]{1,3,2,0:T(8,128)}, ...), condition=%wide.region_10.11_spmd.clone, body=%wide.region_6.10_spmd.clone.sunk | while | flops 813615232 | bytes 10128397 | solution.py:134
  193.7 2.8 fusion.246
  200.6 2.7 fusion.251
  207.8 2.8 fusion.246
  214.7 2.6 fusion.251
  221.8 2.8 fusion.246
  228.7 2.6 fusion.251
  235.9 2.8 fusion.246
  242.7 2.7 fusion.251
  248.6 2.4 fusion.168
  255.4 6.1 collective-permute-start.2
  261.5 3.0 copy.48
  265.8 3.7 collective-permute-done.6
  269.5 7.6 %fusion.148 = (f32[4096]{0:T(1024)S(1)}, f32[128]{0:T(128)S(1)}, f32[128,4096]{1,0:T(8,128)S(1)}) fusion(bf16[1,128,4096]{2,1,0:T(8,128)(2,1)S(1)} %copy-done, f32[128]{0:T(128)S(1)} %get-tuple-element.209, f32[4096]{0:T(1024)S(1)} %bitcast.366, f32[128,4096]{1,0:T(8,128)} %copy.48, bf16[1,4096,1024]{2,1,0:T(8,128)(2,1)} %all-gather.3.cloned.1.call-done, ...), kind=kOutput, calls=%fused_computation.117 | convolution fusion | flops 1078456192 | bytes 16286720 | tf_op jit(solution)/shard_map/dot_general | solution.py:148
  277.8 8.2 %collective-permute-start.7 = (bf16[128,4096]{1,0:T(8,128)(2,1)S(1)}, bf16[128,4096]{1,0:T(8,128)(2,1)S(1)}, u32[]{:S(2)}, u32[]{:S(2)}) collective-permute-start(bf16[128,4096]{1,0:T(8,128)(2,1)S(1)} %fusion.147), channel_id=1, source_target_pairs={{64,0},{128,64},{192,128},{256,192},{320,256},{384,320},{448,384},... | collective-permute-start | bytes 3145736 | tf_op jit(solution)/shard_map/ppermute | solution.py:22
  286.0 359.0 %psum.7 = f32[1,4096]{1,0:T(1,128)} all-reduce(f32[1,4096]{1,0:T(1,128)S(1)} %bitcast.368), channel_id=1, replica_groups=mesh['section'=8,'ctx'=64] {'ctx'}, use_global_device_ids=true, to_apply=%region_13.14 | all-reduce | flops 4096 | bytes 32768 | tf_op jit(solution)/shard_map/psum | solution.py:152
  645.0 2.3 copy.112
  (90 shorter events, 64.8 us)
Async XLA Ops:
  7.2 3.1 copy-start.1
  7.2 134.5 %all-gather.3.cloned.1.call-start = ((), (), s32[]{:S(2)}) async-start(), calls=%async_computation | async-start | bytes 8519680 | tf_op jit(solution)/shard_map/all_gather | solution.py:93
  10.4 1.7 copy-start
  14.1 0.7 copy-start.8
  14.1 1.6 copy-start.4
  141.6 10.4 %copy-start.2 = (bf16[1,4096,1024]{2,1,0:T(8,128)(2,1)S(1)}, bf16[1,4096,1024]{2,1,0:T(8,128)(2,1)}, u32[]{:S(2)}) copy-start(bf16[1,4096,1024]{2,1,0:T(8,128)(2,1)} %all-gather.3.cloned.1.call-done) | copy-start | bytes 25165828
  146.5 11.6 %collective-permute-start.4 = (bf16[128,1024]{1,0:T(8,128)(2,1)S(1)}, bf16[128,1024]{1,0:T(8,128)(2,1)S(1)}, u32[]{:S(2)}, u32[]{:S(2)}) collective-permute-start(bf16[128,1024]{1,0:T(8,128)(2,1)S(1)} %fusion.157), channel_id=1, source_target_pairs={{0,1},{1,2},{2,3},{3,4},{4,5},{5,6},{6,7},{7,8},{8,9},{9,10},{10,1... | collective-permute-start | bytes 786440 | tf_op jit(solution)/shard_map/ppermute | solution.py:16
  148.6 9.4 %collective-permute-start.3 = (bf16[128,1024]{1,0:T(8,128)(2,1)S(1)}, bf16[128,1024]{1,0:T(8,128)(2,1)S(1)}, u32[]{:S(2)}, u32[]{:S(2)}) collective-permute-start(bf16[128,1024]{1,0:T(8,128)(2,1)S(1)} %fusion.157), channel_id=1, source_target_pairs={{0,2},{1,3},{2,4},{3,5},{4,6},{5,7},{6,8},{7,9},{8,10},{9,11},{10,... | collective-permute-start | bytes 786440 | tf_op jit(solution)/shard_map/ppermute | solution.py:16
  153.4 8.4 %collective-permute-start.1 = (bf16[128,1024]{1,0:T(8,128)(2,1)S(1)}, bf16[128,1024]{1,0:T(8,128)(2,1)S(1)}, u32[]{:S(2)}, u32[]{:S(2)}) collective-permute-start(bf16[128,1024]{1,0:T(8,128)(2,1)S(1)} %fusion.154), channel_id=1, source_target_pairs={{0,1},{1,2},{2,3},{3,4},{4,5},{5,6},{6,7},{7,8},{8,9},{9,10},{10,1... | collective-permute-start | bytes 786440 | tf_op jit(solution)/shard_map/ppermute | solution.py:16
  155.9 10.1 %collective-permute-start = (bf16[128,1024]{1,0:T(8,128)(2,1)S(1)}, bf16[128,1024]{1,0:T(8,128)(2,1)S(1)}, u32[]{:S(2)}, u32[]{:S(2)}) collective-permute-start(bf16[128,1024]{1,0:T(8,128)(2,1)S(1)} %fusion.154), channel_id=1, source_target_pairs={{0,2},{1,3},{2,4},{3,5},{4,6},{5,7},{6,8},{7,9},{8,10},{9,11},{10,... | collective-permute-start | bytes 786440 | tf_op jit(solution)/shard_map/ppermute | solution.py:16
  167.9 1.6 copy-start.7
  248.6 5.6 copy-start.3
  251.0 14.8 %collective-permute-start.5 = (f32[128,1024]{0,1:T(8,128)}, f32[128,1024]{0,1:T(8,128)S(1)}, u32[]{:S(2)}, u32[]{:S(2)}) collective-permute-start(f32[128,1024]{0,1:T(8,128)} %get-tuple-element.200), channel_id=1, source_target_pairs={{1,0},{2,1},{3,2},{4,3},{5,4},{6,5},{7,6},{8,7},{9,8},{10,9},{11,1... | collective-permute-start | bytes 1572872 | tf_op jit(solution)/shard_map/ppermute | solution.py:16
  252.9 16.7 %collective-permute-start.6 = (f32[128,1024]{0,1:T(8,128)}, f32[128,1024]{0,1:T(8,128)}, u32[]{:S(2)}, u32[]{:S(2)}) collective-permute-start(f32[128,1024]{0,1:T(8,128)} %get-tuple-element.201), channel_id=1, source_target_pairs={{2,0},{3,1},{4,2},{5,3},{6,4},{7,5},{8,6},{9,7},{10,8},{11,9},{12,... | collective-permute-start | bytes 1572872 | tf_op jit(solution)/shard_map/ppermute | solution.py:16
  255.4 389.6 %collective-permute-start.2 = (bf16[128,4096]{1,0:T(8,128)(2,1)}, bf16[128,4096]{1,0:T(8,128)(2,1)}, u32[]{:S(2)}, u32[]{:S(2)}) collective-permute-start(bf16[128,4096]{1,0:T(8,128)(2,1)} %fusion.141), channel_id=1, source_target_pairs={{448,0},{0,64},{64,128},{128,192},{192,256},{256,320},{320,384},{3... | collective-permute-start | bytes 3145736 | tf_op jit(solution)/shard_map/ppermute | solution.py:22
  261.5 8.1 %copy-start.6 = (f32[4,384,128]{1,2,0:T(8,128)S(1)}, f32[4,384,128]{1,2,0:T(8,128)}, u32[]{:S(2)}) copy-start(f32[4,384,128]{1,2,0:T(8,128)} %get-tuple-element.87) | copy-start | bytes 2359300
  264.5 12.6 %copy-start.5 = (bf16[1,128,4096]{2,1,0:T(8,128)(2,1)S(1)}, bf16[1,128,4096]{2,1,0:T(8,128)(2,1)}, u32[]{:S(2)}) copy-start(bf16[1,128,4096]{2,1,0:T(8,128)(2,1)} %param.11) | copy-start | bytes 3145732
  277.8 367.2 %collective-permute-start.7 = (bf16[128,4096]{1,0:T(8,128)(2,1)S(1)}, bf16[128,4096]{1,0:T(8,128)(2,1)S(1)}, u32[]{:S(2)}, u32[]{:S(2)}) collective-permute-start(bf16[128,4096]{1,0:T(8,128)(2,1)S(1)} %fusion.147), channel_id=1, source_target_pairs={{64,0},{128,64},{192,128},{256,192},{320,256},{384,320},{448,384},... | collective-permute-start | bytes 3145736 | tf_op jit(solution)/shard_map/ppermute | solution.py:22
Sparse Core Ops, SparseCore 0:
  10.2 131.4 all-gather.2
where the time goes:
time: 656 us; the launch traced here: 655 us
  blocking collectives  359 us (55%)
  waiting for transfers between devices  133 us (20%)
  matrix products  81.8 us (12%)
  starting transfers between devices  27.6 us (4%)
  local copies, waits for them, and re-layouts  26.5 us (4%)
  between operations  14.3 us (2%)
  other arithmetic  13.2 us (2%)
    psum x1, blocking collectives, body(): gain_total = lax.psum(jnp.sum(grad_normed * scaled_b, axis=0), 'ctx')  359 us
    all_gather x1, waiting for transfers between devices, body(): w_full = lax.all_gather(kv_weight[0], 'ctx', axis=0, tiled=True)  120 us
    sub x8, matrix products, head_probs(): exp_terms = jnp.exp(logits - row_max)  17.5 us
    ppermute x2, starting transfers between devices, shifted(): return lax.ppermute(block, axis, route)  14.3 us
    ppermute x6, starting transfers between devices, from_behind(): return lax.ppermute(value, axis, pairs)  13.3 us
  transfers between devices with their start and end apart: 9, of which 5 were waited for; matrix products, arithmetic and copies ran while one was open for 4% of the time, Pallas kernels for 0%

commit v1 on v0

v1 whole, which is shorter than its diff:
```python
import functools

import jax
import jax.numpy as jnp
from jax import lax
from jax.experimental import pallas as pl
from jax.experimental.pallas import tpu as pltpu
from jax.sharding import PartitionSpec as P

HD = 128
STEPS = 2
EPSILON = 1e-05
GROUP = 8
KVH = 4
TOK = 128
SPAN = (STEPS + 1) * TOK

X, Z_HI, Y, Z_LO, CORES = 4, 2, 8, 4, 2
Z = Z_HI * Z_LO
CTX = Y * Z_LO * CORES

SCALE = HD ** (-0.5)
LOG2E = 1.4426950408889634


def ctx_pairs(move):
    pairs = []
    for c in range(CTX):
        target = move(c // (Z_LO * CORES), (c // CORES) % Z_LO, c % CORES)
        if target is not None:
            y, z_lo, core = target
            pairs.append((c, (y * Z_LO + z_lo) * CORES + core))
    return pairs


def over_ctx(value, move):
    return lax.ppermute(value, "ctx", ctx_pairs(move))


def grid_pairs(move):
    pairs = []
    for x in range(X):
        for z in range(Z):
            new_x, new_z = move(x, z)
            new_x, new_z = (new_x % X, new_z % Z)
            for y in range(Y):
                for core in range(CORES):
                    source = (x * Z_HI + z // Z_LO) * CTX + (y * Z_LO + z % Z_LO) * CORES + core
                    target = (new_x * Z_HI + new_z // Z_LO) * CTX + (y * Z_LO + new_z % Z_LO) * CORES + core
                    pairs.append((source, target))
    return pairs


def over_grid(value, move):
    return lax.ppermute(value, ("section", "ctx"), grid_pairs(move))


def halfway(value, way):
    return over_grid(value, lambda x, z: (x, z + 2 * way))


def arrive(value, way, distance):
    def move(x, z):
        z_hi = ((z - 2 * way) % Z) // Z_LO
        cross = (1 if z_hi == Z_HI - 1 else 0) if distance == 1 else (-1 if z_hi == 0 else 0)
        return (x + cross, z + 2 * way)

    return over_grid(value, move)


def set_out(upper, lower):
    return halfway(upper, 1), halfway(lower, -1)


def land(halves, distance):
    return arrive(halves[0], 1, distance), arrive(halves[1], -1, distance)


def norm_forward(section_x, gain_row):
    values = section_x.astype(jnp.float32)
    inv_rms = lax.rsqrt(jnp.mean(values * values, axis=-1, keepdims=True) + EPSILON)
    return (values * inv_rms * gain_row).astype(jnp.bfloat16)


def by_head(kv_columns):
    parts = []
    for head in range(KVH):
        parts.append(kv_columns[:, head * HD : (head + 1) * HD])
        parts.append(kv_columns[:, (KVH + head) * HD : (KVH + head + 1) * HD])
    return jnp.concatenate(parts, axis=1)


def gather_weight(own_rows, core, z_lo, y, start_crossing):
    half = own_rows.shape[1] // 2
    columns = by_head(own_rows)
    low, high = columns[:, :half], columns[:, half:]
    keep = jnp.where(core == 0, low, high)
    received = over_ctx(jnp.where(core == 0, high, low), lambda y, z, c: (y, z, 1 - c))
    chip = jnp.concatenate(
        [jnp.where(core == 0, keep, received), jnp.where(core == 0, received, keep)], axis=0
    )
    rows = chip.shape[0]
    pieces = [chip]
    for step in range(1, Z_LO):
        pieces.append(over_ctx(chip, lambda y, z, c, step=step: (y, (z + step) % Z_LO, c)))
    back = pieces[::-1]
    run = lax.dynamic_slice_in_dim(
        jnp.concatenate(back + back[:-1], axis=0), (Z_LO - 1 - z_lo) * rows, Z_LO * rows, 0
    )
    block = Z_LO * rows
    weight = jnp.zeros((Y * block, half), own_rows.dtype)

    def place(weight, piece, at, offset=0):
        return lax.dynamic_update_slice_in_dim(weight, piece, (at % Y) * block + offset, 0)

    def up(piece):
        return over_ctx(piece, lambda y, z, c: ((y + 1) % Y, z, c))

    def down(piece):
        return over_ctx(piece, lambda y, z, c: ((y - 1) % Y, z, c))

    weight = place(weight, run, y)
    rising, falling = run, run
    for step in range(1, Y // 2):
        rising, falling = up(rising), down(falling)
        weight = place(weight, rising, y - step + Y)
        weight = place(weight, falling, y + step)
        if step == 1:
            crossing = start_crossing(run)
        if step == 3:
            (rising, falling), crossing = lax.optimization_barrier(((rising, falling), crossing))
    last_rising, last_falling = up(rising[: block // 2]), down(falling[block // 2 :])
    weight = place(weight, last_rising, y + Y // 2)
    weight = place(weight, last_falling, y + Y // 2, block // 2)
    return weight, crossing


def swap(value):
    return over_ctx(value, lambda y, z, c: (y, z, 1 - c))


def chip_rows(own, partner, core):
    return jnp.concatenate(
        [jnp.where(core == 0, own, partner), jnp.where(core == 0, partner, own)], axis=0
    )


def next_chip(y, z):
    chip = y * Z_LO + z + 1
    return None if chip == Y * Z_LO else (chip // Z_LO, chip % Z_LO)


def to_next(cross):
    def move(y, z, core):
        after = next_chip(y, z)
        return None if after is None else (after[0], after[1], core ^ cross)

    return move


def window(mine, core):
    other = swap(mine)
    same = over_ctx(mine, to_next(0))
    cross = over_ctx(mine, to_next(1))
    rows = jnp.concatenate([same, mine], axis=0)
    others = jnp.concatenate([cross, other], axis=0)
    return jnp.concatenate(
        [jnp.where(core == 0, rows, others), jnp.where(core == 0, others, rows)], axis=1
    )


def stacked(ref, first, count):
    return jnp.concatenate(
        [ref[:, (first + g) * HD : (first + g + 1) * HD] for g in range(count)], axis=0
    )


def masked_scores(keys, queries, block_id):
    scores = lax.dot_general(
        keys, queries, (((1,), (1,)), ((), ())), preferred_element_type=jnp.float32
    )
    across = queries.shape[0]
    parts = []
    for slot in range(STEPS):
        part = scores[slot * TOK : (slot + 1) * TOK]
        parts.append(jnp.where(block_id - STEPS + slot >= 0, part, -1e30))
    seen = lax.broadcasted_iota(jnp.int32, (TOK, across), 0)
    query = lax.broadcasted_iota(jnp.int32, (TOK, across), 1) % TOK
    parts.append(jnp.where(seen <= query, scores[STEPS * TOK :], -1e30))
    return jnp.concatenate(parts, axis=0)


PAIR = 2


def forward_kernel(block_ref, normed_ref, x_ref, kv_ref, out_ref):
    block_id = block_ref[0]
    first = pl.multiple_of((block_id % CORES) * TOK, TOK)
    kv = kv_ref[pl.ds(first, SPAN), :]
    keys, values = kv[:, :HD], kv[:, HD:]
    values_t = values.astype(jnp.float32).T.astype(jnp.bfloat16)
    for pair in range(GROUP // PAIR):
        queries = stacked(normed_ref, pair * PAIR, PAIR)
        scores = masked_scores(keys, queries, block_id)
        top = jnp.max(scores, axis=0, keepdims=True)
        terms = jnp.exp2((scores - top) * (SCALE * LOG2E))
        total = jnp.sum(terms, axis=0, keepdims=True)
        attended = jnp.dot(
            values_t, terms.astype(jnp.bfloat16), preferred_element_type=jnp.float32
        ) * (1.0 / total)
        for g in range(PAIR):
            at = (pair * PAIR + g) * HD
            out = attended[:, g * TOK : (g + 1) * TOK].T + x_ref[:, at : at + HD].astype(jnp.float32)
            out_ref[:, at : at + HD] = out.astype(jnp.bfloat16)


def forward_attention(block_id, normed, x, kv):
    wide = GROUP * HD
    return pl.pallas_call(
        forward_kernel,
        grid=(KVH,),
        in_specs=[
            pl.BlockSpec(memory_space=pltpu.SMEM),
            pl.BlockSpec((TOK, wide), lambda h: (0, h)),
            pl.BlockSpec((TOK, wide), lambda h: (0, h)),
            pl.BlockSpec((4 * TOK, 2 * HD), lambda h: (0, h)),
        ],
        out_specs=pl.BlockSpec((TOK, wide), lambda h: (0, h)),
        out_shape=jax.ShapeDtypeStruct(x.shape, jnp.bfloat16),
        compiler_params=pltpu.CompilerParams(vmem_limit_bytes=32 * 2**20),
        cost_estimate=pl.CostEstimate(
            flops=16 * 10**8, bytes_accessed=4 * 2**20, transcendentals=2 * 10**6
        ),
        name="forward_attention",
    )(block_id, normed, x, kv)


def backward_kernel(
    block_ref, normed_ref, upper_ref, kv_ref, dq_ref, far_ref, near_ref, own_ref, probs_ref, dlog_ref
):
    block_id = block_ref[0]
    first = pl.multiple_of((block_id % CORES) * TOK, TOK)
    kv = kv_ref[pl.ds(first, SPAN), :]
    keys, values = kv[:, :HD], kv[:, HD:]
    keys_t = keys.astype(jnp.float32).T.astype(jnp.bfloat16)
    for pair in range(GROUP // PAIR):
        queries = stacked(normed_ref, pair * PAIR, PAIR)
        upper = stacked(upper_ref, pair * PAIR, PAIR)
        scores = masked_scores(keys, queries, block_id)
        grad_probs = lax.dot_general(
            values, upper, (((1,), (1,)), ((), ())), preferred_element_type=jnp.float32
        )
        top = jnp.max(scores, axis=0, keepdims=True)
        terms = jnp.exp2((scores - top) * (SCALE * LOG2E))
        inverse = 1.0 / jnp.sum(terms, axis=0, keepdims=True)
        row_dot = jnp.sum(terms * grad_probs, axis=0, keepdims=True) * inverse
        probs = terms * inverse
        at = pair * PAIR * TOK
        probs_ref[:, at : at + PAIR * TOK] = probs.astype(jnp.bfloat16)
        dlog_ref[:, at : at + PAIR * TOK] = (probs * ((grad_probs - row_dot) * SCALE)).astype(
            jnp.bfloat16
        )
    dlogits = dlog_ref[...]
    grad_keys = jnp.dot(dlogits, stacked(normed_ref, 0, GROUP), preferred_element_type=jnp.float32)
    grad_values = jnp.dot(
        probs_ref[...], stacked(upper_ref, 0, GROUP), preferred_element_type=jnp.float32
    )
    grad_query = jnp.dot(keys_t, dlogits, preferred_element_type=jnp.float32)
    for g in range(GROUP):
        dq_ref[:, g * HD : (g + 1) * HD] = grad_query[:, g * TOK : (g + 1) * TOK].T
    for slot, ref in enumerate((far_ref, near_ref, own_ref)):
        ref[:, :HD] = grad_keys[slot * TOK : (slot + 1) * TOK].astype(ref.dtype)
        ref[:, HD:] = grad_values[slot * TOK : (slot + 1) * TOK].astype(ref.dtype)


def backward_attention(block_id, normed, upper, kv):
    wide = GROUP * HD
    heads = pl.BlockSpec((TOK, wide), lambda h: (0, h))
    grads = pl.BlockSpec((TOK, 2 * HD), lambda h: (0, h))
    kv_width = kv.shape[1]
    return pl.pallas_call(
        backward_kernel,
        grid=(KVH,),
        in_specs=[
            pl.BlockSpec(memory_space=pltpu.SMEM),
            heads,
            heads,
            pl.BlockSpec((4 * TOK, 2 * HD), lambda h: (0, h)),
        ],
        out_specs=[heads, grads, grads, grads],
        out_shape=[
            jax.ShapeDtypeStruct(normed.shape, jnp.float32),
            jax.ShapeDtypeStruct((TOK, kv_width), jnp.bfloat16),
            jax.ShapeDtypeStruct((TOK, kv_width), jnp.bfloat16),
            jax.ShapeDtypeStruct((TOK, kv_width), jnp.float32),
        ],
        scratch_shapes=[
            pltpu.VMEM((SPAN, wide), jnp.bfloat16),
            pltpu.VMEM((SPAN, wide), jnp.bfloat16),
        ],
        compiler_params=pltpu.CompilerParams(vmem_limit_bytes=32 * 2**20),
        cost_estimate=pl.CostEstimate(
            flops=4 * 10**9, bytes_accessed=8 * 2**20, transcendentals=2 * 10**6
        ),
        name="backward_attention",
    )(block_id, normed, upper, kv)


def input_grad_kernel(
    block_ref, own_ref, near_ref, far_ref, w_mine_ref, w_other_ref, dq_ref, x_ref, upper_ref, gain_ref,
    up_ref, down_ref, gain_grad_ref, grad_kv_ref, inv_ref, inner_ref, grad_ref,
):
    step = pl.program_id(0)
    core = block_ref[0] % CORES
    half = w_mine_ref.shape[1]
    width = w_mine_ref.shape[0]
    features = x_ref.shape[1]

    @pl.when(step == 0)
    def _():
        grad_kv_ref[...] = (
            own_ref[...] + near_ref[...].astype(jnp.float32) + far_ref[...].astype(jnp.float32)
        ).astype(jnp.bfloat16)
        squares = jnp.zeros((TOK, 1), jnp.float32)
        for at in range(0, features, width):
            part = x_ref[:, at : at + width].astype(jnp.float32)
            squares += jnp.sum(part * part, axis=-1, keepdims=True)
        inv_ref[...] = jnp.broadcast_to(lax.rsqrt(squares / features + EPSILON), inv_ref.shape)
        inner_ref[...] = jnp.zeros_like(inner_ref)

    at = pl.ds(pl.multiple_of(step * width, width), width)
    mine = grad_kv_ref[:, pl.ds(pl.multiple_of(core * half, half), half)]
    other = grad_kv_ref[:, pl.ds(pl.multiple_of((1 - core) * half, half), half)]
    contract = (((1,), (1,)), ((), ()))
    grad = dq_ref[...]
    grad += lax.dot_general(mine, w_mine_ref[...], contract, preferred_element_type=jnp.float32)
    grad += lax.dot_general(other, w_other_ref[...], contract, preferred_element_type=jnp.float32)
    inv_rms = inv_ref[:, :1]
    scaled = x_ref[:, at].astype(jnp.float32) * inv_rms
    gain_grad_ref[:, at] = jnp.sum(grad * scaled, axis=0, keepdims=True)
    grad = grad * gain_ref[:, at]
    grad_ref[:, at] = grad
    inner_ref[...] += jnp.broadcast_to(
        jnp.sum(grad * scaled, axis=-1, keepdims=True), inner_ref.shape
    )

    @pl.when(step == pl.num_programs(0) - 1)
    def _():
        for first, ref in ((0, up_ref), (TOK // 2, down_ref)):
            rows = slice(first, first + TOK // 2)
            inv = inv_ref[rows, :1]
            mean = inner_ref[rows, :1] * (1.0 / features)
            for at in range(0, features, width):
                cols = slice(at, at + width)
                scaled = x_ref[rows, cols].astype(jnp.float32) * inv
                out = inv * (grad_ref[rows, cols] - scaled * mean)
                ref[:, cols] = (out + upper_ref[rows, cols].astype(jnp.float32)).astype(jnp.bfloat16)


def input_grad(block_id, own, near, far, w_mine, w_other, dq, x, upper, gain_row):
    features, half = w_mine.shape
    width = 512
    whole = lambda shape: pl.BlockSpec(shape, lambda j: (0, 0))
    tokens = whole((TOK, features))
    return pl.pallas_call(
        input_grad_kernel,
        grid=(features // width,),
        in_specs=[
            pl.BlockSpec(memory_space=pltpu.SMEM),
            whole(own.shape),
            whole(own.shape),
            whole(own.shape),
            pl.BlockSpec((width, half), lambda j: (j, 0)),
            pl.BlockSpec((width, half), lambda j: (j, 0)),
            pl.BlockSpec((TOK, width), lambda j: (0, j)),
            tokens,
            tokens,
            whole((1, features)),
        ],
        out_specs=[
            whole((TOK // 2, features)),
            whole((TOK // 2, features)),
            whole((1, features)),
        ],
        out_shape=[
            jax.ShapeDtypeStruct((TOK // 2, features), jnp.bfloat16),
            jax.ShapeDtypeStruct((TOK // 2, features), jnp.bfloat16),
            jax.ShapeDtypeStruct((1, features), jnp.float32),
        ],
        scratch_shapes=[
            pltpu.VMEM((TOK, 2 * half), jnp.bfloat16),
            pltpu.VMEM((TOK, HD), jnp.float32),
            pltpu.VMEM((TOK, HD), jnp.float32),
            pltpu.VMEM((TOK, features), jnp.float32),
        ],
        compiler_params=pltpu.CompilerParams(vmem_limit_bytes=32 * 2**20),
        cost_estimate=pl.CostEstimate(
            flops=2 * 10**9, bytes_accessed=16 * 2**20, transcendentals=10**3
        ),
        name="input_grad",
    )(block_id, own, near, far, w_mine, w_other, dq, x, upper, gain_row)


def sum_over_ctx(value):
    moves = [lambda y, z, c: (y, z, c ^ 1)]
    moves += [lambda y, z, c, bit=bit: (y, z ^ bit, c) for bit in (1, 2)]
    moves += [lambda y, z, c, bit=bit: (y ^ bit, z, c) for bit in (1, 2, 4)]
    for move in moves:
        value = value + over_ctx(value, move)
    return value


def body(section_in, back_in, upstream, gains, kv_weight):
    index = lax.axis_index("ctx")
    core, z_lo, y = index % CORES, (index // CORES) % Z_LO, index // (CORES * Z_LO)
    block_id = index.astype(jnp.int32).reshape(1)
    x_back, upper_in = back_in[0], upstream[0]

    def start_crossing(after):
        x_fwd, _ = lax.optimization_barrier((section_in[0], after))
        return set_out(x_fwd[: TOK // 2], x_fwd[TOK // 2 :])

    w_mine, crossing = gather_weight(kv_weight[0], core, z_lo, y, start_crossing)
    x_parts = land(crossing, 1)
    peers = lax.axis_size("section")
    next_section = [(i, (i + 1) % peers) for i in range(peers)]
    gain_here = lax.ppermute(gains, "section", next_section)

    normed_back = norm_forward(x_back, gains)
    normed_fwd = norm_forward(section_in[0], gains)
    partner = swap(jnp.concatenate([normed_back, normed_fwd], axis=0))
    chip_back = chip_rows(normed_back, partner[:TOK], core)
    chip_fwd = chip_rows(normed_fwd, partner[TOK:], core)

    def project(normed):
        return jnp.dot(normed, w_mine, preferred_element_type=jnp.float32).astype(jnp.bfloat16)

    kv_back, x_parts = lax.optimization_barrier((project(chip_back), x_parts))
    x_here = jnp.concatenate(x_parts, axis=0)
    window_back = window(kv_back, core)
    kv_fwd, w_later, _ = lax.optimization_barrier((project(chip_fwd), w_mine, window_back))
    w_other = swap(w_later)
    kv_here = lax.ppermute(kv_fwd, "section", next_section)

    dq, far, near, own = backward_attention(block_id, normed_back, upper_in, window_back)
    kv_here, near, far = lax.optimization_barrier((kv_here, near, far))
    near = lax.ppermute(near, "ctx", [(i, i - 1) for i in range(1, CTX)])
    far = lax.ppermute(far, "ctx", [(i, i - 2) for i in range(2, CTX)])
    up, down, gain_part = input_grad(
        block_id, own, near, far, w_mine, w_other, dq, x_back, upper_in, gains
    )
    next_grad = jnp.concatenate(land(set_out(up, down), -1), axis=0)
    gain_total = sum_over_ctx(gain_part)

    window_here = window(kv_here, core)
    x_here, _ = lax.optimization_barrier((x_here, up))
    next_in = forward_attention(block_id, norm_forward(x_here, gain_here), x_here, window_here)
    return (next_in[None], next_grad[None], gain_total)


def solution(mesh):
    in_specs = (
        P("section", "ctx", None),
        P("section", "ctx", None),
        P("section", "ctx", None),
        P("section", None),
        P("section", "ctx", None),
    )
    out_specs = (P("section", "ctx", None), P("section", "ctx", None), P("section", None))
    return jax.shard_map(body, mesh=mesh, in_specs=in_specs, out_specs=out_specs, check_vma=False)
```

time: 656 us -> 284 us (0.43)
  the two profiles are of different devices: /device:TPU:1 before, /device:TPU:112 now
where the time goes in v1:
time: 284 us; the launch traced here: 282 us
  starting transfers between devices  149 us (52%)
  waiting for transfers between devices  81.2 us (29%)
  Pallas kernels  21.2 us (7%)
  local copies, waits for them, and re-layouts  18.2 us (6%)
  other arithmetic  8.89 us (3%)
    ppermute x26, starting transfers between devices, over_ctx(): return lax.ppermute(value, 'ctx', ctx_pairs(move))  95.6 us
    ppermute x26, waiting for transfers between devices, over_ctx(): return lax.ppermute(value, 'ctx', ctx_pairs(move))  41.5 us
    ppermute x8, starting transfers between devices, over_grid(): return lax.ppermute(value, ('section', 'ctx'), grid_pairs(move))  39.7 us
    ppermute x8, waiting for transfers between devices, over_grid(): return lax.ppermute(value, ('section', 'ctx'), grid_pairs(move))  22.2 us
    dynamic_update_slice x9, local copies, waits for them, and re-layouts, place(): lax.dynamic_update_slice_in_dim(weight, piece, at % Y * block + offset, 0)  12.9 us
    ppermute x1, waiting for transfers between devices, body(): kv_here = lax.ppermute(kv_fwd, 'section', next_section)  12.5 us
    pallas_call x1, Pallas kernels, forward_attention(): pl.pallas_call(forward_kernel, grid=(KVH,), in_specs=[pl.BlockSpec(memory...  7.8 us
    pallas_call x1, Pallas kernels, backward_attention(): pl.pallas_call(backward_kernel, grid=(KVH,), in_specs=[pl.BlockSpec(memor...  7.56 us
  transfers between devices with their start and end apart: 38, of which 18 were waited for; matrix products, arithmetic and copies ran while one was open for 9% of the time, Pallas kernels for 7%

profile of v1, /device:TPU:112, one launch (start us, length us, event | category | flops | bytes accessed | tf_op | source)
XLA Modules:
  0.0 282.4 jit_solution(3148225841600383988)
XLA Ops:
  7.4 6.1 %collective-permute-start.3 = (bf16[128,512]{1,0:T(8,128)(2,1)S(1)}, bf16[128,512]{1,0:T(8,128)(2,1)S(1)}, u32[]{:S(2)}, u32[]{:S(2)}) collective-permute-start(bf16[128,512]{1,0:T(8,128)(2,1)S(1)} %pad_maximum_fusion.4), channel_id=1, source_target_pairs={{0,4},{1,5},{2,6},{3,7},{4,0},{5,1},{6,2},{7,3},{8,12},{9,13},{10,... | collective-permute-start | bytes 393224 | tf_op jit(solution)/shard_map/ppermute | solution.py:37
  13.5 4.8 %collective-permute-start.4 = (bf16[128,512]{1,0:T(8,128)(2,1)S(1)}, bf16[128,512]{1,0:T(8,128)(2,1)S(1)}, u32[]{:S(2)}, u32[]{:S(2)}) collective-permute-start(bf16[128,512]{1,0:T(8,128)(2,1)S(1)} %pad_maximum_fusion.4), channel_id=1, source_target_pairs={{0,2},{1,3},{2,4},{3,5},{4,6},{5,7},{6,0},{7,1},{8,10},{9,11},{10,... | collective-permute-start | bytes 393224 | tf_op jit(solution)/shard_map/ppermute | solution.py:37
  27.4 3.3 %collective-permute-start.6 = (bf16[512,512]{1,0:T(8,128)(2,1)S(1)}, bf16[512,512]{1,0:T(8,128)(2,1)S(1)}, u32[]{:S(2)}, u32[]{:S(2)}) collective-permute-start(bf16[512,512]{1,0:T(8,128)(2,1)S(1)} %get-tuple-element.46), channel_id=1, source_target_pairs={{0,56},{1,57},{2,58},{3,59},{4,60},{5,61},{6,62},{7,63},{8,0},{9,1... | collective-permute-start | bytes 1572872 | tf_op jit(solution)/shard_map/ppermute | solution.py:37
  34.8 5.8 %collective-permute-done.5 = bf16[512,512]{1,0:T(8,128)(2,1)S(1)} collective-permute-done((bf16[512,512]{1,0:T(8,128)(2,1)S(1)}, bf16[512,512]{1,0:T(8,128)(2,1)S(1)}, u32[]{:S(2)}, u32[]{:S(2)}) %collective-permute-start.5) | collective-permute-done | bytes 524320 | tf_op jit(solution)/shard_map/ppermute | solution.py:37
  43.2 3.3 %collective-permute-start.8 = (bf16[512,512]{1,0:T(8,128)(2,1)S(1)}, bf16[512,512]{1,0:T(8,128)(2,1)}, u32[]{:S(2)}, u32[]{:S(2)}) collective-permute-start(bf16[512,512]{1,0:T(8,128)(2,1)S(1)} %collective-permute-done.6), channel_id=1, source_target_pairs={{0,56},{1,57},{2,58},{3,59},{4,60},{5,61},{6,62},{7,63},{8,0},{9,1... | collective-permute-start | bytes 1572872 | tf_op jit(solution)/shard_map/ppermute | solution.py:37
  50.6 5.9 %collective-permute-start.12 = (bf16[64,4096]{1,0:T(8,128)(2,1)}, bf16[64,4096]{1,0:T(8,128)(2,1)}, u32[]{:S(2)}, u32[]{:S(2)}) collective-permute-start(bf16[64,4096]{1,0:T(8,128)(2,1)} %get-tuple-element.57), channel_id=1, source_target_pairs={{0,68},{1,69},{8,76},{9,77},{16,84},{17,85},{24,92},{25,93},{32,10... | collective-permute-start | bytes 1572872 | tf_op jit(solution)/shard_map/ppermute | solution.py:55
  59.1 3.3 %collective-permute-start.10 = (bf16[512,512]{1,0:T(8,128)(2,1)}, bf16[512,512]{1,0:T(8,128)(2,1)}, u32[]{:S(2)}, u32[]{:S(2)}) collective-permute-start(bf16[512,512]{1,0:T(8,128)(2,1)} %collective-permute-done.8), channel_id=1, source_target_pairs={{0,56},{1,57},{2,58},{3,59},{4,60},{5,61},{6,62},{7,63},{8,0},{9,1... | collective-permute-start | bytes 1572872 | tf_op jit(solution)/shard_map/ppermute | solution.py:37
  70.6 3.2 %collective-permute-done.10 = bf16[512,512]{1,0:T(8,128)(2,1)} collective-permute-done((bf16[512,512]{1,0:T(8,128)(2,1)}, bf16[512,512]{1,0:T(8,128)(2,1)}, u32[]{:S(2)}, u32[]{:S(2)}) %collective-permute-start.10) | collective-permute-done | bytes 524320 | tf_op jit(solution)/shard_map/ppermute | solution.py:37
  74.8 4.9 %collective-permute-start.13 = (bf16[256,512]{1,0:T(8,128)(2,1)S(1)}, bf16[256,512]{1,0:T(8,128)(2,1)S(1)}, u32[]{:S(2)}, u32[]{:S(2)}) collective-permute-start(bf16[256,512]{1,0:T(8,128)(2,1)S(1)} %slice.57), channel_id=1, source_target_pairs={{0,8},{1,9},{2,10},{3,11},{4,12},{5,13},{6,14},{7,15},{8,16},{9,17... | collective-permute-start | bytes 786440 | tf_op jit(solution)/shard_map/ppermute | solution.py:37
  84.5 12.2 %collective-permute-start.15 = (bf16[64,4096]{1,0:T(8,128)(2,1)}, bf16[64,4096]{1,0:T(8,128)(2,1)S(1)}, u32[]{:S(2)}, u32[]{:S(2)}) collective-permute-start(bf16[64,4096]{1,0:T(8,128)(2,1)} %collective-permute-done.11), channel_id=1, source_target_pairs={{0,132},{1,133},{8,140},{9,141},{16,148},{17,149},{24,156},{25,157... | collective-permute-start | bytes 1572872 | tf_op jit(solution)/shard_map/ppermute | solution.py:55
  108.0 4.1 %collective-permute-done.15 = bf16[64,4096]{1,0:T(8,128)(2,1)S(1)} collective-permute-done((bf16[64,4096]{1,0:T(8,128)(2,1)}, bf16[64,4096]{1,0:T(8,128)(2,1)S(1)}, u32[]{:S(2)}, u32[]{:S(2)}) %collective-permute-start.15) | collective-permute-done | bytes 524320 | tf_op jit(solution)/shard_map/ppermute | solution.py:55
  112.1 5.0 %collective-permute-done.16 = bf16[64,4096]{1,0:T(8,128)(2,1)S(1)} collective-permute-done((bf16[64,4096]{1,0:T(8,128)(2,1)}, bf16[64,4096]{1,0:T(8,128)(2,1)S(1)}, u32[]{:S(2)}, u32[]{:S(2)}) %collective-permute-start.16) | collective-permute-done | bytes 524320 | tf_op jit(solution)/shard_map/ppermute | solution.py:55
  117.1 10.2 %collective-permute-start.17 = (bf16[256,512]{1,0:T(8,128)(2,1)S(1)}, bf16[256,512]{1,0:T(8,128)(2,1)S(1)}, u32[]{:S(2)}, u32[]{:S(2)}) collective-permute-start(bf16[256,512]{1,0:T(8,128)(2,1)S(1)} %fusion.20), channel_id=1, source_target_pairs={{0,2},{1,3},{2,4},{3,5},{4,6},{5,7},{6,8},{7,9},{8,10},{9,11},{10,... | collective-permute-start | bytes 786440 | tf_op jit(solution)/shard_map/ppermute | solution.py:37
  134.0 4.6 %collective-permute-done.18 = bf16[256,512]{1,0:T(8,128)(2,1)S(1)} collective-permute-done((bf16[256,512]{1,0:T(8,128)(2,1)S(1)}, bf16[256,512]{1,0:T(8,128)(2,1)S(1)}, u32[]{:S(2)}, u32[]{:S(2)}) %collective-permute-start.18) | collective-permute-done | bytes 262176 | tf_op jit(solution)/shard_map/ppermute | solution.py:37
  143.2 7.6 %backward_attention.1 = (f32[128,4096]{1,0:T(8,128)S(1)}, bf16[128,1024]{1,0:T(8,128)(2,1)S(1)}, bf16[128,1024]{1,0:T(8,128)(2,1)S(1)}, f32[128,1024]{1,0:T(8,128)S(1)}) custom-call(s32[1]{0:T(128)} %bitcast.block_ref, bf16[128,4096]{1,0:T(8,128)(2,1)S(1)} %get-tuple-element.70.normed_ref, bf16[128,4096]{1,0:T(8,128)(2,1)S(1)} %bitcast.17, ...), custom_call_target="tpu_custom_call" | custom-call | flops 4000000000 | bytes 8388608 | tf_op jit(solution)/shard_map/backward_attention/pallas_call | solution.py:281
  150.7 12.5 %collective-permute-done.20 = bf16[256,512]{1,0:T(8,128)(2,1)S(1)} collective-permute-done((bf16[256,512]{1,0:T(8,128)(2,1)S(1)}, bf16[256,512]{1,0:T(8,128)(2,1)S(1)}, u32[]{:S(2)}, u32[]{:S(2)}) %collective-permute-start.20) | collective-permute-done | bytes 262176 | tf_op jit(solution)/shard_map/ppermute | solution.py:443
  163.2 4.3 %collective-permute-start.25 = (bf16[256,512]{1,0:T(8,128)(2,1)S(1)}, bf16[256,512]{1,0:T(8,128)(2,1)S(1)}, u32[]{:S(2)}, u32[]{:S(2)}) collective-permute-start(bf16[256,512]{1,0:T(8,128)(2,1)S(1)} %collective-permute-done.20), channel_id=1, source_target_pairs={{0,2},{1,3},{2,4},{3,5},{4,6},{5,7},{6,8},{7,9},{8,10},{9,11},{10,... | collective-permute-start | bytes 786440 | tf_op jit(solution)/shard_map/ppermute | solution.py:37
  171.6 3.5 %collective-permute-start.21 = (bf16[128,1024]{1,0:T(8,128)(2,1)S(1)}, bf16[128,1024]{1,0:T(8,128)(2,1)S(1)}, u32[]{:S(2)}, u32[]{:S(2)}) collective-permute-start(bf16[128,1024]{1,0:T(8,128)(2,1)S(1)} %get-tuple-element.36), channel_id=1, source_target_pairs={{1,0},{2,1},{3,2},{4,3},{5,4},{6,5},{7,6},{8,7},{9,8},{10,9},{11,1... | collective-permute-start | bytes 786440 | tf_op jit(solution)/shard_map/ppermute | solution.py:447
  175.1 4.2 %collective-permute-start.22 = (bf16[128,1024]{1,0:T(8,128)(2,1)S(1)}, bf16[128,1024]{1,0:T(8,128)(2,1)S(1)}, u32[]{:S(2)}, u32[]{:S(2)}) collective-permute-start(bf16[128,1024]{1,0:T(8,128)(2,1)S(1)} %get-tuple-element.37), channel_id=1, source_target_pairs={{2,0},{3,1},{4,2},{5,3},{6,4},{7,5},{8,6},{9,7},{10,8},{11,9},{12,... | collective-permute-start | bytes 786440 | tf_op jit(solution)/shard_map/ppermute | solution.py:448
  179.4 3.5 %collective-permute-start.24 = (f32[1,4096]{1,0:T(1,128)S(1)}, f32[1,4096]{1,0:T(1,128)S(1)}, u32[]{:S(2)}, u32[]{:S(2)}) collective-permute-start(f32[1,4096]{1,0:T(1,128)S(1)} %copy-done.4), channel_id=1, source_target_pairs={{0,64},{64,128},{128,192},{192,256},{256,320},{320,384},{384,448},... | collective-permute-start | bytes 49160 | tf_op jit(solution)/shard_map/ppermute | solution.py:427
  183.7 4.4 %collective-permute-done.22.far_ref = bf16[128,1024]{1,0:T(8,128)(2,1)S(1)} collective-permute-done((bf16[128,1024]{1,0:T(8,128)(2,1)S(1)}, bf16[128,1024]{1,0:T(8,128)(2,1)S(1)}, u32[]{:S(2)}, u32[]{:S(2)}) %collective-permute-start.22) | collective-permute-done | bytes 262176 | tf_op jit(solution)/shard_map/ppermute | solution.py:448
  188.1 5.8 %input_grad.1 = (bf16[64,4096]{1,0:T(8,128)(2,1)S(1)}, bf16[64,4096]{1,0:T(8,128)(2,1)S(1)}, f32[1,4096]{1,0:T(1,128)S(1)}) custom-call(s32[1]{0:T(128)} %bitcast.block_ref, f32[128,1024]{1,0:T(8,128)S(1)} %get-tuple-element.32.own_ref, bf16[128,1024]{1,0:T(8,128)(2,1)S(1)} %collective-permute-done.21.near_ref, ...), custom_call_target="tpu_custom_call" | custom-call | flops 2000000000 | bytes 16777216 | tf_op jit(solution)/shard_map/input_grad/pallas_call | solution.py:365
  198.6 4.1 %collective-permute-start.28 = (bf16[64,4096]{1,0:T(8,128)(2,1)S(1)}, bf16[64,4096]{1,0:T(8,128)(2,1)S(1)}, u32[]{:S(2)}, u32[]{:S(2)}) collective-permute-start(bf16[64,4096]{1,0:T(8,128)(2,1)S(1)} %get-tuple-element.40), channel_id=1, source_target_pairs={{0,4},{1,5},{8,12},{9,13},{16,20},{17,21},{24,28},{25,29},{32,36},... | collective-permute-start | bytes 1572872 | tf_op jit(solution)/shard_map/ppermute | solution.py:55
  202.7 3.4 %collective-permute-start.33 = (f32[1,4096]{1,0:T(1,128)S(1)}, f32[1,4096]{1,0:T(1,128)S(1)}, u32[]{:S(2)}, u32[]{:S(2)}) collective-permute-start(f32[1,4096]{1,0:T(1,128)S(1)} %add.173), channel_id=1, source_target_pairs={{0,2},{1,3},{2,0},{3,1},{4,6},{5,7},{6,4},{7,5},{8,10},{9,11},{10,... | collective-permute-start | bytes 49160 | tf_op jit(solution)/shard_map/ppermute | solution.py:37
  206.2 15.8 %collective-permute-done.33 = f32[1,4096]{1,0:T(1,128)S(1)} collective-permute-done((f32[1,4096]{1,0:T(1,128)S(1)}, f32[1,4096]{1,0:T(1,128)S(1)}, u32[]{:S(2)}, u32[]{:S(2)}) %collective-permute-start.33) | collective-permute-done | bytes 16416 | tf_op jit(solution)/shard_map/ppermute | solution.py:37
  222.1 9.0 %collective-permute-start.34 = (f32[1,4096]{1,0:T(1,128)S(1)}, f32[1,4096]{1,0:T(1,128)S(1)}, u32[]{:S(2)}, u32[]{:S(2)}) collective-permute-start(f32[1,4096]{1,0:T(1,128)S(1)} %add.174), channel_id=1, source_target_pairs={{0,4},{1,5},{2,6},{3,7},{4,0},{5,1},{6,2},{7,3},{8,12},{9,13},{10,... | collective-permute-start | bytes 49160 | tf_op jit(solution)/shard_map/ppermute | solution.py:37
  232.8 4.8 %collective-permute-start.35 = (f32[1,4096]{1,0:T(1,128)S(1)}, f32[1,4096]{1,0:T(1,128)S(1)}, u32[]{:S(2)}, u32[]{:S(2)}) collective-permute-start(f32[1,4096]{1,0:T(1,128)S(1)} %add.175), channel_id=1, source_target_pairs={{0,8},{1,9},{2,10},{3,11},{4,12},{5,13},{6,14},{7,15},{8,0},{9,1},... | collective-permute-start | bytes 49160 | tf_op jit(solution)/shard_map/ppermute | solution.py:37
  239.4 9.2 %collective-permute-start.36 = (f32[1,4096]{1,0:T(1,128)S(1)}, f32[1,4096]{1,0:T(1,128)S(1)}, u32[]{:S(2)}, u32[]{:S(2)}) collective-permute-start(f32[1,4096]{1,0:T(1,128)S(1)} %add.176), channel_id=1, source_target_pairs={{0,16},{1,17},{2,18},{3,19},{4,20},{5,21},{6,22},{7,23},{8,24},{9,... | collective-permute-start | bytes 49160 | tf_op jit(solution)/shard_map/ppermute | solution.py:37
  248.6 8.0 %collective-permute-start.31 = (bf16[64,4096]{1,0:T(8,128)(2,1)S(1)}, bf16[64,4096]{1,0:T(8,128)(2,1)S(1)}, u32[]{:S(2)}, u32[]{:S(2)}) collective-permute-start(bf16[64,4096]{1,0:T(8,128)(2,1)S(1)} %collective-permute-done.30), channel_id=1, source_target_pairs={{0,452},{1,453},{8,460},{9,461},{16,468},{17,469},{24,476},{25,477... | collective-permute-start | bytes 1572872 | tf_op jit(solution)/shard_map/ppermute | solution.py:55
  260.9 7.8 %forward_attention.1 = bf16[128,4096]{1,0:T(8,128)(2,1)} custom-call(s32[1]{0:T(128)} %bitcast.block_ref, bf16[128,4096]{1,0:T(8,128)(2,1)S(1)} %fusion.8.normed_ref, bf16[128,4096]{1,0:T(8,128)(2,1)S(1)} %pad_maximum_fusion.1.x_ref, bf16[512,1024]{1,0:T(8,128)(2,1)S(1)} %pad_maximum_fusion.3.kv_ref), custom_call_target="tpu_custom_call" | custom-call | flops 1600000000 | bytes 4194304 | tf_op jit(solution)/shard_map/forward_attention/pallas_call | solution.py:219
  269.3 4.6 %collective-permute-done.31 = bf16[64,4096]{1,0:T(8,128)(2,1)S(1)} collective-permute-done((bf16[64,4096]{1,0:T(8,128)(2,1)S(1)}, bf16[64,4096]{1,0:T(8,128)(2,1)S(1)}, u32[]{:S(2)}, u32[]{:S(2)}) %collective-permute-start.31) | collective-permute-done | bytes 524320 | tf_op jit(solution)/shard_map/ppermute | solution.py:55
  273.9 7.4 %collective-permute-done.29 = bf16[64,4096]{1,0:T(8,128)(2,1)S(1)} collective-permute-done((bf16[64,4096]{1,0:T(8,128)(2,1)S(1)}, bf16[64,4096]{1,0:T(8,128)(2,1)S(1)}, u32[]{:S(2)}, u32[]{:S(2)}) %collective-permute-start.29) | collective-permute-done | bytes 524320 | tf_op jit(solution)/shard_map/ppermute | solution.py:55
  (119 shorter events, 84.2 us)
Async XLA Ops:
  5.4 12.9 %collective-permute-start.2 = (bf16[128,512]{1,0:T(8,128)(2,1)S(1)}, bf16[128,512]{1,0:T(8,128)(2,1)S(1)}, u32[]{:S(2)}, u32[]{:S(2)}) collective-permute-start(bf16[128,512]{1,0:T(8,128)(2,1)S(1)} %pad_maximum_fusion.4), channel_id=1, source_target_pairs={{0,6},{1,7},{2,0},{3,1},{4,2},{5,3},{6,4},{7,5},{8,14},{9,15},{10,... | collective-permute-start | bytes 393224 | tf_op jit(solution)/shard_map/ppermute | solution.py:37
  7.4 14.2 %collective-permute-start.3 = (bf16[128,512]{1,0:T(8,128)(2,1)S(1)}, bf16[128,512]{1,0:T(8,128)(2,1)S(1)}, u32[]{:S(2)}, u32[]{:S(2)}) collective-permute-start(bf16[128,512]{1,0:T(8,128)(2,1)S(1)} %pad_maximum_fusion.4), channel_id=1, source_target_pairs={{0,4},{1,5},{2,6},{3,7},{4,0},{5,1},{6,2},{7,3},{8,12},{9,13},{10,... | collective-permute-start | bytes 393224 | tf_op jit(solution)/shard_map/ppermute | solution.py:37
  13.5 10.8 %collective-permute-start.4 = (bf16[128,512]{1,0:T(8,128)(2,1)S(1)}, bf16[128,512]{1,0:T(8,128)(2,1)S(1)}, u32[]{:S(2)}, u32[]{:S(2)}) collective-permute-start(bf16[128,512]{1,0:T(8,128)(2,1)S(1)} %pad_maximum_fusion.4), channel_id=1, source_target_pairs={{0,2},{1,3},{2,4},{3,5},{4,6},{5,7},{6,0},{7,1},{8,10},{9,11},{10,... | collective-permute-start | bytes 393224 | tf_op jit(solution)/shard_map/ppermute | solution.py:37
  24.8 15.8 %collective-permute-start.5 = (bf16[512,512]{1,0:T(8,128)(2,1)S(1)}, bf16[512,512]{1,0:T(8,128)(2,1)S(1)}, u32[]{:S(2)}, u32[]{:S(2)}) collective-permute-start(bf16[512,512]{1,0:T(8,128)(2,1)S(1)} %get-tuple-element.46), channel_id=1, source_target_pairs={{0,8},{1,9},{2,10},{3,11},{4,12},{5,13},{6,14},{7,15},{8,16},{9,17... | collective-permute-start | bytes 1572872 | tf_op jit(solution)/shard_map/ppermute | solution.py:37
  27.4 15.8 %collective-permute-start.6 = (bf16[512,512]{1,0:T(8,128)(2,1)S(1)}, bf16[512,512]{1,0:T(8,128)(2,1)S(1)}, u32[]{:S(2)}, u32[]{:S(2)}) collective-permute-start(bf16[512,512]{1,0:T(8,128)(2,1)S(1)} %get-tuple-element.46), channel_id=1, source_target_pairs={{0,56},{1,57},{2,58},{3,59},{4,60},{5,61},{6,62},{7,63},{8,0},{9,1... | collective-permute-start | bytes 1572872 | tf_op jit(solution)/shard_map/ppermute | solution.py:37
  32.9 71.0 %collective-permute-start = (bf16[256,4096]{1,0:T(8,128)(2,1)}, bf16[256,4096]{1,0:T(8,128)(2,1)}, u32[]{:S(2)}, u32[]{:S(2)}) collective-permute-start(bf16[256,4096]{1,0:T(8,128)(2,1)} %pad_maximum_fusion), channel_id=1, source_target_pairs={{0,1},{1,0},{2,3},{3,2},{4,5},{5,4},{6,7},{7,6},{8,9},{9,8},{10,11... | collective-permute-start | bytes 6291464 | tf_op jit(solution)/shard_map/ppermute | solution.py:37
  40.6 15.8 %collective-permute-start.7 = (bf16[512,512]{1,0:T(8,128)(2,1)S(1)}, bf16[512,512]{1,0:T(8,128)(2,1)}, u32[]{:S(2)}, u32[]{:S(2)}) collective-permute-start(bf16[512,512]{1,0:T(8,128)(2,1)S(1)} %collective-permute-done.5), channel_id=1, source_target_pairs={{0,8},{1,9},{2,10},{3,11},{4,12},{5,13},{6,14},{7,15},{8,16},{9,17... | collective-permute-start | bytes 1572872 | tf_op jit(solution)/shard_map/ppermute | solution.py:37
  43.2 15.9 %collective-permute-start.8 = (bf16[512,512]{1,0:T(8,128)(2,1)S(1)}, bf16[512,512]{1,0:T(8,128)(2,1)}, u32[]{:S(2)}, u32[]{:S(2)}) collective-permute-start(bf16[512,512]{1,0:T(8,128)(2,1)S(1)} %collective-permute-done.6), channel_id=1, source_target_pairs={{0,56},{1,57},{2,58},{3,59},{4,60},{5,61},{6,62},{7,63},{8,0},{9,1... | collective-permute-start | bytes 1572872 | tf_op jit(solution)/shard_map/ppermute | solution.py:37
  47.5 20.6 %collective-permute-start.11 = (bf16[64,4096]{1,0:T(8,128)(2,1)}, bf16[64,4096]{1,0:T(8,128)(2,1)}, u32[]{:S(2)}, u32[]{:S(2)}) collective-permute-start(bf16[64,4096]{1,0:T(8,128)(2,1)} %get-tuple-element.58), channel_id=1, source_target_pairs={{0,4},{1,5},{8,12},{9,13},{16,20},{17,21},{24,28},{25,29},{32,36},... | collective-permute-start | bytes 1572872 | tf_op jit(solution)/shard_map/ppermute | solution.py:55
  50.6 18.6 %collective-permute-start.12 = (bf16[64,4096]{1,0:T(8,128)(2,1)}, bf16[64,4096]{1,0:T(8,128)(2,1)}, u32[]{:S(2)}, u32[]{:S(2)}) collective-permute-start(bf16[64,4096]{1,0:T(8,128)(2,1)} %get-tuple-element.57), channel_id=1, source_target_pairs={{0,68},{1,69},{8,76},{9,77},{16,84},{17,85},{24,92},{25,93},{32,10... | collective-permute-start | bytes 1572872 | tf_op jit(solution)/shard_map/ppermute | solution.py:55
  56.5 14.2 %collective-permute-start.9 = (bf16[512,512]{1,0:T(8,128)(2,1)}, bf16[512,512]{1,0:T(8,128)(2,1)}, u32[]{:S(2)}, u32[]{:S(2)}) collective-permute-start(bf16[512,512]{1,0:T(8,128)(2,1)} %collective-permute-done.7), channel_id=1, source_target_pairs={{0,8},{1,9},{2,10},{3,11},{4,12},{5,13},{6,14},{7,15},{8,16},{9,17... | collective-permute-start | bytes 1572872 | tf_op jit(solution)/shard_map/ppermute | solution.py:37
  59.1 14.8 %collective-permute-start.10 = (bf16[512,512]{1,0:T(8,128)(2,1)}, bf16[512,512]{1,0:T(8,128)(2,1)}, u32[]{:S(2)}, u32[]{:S(2)}) collective-permute-start(bf16[512,512]{1,0:T(8,128)(2,1)} %collective-permute-done.8), channel_id=1, source_target_pairs={{0,56},{1,57},{2,58},{3,59},{4,60},{5,61},{6,62},{7,63},{8,0},{9,1... | collective-permute-start | bytes 1572872 | tf_op jit(solution)/shard_map/ppermute | solution.py:37
  74.8 27.6 %collective-permute-start.13 = (bf16[256,512]{1,0:T(8,128)(2,1)S(1)}, bf16[256,512]{1,0:T(8,128)(2,1)S(1)}, u32[]{:S(2)}, u32[]{:S(2)}) collective-permute-start(bf16[256,512]{1,0:T(8,128)(2,1)S(1)} %slice.57), channel_id=1, source_target_pairs={{0,8},{1,9},{2,10},{3,11},{4,12},{5,13},{6,14},{7,15},{8,16},{9,17... | collective-permute-start | bytes 786440 | tf_op jit(solution)/shard_map/ppermute | solution.py:37
  82.6 20.6 %collective-permute-start.14 = (bf16[256,512]{1,0:T(8,128)(2,1)S(1)}, bf16[256,512]{1,0:T(8,128)(2,1)S(1)}, u32[]{:S(2)}, u32[]{:S(2)}) collective-permute-start(bf16[256,512]{1,0:T(8,128)(2,1)S(1)} %slice.58), channel_id=1, source_target_pairs={{0,56},{1,57},{2,58},{3,59},{4,60},{5,61},{6,62},{7,63},{8,0},{9,1... | collective-permute-start | bytes 786440 | tf_op jit(solution)/shard_map/ppermute | solution.py:37
  84.5 27.6 %collective-permute-start.15 = (bf16[64,4096]{1,0:T(8,128)(2,1)}, bf16[64,4096]{1,0:T(8,128)(2,1)S(1)}, u32[]{:S(2)}, u32[]{:S(2)}) collective-permute-start(bf16[64,4096]{1,0:T(8,128)(2,1)} %collective-permute-done.11), channel_id=1, source_target_pairs={{0,132},{1,133},{8,140},{9,141},{16,148},{17,149},{24,156},{25,157... | collective-permute-start | bytes 1572872 | tf_op jit(solution)/shard_map/ppermute | solution.py:55
  96.7 20.4 %collective-permute-start.16 = (bf16[64,4096]{1,0:T(8,128)(2,1)}, bf16[64,4096]{1,0:T(8,128)(2,1)S(1)}, u32[]{:S(2)}, u32[]{:S(2)}) collective-permute-start(bf16[64,4096]{1,0:T(8,128)(2,1)} %collective-permute-done.12), channel_id=1, source_target_pairs={{0,68},{1,69},{8,76},{9,77},{16,84},{17,85},{24,92},{25,93},{32,10... | collective-permute-start | bytes 1572872 | tf_op jit(solution)/shard_map/ppermute | solution.py:55
  117.1 16.8 %collective-permute-start.17 = (bf16[256,512]{1,0:T(8,128)(2,1)S(1)}, bf16[256,512]{1,0:T(8,128)(2,1)S(1)}, u32[]{:S(2)}, u32[]{:S(2)}) collective-permute-start(bf16[256,512]{1,0:T(8,128)(2,1)S(1)} %fusion.20), channel_id=1, source_target_pairs={{0,2},{1,3},{2,4},{3,5},{4,6},{5,7},{6,8},{7,9},{8,10},{9,11},{10,... | collective-permute-start | bytes 786440 | tf_op jit(solution)/shard_map/ppermute | solution.py:37
  127.3 11.3 %collective-permute-start.18 = (bf16[256,512]{1,0:T(8,128)(2,1)S(1)}, bf16[256,512]{1,0:T(8,128)(2,1)S(1)}, u32[]{:S(2)}, u32[]{:S(2)}) collective-permute-start(bf16[256,512]{1,0:T(8,128)(2,1)S(1)} %fusion.20), channel_id=1, source_target_pairs={{0,3},{1,2},{2,5},{3,4},{4,7},{5,6},{6,9},{7,8},{8,11},{9,10},{10,... | collective-permute-start | bytes 786440 | tf_op jit(solution)/shard_map/ppermute | solution.py:37
  138.9 49.2 %collective-permute-start.23 = (bf16[4096,512]{1,0:T(8,128)(2,1)S(1)}, bf16[4096,512]{1,0:T(8,128)(2,1)S(1)}, u32[]{:S(2)}, u32[]{:S(2)}) collective-permute-start(bf16[4096,512]{1,0:T(8,128)(2,1)S(1)} %copy-done.1), channel_id=1, source_target_pairs={{0,1},{1,0},{2,3},{3,2},{4,5},{5,4},{6,7},{7,6},{8,9},{9,8},{10,11... | collective-permute-start | bytes 12582920 | tf_op jit(solution)/shard_map/ppermute | solution.py:37
  141.0 22.2 %collective-permute-start.20 = (bf16[256,512]{1,0:T(8,128)(2,1)S(1)}, bf16[256,512]{1,0:T(8,128)(2,1)S(1)}, u32[]{:S(2)}, u32[]{:S(2)}) collective-permute-start(bf16[256,512]{1,0:T(8,128)(2,1)S(1)} %fusion.17), channel_id=1, source_target_pairs={{0,64},{64,128},{128,192},{192,256},{256,320},{320,384},{384,448},... | collective-permute-start | bytes 786440 | tf_op jit(solution)/shard_map/ppermute | solution.py:443
  163.2 11.9 %collective-permute-start.25 = (bf16[256,512]{1,0:T(8,128)(2,1)S(1)}, bf16[256,512]{1,0:T(8,128)(2,1)S(1)}, u32[]{:S(2)}, u32[]{:S(2)}) collective-permute-start(bf16[256,512]{1,0:T(8,128)(2,1)S(1)} %collective-permute-done.20), channel_id=1, source_target_pairs={{0,2},{1,3},{2,4},{3,5},{4,6},{5,7},{6,8},{7,9},{8,10},{9,11},{10,... | collective-permute-start | bytes 786440 | tf_op jit(solution)/shard_map/ppermute | solution.py:37
  167.5 11.9 %collective-permute-start.26 = (bf16[256,512]{1,0:T(8,128)(2,1)S(1)}, bf16[256,512]{1,0:T(8,128)(2,1)S(1)}, u32[]{:S(2)}, u32[]{:S(2)}) collective-permute-start(bf16[256,512]{1,0:T(8,128)(2,1)S(1)} %collective-permute-done.20), channel_id=1, source_target_pairs={{0,3},{1,2},{2,5},{3,4},{4,7},{5,6},{6,9},{7,8},{8,11},{9,10},{10,... | collective-permute-start | bytes 786440 | tf_op jit(solution)/shard_map/ppermute | solution.py:37
  169.5 13.5 %collective-permute-start.27 = (bf16[256,512]{1,0:T(8,128)(2,1)S(1)}, bf16[256,512]{1,0:T(8,128)(2,1)S(1)}, u32[]{:S(2)}, u32[]{:S(2)}) collective-permute-start(bf16[256,512]{1,0:T(8,128)(2,1)S(1)} %collective-permute-done.20), channel_id=1, source_target_pairs={{0,1},{1,0},{2,3},{3,2},{4,5},{5,4},{6,7},{7,6},{8,9},{9,8},{10,11... | collective-permute-start | bytes 786440 | tf_op jit(solution)/shard_map/ppermute | solution.py:37
  171.6 12.1 %collective-permute-start.21 = (bf16[128,1024]{1,0:T(8,128)(2,1)S(1)}, bf16[128,1024]{1,0:T(8,128)(2,1)S(1)}, u32[]{:S(2)}, u32[]{:S(2)}) collective-permute-start(bf16[128,1024]{1,0:T(8,128)(2,1)S(1)} %get-tuple-element.36), channel_id=1, source_target_pairs={{1,0},{2,1},{3,2},{4,3},{5,4},{6,5},{7,6},{8,7},{9,8},{10,9},{11,1... | collective-permute-start | bytes 786440 | tf_op jit(solution)/shard_map/ppermute | solution.py:447
  175.1 12.9 %collective-permute-start.22 = (bf16[128,1024]{1,0:T(8,128)(2,1)S(1)}, bf16[128,1024]{1,0:T(8,128)(2,1)S(1)}, u32[]{:S(2)}, u32[]{:S(2)}) collective-permute-start(bf16[128,1024]{1,0:T(8,128)(2,1)S(1)} %get-tuple-element.37), channel_id=1, source_target_pairs={{2,0},{3,1},{4,2},{5,3},{6,4},{7,5},{8,6},{9,7},{10,8},{11,9},{12,... | collective-permute-start | bytes 786440 | tf_op jit(solution)/shard_map/ppermute | solution.py:448
  179.4 79.2 %collective-permute-start.24 = (f32[1,4096]{1,0:T(1,128)S(1)}, f32[1,4096]{1,0:T(1,128)S(1)}, u32[]{:S(2)}, u32[]{:S(2)}) collective-permute-start(f32[1,4096]{1,0:T(1,128)S(1)} %copy-done.4), channel_id=1, source_target_pairs={{0,64},{64,128},{128,192},{192,256},{256,320},{320,384},{384,448},... | collective-permute-start | bytes 49160 | tf_op jit(solution)/shard_map/ppermute | solution.py:427
  195.9 52.7 %collective-permute-start.30 = (bf16[64,4096]{1,0:T(8,128)(2,1)S(1)}, bf16[64,4096]{1,0:T(8,128)(2,1)S(1)}, u32[]{:S(2)}, u32[]{:S(2)}) collective-permute-start(bf16[64,4096]{1,0:T(8,128)(2,1)S(1)} %get-tuple-element.43), channel_id=1, source_target_pairs={{0,68},{1,69},{8,76},{9,77},{16,84},{17,85},{24,92},{25,93},{32,10... | collective-permute-start | bytes 1572872 | tf_op jit(solution)/shard_map/ppermute | solution.py:55
  198.6 58.1 %collective-permute-start.28 = (bf16[64,4096]{1,0:T(8,128)(2,1)S(1)}, bf16[64,4096]{1,0:T(8,128)(2,1)S(1)}, u32[]{:S(2)}, u32[]{:S(2)}) collective-permute-start(bf16[64,4096]{1,0:T(8,128)(2,1)S(1)} %get-tuple-element.40), channel_id=1, source_target_pairs={{0,4},{1,5},{8,12},{9,13},{16,20},{17,21},{24,28},{25,29},{32,36},... | collective-permute-start | bytes 1572872 | tf_op jit(solution)/shard_map/ppermute | solution.py:55
  202.7 19.4 %collective-permute-start.33 = (f32[1,4096]{1,0:T(1,128)S(1)}, f32[1,4096]{1,0:T(1,128)S(1)}, u32[]{:S(2)}, u32[]{:S(2)}) collective-permute-start(f32[1,4096]{1,0:T(1,128)S(1)} %add.173), channel_id=1, source_target_pairs={{0,2},{1,3},{2,0},{3,1},{4,6},{5,7},{6,4},{7,5},{8,10},{9,11},{10,... | collective-permute-start | bytes 49160 | tf_op jit(solution)/shard_map/ppermute | solution.py:37
  239.4 19.6 %collective-permute-start.36 = (f32[1,4096]{1,0:T(1,128)S(1)}, f32[1,4096]{1,0:T(1,128)S(1)}, u32[]{:S(2)}, u32[]{:S(2)}) collective-permute-start(f32[1,4096]{1,0:T(1,128)S(1)} %add.176), channel_id=1, source_target_pairs={{0,16},{1,17},{2,18},{3,19},{4,20},{5,21},{6,22},{7,23},{8,24},{9,... | collective-permute-start | bytes 49160 | tf_op jit(solution)/shard_map/ppermute | solution.py:37
  248.6 25.3 %collective-permute-start.31 = (bf16[64,4096]{1,0:T(8,128)(2,1)S(1)}, bf16[64,4096]{1,0:T(8,128)(2,1)S(1)}, u32[]{:S(2)}, u32[]{:S(2)}) collective-permute-start(bf16[64,4096]{1,0:T(8,128)(2,1)S(1)} %collective-permute-done.30), channel_id=1, source_target_pairs={{0,452},{1,453},{8,460},{9,461},{16,468},{17,469},{24,476},{25,477... | collective-permute-start | bytes 1572872 | tf_op jit(solution)/shard_map/ppermute | solution.py:55
  256.7 24.7 %collective-permute-start.29 = (bf16[64,4096]{1,0:T(8,128)(2,1)S(1)}, bf16[64,4096]{1,0:T(8,128)(2,1)S(1)}, u32[]{:S(2)}, u32[]{:S(2)}) collective-permute-start(bf16[64,4096]{1,0:T(8,128)(2,1)S(1)} %collective-permute-done.28), channel_id=1, source_target_pairs={{0,4},{1,5},{8,12},{9,13},{16,20},{17,21},{24,28},{25,29},{32,36},... | collective-permute-start | bytes 1572872 | tf_op jit(solution)/shard_map/ppermute | solution.py:55
  (14 other events, 98.7 us)

commit v2 on v0

v2 whole, which is shorter than its diff:
```python
import functools

import jax
import jax.numpy as jnp
from jax import lax
from jax.experimental import pallas as pl
from jax.experimental.pallas import tpu as pltpu
from jax.sharding import PartitionSpec as P

HD = 128
STEPS = 2
EPSILON = 1e-05
GROUP = 8
KVH = 4
TOK = 128
SPAN = (STEPS + 1) * TOK

X, Z_HI, Y, Z_LO, CORES = 4, 2, 8, 4, 2
Z = Z_HI * Z_LO
CHIPS = Y * Z_LO
CTX = Y * Z_LO * CORES

HEADS = KVH // CORES
CHIP_TOK = CORES * TOK
HALF = HEADS * GROUP * HD

SCALE = HD ** (-0.5)
LOG2E = 1.4426950408889634


def ctx_pairs(move):
    pairs = []
    for c in range(CTX):
        target = move(c // (Z_LO * CORES), (c // CORES) % Z_LO, c % CORES)
        if target is not None:
            y, z_lo, core = target
            pairs.append((c, (y * Z_LO + z_lo) * CORES + core))
    return pairs


def over_ctx(value, move):
    return lax.ppermute(value, "ctx", ctx_pairs(move))


def grid_pairs(move):
    pairs = []
    for x in range(X):
        for z in range(Z):
            new_x, new_z = move(x, z)
            new_x, new_z = (new_x % X, new_z % Z)
            for y in range(Y):
                for core in range(CORES):
                    source = (x * Z_HI + z // Z_LO) * CTX + (y * Z_LO + z % Z_LO) * CORES + core
                    target = (new_x * Z_HI + new_z // Z_LO) * CTX + (y * Z_LO + new_z % Z_LO) * CORES + core
                    pairs.append((source, target))
    return pairs


def over_grid(value, move):
    return lax.ppermute(value, ("section", "ctx"), grid_pairs(move))


def halfway(value, way):
    return over_grid(value, lambda x, z: (x, z + 2 * way))


def arrive(value, way, distance):
    def move(x, z):
        z_hi = ((z - 2 * way) % Z) // Z_LO
        cross = (1 if z_hi == Z_HI - 1 else 0) if distance == 1 else (-1 if z_hi == 0 else 0)
        return (x + cross, z + 2 * way)

    return over_grid(value, move)


def set_out(upper, lower):
    return halfway(upper, 1), halfway(lower, -1)


def land(halves, distance):
    return arrive(halves[0], 1, distance), arrive(halves[1], -1, distance)


def norm_forward(section_x, gain_row):
    values = section_x.astype(jnp.float32)
    inv_rms = lax.rsqrt(jnp.mean(values * values, axis=-1, keepdims=True) + EPSILON)
    return (values * inv_rms * gain_row).astype(jnp.bfloat16)


def by_head(kv_columns):
    parts = []
    for head in range(KVH):
        parts.append(kv_columns[:, head * HD : (head + 1) * HD])
        parts.append(kv_columns[:, (KVH + head) * HD : (KVH + head + 1) * HD])
    return jnp.concatenate(parts, axis=1)


def gather_weight(own_rows, core):
    half = own_rows.shape[1] // 2
    columns = by_head(own_rows)
    low, high = columns[:, :half], columns[:, half:]
    keep = jnp.where(core == 0, low, high)
    received = swap(jnp.where(core == 0, high, low))
    chip = chip_rows(keep, received, core)
    same_core = [[chip * CORES + c for chip in range(Y * Z_LO)] for c in range(CORES)]
    return lax.all_gather(chip, "ctx", axis_index_groups=same_core, axis=0, tiled=True)


def swap(value):
    return over_ctx(value, lambda y, z, c: (y, z, 1 - c))


def chip_rows(own, partner, core):
    return jnp.concatenate(
        [jnp.where(core == 0, own, partner), jnp.where(core == 0, partner, own)], axis=0
    )


def to_next_chip(value):
    pairs = [(i, i + CORES) for i in range(CTX - CORES)]
    return lax.ppermute(value, "ctx", pairs)


def to_chip_before(value):
    pairs = [(i, i - CORES) for i in range(CORES, CTX)]
    return lax.ppermute(value, "ctx", pairs)


def columns_of(value, core):
    return lax.dynamic_slice_in_dim(value, core * HALF, HALF, 1)


def chip_columns(value, core):
    return chip_rows(columns_of(value, core), swap(columns_of(value, 1 - core)), core)


def stacked(ref, tokens):
    rows = slice(tokens * TOK, (tokens + 1) * TOK)
    return jnp.concatenate([ref[rows, g * HD : (g + 1) * HD] for g in range(GROUP)], axis=0)


def masked_scores(keys, queries, tokens, any_before):
    scores = lax.dot_general(
        keys, queries, (((1,), (1,)), ((), ())), preferred_element_type=jnp.float32
    )
    across = queries.shape[0]
    before = (STEPS - tokens) * TOK
    seen = lax.broadcasted_iota(jnp.int32, (TOK, across), 0)
    query = lax.broadcasted_iota(jnp.int32, (TOK, across), 1) % TOK
    parts = [jnp.where(any_before, scores[:before], -1e30)]
    if tokens:
        parts.append(scores[before : STEPS * TOK])
    parts.append(jnp.where(seen <= query, scores[STEPS * TOK :], -1e30))
    return jnp.concatenate(parts, axis=0)


PAIR = 2
WIDE = GROUP * HD


def forward_kernel(index_ref, normed_ref, x_ref, before_ref, own_ref, out_ref):
    any_before = index_ref[0] >= CORES
    keys = jnp.concatenate([before_ref[:, :HD], own_ref[:, :HD]], axis=0)
    values = jnp.concatenate([before_ref[:, HD:], own_ref[:, HD:]], axis=0)
    values_t = values.astype(jnp.float32).T.astype(jnp.bfloat16)
    for tokens in range(CORES):
        span = slice(tokens * TOK, tokens * TOK + SPAN)
        rows = slice(tokens * TOK, (tokens + 1) * TOK)
        queries = stacked(normed_ref, tokens)
        for pair in range(GROUP // PAIR):
            these = queries[pair * PAIR * TOK : (pair + 1) * PAIR * TOK]
            scores = masked_scores(keys[span], these, tokens, any_before)
            top = jnp.max(scores, axis=0, keepdims=True)
            terms = jnp.exp2((scores - top) * (SCALE * LOG2E))
            total = jnp.sum(terms, axis=0, keepdims=True)
            attended = jnp.dot(
                values_t[:, span], terms.astype(jnp.bfloat16), preferred_element_type=jnp.float32
            ) * (1.0 / total)
            for g in range(PAIR):
                at = (pair * PAIR + g) * HD
                cols = slice(at, at + HD)
                out = attended[:, g * TOK : (g + 1) * TOK].T + x_ref[rows, cols].astype(jnp.float32)
                out_ref[rows, cols] = out.astype(jnp.bfloat16)


def forward_attention(index, normed, x, before, own):
    heads = pl.BlockSpec((CHIP_TOK, WIDE), lambda h, index: (0, h))
    kv = pl.BlockSpec((CHIP_TOK, 2 * HD), lambda h, index: (0, h))
    return pl.pallas_call(
        forward_kernel,
        grid_spec=pltpu.PrefetchScalarGridSpec(
            num_scalar_prefetch=1,
            grid=(HEADS,),
            in_specs=[heads, heads, kv, kv],
            out_specs=heads,
        ),
        out_shape=jax.ShapeDtypeStruct(x.shape, jnp.bfloat16),
        compiler_params=pltpu.CompilerParams(vmem_limit_bytes=32 * 2**20),
        cost_estimate=pl.CostEstimate(
            flops=4 * 10**9, bytes_accessed=8 * 2**20, transcendentals=2 * 10**6
        ),
        name="forward_attention",
    )(index, normed, x, before, own)


def backward_kernel(
    index_ref, normed_ref, upper_ref, before_ref, own_ref, dq_ref, grad_before_ref, grad_own_ref,
    probs_ref, dlog_ref,
):
    any_before = index_ref[0] >= CORES
    keys = jnp.concatenate([before_ref[:, :HD], own_ref[:, :HD]], axis=0)
    values = jnp.concatenate([before_ref[:, HD:], own_ref[:, HD:]], axis=0)
    keys_t = keys.astype(jnp.float32).T.astype(jnp.bfloat16)
    queries = [stacked(normed_ref, tokens) for tokens in range(CORES)]
    uppers = [stacked(upper_ref, tokens) for tokens in range(CORES)]
    for tokens in range(CORES):
        span = slice(tokens * TOK, tokens * TOK + SPAN)
        for pair in range(GROUP // PAIR):
            these = slice(pair * PAIR * TOK, (pair + 1) * PAIR * TOK)
            scores = masked_scores(keys[span], queries[tokens][these], tokens, any_before)
            grad_probs = lax.dot_general(
                values[span],
                uppers[tokens][these],
                (((1,), (1,)), ((), ())),
                preferred_element_type=jnp.float32,
            )
            top = jnp.max(scores, axis=0, keepdims=True)
            terms = jnp.exp2((scores - top) * (SCALE * LOG2E))
            inverse = 1.0 / jnp.sum(terms, axis=0, keepdims=True)
            row_dot = jnp.sum(terms * grad_probs, axis=0, keepdims=True) * inverse
            probs = terms * inverse
            cols = slice(tokens * WIDE + these.start, tokens * WIDE + these.stop)
            probs_ref[span, cols] = probs.astype(jnp.bfloat16)
            dlog_ref[span, cols] = (probs * ((grad_probs - row_dot) * SCALE)).astype(jnp.bfloat16)
        dlogits = dlog_ref[span, tokens * WIDE : (tokens + 1) * WIDE]
        grad_query = jnp.dot(keys_t[:, span], dlogits, preferred_element_type=jnp.float32)
        rows = slice(tokens * TOK, (tokens + 1) * TOK)
        for g in range(GROUP):
            dq_ref[rows, g * HD : (g + 1) * HD] = grad_query[:, g * TOK : (g + 1) * TOK].T
    for left, factors, first in ((dlog_ref, queries, 0), (probs_ref, uppers, HD)):
        cols = slice(first, first + HD)

        def product(rows, tokens, last):
            factor = jnp.concatenate(factors[tokens:last], axis=0)
            return jnp.dot(
                left[rows, tokens * WIDE : last * WIDE], factor, preferred_element_type=jnp.float32
            )

        middle = product(slice(TOK, 3 * TOK), 0, 2)
        grad_before_ref[:TOK, cols] = product(slice(0, TOK), 0, 1).astype(jnp.bfloat16)
        grad_before_ref[TOK:, cols] = middle[:TOK].astype(jnp.bfloat16)
        grad_own_ref[:TOK, cols] = middle[TOK:]
        grad_own_ref[TOK:, cols] = product(slice(3 * TOK, 4 * TOK), 1, 2)


def backward_attention(index, normed, upper, before, own):
    kv = pl.BlockSpec((CHIP_TOK, 2 * HD), lambda h, index: (0, h))
    heads = pl.BlockSpec((CHIP_TOK, WIDE), lambda h, index: (0, h))
    return pl.pallas_call(
        backward_kernel,
        grid_spec=pltpu.PrefetchScalarGridSpec(
            num_scalar_prefetch=1,
            grid=(HEADS,),
            in_specs=[
                pl.BlockSpec((CHIP_TOK, WIDE), lambda h, index: (0, (index[0] % CORES) * HEADS + h)),
                heads,
                kv,
                kv,
            ],
            out_specs=[heads, kv, kv],
            scratch_shapes=[
                pltpu.VMEM((4 * TOK, CORES * WIDE), jnp.bfloat16),
                pltpu.VMEM((4 * TOK, CORES * WIDE), jnp.bfloat16),
            ],
        ),
        out_shape=[
            jax.ShapeDtypeStruct((CHIP_TOK, HALF), jnp.float32),
            jax.ShapeDtypeStruct(before.shape, jnp.bfloat16),
            jax.ShapeDtypeStruct(own.shape, jnp.float32),
        ],
        compiler_params=pltpu.CompilerParams(vmem_limit_bytes=40 * 2**20),
        cost_estimate=pl.CostEstimate(
            flops=4 * 10**9, bytes_accessed=8 * 2**20, transcendentals=2 * 10**6
        ),
        name="backward_attention",
    )(index, normed, upper, before, own)


def partial_kernel(where_ref, own_ref, after_ref, weight_ref, dq_ref, out_ref, grad_kv_ref):
    step = pl.program_id(0)
    steps = pl.num_programs(0) // CORES

    @pl.when(step == 0)
    def _():
        grad_kv_ref[...] = (own_ref[...] + after_ref[...].astype(jnp.float32)).astype(jnp.bfloat16)

    product = lax.dot_general(
        grad_kv_ref[...], weight_ref[...], (((1,), (1,)), ((), ())), preferred_element_type=jnp.float32
    )
    here = step // steps == where_ref[1]

    @pl.when(here)
    def _():
        out_ref[...] = (product + dq_ref[...]).astype(out_ref.dtype)

    @pl.when(jnp.logical_not(here))
    def _():
        out_ref[...] = product.astype(out_ref.dtype)


def partial_grad(row, core, own, after, weight, dq, kind):
    features, half = weight.shape
    width = 1024
    steps = features // width // CORES
    rows = pl.BlockSpec((TOK, half), lambda j, where: (where[0], 0))
    return pl.pallas_call(
        partial_kernel,
        grid_spec=pltpu.PrefetchScalarGridSpec(
            num_scalar_prefetch=1,
            grid=(features // width,),
            in_specs=[
                rows,
                rows,
                pl.BlockSpec((width, half), lambda j, where: (j, 0)),
                pl.BlockSpec((TOK, width), lambda j, where: (where[0], j % steps)),
            ],
            out_specs=pl.BlockSpec((TOK, width), lambda j, where: (0, j)),
            scratch_shapes=[pltpu.VMEM((TOK, half), jnp.bfloat16)],
        ),
        out_shape=jax.ShapeDtypeStruct((TOK, features), kind),
        compiler_params=pltpu.CompilerParams(vmem_limit_bytes=32 * 2**20),
        cost_estimate=pl.CostEstimate(
            flops=10**9, bytes_accessed=8 * 2**20, transcendentals=0
        ),
        name="partial_grad",
    )(jnp.stack([row, core]).astype(jnp.int32), own, after, weight, dq)


def input_grad_kernel(
    own_ref, other_ref, x_ref, upper_ref, gain_ref, up_ref, down_ref, gain_grad_ref, grad_ref
):
    features = x_ref.shape[1]
    width = 512
    blocks = [slice(at, at + width) for at in range(0, features, width)]
    squares = jnp.zeros((TOK, 1), jnp.float32)
    for cols in blocks:
        part = x_ref[:, cols].astype(jnp.float32)
        squares += jnp.sum(part * part, axis=-1, keepdims=True)
    inv_rms = lax.rsqrt(squares / features + EPSILON)
    inner = jnp.zeros((TOK, 1), jnp.float32)
    for cols in blocks:
        grad = own_ref[:, cols] + other_ref[:, cols].astype(jnp.float32)
        scaled = x_ref[:, cols].astype(jnp.float32) * inv_rms
        product = grad * scaled
        gain_grad_ref[:, cols] = jnp.sum(product, axis=0, keepdims=True)
        gain = gain_ref[:, cols]
        inner += jnp.sum(product * gain, axis=-1, keepdims=True)
        grad_ref[:, cols] = grad * gain
    mean = inner * (1.0 / features)
    for first, ref in ((0, up_ref), (TOK // 2, down_ref)):
        rows = slice(first, first + TOK // 2)
        inv = inv_rms[rows]
        for cols in blocks:
            scaled = x_ref[rows, cols].astype(jnp.float32) * inv
            out = inv * (grad_ref[rows, cols] - scaled * mean[rows])
            ref[:, cols] = (out + upper_ref[rows, cols].astype(jnp.float32)).astype(jnp.bfloat16)


def input_grad(own, other, x, upper, gain_row):
    features = x.shape[1]
    return pl.pallas_call(
        input_grad_kernel,
        out_shape=[
            jax.ShapeDtypeStruct((TOK // 2, features), jnp.bfloat16),
            jax.ShapeDtypeStruct((TOK // 2, features), jnp.bfloat16),
            jax.ShapeDtypeStruct((1, features), jnp.float32),
        ],
        scratch_shapes=[pltpu.VMEM((TOK, features), jnp.float32)],
        compiler_params=pltpu.CompilerParams(vmem_limit_bytes=32 * 2**20),
        cost_estimate=pl.CostEstimate(
            flops=10**7, bytes_accessed=8 * 2**20, transcendentals=10**3
        ),
        name="input_grad",
    )(own, other, x, upper, gain_row)


def body(section_in, back_in, upstream, gains, kv_weight):
    index = lax.axis_index("ctx").astype(jnp.int32)
    core = index % CORES
    place = index.reshape(1)
    x_back, upper_in = back_in[0], upstream[0]

    w_mine = gather_weight(kv_weight[0], core)
    x_parts = land(set_out(section_in[0, : TOK // 2], section_in[0, TOK // 2 :]), 1)
    peers = lax.axis_size("section")
    next_section = [(i, (i + 1) % peers) for i in range(peers)]
    gain_here = lax.ppermute(gains, "section", next_section)

    normed_back = norm_forward(x_back, gains)
    normed_fwd = norm_forward(section_in[0], gains)
    partner = swap(jnp.concatenate([normed_back, normed_fwd], axis=0))
    chip_back = chip_rows(normed_back, partner[:TOK], core)
    chip_fwd = chip_rows(normed_fwd, partner[TOK:], core)
    chip_upper = chip_columns(upper_in, core)

    x_here = jnp.concatenate(x_parts, axis=0)
    normed_here = norm_forward(x_here, gain_here)
    swapped = swap(
        jnp.concatenate([columns_of(normed_here, 1 - core), columns_of(x_here, 1 - core)], axis=0)
    )
    chip_normed_here = chip_rows(columns_of(normed_here, core), swapped[:TOK], core)
    chip_x_here = chip_rows(columns_of(x_here, core), swapped[TOK:], core)

    chip_back, chip_fwd, chip_upper, chip_normed_here, chip_x_here = lax.optimization_barrier(
        (chip_back, chip_fwd, chip_upper, chip_normed_here, chip_x_here)
    )

    def project(normed):
        return jnp.dot(normed, w_mine, preferred_element_type=jnp.float32).astype(jnp.bfloat16)

    kv_back = project(chip_back)
    before = to_next_chip(kv_back)
    kv_fwd = project(chip_fwd)
    kv_here = lax.ppermute(kv_fwd, "section", next_section)

    dq, grad_before, grad_own = backward_attention(place, chip_back, chip_upper, before, kv_back)
    after, kv_here = lax.optimization_barrier((to_chip_before(grad_before), kv_here))
    before_here = to_next_chip(kv_here)

    away = partial_grad(1 - core, core, grad_own, after, w_mine, dq, jnp.bfloat16)
    home = partial_grad(core, core, grad_own, after, w_mine, dq, jnp.float32)
    away, home, before_here = lax.optimization_barrier((swap(away), home, before_here))
    up, down, gain_part = input_grad(home, away, x_back, upper_in, gains)
    next_grad = jnp.concatenate(land(set_out(up, down), -1), axis=0)
    gain_total = jnp.sum(
        lax.all_gather(gain_part, "ctx", axis=0, tiled=True), axis=0, keepdims=True
    )

    chip_x_here, _ = lax.optimization_barrier((chip_x_here, up))
    out = forward_attention(place, chip_normed_here, chip_x_here, before_here, kv_here)
    first, second = out[:TOK], out[TOK:]
    mine = jnp.where(core == 0, first, second)
    other = swap(jnp.where(core == 0, second, first))
    next_in = jnp.concatenate(
        [jnp.where(core == 0, mine, other), jnp.where(core == 0, other, mine)], axis=1
    )
    return (next_in[None], next_grad[None], gain_total)


def solution(mesh):
    in_specs = (
        P("section", "ctx", None),
        P("section", "ctx", None),
        P("section", "ctx", None),
        P("section", None),
        P("section", "ctx", None),
    )
    out_specs = (P("section", "ctx", None), P("section", "ctx", None), P("section", None))
    return jax.shard_map(body, mesh=mesh, in_specs=in_specs, out_specs=out_specs, check_vma=False)
```

time: 656 us -> 401 us (0.61)
  blocking collectives: 359 us -> 0 us
  waiting for transfers between devices: 133 us -> 232 us
  matrix products: 81.8 us -> 5.45 us
  starting transfers between devices: 27.6 us -> 102 us
  Pallas kernels: 0 us -> 21.9 us
  local copies, waits for them, and re-layouts: 26.5 us -> 4.7 us
  other arithmetic: 13.2 us -> 20.4 us
    psum x1 -> x0, blocking collectives: 359 us -> none  [body(): gain_total = lax.psum(jnp.sum(grad_normed * scaled_b, axis=0), 'ctx')]
    ppermute x8 -> x19, starting transfers between devices: 27.6 us -> 102 us  [the longest x8 46.4 us: over_grid(): return lax.ppermute(value, ('section', 'ctx'), grid_pairs(move))]
    dot_general x27 -> x2, matrix products: 64.4 us -> 5.45 us  [project(): jnp.dot(normed, w_mine, preferred_element_type=jnp.float32)]
    ppermute x8 -> x19, waiting for transfers between devices: 12 us -> 64 us  [the longest x8 53.5 us: over_grid(): return lax.ppermute(value, ('section', 'ctx'), grid_pairs(move))]
    all_gather x1 -> x2, waiting for transfers between devices: 120 us -> 168 us  [the longest x1 85.5 us: body(): lax.all_gather(gain_part, 'ctx', axis=0, tiled=True)]
    pallas_call x0 -> x5, Pallas kernels: none -> 21.9 us  [the longest x1 7.03 us: backward_attention(): pl.pallas_call(backward_kernel, grid_spec=pltpu.PrefetchScalarGridSpec(nu...]
    sub x8 -> x0, matrix products: 17.5 us -> none  [head_probs(): exp_terms = jnp.exp(logits - row_max)]
    reshape x6 -> x0, local copies, waits for them, and re-layouts: 8.66 us -> none  [the longest x2 5.99 us: merge_heads(): return moved.reshape(moved.shape[0], -1)]
  transfers between devices with their start and end apart: 9 -> 21, of which waited for: 5 -> 10; matrix products, arithmetic and copies ran while one was open for 4% -> 5% of each run, Pallas kernels for 0% -> 4%
where the time goes in v2:
time: 401 us
  waiting for transfers between devices  232 us (58%)
  starting transfers between devices  102 us (25%)
  Pallas kernels  21.9 us (5%)
  other arithmetic  20.4 us (5%)
  between operations  14.6 us (4%)
  matrix products  5.45 us (1%)
  local copies, waits for them, and re-layouts  4.7 us (1%)
    all_gather x1, waiting for transfers between devices, body(): lax.all_gather(gain_part, 'ctx', axis=0, tiled=True)  85.5 us
    all_gather x1, waiting for transfers between devices, gather_weight(): lax.all_gather(chip, 'ctx', axis_index_groups=same_core, axis=0, tiled=True)  82.4 us
    ppermute x8, waiting for transfers between devices, over_grid(): return lax.ppermute(value, ('section', 'ctx'), grid_pairs(move))  53.5 us
    ppermute x8, starting transfers between devices, over_grid(): return lax.ppermute(value, ('section', 'ctx'), grid_pairs(move))  46.4 us
    ppermute x6, starting transfers between devices, over_ctx(): return lax.ppermute(value, 'ctx', ctx_pairs(move))  38.9 us
  transfers between devices with their start and end apart: 21, of which 10 were waited for; matrix products, arithmetic and copies ran while one was open for 5% of the time, Pallas kernels for 4%

profile of v2, /device:TPU:1, one launch (start us, length us, event | category | flops | bytes accessed | tf_op | source)
XLA Modules:
  0.0 400.6 jit_solution(8671258660912032631)
XLA Ops:
  8.7 6.6 %collective-permute-start.2 = (bf16[64,4096]{1,0:T(8,128)(2,1)S(1)}, bf16[64,4096]{1,0:T(8,128)(2,1)}, u32[]{:S(2)}, u32[]{:S(2)}) collective-permute-start(bf16[64,4096]{1,0:T(8,128)(2,1)S(1)} %get-tuple-element.54), channel_id=1, source_target_pairs={{0,4},{1,5},{8,12},{9,13},{16,20},{17,21},{24,28},{25,29},{32,36},... | collective-permute-start | bytes 1572872 | tf_op jit(solution)/shard_map/ppermute | solution.py:60
  15.3 6.8 %collective-permute-start.4 = (bf16[64,4096]{1,0:T(8,128)(2,1)S(1)}, bf16[64,4096]{1,0:T(8,128)(2,1)}, u32[]{:S(2)}, u32[]{:S(2)}) collective-permute-start(bf16[64,4096]{1,0:T(8,128)(2,1)S(1)} %get-tuple-element.53), channel_id=1, source_target_pairs={{0,68},{1,69},{8,76},{9,77},{16,84},{17,85},{24,92},{25,93},{32,10... | collective-permute-start | bytes 1572872 | tf_op jit(solution)/shard_map/ppermute | solution.py:60
  22.1 5.5 %collective-permute-start.6 = (f32[1,4096]{1,0:T(1,128)S(1)}, f32[1,4096]{1,0:T(1,128)S(1)}, u32[]{:S(2)}, u32[]{:S(2)}) collective-permute-start(f32[1,4096]{1,0:T(1,128)S(1)} %copy-done.6), channel_id=1, source_target_pairs={{0,64},{64,128},{128,192},{192,256},{256,320},{320,384},{384,448},... | collective-permute-start | bytes 49160 | tf_op jit(solution)/shard_map/ppermute | solution.py:397
  27.6 3.4 collective-permute-start.8
  32.7 12.6 %collective-permute-start.3 = (bf16[64,4096]{1,0:T(8,128)(2,1)}, bf16[64,4096]{1,0:T(8,128)(2,1)S(1)}, u32[]{:S(2)}, u32[]{:S(2)}) collective-permute-start(bf16[64,4096]{1,0:T(8,128)(2,1)} %collective-permute-done.2), channel_id=1, source_target_pairs={{0,132},{1,133},{8,140},{9,141},{16,148},{17,149},{24,156},{25,157... | collective-permute-start | bytes 1572872 | tf_op jit(solution)/shard_map/ppermute | solution.py:60
  45.4 3.7 collective-permute-start.5
  51.1 30.0 %collective-permute-done.3 = bf16[64,4096]{1,0:T(8,128)(2,1)S(1)} collective-permute-done((bf16[64,4096]{1,0:T(8,128)(2,1)}, bf16[64,4096]{1,0:T(8,128)(2,1)S(1)}, u32[]{:S(2)}, u32[]{:S(2)}) %collective-permute-start.3) | collective-permute-done | bytes 524320 | tf_op jit(solution)/shard_map/ppermute | solution.py:60
  83.1 4.2 %collective-permute-start.7 = (bf16[256,2048]{1,0:T(8,128)(2,1)}, bf16[256,2048]{1,0:T(8,128)(2,1)}, u32[]{:S(2)}, u32[]{:S(2)}) collective-permute-start(bf16[256,2048]{1,0:T(8,128)(2,1)} %pad_maximum_fusion.4), channel_id=1, source_target_pairs={{0,1},{1,0},{2,3},{3,2},{4,5},{5,4},{6,7},{7,6},{8,9},{9,8},{10,11... | collective-permute-start | bytes 3145736 | tf_op jit(solution)/shard_map/ppermute | solution.py:42
  91.7 2.4 collective-permute-start.1
  102.4 2.3 pad_maximum_fusion.1
  104.7 82.4 %all-gather.4.cloned.1.call-done.weight_ref = bf16[4096,512]{1,0:T(8,128)(2,1)} async-done(((bf16[128,512]{1,0:T(8,128)(2,1)}), bf16[4096,512]{1,0:T(8,128)(2,1)}) %all-gather.4.cloned.1.call-update) | async-done | bytes 4194320 | tf_op jit(solution)/shard_map/all_gather | solution.py:106
  187.1 4.2 %convolution_convert_fusion.1.own_ref = bf16[256,512]{1,0:T(8,128)(2,1)S(1)} fusion(bf16[256,4096]{1,0:T(8,128)(2,1)} %get-tuple-element.22.normed_ref, bf16[4096,512]{1,0:T(8,128)(2,1)} %all-gather.4.cloned.1.call-done.weight_ref), kind=kOutput, calls=%fused_computation.19 | convolution fusion | flops 1073872896 | bytes 6553600 | tf_op jit(solution)/shard_map/dot_general | solution.py:419
  194.2 4.0 %collective-permute-start.11 = (bf16[256,512]{1,0:T(8,128)(2,1)S(1)}, bf16[256,512]{1,0:T(8,128)(2,1)S(1)}, u32[]{:S(2)}, u32[]{:S(2)}) collective-permute-start(bf16[256,512]{1,0:T(8,128)(2,1)S(1)} %convolution_convert_fusion), channel_id=1, source_target_pairs={{0,64},{64,128},{128,192},{192,256},{256,320},{320,384},{384,448},... | collective-permute-start | bytes 786440 | tf_op jit(solution)/shard_map/ppermute | solution.py:424
  198.3 7.0 %backward_attention.1 = (f32[256,2048]{1,0:T(8,128)S(1)}, bf16[256,512]{1,0:T(8,128)(2,1)S(1)}, f32[256,512]{1,0:T(8,128)S(1)}) custom-call(s32[1]{0:T(128)} %bitcast.index_ref, bf16[256,4096]{1,0:T(8,128)(2,1)S(1)} %copy-done.3, bf16[256,2048]{1,0:T(8,128)(2,1)S(1)} %copy-done.5, bf16[256,512]{1,0:T(8,128)(2,1)S(1)} %collective-permute-done.9.before_ref, ...), custom_call_target="tpu_custom_call" | custom-call | flops 4000000000 | bytes 8388608 | tf_op jit(solution)/shard_map/backward_attention/pallas_call | solution.py:259
  206.7 3.1 collective-permute-done.11.own_ref
  209.9 2.8 collective-permute-done.10.after_ref
  212.6 3.0 partial_grad.2
  215.6 24.0 %collective-permute-start.12 = (bf16[128,4096]{1,0:T(8,128)(2,1)S(1)}, bf16[128,4096]{1,0:T(8,128)(2,1)S(1)}, u32[]{:S(2)}, u32[]{:S(2)}) collective-permute-start(bf16[128,4096]{1,0:T(8,128)(2,1)S(1)} %partial_grad.2), channel_id=1, source_target_pairs={{0,1},{1,0},{2,3},{3,2},{4,5},{5,4},{6,7},{7,6},{8,9},{9,8},{10,11... | collective-permute-start | bytes 3145736 | tf_op jit(solution)/shard_map/ppermute | solution.py:42
  239.6 3.8 collective-permute-start.13
  243.6 3.0 partial_grad.3.own_ref
  246.6 2.4 collective-permute-done.13.before_ref
  249.0 2.3 input_grad.1
  251.3 4.7 %collective-permute-start.15 = (bf16[64,4096]{1,0:T(8,128)(2,1)}, bf16[64,4096]{1,0:T(8,128)(2,1)}, u32[]{:S(2)}, u32[]{:S(2)}) collective-permute-start(bf16[64,4096]{1,0:T(8,128)(2,1)} %get-tuple-element.32), channel_id=1, source_target_pairs={{0,4},{1,5},{8,12},{9,13},{16,20},{17,21},{24,28},{25,29},{32,36},... | collective-permute-start | bytes 1572872 | tf_op jit(solution)/shard_map/ppermute | solution.py:60
  256.0 3.5 collective-permute-start.17
  261.8 6.6 %forward_attention.1 = bf16[256,2048]{1,0:T(8,128)(2,1)S(1)} custom-call(s32[1]{0:T(128)} %bitcast.index_ref, bf16[256,2048]{1,0:T(8,128)(2,1)S(1)} %copy-done.4, bf16[256,2048]{1,0:T(8,128)(2,1)S(1)} %pad_maximum_fusion.6.x_ref, bf16[256,512]{1,0:T(8,128)(2,1)S(1)} %copy-done.8, bf16[256,512]{1,0:T(8,128)(2,1)S(1)} %collective-permute-done.11.own_ref), custom_call_target="tpu_custom_call" | custom-call | flops 4000000000 | bytes 8388608 | tf_op jit(solution)/shard_map/forward_attention/pallas_call | solution.py:189
  268.4 3.0 collective-permute-start.14
  271.4 2.9 collective-permute-start.16
  274.4 5.5 %collective-permute-start.18 = (bf16[64,4096]{1,0:T(8,128)(2,1)}, bf16[64,4096]{1,0:T(8,128)(2,1)S(1)}, u32[]{:S(2)}, u32[]{:S(2)}) collective-permute-start(bf16[64,4096]{1,0:T(8,128)(2,1)} %collective-permute-done.17), channel_id=1, source_target_pairs={{0,452},{1,453},{8,460},{9,461},{16,468},{17,469},{24,476},{25,477... | collective-permute-start | bytes 1572872 | tf_op jit(solution)/shard_map/ppermute | solution.py:60
  281.0 19.2 %collective-permute-done.16 = bf16[64,4096]{1,0:T(8,128)(2,1)S(1)} collective-permute-done((bf16[64,4096]{1,0:T(8,128)(2,1)}, bf16[64,4096]{1,0:T(8,128)(2,1)S(1)}, u32[]{:S(2)}, u32[]{:S(2)}) %collective-permute-start.16) | collective-permute-done | bytes 524320 | tf_op jit(solution)/shard_map/ppermute | solution.py:60
  300.3 4.3 %collective-permute-done.18 = bf16[64,4096]{1,0:T(8,128)(2,1)S(1)} collective-permute-done((bf16[64,4096]{1,0:T(8,128)(2,1)}, bf16[64,4096]{1,0:T(8,128)(2,1)S(1)}, u32[]{:S(2)}, u32[]{:S(2)}) %collective-permute-start.18) | collective-permute-done | bytes 524320 | tf_op jit(solution)/shard_map/ppermute | solution.py:60
  305.6 85.5 %all-gather.6.cloned.1.call-done = f32[64,1,4096]{2,1,0:T(1,128)} async-done(((f32[1,1,4096]{2,1,0:T(1,128)}), f32[64,1,4096]{2,1,0:T(1,128)}) %all-gather.6.cloned.1.call-update) | async-done | bytes 1048592 | tf_op jit(solution)/shard_map/all_gather | solution.py:436
  391.1 2.7 reduce_sum.39
  (86 shorter events, 28.5 us)
Async XLA Ops:
  7.2 23.9 %copy-start.9 = (bf16[1,128,4096]{2,1,0:T(8,128)(2,1)S(1)}, bf16[1,128,4096]{2,1,0:T(8,128)(2,1)}, u32[]{:S(2)}) copy-start(bf16[1,128,4096]{2,1,0:T(8,128)(2,1)} %param.5) | copy-start | bytes 3145732
  7.2 14.9 %copy-start.6 = (f32[1,4096]{1,0:T(1,128)S(1)}, f32[1,4096]{1,0:T(1,128)}, u32[]{:S(2)}) copy-start(f32[1,4096]{1,0:T(1,128)} %gain_ref.1) | copy-start | bytes 49156
  7.2 20.4 %copy-start.16 = (bf16[1,64,1024]{2,1,0:T(8,128)(2,1)S(1)}, bf16[1,64,1024]{2,1,0:T(8,128)(2,1)}, u32[]{:S(2)}) copy-start(bf16[1,64,1024]{2,1,0:T(8,128)(2,1)} %param.9) | copy-start | bytes 393220
  7.2 24.2 %copy-start.1 = (bf16[1,128,4096]{2,1,0:T(8,128)(2,1)S(1)}, bf16[1,128,4096]{2,1,0:T(8,128)(2,1)}, u32[]{:S(2)}) copy-start(bf16[1,128,4096]{2,1,0:T(8,128)(2,1)} %param.6) | copy-start | bytes 3145732
  7.2 179.9 %all-gather.4.cloned.1.call-start = ((), (), s32[]{:S(2)}) async-start(), calls=%async_computation | async-start | bytes 4325376 | tf_op jit(solution)/shard_map/all_gather | solution.py:106
  8.7 24.1 %collective-permute-start.2 = (bf16[64,4096]{1,0:T(8,128)(2,1)S(1)}, bf16[64,4096]{1,0:T(8,128)(2,1)}, u32[]{:S(2)}, u32[]{:S(2)}) collective-permute-start(bf16[64,4096]{1,0:T(8,128)(2,1)S(1)} %get-tuple-element.54), channel_id=1, source_target_pairs={{0,4},{1,5},{8,12},{9,13},{16,20},{17,21},{24,28},{25,29},{32,36},... | collective-permute-start | bytes 1572872 | tf_op jit(solution)/shard_map/ppermute | solution.py:60
  15.3 30.0 %collective-permute-start.4 = (bf16[64,4096]{1,0:T(8,128)(2,1)S(1)}, bf16[64,4096]{1,0:T(8,128)(2,1)}, u32[]{:S(2)}, u32[]{:S(2)}) collective-permute-start(bf16[64,4096]{1,0:T(8,128)(2,1)S(1)} %get-tuple-element.53), channel_id=1, source_target_pairs={{0,68},{1,69},{8,76},{9,77},{16,84},{17,85},{24,92},{25,93},{32,10... | collective-permute-start | bytes 1572872 | tf_op jit(solution)/shard_map/ppermute | solution.py:60
  22.1 59.5 %collective-permute-start.6 = (f32[1,4096]{1,0:T(1,128)S(1)}, f32[1,4096]{1,0:T(1,128)S(1)}, u32[]{:S(2)}, u32[]{:S(2)}) collective-permute-start(f32[1,4096]{1,0:T(1,128)S(1)} %copy-done.6), channel_id=1, source_target_pairs={{0,64},{64,128},{128,192},{192,256},{256,320},{320,384},{384,448},... | collective-permute-start | bytes 49160 | tf_op jit(solution)/shard_map/ppermute | solution.py:397
  27.6 4.3 %collective-permute-start.8 = (bf16[64,512]{1,0:T(8,128)(2,1)S(1)}, bf16[64,512]{1,0:T(8,128)(2,1)S(1)}, u32[]{:S(2)}, u32[]{:S(2)}) collective-permute-start(bf16[64,512]{1,0:T(8,128)(2,1)S(1)} %broadcast_select_fusion.14), channel_id=1, source_target_pairs={{0,1},{1,0},{2,3},{3,2},{4,5},{5,4},{6,7},{7,6},{8,9},{9,8},{10,11... | collective-permute-start | bytes 196616 | tf_op jit(solution)/shard_map/ppermute | solution.py:42
  32.7 358.4 %all-gather.6.cloned.1.call-start = ((), (), s32[]{:S(2)}) async-start(), calls=%async_computation.1 | async-start | bytes 1064960 | tf_op jit(solution)/shard_map/all_gather | solution.py:436
  32.7 48.4 %collective-permute-start.3 = (bf16[64,4096]{1,0:T(8,128)(2,1)}, bf16[64,4096]{1,0:T(8,128)(2,1)S(1)}, u32[]{:S(2)}, u32[]{:S(2)}) collective-permute-start(bf16[64,4096]{1,0:T(8,128)(2,1)} %collective-permute-done.2), channel_id=1, source_target_pairs={{0,132},{1,133},{8,140},{9,141},{16,148},{17,149},{24,156},{25,157... | collective-permute-start | bytes 1572872 | tf_op jit(solution)/shard_map/ppermute | solution.py:60
  45.4 35.8 %collective-permute-start.5 = (bf16[64,4096]{1,0:T(8,128)(2,1)}, bf16[64,4096]{1,0:T(8,128)(2,1)S(1)}, u32[]{:S(2)}, u32[]{:S(2)}) collective-permute-start(bf16[64,4096]{1,0:T(8,128)(2,1)} %collective-permute-done.4), channel_id=1, source_target_pairs={{0,68},{1,69},{8,76},{9,77},{16,84},{17,85},{24,92},{25,93},{32,10... | collective-permute-start | bytes 1572872 | tf_op jit(solution)/shard_map/ppermute | solution.py:60
  81.9 5.3 %copy-start.14 = (bf16[128,4096]{1,0:T(8,128)(2,1)}, bf16[128,4096]{1,0:T(8,128)(2,1)S(1)}, u32[]{:S(2)}) copy-start(bf16[128,4096]{1,0:T(8,128)(2,1)S(1)} %fusion.5) | copy-start | bytes 3145732
  81.9 5.3 %copy-start.10 = (bf16[128,4096]{1,0:T(8,128)(2,1)S(1)}, bf16[128,4096]{1,0:T(8,128)(2,1)}, u32[]{:S(2)}) copy-start(bf16[128,4096]{1,0:T(8,128)(2,1)} %get-tuple-element.65) | copy-start | bytes 3145732
  81.9 5.3 %copy-start.12 = (bf16[128,4096]{1,0:T(8,128)(2,1)S(1)}, bf16[128,4096]{1,0:T(8,128)(2,1)}, u32[]{:S(2)}) copy-start(bf16[128,4096]{1,0:T(8,128)(2,1)} %get-tuple-element.66) | copy-start | bytes 3145732
  83.1 13.0 %collective-permute-start.7 = (bf16[256,2048]{1,0:T(8,128)(2,1)}, bf16[256,2048]{1,0:T(8,128)(2,1)}, u32[]{:S(2)}, u32[]{:S(2)}) collective-permute-start(bf16[256,2048]{1,0:T(8,128)(2,1)} %pad_maximum_fusion.4), channel_id=1, source_target_pairs={{0,1},{1,0},{2,3},{3,2},{4,5},{5,4},{6,7},{7,6},{8,9},{9,8},{10,11... | collective-permute-start | bytes 3145736 | tf_op jit(solution)/shard_map/ppermute | solution.py:42
  88.9 11.7 %collective-permute-start = (bf16[256,4096]{1,0:T(8,128)(2,1)}, bf16[256,4096]{1,0:T(8,128)(2,1)}, u32[]{:S(2)}, u32[]{:S(2)}) collective-permute-start(bf16[256,4096]{1,0:T(8,128)(2,1)} %pad_maximum_fusion), channel_id=1, source_target_pairs={{0,1},{1,0},{2,3},{3,2},{4,5},{5,4},{6,7},{7,6},{8,9},{9,8},{10,11... | collective-permute-start | bytes 6291464 | tf_op jit(solution)/shard_map/ppermute | solution.py:42
  91.7 4.3 %collective-permute-start.1 = (bf16[128,2048]{1,0:T(8,128)(2,1)}, bf16[128,2048]{1,0:T(8,128)(2,1)}, u32[]{:S(2)}, u32[]{:S(2)}) collective-permute-start(bf16[128,2048]{1,0:T(8,128)(2,1)} %dynamic-slice_bitcast_fusion), channel_id=1, source_target_pairs={{0,1},{1,0},{2,3},{3,2},{4,5},{5,4},{6,7},{7,6},{8,9},{9,8},{10,11... | collective-permute-start | bytes 1572872 | tf_op jit(solution)/shard_map/ppermute | solution.py:42
  187.1 5.9 %copy-start = (bf16[4096,512]{1,0:T(8,128)(2,1)S(1)}, bf16[4096,512]{1,0:T(8,128)(2,1)}, u32[]{:S(2)}) copy-start(bf16[4096,512]{1,0:T(8,128)(2,1)} %all-gather.4.cloned.1.call-done.weight_ref) | copy-start | bytes 12582916
  187.1 5.9 %copy-start.15 = (bf16[256,4096]{1,0:T(8,128)(2,1)S(1)}, bf16[256,4096]{1,0:T(8,128)(2,1)}, u32[]{:S(2)}) copy-start(bf16[256,4096]{1,0:T(8,128)(2,1)} %get-tuple-element.26) | copy-start | bytes 6291460
  191.3 7.0 %copy-start.3 = (bf16[256,4096]{1,0:T(8,128)(2,1)S(1)}, bf16[256,4096]{1,0:T(8,128)(2,1)}, u32[]{:S(2)}) copy-start(bf16[256,4096]{1,0:T(8,128)(2,1)} %get-tuple-element.22.normed_ref) | copy-start | bytes 6291460
  191.3 7.0 %copy-start.5 = (bf16[256,2048]{1,0:T(8,128)(2,1)S(1)}, bf16[256,2048]{1,0:T(8,128)(2,1)}, u32[]{:S(2)}) copy-start(bf16[256,2048]{1,0:T(8,128)(2,1)} %pad_maximum_fusion.3.upper_ref) | copy-start | bytes 3145732
  191.3 6.9 %collective-permute-start.9 = (bf16[256,512]{1,0:T(8,128)(2,1)S(1)}, bf16[256,512]{1,0:T(8,128)(2,1)S(1)}, u32[]{:S(2)}, u32[]{:S(2)}) collective-permute-start(bf16[256,512]{1,0:T(8,128)(2,1)S(1)} %convolution_convert_fusion.1.own_ref), channel_id=1, source_target_pairs={{0,2},{1,3},{2,4},{3,5},{4,6},{5,7},{6,8},{7,9},{8,10},{9,11},{10,... | collective-permute-start | bytes 786440 | tf_op jit(solution)/shard_map/ppermute | solution.py:121
  194.2 15.6 %collective-permute-start.11 = (bf16[256,512]{1,0:T(8,128)(2,1)S(1)}, bf16[256,512]{1,0:T(8,128)(2,1)S(1)}, u32[]{:S(2)}, u32[]{:S(2)}) collective-permute-start(bf16[256,512]{1,0:T(8,128)(2,1)S(1)} %convolution_convert_fusion), channel_id=1, source_target_pairs={{0,64},{64,128},{128,192},{192,256},{256,320},{320,384},{384,448},... | collective-permute-start | bytes 786440 | tf_op jit(solution)/shard_map/ppermute | solution.py:424
  205.3 7.3 %collective-permute-start.10 = (bf16[256,512]{1,0:T(8,128)(2,1)S(1)}, bf16[256,512]{1,0:T(8,128)(2,1)S(1)}, u32[]{:S(2)}, u32[]{:S(2)}) collective-permute-start(bf16[256,512]{1,0:T(8,128)(2,1)S(1)} %get-tuple-element.25), channel_id=1, source_target_pairs={{2,0},{3,1},{4,2},{5,3},{6,4},{7,5},{8,6},{9,7},{10,8},{11,9},{12,... | collective-permute-start | bytes 786440 | tf_op jit(solution)/shard_map/ppermute | solution.py:126
  215.6 33.4 %collective-permute-start.12 = (bf16[128,4096]{1,0:T(8,128)(2,1)S(1)}, bf16[128,4096]{1,0:T(8,128)(2,1)S(1)}, u32[]{:S(2)}, u32[]{:S(2)}) collective-permute-start(bf16[128,4096]{1,0:T(8,128)(2,1)S(1)} %partial_grad.2), channel_id=1, source_target_pairs={{0,1},{1,0},{2,3},{3,2},{4,5},{5,4},{6,7},{7,6},{8,9},{9,8},{10,11... | collective-permute-start | bytes 3145736 | tf_op jit(solution)/shard_map/ppermute | solution.py:42
  239.6 9.4 %collective-permute-start.13 = (bf16[256,512]{1,0:T(8,128)(2,1)S(1)}, bf16[256,512]{1,0:T(8,128)(2,1)S(1)}, u32[]{:S(2)}, u32[]{:S(2)}) collective-permute-start(bf16[256,512]{1,0:T(8,128)(2,1)S(1)} %collective-permute-done.11.own_ref), channel_id=1, source_target_pairs={{0,2},{1,3},{2,4},{3,5},{4,6},{5,7},{6,8},{7,9},{8,10},{9,11},{10,... | collective-permute-start | bytes 786440 | tf_op jit(solution)/shard_map/ppermute | solution.py:121
  251.3 20.1 %collective-permute-start.15 = (bf16[64,4096]{1,0:T(8,128)(2,1)}, bf16[64,4096]{1,0:T(8,128)(2,1)}, u32[]{:S(2)}, u32[]{:S(2)}) collective-permute-start(bf16[64,4096]{1,0:T(8,128)(2,1)} %get-tuple-element.32), channel_id=1, source_target_pairs={{0,4},{1,5},{8,12},{9,13},{16,20},{17,21},{24,28},{25,29},{32,36},... | collective-permute-start | bytes 1572872 | tf_op jit(solution)/shard_map/ppermute | solution.py:60
  256.0 18.3 %collective-permute-start.17 = (bf16[64,4096]{1,0:T(8,128)(2,1)}, bf16[64,4096]{1,0:T(8,128)(2,1)}, u32[]{:S(2)}, u32[]{:S(2)}) collective-permute-start(bf16[64,4096]{1,0:T(8,128)(2,1)} %get-tuple-element.35), channel_id=1, source_target_pairs={{0,68},{1,69},{8,76},{9,77},{16,84},{17,85},{24,92},{25,93},{32,10... | collective-permute-start | bytes 1572872 | tf_op jit(solution)/shard_map/ppermute | solution.py:60
  268.4 11.5 %collective-permute-start.14 = (bf16[128,2048]{1,0:T(8,128)(2,1)S(1)}, bf16[128,2048]{1,0:T(8,128)(2,1)S(1)}, u32[]{:S(2)}, u32[]{:S(2)}) collective-permute-start(bf16[128,2048]{1,0:T(8,128)(2,1)S(1)} %broadcast_select_fusion.6), channel_id=1, source_target_pairs={{0,1},{1,0},{2,3},{3,2},{4,5},{5,4},{6,7},{7,6},{8,9},{9,8},{10,11... | collective-permute-start | bytes 1572872 | tf_op jit(solution)/shard_map/ppermute | solution.py:42
  271.4 28.9 %collective-permute-start.16 = (bf16[64,4096]{1,0:T(8,128)(2,1)}, bf16[64,4096]{1,0:T(8,128)(2,1)S(1)}, u32[]{:S(2)}, u32[]{:S(2)}) collective-permute-start(bf16[64,4096]{1,0:T(8,128)(2,1)} %collective-permute-done.15), channel_id=1, source_target_pairs={{0,4},{1,5},{8,12},{9,13},{16,20},{17,21},{24,28},{25,29},{32,36},... | collective-permute-start | bytes 1572872 | tf_op jit(solution)/shard_map/ppermute | solution.py:60
  274.4 30.2 %collective-permute-start.18 = (bf16[64,4096]{1,0:T(8,128)(2,1)}, bf16[64,4096]{1,0:T(8,128)(2,1)S(1)}, u32[]{:S(2)}, u32[]{:S(2)}) collective-permute-start(bf16[64,4096]{1,0:T(8,128)(2,1)} %collective-permute-done.17), channel_id=1, source_target_pairs={{0,452},{1,453},{8,460},{9,461},{16,468},{17,469},{24,476},{25,477... | collective-permute-start | bytes 1572872 | tf_op jit(solution)/shard_map/ppermute | solution.py:60
  (6 other events, 12.3 us)
Sparse Core Ops, SparseCore 0:
  32.8 154.2 all-gather.3
  259.7 131.3 all-gather.5

commit v3 on v2

--- a/solution.py
+++ b/solution.py
@@ -73,18 +73,15 @@
     return over_grid(value, move)
 
 
-def set_out(upper, lower):
-    return halfway(upper, 1), halfway(lower, -1)
-
-
-def land(halves, distance):
-    return arrive(halves[0], 1, distance), arrive(halves[1], -1, distance)
+def direct(value, distance):
+    peers = Z_HI * X
+    return lax.ppermute(value, "section", [(i, (i + distance) % peers) for i in range(peers)])
 
 
 def norm_forward(section_x, gain_row):
     values = section_x.astype(jnp.float32)
     inv_rms = lax.rsqrt(jnp.mean(values * values, axis=-1, keepdims=True) + EPSILON)
-    return (values * inv_rms * gain_row).astype(jnp.bfloat16)
+    return (values * inv_rms * gain_row).astype(jnp.bfloat16), inv_rms
 
 
 def by_head(kv_columns):
@@ -95,15 +92,47 @@
     return jnp.concatenate(parts, axis=1)
 
 
-def gather_weight(own_rows, core):
+def gather_run(own_rows, core, z_lo):
     half = own_rows.shape[1] // 2
     columns = by_head(own_rows)
     low, high = columns[:, :half], columns[:, half:]
     keep = jnp.where(core == 0, low, high)
     received = swap(jnp.where(core == 0, high, low))
     chip = chip_rows(keep, received, core)
-    same_core = [[chip * CORES + c for chip in range(Y * Z_LO)] for c in range(CORES)]
-    return lax.all_gather(chip, "ctx", axis_index_groups=same_core, axis=0, tiled=True)
+    rows = chip.shape[0]
+    pieces = [chip]
+    for step in range(1, Z_LO):
+        pieces.append(over_ctx(chip, lambda y, z, c, step=step: (y, (z + step) % Z_LO, c)))
+    back = pieces[::-1]
+    return lax.dynamic_slice_in_dim(
+        jnp.concatenate(back + back[:-1], axis=0), (Z_LO - 1 - z_lo) * rows, Z_LO * rows, 0
+    )
+
+
+def gather_weight(run, set_out):
+    def up(piece):
+        return over_ctx(piece, lambda y, z, c: ((y + 1) % Y, z, c))
+
+    def down(piece):
+        return over_ctx(piece, lambda y, z, c: ((y - 1) % Y, z, c))
+
+    first_out, second_out, first_in = set_out
+    rising, falling = [up(run)], [down(run)]
+    first = first_out(run)
+    rising.append(up(rising[0]))
+    falling.append(down(falling[0]))
+    second = second_out(rising[0])
+    rising[1], falling[1], first = lax.optimization_barrier((rising[1], falling[1], first))
+    rising.append(up(rising[1]))
+    falling.append(down(falling[1]))
+    first = first_in(first)
+    rising[2], falling[2], second = lax.optimization_barrier((rising[2], falling[2], second))
+    middle = run.shape[0] // 2
+    rising.append(up(rising[2][:middle]))
+    falling.append(down(falling[2][middle:]))
+    rising[3], falling[3], first = lax.optimization_barrier((rising[3], falling[3], first))
+    pieces = [run, *falling[:3], rising[3], falling[3], *rising[:3][::-1]]
+    return pieces, first, second
 
 
 def swap(value):
@@ -157,50 +186,65 @@
 PAIR = 2
 WIDE = GROUP * HD
 
-
-def forward_kernel(index_ref, normed_ref, x_ref, before_ref, own_ref, out_ref):
+BRIEF = pl.CostEstimate(flops=1000, bytes_accessed=1000, transcendentals=0)
+
+
+def forward_kernel(
+    index_ref, first_ref, second_ref, inv_ref, gain_ref, before_ref, own_ref, out_ref
+):
     any_before = index_ref[0] >= CORES
     keys = jnp.concatenate([before_ref[:, :HD], own_ref[:, :HD]], axis=0)
     values = jnp.concatenate([before_ref[:, HD:], own_ref[:, HD:]], axis=0)
     values_t = values.astype(jnp.float32).T.astype(jnp.bfloat16)
-    for tokens in range(CORES):
+    for tokens, x_ref in enumerate((first_ref, second_ref)):
         span = slice(tokens * TOK, tokens * TOK + SPAN)
         rows = slice(tokens * TOK, (tokens + 1) * TOK)
-        queries = stacked(normed_ref, tokens)
+        inv = inv_ref[rows, :]
         for pair in range(GROUP // PAIR):
-            these = queries[pair * PAIR * TOK : (pair + 1) * PAIR * TOK]
-            scores = masked_scores(keys[span], these, tokens, any_before)
+            cols = [
+                slice(g * HD, (g + 1) * HD) for g in range(pair * PAIR, (pair + 1) * PAIR)
+            ]
+            x = [x_ref[:, at].astype(jnp.float32) for at in cols]
+            queries = jnp.concatenate(
+                [(part * inv * gain_ref[:, at]).astype(jnp.bfloat16) for part, at in zip(x, cols)],
+                axis=0,
+            )
+            scores = masked_scores(keys[span], queries, tokens, any_before)
             top = jnp.max(scores, axis=0, keepdims=True)
             terms = jnp.exp2((scores - top) * (SCALE * LOG2E))
             total = jnp.sum(terms, axis=0, keepdims=True)
             attended = jnp.dot(
                 values_t[:, span], terms.astype(jnp.bfloat16), preferred_element_type=jnp.float32
             ) * (1.0 / total)
-            for g in range(PAIR):
-                at = (pair * PAIR + g) * HD
-                cols = slice(at, at + HD)
-                out = attended[:, g * TOK : (g + 1) * TOK].T + x_ref[rows, cols].astype(jnp.float32)
-                out_ref[rows, cols] = out.astype(jnp.bfloat16)
-
-
-def forward_attention(index, normed, x, before, own):
+            for g, at in enumerate(cols):
+                out = attended[:, g * TOK : (g + 1) * TOK].T + x[g]
+                out_ref[rows, at] = out.astype(jnp.bfloat16)
+
+
+def forward_attention(index, first, second, inv_rms, gain, before, own):
     heads = pl.BlockSpec((CHIP_TOK, WIDE), lambda h, index: (0, h))
+    tokens = pl.BlockSpec((TOK, WIDE), lambda h, index: (0, h))
     kv = pl.BlockSpec((CHIP_TOK, 2 * HD), lambda h, index: (0, h))
     return pl.pallas_call(
         forward_kernel,
         grid_spec=pltpu.PrefetchScalarGridSpec(
             num_scalar_prefetch=1,
             grid=(HEADS,),
-            in_specs=[heads, heads, kv, kv],
+            in_specs=[
+                tokens,
+                tokens,
+                pl.BlockSpec((CHIP_TOK, 1), lambda h, index: (0, 0)),
+                pl.BlockSpec((1, WIDE), lambda h, index: (0, h)),
+                kv,
+                kv,
+            ],
             out_specs=heads,
         ),
-        out_shape=jax.ShapeDtypeStruct(x.shape, jnp.bfloat16),
+        out_shape=jax.ShapeDtypeStruct((CHIP_TOK, HALF), jnp.bfloat16),
         compiler_params=pltpu.CompilerParams(vmem_limit_bytes=32 * 2**20),
-        cost_estimate=pl.CostEstimate(
-            flops=4 * 10**9, bytes_accessed=8 * 2**20, transcendentals=2 * 10**6
-        ),
+        cost_estimate=BRIEF,
         name="forward_attention",
-    )(index, normed, x, before, own)
+    )(index, first, second, inv_rms, gain, before, own)
 
 
 def backward_kernel(
@@ -279,83 +323,92 @@
             jax.ShapeDtypeStruct(own.shape, jnp.float32),
         ],
         compiler_params=pltpu.CompilerParams(vmem_limit_bytes=40 * 2**20),
-        cost_estimate=pl.CostEstimate(
-            flops=4 * 10**9, bytes_accessed=8 * 2**20, transcendentals=2 * 10**6
-        ),
+        cost_estimate=BRIEF,
         name="backward_attention",
     )(index, normed, upper, before, own)
 
 
-def partial_kernel(where_ref, own_ref, after_ref, weight_ref, dq_ref, out_ref, grad_kv_ref):
-    step = pl.program_id(0)
-    steps = pl.num_programs(0) // CORES
-
-    @pl.when(step == 0)
-    def _():
-        grad_kv_ref[...] = (own_ref[...] + after_ref[...].astype(jnp.float32)).astype(jnp.bfloat16)
-
-    product = lax.dot_general(
-        grad_kv_ref[...], weight_ref[...], (((1,), (1,)), ((), ())), preferred_element_type=jnp.float32
-    )
-    here = step // steps == where_ref[1]
-
-    @pl.when(here)
-    def _():
-        out_ref[...] = (product + dq_ref[...]).astype(out_ref.dtype)
-
-    @pl.when(jnp.logical_not(here))
-    def _():
-        out_ref[...] = product.astype(out_ref.dtype)
-
-
-def partial_grad(row, core, own, after, weight, dq, kind):
-    features, half = weight.shape
-    width = 1024
-    steps = features // width // CORES
-    rows = pl.BlockSpec((TOK, half), lambda j, where: (where[0], 0))
+def piece_columns(y, pieces):
+    firsts, at = [], 0
+    block = pieces[0].shape[0]
+    for piece in pieces:
+        firsts.append(pl.multiple_of(((y + at // block) % Y) * block, block) + at % block)
+        at += piece.shape[0]
+    return firsts
+
+
+def project_kernel(y_ref, normed_ref, *refs):
+    *pieces, out_ref = refs
+    total = jnp.zeros(out_ref.shape, jnp.float32)
+    for first, piece in zip(piece_columns(y_ref[0], pieces), pieces):
+        rows = piece.shape[0]
+        part = normed_ref[:, pl.ds(pl.multiple_of(first, rows), rows)]
+        total += jnp.dot(part, piece[...], preferred_element_type=jnp.float32)
+    out_ref[...] = total.astype(out_ref.dtype)
+
+
+SCALARS = pl.BlockSpec(memory_space=pltpu.SMEM)
+WHOLE = pl.BlockSpec(memory_space=pltpu.VMEM)
+
+
+def project(y, normed, pieces):
+    return pl.pallas_call(
+        project_kernel,
+        in_specs=[SCALARS] + [WHOLE] * (1 + len(pieces)),
+        out_specs=WHOLE,
+        out_shape=jax.ShapeDtypeStruct((normed.shape[0], pieces[0].shape[1]), jnp.bfloat16),
+        compiler_params=pltpu.CompilerParams(vmem_limit_bytes=32 * 2**20),
+        cost_estimate=BRIEF,
+        name="project",
+    )(y, normed, *pieces)
+
+
+def partial_kernel(where_ref, own_ref, after_ref, dq_ref, x_ref, inv_ref, gain_in_ref, *refs):
+    *pieces, out_ref, gain_ref = refs
+    core, y = where_ref[1], where_ref[2]
+    rows = pl.ds(pl.multiple_of(where_ref[0] * TOK, TOK), TOK)
+    grad_kv = (own_ref[rows, :] + after_ref[rows, :].astype(jnp.float32)).astype(jnp.bfloat16)
+    inv = inv_ref[rows, :]
+    for first, piece in zip(piece_columns(y, pieces), pieces):
+        count = piece.shape[0]
+        cols = pl.ds(pl.multiple_of(first, count), count)
+        grad = lax.dot_general(
+            grad_kv, piece[...], (((1,), (1,)), ((), ())), preferred_element_type=jnp.float32
+        )
+        dq = dq_ref[rows, pl.ds(pl.multiple_of(first % HALF, count), count)]
+        grad += jnp.where(first // HALF == core, dq, 0.0)
+        out_ref[:, cols] = grad.astype(out_ref.dtype)
+        scaled = x_ref[rows, cols].astype(jnp.float32) * inv
+        gain_ref[:, cols] = gain_in_ref[:, cols] + jnp.sum(grad * scaled, axis=0, keepdims=True)
+
+
+def partial_grad(where, own, after, dq, x, inv_rms, gain_grad, pieces, kind):
+    features = x.shape[1]
     return pl.pallas_call(
         partial_kernel,
-        grid_spec=pltpu.PrefetchScalarGridSpec(
-            num_scalar_prefetch=1,
-            grid=(features // width,),
-            in_specs=[
-                rows,
-                rows,
-                pl.BlockSpec((width, half), lambda j, where: (j, 0)),
-                pl.BlockSpec((TOK, width), lambda j, where: (where[0], j % steps)),
-            ],
-            out_specs=pl.BlockSpec((TOK, width), lambda j, where: (0, j)),
-            scratch_shapes=[pltpu.VMEM((TOK, half), jnp.bfloat16)],
-        ),
-        out_shape=jax.ShapeDtypeStruct((TOK, features), kind),
-        compiler_params=pltpu.CompilerParams(vmem_limit_bytes=32 * 2**20),
-        cost_estimate=pl.CostEstimate(
-            flops=10**9, bytes_accessed=8 * 2**20, transcendentals=0
-        ),
+        in_specs=[SCALARS] + [WHOLE] * (6 + len(pieces)),
+        out_specs=[WHOLE, WHOLE],
+        out_shape=[
+            jax.ShapeDtypeStruct((TOK, features), kind),
+            jax.ShapeDtypeStruct((1, features), jnp.float32),
+        ],
+        compiler_params=pltpu.CompilerParams(vmem_limit_bytes=40 * 2**20),
+        cost_estimate=BRIEF,
         name="partial_grad",
-    )(jnp.stack([row, core]).astype(jnp.int32), own, after, weight, dq)
-
-
-def input_grad_kernel(
-    own_ref, other_ref, x_ref, upper_ref, gain_ref, up_ref, down_ref, gain_grad_ref, grad_ref
-):
+    )(where, own, after, dq, x, inv_rms, gain_grad, *pieces)
+
+
+def input_grad_kernel(own_ref, other_ref, x_ref, inv_ref, upper_ref, gain_ref, up_ref, down_ref, grad_ref):
     features = x_ref.shape[1]
     width = 512
     blocks = [slice(at, at + width) for at in range(0, features, width)]
-    squares = jnp.zeros((TOK, 1), jnp.float32)
-    for cols in blocks:
-        part = x_ref[:, cols].astype(jnp.float32)
-        squares += jnp.sum(part * part, axis=-1, keepdims=True)
-    inv_rms = lax.rsqrt(squares / features + EPSILON)
+    inv_rms = inv_ref[...]
     inner = jnp.zeros((TOK, 1), jnp.float32)
     for cols in blocks:
-        grad = own_ref[:, cols] + other_ref[:, cols].astype(jnp.float32)
+        grad = (own_ref[:, cols] + other_ref[:, cols].astype(jnp.float32)) * gain_ref[:, cols]
         scaled = x_ref[:, cols].astype(jnp.float32) * inv_rms
-        product = grad * scaled
-        gain_grad_ref[:, cols] = jnp.sum(product, axis=0, keepdims=True)
-        gain = gain_ref[:, cols]
-        inner += jnp.sum(product * gain, axis=-1, keepdims=True)
-        grad_ref[:, cols] = grad * gain
+        inner += jnp.sum(grad * scaled, axis=-1, keepdims=True)
+        grad_ref[:, cols] = grad
     mean = inner * (1.0 / features)
     for first, ref in ((0, up_ref), (TOK // 2, down_ref)):
         rows = slice(first, first + TOK // 2)
@@ -366,78 +419,98 @@
             ref[:, cols] = (out + upper_ref[rows, cols].astype(jnp.float32)).astype(jnp.bfloat16)
 
 
-def input_grad(own, other, x, upper, gain_row):
+def input_grad(own, other, x, inv_rms, upper, gain_row):
     features = x.shape[1]
     return pl.pallas_call(
         input_grad_kernel,
-        out_shape=[
-            jax.ShapeDtypeStruct((TOK // 2, features), jnp.bfloat16),
-            jax.ShapeDtypeStruct((TOK // 2, features), jnp.bfloat16),
-            jax.ShapeDtypeStruct((1, features), jnp.float32),
-        ],
+        in_specs=[WHOLE] * 6,
+        out_specs=[WHOLE, WHOLE],
+        out_shape=[jax.ShapeDtypeStruct((TOK // 2, features), jnp.bfloat16)] * 2,
         scratch_shapes=[pltpu.VMEM((TOK, features), jnp.float32)],
         compiler_params=pltpu.CompilerParams(vmem_limit_bytes=32 * 2**20),
-        cost_estimate=pl.CostEstimate(
-            flops=10**7, bytes_accessed=8 * 2**20, transcendentals=10**3
-        ),
+        cost_estimate=BRIEF,
         name="input_grad",
-    )(own, other, x, upper, gain_row)
+    )(own, other, x, inv_rms, upper, gain_row)
 
 
 def body(section_in, back_in, upstream, gains, kv_weight):
     index = lax.axis_index("ctx").astype(jnp.int32)
-    core = index % CORES
-    place = index.reshape(1)
+    core, z_lo, y = index % CORES, (index // CORES) % Z_LO, index // (CORES * Z_LO)
+    place, y_place = index.reshape(1), y.reshape(1)
     x_back, upper_in = back_in[0], upstream[0]
 
-    w_mine = gather_weight(kv_weight[0], core)
-    x_parts = land(set_out(section_in[0, : TOK // 2], section_in[0, TOK // 2 :]), 1)
-    peers = lax.axis_size("section")
-    next_section = [(i, (i + 1) % peers) for i in range(peers)]
-    gain_here = lax.ppermute(gains, "section", next_section)
-
-    normed_back = norm_forward(x_back, gains)
-    normed_fwd = norm_forward(section_in[0], gains)
-    partner = swap(jnp.concatenate([normed_back, normed_fwd], axis=0))
-    chip_back = chip_rows(normed_back, partner[:TOK], core)
-    chip_fwd = chip_rows(normed_fwd, partner[TOK:], core)
-    chip_upper = chip_columns(upper_in, core)
-
-    x_here = jnp.concatenate(x_parts, axis=0)
-    normed_here = norm_forward(x_here, gain_here)
-    swapped = swap(
-        jnp.concatenate([columns_of(normed_here, 1 - core), columns_of(x_here, 1 - core)], axis=0)
-    )
-    chip_normed_here = chip_rows(columns_of(normed_here, core), swapped[:TOK], core)
-    chip_x_here = chip_rows(columns_of(x_here, core), swapped[TOK:], core)
-
-    chip_back, chip_fwd, chip_upper, chip_normed_here, chip_x_here = lax.optimization_barrier(
-        (chip_back, chip_fwd, chip_upper, chip_normed_here, chip_x_here)
-    )
-
-    def project(normed):
-        return jnp.dot(normed, w_mine, preferred_element_type=jnp.float32).astype(jnp.bfloat16)
-
-    kv_back = project(chip_back)
+    chip_x_fwd = chip_rows(section_in[0], swap(section_in[0]), core)
+    run = gather_run(kv_weight[0], core, z_lo)
+    later_x, later_upper, run = lax.optimization_barrier((x_back, upper_in, run))
+    chip_x_back = chip_rows(x_back, swap(later_x), core)
+    chip_back, inv_back = norm_forward(chip_x_back, gains)
+    chip_fwd, inv_fwd = norm_forward(chip_x_fwd, gains)
+    chip_upper = chip_columns(later_upper, core)
+
+    crossing = columns_of(chip_x_fwd, core)
+    norms = direct(
+        jnp.concatenate([columns_of(gains, core), inv_fwd.reshape(1, CHIP_TOK)], axis=1), 1
+    )
+
+    def first_out(after):
+        part, _ = lax.optimization_barrier((crossing[:TOK], after))
+        return halfway(part, 1)
+
+    def second_out(after):
+        part, _ = lax.optimization_barrier((crossing[TOK:], after))
+        return halfway(part, -1)
+
+    def first_in(part):
+        return arrive(part, 1, 1)
+
+    pieces, first_here, second_half = gather_weight(run, (first_out, second_out, first_in))
+    chip_back, chip_fwd, chip_upper, norms = lax.optimization_barrier(
+        (chip_back, chip_fwd, chip_upper, norms)
+    )
+    second_here = arrive(second_half, -1, 1)
+
+    kv_back = project(y_place, chip_back, pieces)
     before = to_next_chip(kv_back)
-    kv_fwd = project(chip_fwd)
-    kv_here = lax.ppermute(kv_fwd, "section", next_section)
+    kv_here = direct(project(y_place, chip_fwd, pieces), 1)
 
     dq, grad_before, grad_own = backward_attention(place, chip_back, chip_upper, before, kv_back)
-    after, kv_here = lax.optimization_barrier((to_chip_before(grad_before), kv_here))
-    before_here = to_next_chip(kv_here)
-
-    away = partial_grad(1 - core, core, grad_own, after, w_mine, dq, jnp.bfloat16)
-    home = partial_grad(core, core, grad_own, after, w_mine, dq, jnp.float32)
-    away, home, before_here = lax.optimization_barrier((swap(away), home, before_here))
-    up, down, gain_part = input_grad(home, away, x_back, upper_in, gains)
-    next_grad = jnp.concatenate(land(set_out(up, down), -1), axis=0)
-    gain_total = jnp.sum(
-        lax.all_gather(gain_part, "ctx", axis=0, tiled=True), axis=0, keepdims=True
-    )
-
-    chip_x_here, _ = lax.optimization_barrier((chip_x_here, up))
-    out = forward_attention(place, chip_normed_here, chip_x_here, before_here, kv_here)
+    after, kv_here, second_here = lax.optimization_barrier(
+        (to_chip_before(grad_before), kv_here, second_here)
+    )
+
+    def partial(row, gain_grad, kind):
+        where = jnp.stack([row, core, y])
+        return partial_grad(
+            where, grad_own, after, dq, chip_x_back, inv_back, gain_grad, pieces, kind
+        )
+
+    away, gain_grad = partial(1 - core, jnp.zeros_like(gains), jnp.bfloat16)
+    away = swap(away)
+    home, gain_grad = partial(core, gain_grad, jnp.float32)
+    gain_grad = gain_grad + over_ctx(gain_grad, lambda y, z, c: (y, z ^ 1, c))
+    gain_grad = gain_grad + over_ctx(gain_grad, lambda y, z, c: (y, z ^ 2, c))
+    inv_own = lax.dynamic_slice_in_dim(inv_back, core * TOK, TOK, 0)
+    up, down = input_grad(home, away, x_back, inv_own, upper_in, gains)
+    up, gain_grad = lax.optimization_barrier((up, gain_grad))
+    up_half, down_half = halfway(up, 1), halfway(down, -1)
+
+    gain_grad = gain_grad + swap(gain_grad)
+    up_half, down_half, gain_grad = lax.optimization_barrier((up_half, down_half, gain_grad))
+    next_grad = jnp.concatenate([arrive(up_half, 1, -1), arrive(down_half, -1, -1)], axis=0)
+    rings = [[(y * Z_LO + z) * CORES + c for y in range(Y)] for z in range(Z_LO) for c in range(CORES)]
+    gathered = lax.all_gather(gain_grad, "ctx", axis_index_groups=rings, axis=0, tiled=True)
+    gain_total = jnp.sum(gathered, axis=0, keepdims=True)
+
+    kv_here, norms, _ = lax.optimization_barrier((kv_here, norms, up))
+    out = forward_attention(
+        place,
+        first_here,
+        second_here,
+        norms[:, HALF:].reshape(CHIP_TOK, 1),
+        norms[:, :HALF],
+        to_next_chip(kv_here),
+        kv_here,
+    )
     first, second = out[:TOK], out[TOK:]
     mine = jnp.where(core == 0, first, second)
     other = swap(jnp.where(core == 0, second, first))

time: 401 us -> 272 us (0.68)
  the two profiles are of different devices: /device:TPU:1 before, /device:TPU:84 now
where the time goes in v3:
time: 272 us; the launch traced here: 270 us
  starting transfers between devices  131 us (48%)
  waiting for transfers between devices  56.5 us (21%)
  blocking collectives  27.8 us (10%)
  Pallas kernels  27.4 us (10%)
  local copies, waits for them, and re-layouts  13.8 us (5%)
  other arithmetic  11.9 us (4%)
    ppermute x20, starting transfers between devices, over_ctx(): return lax.ppermute(value, 'ctx', ctx_pairs(move))  56.7 us
    ppermute x8, starting transfers between devices, over_grid(): return lax.ppermute(value, ('section', 'ctx'), grid_pairs(move))  46.4 us
    all_gather x1, blocking collectives, body(): lax.all_gather(gain_grad, 'ctx', axis_index_groups=rings, axis=0, tiled=T...  27.8 us
    ppermute x2, starting transfers between devices, direct(): lax.ppermute(value, 'section', [(i, (i + distance) % peers) for i in rang...  19.6 us
    ppermute x20, waiting for transfers between devices, over_ctx(): return lax.ppermute(value, 'ctx', ctx_pairs(move))  19 us
    ppermute x8, waiting for transfers between devices, over_grid(): return lax.ppermute(value, ('section', 'ctx'), grid_pairs(move))  11.9 us
    ppermute x2, waiting for transfers between devices, to_next_chip(): return lax.ppermute(value, 'ctx', pairs)  11 us
    unnamed x91, local copies, waits for them, and re-layouts  10.9 us
  transfers between devices with their start and end apart: 33, of which 13 were waited for; matrix products, arithmetic and copies ran while one was open for 5% of the time, Pallas kernels for 7%

profile of v3, /device:TPU:84, one launch (start us, length us, event | category | flops | bytes accessed | tf_op | source)
XLA Modules:
  0.0 270.3 jit_solution(12040948536058660950)
XLA Ops:
  6.8 6.1 %collective-permute-start.2 = (bf16[128,512]{1,0:T(8,128)(2,1)S(1)}, bf16[128,512]{1,0:T(8,128)(2,1)S(1)}, u32[]{:S(2)}, u32[]{:S(2)}) collective-permute-start(bf16[128,512]{1,0:T(8,128)(2,1)S(1)} %pad_maximum_fusion.3), channel_id=1, source_target_pairs={{0,4},{1,5},{2,6},{3,7},{4,0},{5,1},{6,2},{7,3},{8,12},{9,13},{10,... | collective-permute-start | bytes 393224 | tf_op jit(solution)/shard_map/ppermute | solution.py:42
  13.0 5.0 %collective-permute-start.3 = (bf16[128,512]{1,0:T(8,128)(2,1)S(1)}, bf16[128,512]{1,0:T(8,128)(2,1)S(1)}, u32[]{:S(2)}, u32[]{:S(2)}) collective-permute-start(bf16[128,512]{1,0:T(8,128)(2,1)S(1)} %pad_maximum_fusion.3), channel_id=1, source_target_pairs={{0,2},{1,3},{2,4},{3,5},{4,6},{5,7},{6,0},{7,1},{8,10},{9,11},{10,... | collective-permute-start | bytes 393224 | tf_op jit(solution)/shard_map/ppermute | solution.py:42
  18.0 2.7 %collective-permute-done.2 = bf16[128,512]{1,0:T(8,128)(2,1)S(1)} collective-permute-done((bf16[128,512]{1,0:T(8,128)(2,1)S(1)}, bf16[128,512]{1,0:T(8,128)(2,1)S(1)}, u32[]{:S(2)}, u32[]{:S(2)}) %collective-permute-start.2) | collective-permute-done | bytes 131104 | tf_op jit(solution)/shard_map/ppermute | solution.py:42
  20.7 2.7 %collective-permute-done.3 = bf16[128,512]{1,0:T(8,128)(2,1)S(1)} collective-permute-done((bf16[128,512]{1,0:T(8,128)(2,1)S(1)}, bf16[128,512]{1,0:T(8,128)(2,1)S(1)}, u32[]{:S(2)}, u32[]{:S(2)}) %collective-permute-start.3) | collective-permute-done | bytes 131104 | tf_op jit(solution)/shard_map/ppermute | solution.py:42
  23.6 3.5 %collective-permute-start.4 = (bf16[512,512]{1,0:T(8,128)(2,1)S(1)}, bf16[512,512]{1,0:T(8,128)(2,1)S(1)}, u32[]{:S(2)}, u32[]{:S(2)}) collective-permute-start(bf16[512,512]{1,0:T(8,128)(2,1)S(1)} %constant_dynamic-slice_fusion.2.refs_0_), channel_id=1, source_target_pairs={{0,8},{1,9},{2,10},{3,11},{4,12},{5,13},{6,14},{7,15},{8,16},{9,17... | collective-permute-start | bytes 1572872 | tf_op jit(solution)/shard_map/ppermute | solution.py:42
  31.4 2.4 collective-permute-start.8
  36.0 3.4 %collective-permute-done.4.refs_8_ = bf16[512,512]{1,0:T(8,128)(2,1)S(1)} collective-permute-done((bf16[512,512]{1,0:T(8,128)(2,1)S(1)}, bf16[512,512]{1,0:T(8,128)(2,1)S(1)}, u32[]{:S(2)}, u32[]{:S(2)}) %collective-permute-start.4) | collective-permute-done | bytes 524320 | tf_op jit(solution)/shard_map/ppermute | solution.py:42
  39.3 3.8 %collective-permute-start.5 = (bf16[512,512]{1,0:T(8,128)(2,1)S(1)}, bf16[512,512]{1,0:T(8,128)(2,1)S(1)}, u32[]{:S(2)}, u32[]{:S(2)}) collective-permute-start(bf16[512,512]{1,0:T(8,128)(2,1)S(1)} %collective-permute-done.4.refs_8_), channel_id=1, source_target_pairs={{0,8},{1,9},{2,10},{3,11},{4,12},{5,13},{6,14},{7,15},{8,16},{9,17... | collective-permute-start | bytes 1572872 | tf_op jit(solution)/shard_map/ppermute | solution.py:42
  49.5 3.0 %collective-permute-start.9 = (bf16[128,2048]{1,0:T(8,128)(2,1)S(1)}, bf16[128,2048]{1,0:T(8,128)(2,1)S(1)}, u32[]{:S(2)}, u32[]{:S(2)}) collective-permute-start(bf16[128,2048]{1,0:T(8,128)(2,1)S(1)} %get-tuple-element.41), channel_id=1, source_target_pairs={{0,4},{1,5},{8,12},{9,13},{16,20},{17,21},{24,28},{25,29},{32,36},... | collective-permute-start | bytes 1572872 | tf_op jit(solution)/shard_map/ppermute | solution.py:60
  53.1 8.2 %collective-permute-start.18 = (f32[1,2304]{1,0:T(1,128)S(1)}, f32[1,2304]{1,0:T(1,128)S(1)}, u32[]{:S(2)}, u32[]{:S(2)}) collective-permute-start(f32[1,2304]{1,0:T(1,128)S(1)} %pad_maximum_fusion.6), channel_id=1, source_target_pairs={{0,64},{64,128},{128,192},{192,256},{256,320},{320,384},{384,448},... | collective-permute-start | bytes 27656 | tf_op jit(solution)/shard_map/ppermute | solution.py:78
  61.3 5.5 %collective-permute-start.12 = (bf16[128,2048]{1,0:T(8,128)(2,1)S(1)}, bf16[128,2048]{1,0:T(8,128)(2,1)}, u32[]{:S(2)}, u32[]{:S(2)}) collective-permute-start(bf16[128,2048]{1,0:T(8,128)(2,1)S(1)} %get-tuple-element.44), channel_id=1, source_target_pairs={{0,68},{1,69},{8,76},{9,77},{16,84},{17,85},{24,92},{25,93},{32,10... | collective-permute-start | bytes 1572872 | tf_op jit(solution)/shard_map/ppermute | solution.py:60
  67.5 4.9 %collective-permute-start.10 = (bf16[512,512]{1,0:T(8,128)(2,1)S(1)}, bf16[512,512]{1,0:T(8,128)(2,1)S(1)}, u32[]{:S(2)}, u32[]{:S(2)}) collective-permute-start(bf16[512,512]{1,0:T(8,128)(2,1)S(1)} %collective-permute-done.5.refs_7_), channel_id=1, source_target_pairs={{0,8},{1,9},{2,10},{3,11},{4,12},{5,13},{6,14},{7,15},{8,16},{9,17... | collective-permute-start | bytes 1572872 | tf_op jit(solution)/shard_map/ppermute | solution.py:42
  75.1 15.5 %collective-permute-start.15 = (bf16[128,2048]{1,0:T(8,128)(2,1)S(1)}, bf16[128,2048]{1,0:T(8,128)(2,1)S(1)}, u32[]{:S(2)}, u32[]{:S(2)}) collective-permute-start(bf16[128,2048]{1,0:T(8,128)(2,1)S(1)} %collective-permute-done.9), channel_id=1, source_target_pairs={{0,132},{1,133},{8,140},{9,141},{16,148},{17,149},{24,156},{25,157... | collective-permute-start | bytes 1572872 | tf_op jit(solution)/shard_map/ppermute | solution.py:60
  90.7 4.9 %collective-permute-start.13 = (bf16[256,512]{1,0:T(8,128)(2,1)S(1)}, bf16[256,512]{1,0:T(8,128)(2,1)S(1)}, u32[]{:S(2)}, u32[]{:S(2)}) collective-permute-start(bf16[256,512]{1,0:T(8,128)(2,1)S(1)} %slice.62), channel_id=1, source_target_pairs={{0,8},{1,9},{2,10},{3,11},{4,12},{5,13},{6,14},{7,15},{8,16},{9,17... | collective-permute-start | bytes 786440 | tf_op jit(solution)/shard_map/ppermute | solution.py:42
  99.6 11.3 %collective-permute-done.15.first_ref = bf16[128,2048]{1,0:T(8,128)(2,1)S(1)} collective-permute-done((bf16[128,2048]{1,0:T(8,128)(2,1)S(1)}, bf16[128,2048]{1,0:T(8,128)(2,1)S(1)}, u32[]{:S(2)}, u32[]{:S(2)}) %collective-permute-start.15) | collective-permute-done | bytes 524320 | tf_op jit(solution)/shard_map/ppermute | solution.py:60
  113.0 4.3 %collective-permute-start.19 = (bf16[256,512]{1,0:T(8,128)(2,1)}, bf16[256,512]{1,0:T(8,128)(2,1)}, u32[]{:S(2)}, u32[]{:S(2)}) collective-permute-start(bf16[256,512]{1,0:T(8,128)(2,1)} %project.2.own_ref), channel_id=1, source_target_pairs={{0,2},{1,3},{2,4},{3,5},{4,6},{5,7},{6,8},{7,9},{8,10},{9,11},{10,... | collective-permute-start | bytes 786440 | tf_op jit(solution)/shard_map/ppermute | solution.py:150
  117.3 5.6 %collective-permute-start.22 = (bf16[128,2048]{1,0:T(8,128)(2,1)}, bf16[128,2048]{1,0:T(8,128)(2,1)}, u32[]{:S(2)}, u32[]{:S(2)}) collective-permute-start(bf16[128,2048]{1,0:T(8,128)(2,1)} %collective-permute-done.12), channel_id=1, source_target_pairs={{0,68},{1,69},{8,76},{9,77},{16,84},{17,85},{24,92},{25,93},{32,10... | collective-permute-start | bytes 1572872 | tf_op jit(solution)/shard_map/ppermute | solution.py:60
  133.4 11.4 %collective-permute-start.21 = (bf16[256,512]{1,0:T(8,128)(2,1)S(1)}, bf16[256,512]{1,0:T(8,128)(2,1)S(1)}, u32[]{:S(2)}, u32[]{:S(2)}) collective-permute-start(bf16[256,512]{1,0:T(8,128)(2,1)S(1)} %project.3), channel_id=1, source_target_pairs={{0,64},{64,128},{128,192},{192,256},{256,320},{320,384},{384,448},... | collective-permute-start | bytes 786440 | tf_op jit(solution)/shard_map/ppermute | solution.py:78
  144.8 7.9 %backward_attention.1 = (f32[256,2048]{1,0:T(8,128)S(1)}, bf16[256,512]{1,0:T(8,128)(2,1)S(1)}, f32[256,512]{1,0:T(8,128)S(1)}) custom-call(s32[1]{0:T(128)} %bitcast.index_ref, bf16[256,4096]{1,0:T(8,128)(2,1)S(1)} %get-tuple-element.51.normed_ref, bf16[256,2048]{1,0:T(8,128)(2,1)S(1)} %copy-done.20, bf16[256,512]{1,0:T(8,128)(2,1)} %collective-permute-done.19.before_ref, ...), custom_call_target="tpu_custom_call" | custom-call | flops 1000 | bytes 1000 | tf_op jit(solution)/shard_map/backward_attention/pallas_call | solution.py:303
  155.2 8.4 %collective-permute-done.21.own_ref = bf16[256,512]{1,0:T(8,128)(2,1)S(1)} collective-permute-done((bf16[256,512]{1,0:T(8,128)(2,1)S(1)}, bf16[256,512]{1,0:T(8,128)(2,1)S(1)}, u32[]{:S(2)}, u32[]{:S(2)}) %collective-permute-start.21) | collective-permute-done | bytes 262176 | tf_op jit(solution)/shard_map/ppermute | solution.py:78
  163.6 6.1 %collective-permute-done.20.after_ref = bf16[256,512]{1,0:T(8,128)(2,1)S(1)} collective-permute-done((bf16[256,512]{1,0:T(8,128)(2,1)S(1)}, bf16[256,512]{1,0:T(8,128)(2,1)S(1)}, u32[]{:S(2)}, u32[]{:S(2)}) %collective-permute-start.20) | collective-permute-done | bytes 262176 | tf_op jit(solution)/shard_map/ppermute | solution.py:155
  169.9 3.1 %partial_grad.2 = (bf16[128,4096]{1,0:T(8,128)(2,1)}, f32[1,4096]{1,0:T(1,128)S(1)}) custom-call(s32[3]{0:T(128)S(1)} %copy-done.33, f32[256,512]{1,0:T(8,128)S(1)} %get-tuple-element.61.own_ref, bf16[256,512]{1,0:T(8,128)(2,1)S(1)} %collective-permute-done.20.after_ref, f32[256,2048]{1,0:T(8,128)S(1)} %get-tuple-element.63.dq_ref, ...), custom_call_target="tpu_custom_call" | custom-call | flops 1000 | bytes 1000 | tf_op jit(solution)/shard_map/partial_grad/pallas_call | solution.py:387
  175.1 2.7 partial_grad.3
  181.0 3.9 %collective-permute-done.24 = f32[1,4096]{1,0:T(1,128)S(1)} collective-permute-done((f32[1,4096]{1,0:T(1,128)}, f32[1,4096]{1,0:T(1,128)S(1)}, u32[]{:S(2)}, u32[]{:S(2)}) %collective-permute-start.24) | collective-permute-done | bytes 16416 | tf_op jit(solution)/shard_map/ppermute | solution.py:42
  188.5 3.7 %collective-permute-done.25 = f32[1,4096]{1,0:T(1,128)S(1)} collective-permute-done((f32[1,4096]{1,0:T(1,128)S(1)}, f32[1,4096]{1,0:T(1,128)S(1)}, u32[]{:S(2)}, u32[]{:S(2)}) %collective-permute-start.25) | collective-permute-done | bytes 16416 | tf_op jit(solution)/shard_map/ppermute | solution.py:42
  193.9 3.1 %input_grad.1 = (bf16[64,4096]{1,0:T(8,128)(2,1)}, bf16[64,4096]{1,0:T(8,128)(2,1)S(1)}) custom-call(f32[128,4096]{1,0:T(8,128)S(1)} %copy-done.27, bf16[128,4096]{1,0:T(8,128)(2,1)} %collective-permute-done.23.other_ref, bf16[128,4096]{1,0:T(8,128)(2,1)S(1)} %bitcast.26, f32[128,1]{1,0:T(8,128)S(1)} %copy.15.inv_ref, bf16[128,4096]{1,0:T(8,128)(2,1)S(1)} %bitcast.29, ...), custom_call_target="tpu_custom_call" | custom-call | flops 1000 | bytes 1000 | tf_op jit(solution)/shard_map/input_grad/pallas_call | solution.py:424
  198.9 6.6 %collective-permute-start.28 = (bf16[64,4096]{1,0:T(8,128)(2,1)}, bf16[64,4096]{1,0:T(8,128)(2,1)}, u32[]{:S(2)}, u32[]{:S(2)}) collective-permute-start(bf16[64,4096]{1,0:T(8,128)(2,1)} %get-tuple-element.69), channel_id=1, source_target_pairs={{0,4},{1,5},{8,12},{9,13},{16,20},{17,21},{24,28},{25,29},{32,36},... | collective-permute-start | bytes 1572872 | tf_op jit(solution)/shard_map/ppermute | solution.py:60
  207.6 11.0 %collective-permute-done.26.before_ref = bf16[256,512]{1,0:T(8,128)(2,1)S(1)} collective-permute-done((bf16[256,512]{1,0:T(8,128)(2,1)S(1)}, bf16[256,512]{1,0:T(8,128)(2,1)S(1)}, u32[]{:S(2)}, u32[]{:S(2)}) %collective-permute-start.26) | collective-permute-done | bytes 262176 | tf_op jit(solution)/shard_map/ppermute | solution.py:150
  218.6 7.5 %forward_attention.1 = bf16[256,2048]{1,0:T(8,128)(2,1)S(1)} custom-call(s32[1]{0:T(128)} %bitcast.index_ref, bf16[128,2048]{1,0:T(8,128)(2,1)S(1)} %copy-done.29, bf16[128,2048]{1,0:T(8,128)(2,1)} %collective-permute-done.22.second_ref, f32[256,1]{1,0:T(8,128)S(1)} %copy.16.inv_ref, f32[1,2048]{1,0:T(1,128)S(1)} %slice.65.gain_ref, ...), custom_call_target="tpu_custom_call" | custom-call | flops 1000 | bytes 1000 | tf_op jit(solution)/shard_map/forward_attention/pallas_call | solution.py:228
  231.3 2.4 collective-permute-start.31
  233.7 5.8 %collective-permute-start.32 = (bf16[64,4096]{1,0:T(8,128)(2,1)}, bf16[64,4096]{1,0:T(8,128)(2,1)S(1)}, u32[]{:S(2)}, u32[]{:S(2)}) collective-permute-start(bf16[64,4096]{1,0:T(8,128)(2,1)} %collective-permute-done.29), channel_id=1, source_target_pairs={{0,452},{1,453},{8,460},{9,461},{16,468},{17,469},{24,476},{25,477... | collective-permute-start | bytes 1572872 | tf_op jit(solution)/shard_map/ppermute | solution.py:60
  239.6 27.8 %all-gather = f32[8,1,4096]{2,1,0:T(1,128)S(1)} all-gather(f32[1,1,4096]{2,1,0:T(1,128)S(1)} %bitcast.33), channel_id=1, replica_groups={{0,8,16,24,32,40,48,56},{1,9,17,25,33,41,49,57},{2,10,18,26,34,42,50,58..., dimensions={0}, use_global_device_ids=true | all-gather | bytes 147456 | tf_op jit(solution)/shard_map/all_gather | solution.py:501
  (173 shorter events, 64.4 us)
Async XLA Ops:
  4.8 13.2 %collective-permute-start.1 = (bf16[128,512]{1,0:T(8,128)(2,1)S(1)}, bf16[128,512]{1,0:T(8,128)(2,1)S(1)}, u32[]{:S(2)}, u32[]{:S(2)}) collective-permute-start(bf16[128,512]{1,0:T(8,128)(2,1)S(1)} %pad_maximum_fusion.3), channel_id=1, source_target_pairs={{0,6},{1,7},{2,0},{3,1},{4,2},{5,3},{6,4},{7,5},{8,14},{9,15},{10,... | collective-permute-start | bytes 393224 | tf_op jit(solution)/shard_map/ppermute | solution.py:42
  6.8 13.9 %collective-permute-start.2 = (bf16[128,512]{1,0:T(8,128)(2,1)S(1)}, bf16[128,512]{1,0:T(8,128)(2,1)S(1)}, u32[]{:S(2)}, u32[]{:S(2)}) collective-permute-start(bf16[128,512]{1,0:T(8,128)(2,1)S(1)} %pad_maximum_fusion.3), channel_id=1, source_target_pairs={{0,4},{1,5},{2,6},{3,7},{4,0},{5,1},{6,2},{7,3},{8,12},{9,13},{10,... | collective-permute-start | bytes 393224 | tf_op jit(solution)/shard_map/ppermute | solution.py:42
  13.0 10.5 %collective-permute-start.3 = (bf16[128,512]{1,0:T(8,128)(2,1)S(1)}, bf16[128,512]{1,0:T(8,128)(2,1)S(1)}, u32[]{:S(2)}, u32[]{:S(2)}) collective-permute-start(bf16[128,512]{1,0:T(8,128)(2,1)S(1)} %pad_maximum_fusion.3), channel_id=1, source_target_pairs={{0,2},{1,3},{2,4},{3,5},{4,6},{5,7},{6,0},{7,1},{8,10},{9,11},{10,... | collective-permute-start | bytes 393224 | tf_op jit(solution)/shard_map/ppermute | solution.py:42
  23.6 15.7 %collective-permute-start.4 = (bf16[512,512]{1,0:T(8,128)(2,1)S(1)}, bf16[512,512]{1,0:T(8,128)(2,1)S(1)}, u32[]{:S(2)}, u32[]{:S(2)}) collective-permute-start(bf16[512,512]{1,0:T(8,128)(2,1)S(1)} %constant_dynamic-slice_fusion.2.refs_0_), channel_id=1, source_target_pairs={{0,8},{1,9},{2,10},{3,11},{4,12},{5,13},{6,14},{7,15},{8,16},{9,17... | collective-permute-start | bytes 1572872 | tf_op jit(solution)/shard_map/ppermute | solution.py:42
  27.1 16.5 %collective-permute-start.6 = (bf16[512,512]{1,0:T(8,128)(2,1)S(1)}, bf16[512,512]{1,0:T(8,128)(2,1)S(1)}, u32[]{:S(2)}, u32[]{:S(2)}) collective-permute-start(bf16[512,512]{1,0:T(8,128)(2,1)S(1)} %constant_dynamic-slice_fusion.2.refs_0_), channel_id=1, source_target_pairs={{0,56},{1,57},{2,58},{3,59},{4,60},{5,61},{6,62},{7,63},{8,0},{9,1... | collective-permute-start | bytes 1572872 | tf_op jit(solution)/shard_map/ppermute | solution.py:42
  29.5 16.0 %collective-permute-start.17 = (bf16[128,2048]{1,0:T(8,128)(2,1)S(1)}, bf16[128,2048]{1,0:T(8,128)(2,1)}, u32[]{:S(2)}, u32[]{:S(2)}) collective-permute-start(bf16[128,2048]{1,0:T(8,128)(2,1)S(1)} %constant_dynamic-slice_fusion.1), channel_id=1, source_target_pairs={{0,1},{1,0},{2,3},{3,2},{4,5},{5,4},{6,7},{7,6},{8,9},{9,8},{10,11... | collective-permute-start | bytes 1572872 | tf_op jit(solution)/shard_map/ppermute | solution.py:42
  31.4 16.6 %collective-permute-start.8 = (bf16[128,4096]{1,0:T(8,128)(2,1)}, bf16[128,4096]{1,0:T(8,128)(2,1)}, u32[]{:S(2)}, u32[]{:S(2)}) collective-permute-start(bf16[128,4096]{1,0:T(8,128)(2,1)} %bitcast.31), channel_id=1, source_target_pairs={{0,1},{1,0},{2,3},{3,2},{4,5},{5,4},{6,7},{7,6},{8,9},{9,8},{10,11... | collective-permute-start | bytes 3145736 | tf_op jit(solution)/shard_map/ppermute | solution.py:42
  33.9 40.4 %collective-permute-start.16 = (bf16[128,4096]{1,0:T(8,128)(2,1)S(1)}, bf16[128,4096]{1,0:T(8,128)(2,1)S(1)}, u32[]{:S(2)}, u32[]{:S(2)}) collective-permute-start(bf16[128,4096]{1,0:T(8,128)(2,1)S(1)} %bitcast.25), channel_id=1, source_target_pairs={{0,1},{1,0},{2,3},{3,2},{4,5},{5,4},{6,7},{7,6},{8,9},{9,8},{10,11... | collective-permute-start | bytes 3145736 | tf_op jit(solution)/shard_map/ppermute | solution.py:42
  39.3 22.0 %collective-permute-start.5 = (bf16[512,512]{1,0:T(8,128)(2,1)S(1)}, bf16[512,512]{1,0:T(8,128)(2,1)S(1)}, u32[]{:S(2)}, u32[]{:S(2)}) collective-permute-start(bf16[512,512]{1,0:T(8,128)(2,1)S(1)} %collective-permute-done.4.refs_8_), channel_id=1, source_target_pairs={{0,8},{1,9},{2,10},{3,11},{4,12},{5,13},{6,14},{7,15},{8,16},{9,17... | collective-permute-start | bytes 1572872 | tf_op jit(solution)/shard_map/ppermute | solution.py:42
  43.6 23.3 %collective-permute-start.7 = (bf16[512,512]{1,0:T(8,128)(2,1)S(1)}, bf16[512,512]{1,0:T(8,128)(2,1)S(1)}, u32[]{:S(2)}, u32[]{:S(2)}) collective-permute-start(bf16[512,512]{1,0:T(8,128)(2,1)S(1)} %collective-permute-done.6.refs_1_), channel_id=1, source_target_pairs={{0,56},{1,57},{2,58},{3,59},{4,60},{5,61},{6,62},{7,63},{8,0},{9,1... | collective-permute-start | bytes 1572872 | tf_op jit(solution)/shard_map/ppermute | solution.py:42
  49.5 18.0 %collective-permute-start.9 = (bf16[128,2048]{1,0:T(8,128)(2,1)S(1)}, bf16[128,2048]{1,0:T(8,128)(2,1)S(1)}, u32[]{:S(2)}, u32[]{:S(2)}) collective-permute-start(bf16[128,2048]{1,0:T(8,128)(2,1)S(1)} %get-tuple-element.41), channel_id=1, source_target_pairs={{0,4},{1,5},{8,12},{9,13},{16,20},{17,21},{24,28},{25,29},{32,36},... | collective-permute-start | bytes 1572872 | tf_op jit(solution)/shard_map/ppermute | solution.py:60
  53.1 46.5 %collective-permute-start.18 = (f32[1,2304]{1,0:T(1,128)S(1)}, f32[1,2304]{1,0:T(1,128)S(1)}, u32[]{:S(2)}, u32[]{:S(2)}) collective-permute-start(f32[1,2304]{1,0:T(1,128)S(1)} %pad_maximum_fusion.6), channel_id=1, source_target_pairs={{0,64},{64,128},{128,192},{192,256},{256,320},{320,384},{384,448},... | collective-permute-start | bytes 27656 | tf_op jit(solution)/shard_map/ppermute | solution.py:78
  61.3 29.3 %collective-permute-start.12 = (bf16[128,2048]{1,0:T(8,128)(2,1)S(1)}, bf16[128,2048]{1,0:T(8,128)(2,1)}, u32[]{:S(2)}, u32[]{:S(2)}) collective-permute-start(bf16[128,2048]{1,0:T(8,128)(2,1)S(1)} %get-tuple-element.44), channel_id=1, source_target_pairs={{0,68},{1,69},{8,76},{9,77},{16,84},{17,85},{24,92},{25,93},{32,10... | collective-permute-start | bytes 1572872 | tf_op jit(solution)/shard_map/ppermute | solution.py:60
  67.5 23.1 %collective-permute-start.10 = (bf16[512,512]{1,0:T(8,128)(2,1)S(1)}, bf16[512,512]{1,0:T(8,128)(2,1)S(1)}, u32[]{:S(2)}, u32[]{:S(2)}) collective-permute-start(bf16[512,512]{1,0:T(8,128)(2,1)S(1)} %collective-permute-done.5.refs_7_), channel_id=1, source_target_pairs={{0,8},{1,9},{2,10},{3,11},{4,12},{5,13},{6,14},{7,15},{8,16},{9,17... | collective-permute-start | bytes 1572872 | tf_op jit(solution)/shard_map/ppermute | solution.py:42
  72.4 18.3 %collective-permute-start.11 = (bf16[512,512]{1,0:T(8,128)(2,1)S(1)}, bf16[512,512]{1,0:T(8,128)(2,1)S(1)}, u32[]{:S(2)}, u32[]{:S(2)}) collective-permute-start(bf16[512,512]{1,0:T(8,128)(2,1)S(1)} %collective-permute-done.7.refs_2_), channel_id=1, source_target_pairs={{0,56},{1,57},{2,58},{3,59},{4,60},{5,61},{6,62},{7,63},{8,0},{9,1... | collective-permute-start | bytes 1572872 | tf_op jit(solution)/shard_map/ppermute | solution.py:42
  75.1 35.8 %collective-permute-start.15 = (bf16[128,2048]{1,0:T(8,128)(2,1)S(1)}, bf16[128,2048]{1,0:T(8,128)(2,1)S(1)}, u32[]{:S(2)}, u32[]{:S(2)}) collective-permute-start(bf16[128,2048]{1,0:T(8,128)(2,1)S(1)} %collective-permute-done.9), channel_id=1, source_target_pairs={{0,132},{1,133},{8,140},{9,141},{16,148},{17,149},{24,156},{25,157... | collective-permute-start | bytes 1572872 | tf_op jit(solution)/shard_map/ppermute | solution.py:60
  90.7 20.2 %collective-permute-start.13 = (bf16[256,512]{1,0:T(8,128)(2,1)S(1)}, bf16[256,512]{1,0:T(8,128)(2,1)S(1)}, u32[]{:S(2)}, u32[]{:S(2)}) collective-permute-start(bf16[256,512]{1,0:T(8,128)(2,1)S(1)} %slice.62), channel_id=1, source_target_pairs={{0,8},{1,9},{2,10},{3,11},{4,12},{5,13},{6,14},{7,15},{8,16},{9,17... | collective-permute-start | bytes 786440 | tf_op jit(solution)/shard_map/ppermute | solution.py:42
  95.6 15.3 %collective-permute-start.14 = (bf16[256,512]{1,0:T(8,128)(2,1)S(1)}, bf16[256,512]{1,0:T(8,128)(2,1)S(1)}, u32[]{:S(2)}, u32[]{:S(2)}) collective-permute-start(bf16[256,512]{1,0:T(8,128)(2,1)S(1)} %slice.63), channel_id=1, source_target_pairs={{0,56},{1,57},{2,58},{3,59},{4,60},{5,61},{6,62},{7,63},{8,0},{9,1... | collective-permute-start | bytes 786440 | tf_op jit(solution)/shard_map/ppermute | solution.py:42
  113.0 31.8 %collective-permute-start.19 = (bf16[256,512]{1,0:T(8,128)(2,1)}, bf16[256,512]{1,0:T(8,128)(2,1)}, u32[]{:S(2)}, u32[]{:S(2)}) collective-permute-start(bf16[256,512]{1,0:T(8,128)(2,1)} %project.2.own_ref), channel_id=1, source_target_pairs={{0,2},{1,3},{2,4},{3,5},{4,6},{5,7},{6,8},{7,9},{8,10},{9,11},{10,... | collective-permute-start | bytes 786440 | tf_op jit(solution)/shard_map/ppermute | solution.py:150
  117.3 46.4 %collective-permute-start.22 = (bf16[128,2048]{1,0:T(8,128)(2,1)}, bf16[128,2048]{1,0:T(8,128)(2,1)}, u32[]{:S(2)}, u32[]{:S(2)}) collective-permute-start(bf16[128,2048]{1,0:T(8,128)(2,1)} %collective-permute-done.12), channel_id=1, source_target_pairs={{0,68},{1,69},{8,76},{9,77},{16,84},{17,85},{24,92},{25,93},{32,10... | collective-permute-start | bytes 1572872 | tf_op jit(solution)/shard_map/ppermute | solution.py:60
  133.4 30.2 %collective-permute-start.21 = (bf16[256,512]{1,0:T(8,128)(2,1)S(1)}, bf16[256,512]{1,0:T(8,128)(2,1)S(1)}, u32[]{:S(2)}, u32[]{:S(2)}) collective-permute-start(bf16[256,512]{1,0:T(8,128)(2,1)S(1)} %project.3), channel_id=1, source_target_pairs={{0,64},{64,128},{128,192},{192,256},{256,320},{320,384},{384,448},... | collective-permute-start | bytes 786440 | tf_op jit(solution)/shard_map/ppermute | solution.py:78
  152.8 17.0 %collective-permute-start.20 = (bf16[256,512]{1,0:T(8,128)(2,1)S(1)}, bf16[256,512]{1,0:T(8,128)(2,1)S(1)}, u32[]{:S(2)}, u32[]{:S(2)}) collective-permute-start(bf16[256,512]{1,0:T(8,128)(2,1)S(1)} %get-tuple-element.55), channel_id=1, source_target_pairs={{2,0},{3,1},{4,2},{5,3},{6,4},{7,5},{8,6},{9,7},{10,8},{11,9},{12,... | collective-permute-start | bytes 786440 | tf_op jit(solution)/shard_map/ppermute | solution.py:155
  172.9 19.3 %collective-permute-start.23 = (bf16[128,4096]{1,0:T(8,128)(2,1)}, bf16[128,4096]{1,0:T(8,128)(2,1)}, u32[]{:S(2)}, u32[]{:S(2)}) collective-permute-start(bf16[128,4096]{1,0:T(8,128)(2,1)} %get-tuple-element.66), channel_id=1, source_target_pairs={{0,1},{1,0},{2,3},{3,2},{4,5},{5,4},{6,7},{7,6},{8,9},{9,8},{10,11... | collective-permute-start | bytes 3145736 | tf_op jit(solution)/shard_map/ppermute | solution.py:42
  179.1 5.8 %collective-permute-start.24 = (f32[1,4096]{1,0:T(1,128)}, f32[1,4096]{1,0:T(1,128)S(1)}, u32[]{:S(2)}, u32[]{:S(2)}) collective-permute-start(f32[1,4096]{1,0:T(1,128)} %get-tuple-element.68), channel_id=1, source_target_pairs={{0,2},{1,3},{2,0},{3,1},{4,6},{5,7},{6,4},{7,5},{8,10},{9,11},{10,... | collective-permute-start | bytes 49160 | tf_op jit(solution)/shard_map/ppermute | solution.py:42
  185.7 6.5 %collective-permute-start.25 = (f32[1,4096]{1,0:T(1,128)S(1)}, f32[1,4096]{1,0:T(1,128)S(1)}, u32[]{:S(2)}, u32[]{:S(2)}) collective-permute-start(f32[1,4096]{1,0:T(1,128)S(1)} %add.69), channel_id=1, source_target_pairs={{0,4},{1,5},{2,6},{3,7},{4,0},{5,1},{6,2},{7,3},{8,12},{9,13},{10,... | collective-permute-start | bytes 49160 | tf_op jit(solution)/shard_map/ppermute | solution.py:42
  196.9 21.6 %collective-permute-start.26 = (bf16[256,512]{1,0:T(8,128)(2,1)S(1)}, bf16[256,512]{1,0:T(8,128)(2,1)S(1)}, u32[]{:S(2)}, u32[]{:S(2)}) collective-permute-start(bf16[256,512]{1,0:T(8,128)(2,1)S(1)} %copy-done.31), channel_id=1, source_target_pairs={{0,2},{1,3},{2,4},{3,5},{4,6},{5,7},{6,8},{7,9},{8,10},{9,11},{10,... | collective-permute-start | bytes 786440 | tf_op jit(solution)/shard_map/ppermute | solution.py:150
  198.9 32.4 %collective-permute-start.28 = (bf16[64,4096]{1,0:T(8,128)(2,1)}, bf16[64,4096]{1,0:T(8,128)(2,1)}, u32[]{:S(2)}, u32[]{:S(2)}) collective-permute-start(bf16[64,4096]{1,0:T(8,128)(2,1)} %get-tuple-element.69), channel_id=1, source_target_pairs={{0,4},{1,5},{8,12},{9,13},{16,20},{17,21},{24,28},{25,29},{32,36},... | collective-permute-start | bytes 1572872 | tf_op jit(solution)/shard_map/ppermute | solution.py:60
  205.4 25.8 %collective-permute-start.29 = (bf16[64,4096]{1,0:T(8,128)(2,1)S(1)}, bf16[64,4096]{1,0:T(8,128)(2,1)}, u32[]{:S(2)}, u32[]{:S(2)}) collective-permute-start(bf16[64,4096]{1,0:T(8,128)(2,1)S(1)} %get-tuple-element.72), channel_id=1, source_target_pairs={{0,68},{1,69},{8,76},{9,77},{16,84},{17,85},{24,92},{25,93},{32,10... | collective-permute-start | bytes 1572872 | tf_op jit(solution)/shard_map/ppermute | solution.py:60
  226.1 42.0 %collective-permute-start.27 = (bf16[128,2048]{1,0:T(8,128)(2,1)S(1)}, bf16[128,2048]{1,0:T(8,128)(2,1)S(1)}, u32[]{:S(2)}, u32[]{:S(2)}) collective-permute-start(bf16[128,2048]{1,0:T(8,128)(2,1)S(1)} %broadcast_select_fusion.6), channel_id=1, source_target_pairs={{0,1},{1,0},{2,3},{3,2},{4,5},{5,4},{6,7},{7,6},{8,9},{9,8},{10,11... | collective-permute-start | bytes 1572872 | tf_op jit(solution)/shard_map/ppermute | solution.py:42
  228.0 3.2 %collective-permute-start.30 = (f32[1,4096]{1,0:T(1,128)S(1)}, f32[1,4096]{1,0:T(1,128)S(1)}, u32[]{:S(2)}, u32[]{:S(2)}) collective-permute-start(f32[1,4096]{1,0:T(1,128)S(1)} %add.70), channel_id=1, source_target_pairs={{0,1},{1,0},{2,3},{3,2},{4,5},{5,4},{6,7},{7,6},{8,9},{9,8},{10,11... | collective-permute-start | bytes 49160 | tf_op jit(solution)/shard_map/ppermute | solution.py:42
  231.3 37.9 %collective-permute-start.31 = (bf16[64,4096]{1,0:T(8,128)(2,1)}, bf16[64,4096]{1,0:T(8,128)(2,1)S(1)}, u32[]{:S(2)}, u32[]{:S(2)}) collective-permute-start(bf16[64,4096]{1,0:T(8,128)(2,1)} %collective-permute-done.28), channel_id=1, source_target_pairs={{0,4},{1,5},{8,12},{9,13},{16,20},{17,21},{24,28},{25,29},{32,36},... | collective-permute-start | bytes 1572872 | tf_op jit(solution)/shard_map/ppermute | solution.py:60
  233.7 35.5 %collective-permute-start.32 = (bf16[64,4096]{1,0:T(8,128)(2,1)}, bf16[64,4096]{1,0:T(8,128)(2,1)S(1)}, u32[]{:S(2)}, u32[]{:S(2)}) collective-permute-start(bf16[64,4096]{1,0:T(8,128)(2,1)} %collective-permute-done.29), channel_id=1, source_target_pairs={{0,452},{1,453},{8,460},{9,461},{16,468},{17,469},{24,476},{25,477... | collective-permute-start | bytes 1572872 | tf_op jit(solution)/shard_map/ppermute | solution.py:60
  (43 other events, 622.1 us)

commit v4 on v3

--- a/solution.py
+++ b/solution.py
@@ -46,10 +46,10 @@
     pairs = []
     for x in range(X):
         for z in range(Z):
-            new_x, new_z = move(x, z)
-            new_x, new_z = (new_x % X, new_z % Z)
-            for y in range(Y):
-                for core in range(CORES):
+            for core in range(CORES):
+                new_x, new_z = move(x, z, core)
+                new_x, new_z = (new_x % X, new_z % Z)
+                for y in range(Y):
                     source = (x * Z_HI + z // Z_LO) * CTX + (y * Z_LO + z % Z_LO) * CORES + core
                     target = (new_x * Z_HI + new_z // Z_LO) * CTX + (y * Z_LO + new_z % Z_LO) * CORES + core
                     pairs.append((source, target))
@@ -60,15 +60,18 @@
     return lax.ppermute(value, ("section", "ctx"), grid_pairs(move))
 
 
-def halfway(value, way):
-    return over_grid(value, lambda x, z: (x, z + 2 * way))
-
-
-def arrive(value, way, distance):
-    def move(x, z):
-        z_hi = ((z - 2 * way) % Z) // Z_LO
+WAY = (2, -2)
+
+
+def halfway(value):
+    return over_grid(value, lambda x, z, core: (x, z + WAY[core]))
+
+
+def arrive(value, distance):
+    def move(x, z, core):
+        z_hi = ((z - WAY[core]) % Z) // Z_LO
         cross = (1 if z_hi == Z_HI - 1 else 0) if distance == 1 else (-1 if z_hi == 0 else 0)
-        return (x + cross, z + 2 * way)
+        return (x + cross, z + WAY[core])
 
     return over_grid(value, move)
 
@@ -109,30 +112,26 @@
     )
 
 
-def gather_weight(run, set_out):
+def gather_weight(run, crossing):
     def up(piece):
         return over_ctx(piece, lambda y, z, c: ((y + 1) % Y, z, c))
 
     def down(piece):
         return over_ctx(piece, lambda y, z, c: ((y - 1) % Y, z, c))
 
-    first_out, second_out, first_in = set_out
+    crossing = halfway(crossing)
     rising, falling = [up(run)], [down(run)]
-    first = first_out(run)
     rising.append(up(rising[0]))
     falling.append(down(falling[0]))
-    second = second_out(rising[0])
-    rising[1], falling[1], first = lax.optimization_barrier((rising[1], falling[1], first))
+    rising[1], falling[1], crossing = lax.optimization_barrier((rising[1], falling[1], crossing))
+    crossing = arrive(crossing, 1)
     rising.append(up(rising[1]))
     falling.append(down(falling[1]))
-    first = first_in(first)
-    rising[2], falling[2], second = lax.optimization_barrier((rising[2], falling[2], second))
     middle = run.shape[0] // 2
     rising.append(up(rising[2][:middle]))
     falling.append(down(falling[2][middle:]))
-    rising[3], falling[3], first = lax.optimization_barrier((rising[3], falling[3], first))
-    pieces = [run, *falling[:3], rising[3], falling[3], *rising[:3][::-1]]
-    return pieces, first, second
+    rising[3], falling[3], crossing = lax.optimization_barrier((rising[3], falling[3], crossing))
+    return [run, *falling[:3], rising[3], falling[3], *rising[:3][::-1]], crossing
 
 
 def swap(value):
@@ -189,22 +188,21 @@
 BRIEF = pl.CostEstimate(flops=1000, bytes_accessed=1000, transcendentals=0)
 
 
-def forward_kernel(
-    index_ref, first_ref, second_ref, inv_ref, gain_ref, before_ref, own_ref, out_ref
-):
+def forward_kernel(index_ref, x_ref, inv_ref, gain_ref, before_ref, own_ref, out_ref):
     any_before = index_ref[0] >= CORES
     keys = jnp.concatenate([before_ref[:, :HD], own_ref[:, :HD]], axis=0)
     values = jnp.concatenate([before_ref[:, HD:], own_ref[:, HD:]], axis=0)
     values_t = values.astype(jnp.float32).T.astype(jnp.bfloat16)
-    for tokens, x_ref in enumerate((first_ref, second_ref)):
+    for tokens in range(CORES):
         span = slice(tokens * TOK, tokens * TOK + SPAN)
         rows = slice(tokens * TOK, (tokens + 1) * TOK)
-        inv = inv_ref[rows, :]
+        terms = inv_ref[rows, :].astype(jnp.float32)
+        inv = terms[:, 0:1] + terms[:, 1:2] + terms[:, 2:3]
         for pair in range(GROUP // PAIR):
             cols = [
                 slice(g * HD, (g + 1) * HD) for g in range(pair * PAIR, (pair + 1) * PAIR)
             ]
-            x = [x_ref[:, at].astype(jnp.float32) for at in cols]
+            x = [x_ref[rows, at].astype(jnp.float32) for at in cols]
             queries = jnp.concatenate(
                 [(part * inv * gain_ref[:, at]).astype(jnp.bfloat16) for part, at in zip(x, cols)],
                 axis=0,
@@ -221,9 +219,8 @@
                 out_ref[rows, at] = out.astype(jnp.bfloat16)
 
 
-def forward_attention(index, first, second, inv_rms, gain, before, own):
+def forward_attention(index, crossed, gain, before, own):
     heads = pl.BlockSpec((CHIP_TOK, WIDE), lambda h, index: (0, h))
-    tokens = pl.BlockSpec((TOK, WIDE), lambda h, index: (0, h))
     kv = pl.BlockSpec((CHIP_TOK, 2 * HD), lambda h, index: (0, h))
     return pl.pallas_call(
         forward_kernel,
@@ -231,9 +228,8 @@
             num_scalar_prefetch=1,
             grid=(HEADS,),
             in_specs=[
-                tokens,
-                tokens,
-                pl.BlockSpec((CHIP_TOK, 1), lambda h, index: (0, 0)),
+                heads,
+                pl.BlockSpec((CHIP_TOK, HD), lambda h, index: (0, 2 * HEADS)),
                 pl.BlockSpec((1, WIDE), lambda h, index: (0, h)),
                 kv,
                 kv,
@@ -241,10 +237,10 @@
             out_specs=heads,
         ),
         out_shape=jax.ShapeDtypeStruct((CHIP_TOK, HALF), jnp.bfloat16),
-        compiler_params=pltpu.CompilerParams(vmem_limit_bytes=32 * 2**20),
+        compiler_params=pltpu.CompilerParams(vmem_limit_bytes=20 * 2**20),
         cost_estimate=BRIEF,
         name="forward_attention",
-    )(index, first, second, inv_rms, gain, before, own)
+    )(index, crossed, own, gain, before, own)
 
 
 def backward_kernel(
@@ -322,7 +318,7 @@
             jax.ShapeDtypeStruct(before.shape, jnp.bfloat16),
             jax.ShapeDtypeStruct(own.shape, jnp.float32),
         ],
-        compiler_params=pltpu.CompilerParams(vmem_limit_bytes=40 * 2**20),
+        compiler_params=pltpu.CompilerParams(vmem_limit_bytes=24 * 2**20),
         cost_estimate=BRIEF,
         name="backward_attention",
     )(index, normed, upper, before, own)
@@ -337,100 +333,113 @@
     return firsts
 
 
-def project_kernel(y_ref, normed_ref, *refs):
+def project_kernel(y_ref, normed_ref, beside_ref, *refs):
     *pieces, out_ref = refs
-    total = jnp.zeros(out_ref.shape, jnp.float32)
+    width = pieces[0].shape[1]
+    total = jnp.zeros((normed_ref.shape[0], width), jnp.float32)
     for first, piece in zip(piece_columns(y_ref[0], pieces), pieces):
         rows = piece.shape[0]
         part = normed_ref[:, pl.ds(pl.multiple_of(first, rows), rows)]
         total += jnp.dot(part, piece[...], preferred_element_type=jnp.float32)
-    out_ref[...] = total.astype(out_ref.dtype)
+    out_ref[:, :width] = total.astype(out_ref.dtype)
+    if out_ref.shape[1] > width:
+        out_ref[:, width:] = beside_ref[...]
 
 
 SCALARS = pl.BlockSpec(memory_space=pltpu.SMEM)
 WHOLE = pl.BlockSpec(memory_space=pltpu.VMEM)
 
 
-def project(y, normed, pieces):
+def project(y, normed, pieces, beside, with_beside):
+    width = pieces[0].shape[1] + (beside.shape[1] if with_beside else 0)
     return pl.pallas_call(
         project_kernel,
-        in_specs=[SCALARS] + [WHOLE] * (1 + len(pieces)),
+        in_specs=[SCALARS] + [WHOLE] * (2 + len(pieces)),
         out_specs=WHOLE,
-        out_shape=jax.ShapeDtypeStruct((normed.shape[0], pieces[0].shape[1]), jnp.bfloat16),
-        compiler_params=pltpu.CompilerParams(vmem_limit_bytes=32 * 2**20),
+        out_shape=jax.ShapeDtypeStruct((normed.shape[0], width), jnp.bfloat16),
+        compiler_params=pltpu.CompilerParams(vmem_limit_bytes=16 * 2**20),
         cost_estimate=BRIEF,
         name="project",
-    )(y, normed, *pieces)
-
-
-def partial_kernel(where_ref, own_ref, after_ref, dq_ref, x_ref, inv_ref, gain_in_ref, *refs):
-    *pieces, out_ref, gain_ref = refs
+    )(y, normed, beside, *pieces)
+
+
+def partial_kernel(where_ref, own_ref, after_ref, dq_ref, *refs):
+    *pieces, out_ref = refs
     core, y = where_ref[1], where_ref[2]
     rows = pl.ds(pl.multiple_of(where_ref[0] * TOK, TOK), TOK)
     grad_kv = (own_ref[rows, :] + after_ref[rows, :].astype(jnp.float32)).astype(jnp.bfloat16)
-    inv = inv_ref[rows, :]
     for first, piece in zip(piece_columns(y, pieces), pieces):
         count = piece.shape[0]
-        cols = pl.ds(pl.multiple_of(first, count), count)
         grad = lax.dot_general(
             grad_kv, piece[...], (((1,), (1,)), ((), ())), preferred_element_type=jnp.float32
         )
         dq = dq_ref[rows, pl.ds(pl.multiple_of(first % HALF, count), count)]
         grad += jnp.where(first // HALF == core, dq, 0.0)
-        out_ref[:, cols] = grad.astype(out_ref.dtype)
-        scaled = x_ref[rows, cols].astype(jnp.float32) * inv
-        gain_ref[:, cols] = gain_in_ref[:, cols] + jnp.sum(grad * scaled, axis=0, keepdims=True)
-
-
-def partial_grad(where, own, after, dq, x, inv_rms, gain_grad, pieces, kind):
-    features = x.shape[1]
+        out_ref[:, pl.ds(pl.multiple_of(first, count), count)] = grad.astype(out_ref.dtype)
+
+
+def partial_grad(where, own, after, dq, pieces, kind):
     return pl.pallas_call(
         partial_kernel,
-        in_specs=[SCALARS] + [WHOLE] * (6 + len(pieces)),
-        out_specs=[WHOLE, WHOLE],
-        out_shape=[
-            jax.ShapeDtypeStruct((TOK, features), kind),
-            jax.ShapeDtypeStruct((1, features), jnp.float32),
-        ],
-        compiler_params=pltpu.CompilerParams(vmem_limit_bytes=40 * 2**20),
+        in_specs=[SCALARS] + [WHOLE] * (3 + len(pieces)),
+        out_specs=WHOLE,
+        out_shape=jax.ShapeDtypeStruct((TOK, CORES * HALF), kind),
+        compiler_params=pltpu.CompilerParams(vmem_limit_bytes=20 * 2**20),
         cost_estimate=BRIEF,
         name="partial_grad",
-    )(where, own, after, dq, x, inv_rms, gain_grad, *pieces)
-
-
-def input_grad_kernel(own_ref, other_ref, x_ref, inv_ref, upper_ref, gain_ref, up_ref, down_ref, grad_ref):
+    )(where, own, after, dq, *pieces)
+
+
+def input_grad_kernel(own_ref, other_ref, x_ref, upper_ref, gain_ref, out_ref, gain_grad_ref, grad_ref):
     features = x_ref.shape[1]
     width = 512
     blocks = [slice(at, at + width) for at in range(0, features, width)]
-    inv_rms = inv_ref[...]
+    squares = jnp.zeros((TOK, 1), jnp.float32)
+    for cols in blocks:
+        part = x_ref[:, cols].astype(jnp.float32)
+        squares += jnp.sum(part * part, axis=-1, keepdims=True)
+    inv_rms = lax.rsqrt(squares / features + EPSILON)
     inner = jnp.zeros((TOK, 1), jnp.float32)
     for cols in blocks:
-        grad = (own_ref[:, cols] + other_ref[:, cols].astype(jnp.float32)) * gain_ref[:, cols]
+        grad = own_ref[:, cols] + other_ref[:, cols].astype(jnp.float32)
         scaled = x_ref[:, cols].astype(jnp.float32) * inv_rms
-        inner += jnp.sum(grad * scaled, axis=-1, keepdims=True)
-        grad_ref[:, cols] = grad
+        product = grad * scaled
+        gain_grad_ref[:, cols] = jnp.sum(product, axis=0, keepdims=True)
+        gain = gain_ref[:, cols]
+        inner += jnp.sum(product * gain, axis=-1, keepdims=True)
+        grad_ref[:, cols] = grad * gain
     mean = inner * (1.0 / features)
-    for first, ref in ((0, up_ref), (TOK // 2, down_ref)):
-        rows = slice(first, first + TOK // 2)
-        inv = inv_rms[rows]
-        for cols in blocks:
-            scaled = x_ref[rows, cols].astype(jnp.float32) * inv
-            out = inv * (grad_ref[rows, cols] - scaled * mean[rows])
-            ref[:, cols] = (out + upper_ref[rows, cols].astype(jnp.float32)).astype(jnp.bfloat16)
-
-
-def input_grad(own, other, x, inv_rms, upper, gain_row):
+    for cols in blocks:
+        scaled = x_ref[:, cols].astype(jnp.float32) * inv_rms
+        out = inv_rms * (grad_ref[:, cols] - scaled * mean)
+        out_ref[:, cols] = (out + upper_ref[:, cols].astype(jnp.float32)).astype(jnp.bfloat16)
+
+
+def input_grad(own, other, x, upper, gain_row):
     features = x.shape[1]
     return pl.pallas_call(
         input_grad_kernel,
-        in_specs=[WHOLE] * 6,
+        in_specs=[WHOLE] * 5,
         out_specs=[WHOLE, WHOLE],
-        out_shape=[jax.ShapeDtypeStruct((TOK // 2, features), jnp.bfloat16)] * 2,
+        out_shape=[
+            jax.ShapeDtypeStruct((TOK, features), jnp.bfloat16),
+            jax.ShapeDtypeStruct((1, features), jnp.float32),
+        ],
         scratch_shapes=[pltpu.VMEM((TOK, features), jnp.float32)],
-        compiler_params=pltpu.CompilerParams(vmem_limit_bytes=32 * 2**20),
+        compiler_params=pltpu.CompilerParams(vmem_limit_bytes=16 * 2**20),
         cost_estimate=BRIEF,
         name="input_grad",
-    )(own, other, x, inv_rms, upper, gain_row)
+    )(own, other, x, upper, gain_row)
+
+
+def in_three(value):
+    terms = []
+    for _ in range(3):
+        term = lax.reduce_precision(value, 8, 7)
+        terms.append(term.astype(jnp.bfloat16))
+        value = value - term
+    blank = jnp.zeros((value.shape[0], HD - len(terms)), jnp.bfloat16)
+    return jnp.concatenate(terms + [blank], axis=1)
 
 
 def body(section_in, back_in, upstream, gains, kv_weight):
@@ -440,84 +449,55 @@
     x_back, upper_in = back_in[0], upstream[0]
 
     chip_x_fwd = chip_rows(section_in[0], swap(section_in[0]), core)
+    crossing = columns_of(chip_x_fwd, core)
     run = gather_run(kv_weight[0], core, z_lo)
-    later_x, later_upper, run = lax.optimization_barrier((x_back, upper_in, run))
+    gain_here = direct(columns_of(gains, core), 1)
+    later_x, later_upper, run, gain_here, crossing = lax.optimization_barrier(
+        (x_back, upper_in, run, gain_here, crossing)
+    )
     chip_x_back = chip_rows(x_back, swap(later_x), core)
-    chip_back, inv_back = norm_forward(chip_x_back, gains)
+    chip_back, _ = norm_forward(chip_x_back, gains)
     chip_fwd, inv_fwd = norm_forward(chip_x_fwd, gains)
     chip_upper = chip_columns(later_upper, core)
 
-    crossing = columns_of(chip_x_fwd, core)
-    norms = direct(
-        jnp.concatenate([columns_of(gains, core), inv_fwd.reshape(1, CHIP_TOK)], axis=1), 1
-    )
-
-    def first_out(after):
-        part, _ = lax.optimization_barrier((crossing[:TOK], after))
-        return halfway(part, 1)
-
-    def second_out(after):
-        part, _ = lax.optimization_barrier((crossing[TOK:], after))
-        return halfway(part, -1)
-
-    def first_in(part):
-        return arrive(part, 1, 1)
-
-    pieces, first_here, second_half = gather_weight(run, (first_out, second_out, first_in))
+    pieces, crossed = gather_weight(run, crossing)
     chip_back, chip_fwd, chip_upper, norms = lax.optimization_barrier(
-        (chip_back, chip_fwd, chip_upper, norms)
-    )
-    second_here = arrive(second_half, -1, 1)
-
-    kv_back = project(y_place, chip_back, pieces)
+        (chip_back, chip_fwd, chip_upper, in_three(inv_fwd))
+    )
+
+    kv_back = project(y_place, chip_back, pieces, norms, False)
     before = to_next_chip(kv_back)
-    kv_here = direct(project(y_place, chip_fwd, pieces), 1)
+    kv_here = direct(project(y_place, chip_fwd, pieces, norms, True), 1)
 
     dq, grad_before, grad_own = backward_attention(place, chip_back, chip_upper, before, kv_back)
-    after, kv_here, second_here = lax.optimization_barrier(
-        (to_chip_before(grad_before), kv_here, second_here)
-    )
-
-    def partial(row, gain_grad, kind):
-        where = jnp.stack([row, core, y])
-        return partial_grad(
-            where, grad_own, after, dq, chip_x_back, inv_back, gain_grad, pieces, kind
-        )
-
-    away, gain_grad = partial(1 - core, jnp.zeros_like(gains), jnp.bfloat16)
-    away = swap(away)
-    home, gain_grad = partial(core, gain_grad, jnp.float32)
-    gain_grad = gain_grad + over_ctx(gain_grad, lambda y, z, c: (y, z ^ 1, c))
-    gain_grad = gain_grad + over_ctx(gain_grad, lambda y, z, c: (y, z ^ 2, c))
-    inv_own = lax.dynamic_slice_in_dim(inv_back, core * TOK, TOK, 0)
-    up, down = input_grad(home, away, x_back, inv_own, upper_in, gains)
-    up, gain_grad = lax.optimization_barrier((up, gain_grad))
-    up_half, down_half = halfway(up, 1), halfway(down, -1)
-
-    gain_grad = gain_grad + swap(gain_grad)
-    up_half, down_half, gain_grad = lax.optimization_barrier((up_half, down_half, gain_grad))
-    next_grad = jnp.concatenate([arrive(up_half, 1, -1), arrive(down_half, -1, -1)], axis=0)
-    rings = [[(y * Z_LO + z) * CORES + c for y in range(Y)] for z in range(Z_LO) for c in range(CORES)]
-    gathered = lax.all_gather(gain_grad, "ctx", axis_index_groups=rings, axis=0, tiled=True)
-    gain_total = jnp.sum(gathered, axis=0, keepdims=True)
-
-    kv_here, norms, _ = lax.optimization_barrier((kv_here, norms, up))
-    out = forward_attention(
-        place,
-        first_here,
-        second_here,
-        norms[:, HALF:].reshape(CHIP_TOK, 1),
-        norms[:, :HALF],
-        to_next_chip(kv_here),
-        kv_here,
-    )
+    after, kv_here = lax.optimization_barrier((to_chip_before(grad_before), kv_here))
+
+    def partial(row, kind):
+        return partial_grad(jnp.stack([row, core, y]), grad_own, after, dq, pieces, kind)
+
+    away = swap(partial(1 - core, jnp.bfloat16))
+    home = partial(core, jnp.float32)
+    grad_in, gain_grad = input_grad(home, away, x_back, upper_in, gains)
+    half_sent = halfway(grad_in)
+
+    kv_here, gain_here, _ = lax.optimization_barrier((kv_here, gain_here, grad_in))
+    out = forward_attention(place, crossed, gain_here, to_next_chip(kv_here), kv_here)
     first, second = out[:TOK], out[TOK:]
     mine = jnp.where(core == 0, first, second)
     other = swap(jnp.where(core == 0, second, first))
     next_in = jnp.concatenate(
         [jnp.where(core == 0, mine, other), jnp.where(core == 0, other, mine)], axis=1
     )
-    return (next_in[None], next_grad[None], gain_total)
+
+    gain_grad = gain_grad + swap(gain_grad)
+    half_sent, gain_grad = lax.optimization_barrier((half_sent, gain_grad))
+    next_grad = arrive(half_sent, -1)
+    for bit in (1, 2, 4):
+        gain_grad = gain_grad + over_ctx(gain_grad, lambda y, z, c: (y ^ bit, z, c))
+    next_grad, gain_grad = lax.optimization_barrier((next_grad, gain_grad))
+    for bit in (1, 2):
+        gain_grad = gain_grad + over_ctx(gain_grad, lambda y, z, c: (y, z ^ bit, c))
+    return (next_in[None], next_grad[None], gain_grad)
 
 
 def solution(mesh):

time: 272 us -> 259 us (0.952)
  the two profiles are of different devices: /device:TPU:84 before, /device:TPU:50 now
where the time goes in v4:
time: 259 us; the launch traced here: 258 us
  starting transfers between devices  121 us (47%)
  waiting for transfers between devices  99.3 us (38%)
  Pallas kernels  21.9 us (8%)
  other arithmetic  10.4 us (4%)
  local copies, waits for them, and re-layouts  3.98 us (2%)
    ppermute x23, starting transfers between devices, over_ctx(): return lax.ppermute(value, 'ctx', ctx_pairs(move))  92 us
    ppermute x4, waiting for transfers between devices, over_grid(): return lax.ppermute(value, ('section', 'ctx'), grid_pairs(move))  40.5 us
    ppermute x23, waiting for transfers between devices, over_ctx(): return lax.ppermute(value, 'ctx', ctx_pairs(move))  34.6 us
    ppermute x2, waiting for transfers between devices, to_next_chip(): return lax.ppermute(value, 'ctx', pairs)  13.7 us
    ppermute x4, starting transfers between devices, over_grid(): return lax.ppermute(value, ('section', 'ctx'), grid_pairs(move))  13.3 us
    ppermute x2, starting transfers between devices, direct(): lax.ppermute(value, 'section', [(i, (i + distance) % peers) for i in rang...  10.1 us
    ppermute x1, waiting for transfers between devices, to_chip_before(): return lax.ppermute(value, 'ctx', pairs)  7.42 us
    pallas_call x1, Pallas kernels, backward_attention(): pl.pallas_call(backward_kernel, grid_spec=pltpu.PrefetchScalarGridSpec(nu...  7 us
  transfers between devices with their start and end apart: 32, of which 20 were waited for; matrix products, arithmetic and copies ran while one was open for 5% of the time, Pallas kernels for 7%

profile of v4, /device:TPU:50, one launch (start us, length us, event | category | flops | bytes accessed | tf_op | source)
XLA Modules:
  0.0 258.2 jit_solution(16668426411406453293)
XLA Ops:
  6.0 7.9 %collective-permute-start.1 = (bf16[128,512]{1,0:T(8,128)(2,1)S(1)}, bf16[128,512]{1,0:T(8,128)(2,1)S(1)}, u32[]{:S(2)}, u32[]{:S(2)}) collective-permute-start(bf16[128,512]{1,0:T(8,128)(2,1)S(1)} %pad_maximum_fusion.3), channel_id=1, source_target_pairs={{0,6},{1,7},{2,0},{3,1},{4,2},{5,3},{6,4},{7,5},{8,14},{9,15},{10,... | collective-permute-start | bytes 393224 | tf_op jit(solution)/shard_map/ppermute | solution.py:42
  16.6 8.2 %collective-permute-start.4 = (f32[1,2048]{1,0:T(1,128)S(1)}, f32[1,2048]{1,0:T(1,128)S(1)}, u32[]{:S(2)}, u32[]{:S(2)}) collective-permute-start(f32[1,2048]{1,0:T(1,128)S(1)} %constant_dynamic-slice_fusion.1), channel_id=1, source_target_pairs={{0,64},{64,128},{128,192},{192,256},{256,320},{320,384},{384,448},... | collective-permute-start | bytes 24584 | tf_op jit(solution)/shard_map/ppermute | solution.py:81
  25.5 3.0 %collective-permute-start.3 = (bf16[128,512]{1,0:T(8,128)(2,1)S(1)}, bf16[128,512]{1,0:T(8,128)(2,1)S(1)}, u32[]{:S(2)}, u32[]{:S(2)}) collective-permute-start(bf16[128,512]{1,0:T(8,128)(2,1)S(1)} %pad_maximum_fusion.3), channel_id=1, source_target_pairs={{0,2},{1,3},{2,4},{3,5},{4,6},{5,7},{6,0},{7,1},{8,10},{9,11},{10,... | collective-permute-start | bytes 393224 | tf_op jit(solution)/shard_map/ppermute | solution.py:42
  28.6 5.6 %collective-permute-done.3 = bf16[128,512]{1,0:T(8,128)(2,1)S(1)} collective-permute-done((bf16[128,512]{1,0:T(8,128)(2,1)S(1)}, bf16[128,512]{1,0:T(8,128)(2,1)S(1)}, u32[]{:S(2)}, u32[]{:S(2)}) %collective-permute-start.3) | collective-permute-done | bytes 131104 | tf_op jit(solution)/shard_map/ppermute | solution.py:42
  37.4 2.7 %collective-permute-start.6 = (bf16[512,512]{1,0:T(8,128)(2,1)S(1)}, bf16[512,512]{1,0:T(8,128)(2,1)S(1)}, u32[]{:S(2)}, u32[]{:S(2)}) collective-permute-start(bf16[512,512]{1,0:T(8,128)(2,1)S(1)} %constant_dynamic-slice_fusion.2.refs_0_), channel_id=1, source_target_pairs={{0,8},{1,9},{2,10},{3,11},{4,12},{5,13},{6,14},{7,15},{8,16},{9,17... | collective-permute-start | bytes 1572872 | tf_op jit(solution)/shard_map/ppermute | solution.py:42
  40.1 3.3 %collective-permute-start.8 = (bf16[512,512]{1,0:T(8,128)(2,1)S(1)}, bf16[512,512]{1,0:T(8,128)(2,1)S(1)}, u32[]{:S(2)}, u32[]{:S(2)}) collective-permute-start(bf16[512,512]{1,0:T(8,128)(2,1)S(1)} %constant_dynamic-slice_fusion.2.refs_0_), channel_id=1, source_target_pairs={{0,56},{1,57},{2,58},{3,59},{4,60},{5,61},{6,62},{7,63},{8,0},{9,1... | collective-permute-start | bytes 1572872 | tf_op jit(solution)/shard_map/ppermute | solution.py:42
  48.1 3.0 %collective-permute-start.10 = (bf16[256,2048]{1,0:T(8,128)(2,1)}, bf16[256,2048]{1,0:T(8,128)(2,1)}, u32[]{:S(2)}, u32[]{:S(2)}) collective-permute-start(bf16[256,2048]{1,0:T(8,128)(2,1)} %fusion.6), channel_id=1, source_target_pairs={{0,4},{8,12},{16,20},{24,28},{32,36},{40,44},{48,52},{56,60},{1,69... | collective-permute-start | bytes 3145736 | tf_op jit(solution)/shard_map/ppermute | solution.py:60
  54.7 3.3 %collective-permute-start.9 = (bf16[512,512]{1,0:T(8,128)(2,1)S(1)}, bf16[512,512]{1,0:T(8,128)(2,1)S(1)}, u32[]{:S(2)}, u32[]{:S(2)}) collective-permute-start(bf16[512,512]{1,0:T(8,128)(2,1)S(1)} %collective-permute-done.8.refs_1_), channel_id=1, source_target_pairs={{0,56},{1,57},{2,58},{3,59},{4,60},{5,61},{6,62},{7,63},{8,0},{9,1... | collective-permute-start | bytes 1572872 | tf_op jit(solution)/shard_map/ppermute | solution.py:42
  59.5 7.2 %collective-permute-done.7.refs_7_ = bf16[512,512]{1,0:T(8,128)(2,1)S(1)} collective-permute-done((bf16[512,512]{1,0:T(8,128)(2,1)S(1)}, bf16[512,512]{1,0:T(8,128)(2,1)S(1)}, u32[]{:S(2)}, u32[]{:S(2)}) %collective-permute-start.7) | collective-permute-done | bytes 524320 | tf_op jit(solution)/shard_map/ppermute | solution.py:42
  69.0 7.4 %collective-permute-done.10 = bf16[256,2048]{1,0:T(8,128)(2,1)} collective-permute-done((bf16[256,2048]{1,0:T(8,128)(2,1)}, bf16[256,2048]{1,0:T(8,128)(2,1)}, u32[]{:S(2)}, u32[]{:S(2)}) %collective-permute-start.10) | collective-permute-done | bytes 1048608 | tf_op jit(solution)/shard_map/ppermute | solution.py:60
  79.1 3.3 %collective-permute-start.13 = (bf16[512,512]{1,0:T(8,128)(2,1)S(1)}, bf16[512,512]{1,0:T(8,128)(2,1)S(1)}, u32[]{:S(2)}, u32[]{:S(2)}) collective-permute-start(bf16[512,512]{1,0:T(8,128)(2,1)S(1)} %collective-permute-done.9.refs_2_), channel_id=1, source_target_pairs={{0,56},{1,57},{2,58},{3,59},{4,60},{5,61},{6,62},{7,63},{8,0},{9,1... | collective-permute-start | bytes 1572872 | tf_op jit(solution)/shard_map/ppermute | solution.py:42
  82.3 4.8 %collective-permute-start.15 = (bf16[256,2048]{1,0:T(8,128)(2,1)}, bf16[256,2048]{1,0:T(8,128)(2,1)S(1)}, u32[]{:S(2)}, u32[]{:S(2)}) collective-permute-start(bf16[256,2048]{1,0:T(8,128)(2,1)} %collective-permute-done.10), channel_id=1, source_target_pairs={{0,132},{8,140},{16,148},{24,156},{32,164},{40,172},{48,180},{56,1... | collective-permute-start | bytes 3145736 | tf_op jit(solution)/shard_map/ppermute | solution.py:60
  90.9 2.6 %collective-permute-start.12 = (bf16[256,512]{1,0:T(8,128)(2,1)S(1)}, bf16[256,512]{1,0:T(8,128)(2,1)S(1)}, u32[]{:S(2)}, u32[]{:S(2)}) collective-permute-start(bf16[256,512]{1,0:T(8,128)(2,1)S(1)} %slice.60), channel_id=1, source_target_pairs={{0,8},{1,9},{2,10},{3,11},{4,12},{5,13},{6,14},{7,15},{8,16},{9,17... | collective-permute-start | bytes 786440 | tf_op jit(solution)/shard_map/ppermute | solution.py:42
  93.5 3.4 %collective-permute-start.14 = (bf16[256,512]{1,0:T(8,128)(2,1)S(1)}, bf16[256,512]{1,0:T(8,128)(2,1)S(1)}, u32[]{:S(2)}, u32[]{:S(2)}) collective-permute-start(bf16[256,512]{1,0:T(8,128)(2,1)S(1)} %slice.61), channel_id=1, source_target_pairs={{0,56},{1,57},{2,58},{3,59},{4,60},{5,61},{6,62},{7,63},{8,0},{9,1... | collective-permute-start | bytes 786440 | tf_op jit(solution)/shard_map/ppermute | solution.py:42
  99.5 2.7 %collective-permute-done.14.refs_5_ = bf16[256,512]{1,0:T(8,128)(2,1)S(1)} collective-permute-done((bf16[256,512]{1,0:T(8,128)(2,1)S(1)}, bf16[256,512]{1,0:T(8,128)(2,1)S(1)}, u32[]{:S(2)}, u32[]{:S(2)}) %collective-permute-start.14) | collective-permute-done | bytes 262176 | tf_op jit(solution)/shard_map/ppermute | solution.py:42
  102.2 9.3 %collective-permute-done.15.x_ref = bf16[256,2048]{1,0:T(8,128)(2,1)S(1)} collective-permute-done((bf16[256,2048]{1,0:T(8,128)(2,1)}, bf16[256,2048]{1,0:T(8,128)(2,1)S(1)}, u32[]{:S(2)}, u32[]{:S(2)}) %collective-permute-start.15) | collective-permute-done | bytes 1048608 | tf_op jit(solution)/shard_map/ppermute | solution.py:60
  117.9 8.0 %collective-permute-done.18.before_ref = bf16[256,512]{1,0:T(8,128)(2,1)S(1)} collective-permute-done((bf16[256,512]{1,0:T(8,128)(2,1)S(1)}, bf16[256,512]{1,0:T(8,128)(2,1)S(1)}, u32[]{:S(2)}, u32[]{:S(2)}) %collective-permute-start.18) | collective-permute-done | bytes 262176 | tf_op jit(solution)/shard_map/ppermute | solution.py:149
  125.8 7.0 %backward_attention.1 = (f32[256,2048]{1,0:T(8,128)S(1)}, bf16[256,512]{1,0:T(8,128)(2,1)S(1)}, f32[256,512]{1,0:T(8,128)S(1)}) custom-call(s32[1]{0:T(128)} %bitcast.index_ref, bf16[256,4096]{1,0:T(8,128)(2,1)S(1)} %get-tuple-element.39.normed_ref, bf16[256,2048]{1,0:T(8,128)(2,1)S(1)} %pad_maximum_fusion.2.upper_ref, ...), custom_call_target="tpu_custom_call" | custom-call | flops 1000 | bytes 1000 | tf_op jit(solution)/shard_map/backward_attention/pallas_call | solution.py:299
  134.8 3.0 %collective-permute-done.20.inv_ref.own_ref = bf16[256,640]{1,0:T(8,128)(2,1)S(1)} collective-permute-done((bf16[256,640]{1,0:T(8,128)(2,1)S(1)}, bf16[256,640]{1,0:T(8,128)(2,1)S(1)}, u32[]{:S(2)}, u32[]{:S(2)}) %collective-permute-start.20) | collective-permute-done | bytes 327712 | tf_op jit(solution)/shard_map/ppermute | solution.py:81
  137.8 7.4 %collective-permute-done.19.after_ref = bf16[256,512]{1,0:T(8,128)(2,1)S(1)} collective-permute-done((bf16[256,512]{1,0:T(8,128)(2,1)S(1)}, bf16[256,512]{1,0:T(8,128)(2,1)S(1)}, u32[]{:S(2)}, u32[]{:S(2)}) %collective-permute-start.19) | collective-permute-done | bytes 262176 | tf_op jit(solution)/shard_map/ppermute | solution.py:154
  153.3 2.6 %collective-permute-start.24 = (bf16[128,4096]{1,0:T(8,128)(2,1)S(1)}, bf16[128,4096]{1,0:T(8,128)(2,1)S(1)}, u32[]{:S(2)}, u32[]{:S(2)}) collective-permute-start(bf16[128,4096]{1,0:T(8,128)(2,1)S(1)} %get-tuple-element.51), channel_id=1, source_target_pairs={{0,4},{8,12},{16,20},{24,28},{32,36},{40,44},{48,52},{56,60},{1,69... | collective-permute-start | bytes 3145736 | tf_op jit(solution)/shard_map/ppermute | solution.py:60
  157.8 3.0 %collective-permute-start.25 = (f32[1,4096]{1,0:T(1,128)S(1)}, f32[1,4096]{1,0:T(1,128)S(1)}, u32[]{:S(2)}, u32[]{:S(2)}) collective-permute-start(f32[1,4096]{1,0:T(1,128)S(1)} %get-tuple-element.54), channel_id=1, source_target_pairs={{0,1},{1,0},{2,3},{3,2},{4,5},{5,4},{6,7},{7,6},{8,9},{9,8},{10,11... | collective-permute-start | bytes 49160 | tf_op jit(solution)/shard_map/ppermute | solution.py:42
  161.7 23.8 %collective-permute-done.24 = bf16[128,4096]{1,0:T(8,128)(2,1)S(1)} collective-permute-done((bf16[128,4096]{1,0:T(8,128)(2,1)S(1)}, bf16[128,4096]{1,0:T(8,128)(2,1)S(1)}, u32[]{:S(2)}, u32[]{:S(2)}) %collective-permute-start.24) | collective-permute-done | bytes 1048608 | tf_op jit(solution)/shard_map/ppermute | solution.py:60
  185.4 2.9 %collective-permute-start.26 = (bf16[128,4096]{1,0:T(8,128)(2,1)S(1)}, bf16[128,4096]{1,0:T(8,128)(2,1)S(1)}, u32[]{:S(2)}, u32[]{:S(2)}) collective-permute-start(bf16[128,4096]{1,0:T(8,128)(2,1)S(1)} %collective-permute-done.24), channel_id=1, source_target_pairs={{0,4},{8,12},{16,20},{24,28},{32,36},{40,44},{48,52},{56,60},{1,45... | collective-permute-start | bytes 3145736 | tf_op jit(solution)/shard_map/ppermute | solution.py:60
  188.4 5.8 %collective-permute-done.22.before_ref = bf16[256,640]{1,0:T(8,128)(2,1)S(1)} collective-permute-done((bf16[256,640]{1,0:T(8,128)(2,1)S(1)}, bf16[256,640]{1,0:T(8,128)(2,1)S(1)}, u32[]{:S(2)}, u32[]{:S(2)}) %collective-permute-start.22) | collective-permute-done | bytes 327712 | tf_op jit(solution)/shard_map/ppermute | solution.py:149
  194.2 6.9 %forward_attention.1 = bf16[256,2048]{1,0:T(8,128)(2,1)S(1)} custom-call(s32[1]{0:T(128)} %bitcast.index_ref, bf16[256,2048]{1,0:T(8,128)(2,1)S(1)} %collective-permute-done.15.x_ref, bf16[256,640]{1,0:T(8,128)(2,1)S(1)} %collective-permute-done.20.inv_ref.own_ref, f32[1,2048]{1,0:T(1,128)S(1)} %collective-permute-done.4.gain_ref, ...), custom_call_target="tpu_custom_call" | custom-call | flops 1000 | bytes 1000 | tf_op jit(solution)/shard_map/forward_attention/pallas_call | solution.py:225
  203.0 11.6 %collective-permute-start.27 = (f32[1,4096]{1,0:T(1,128)S(1)}, f32[1,4096]{1,0:T(1,128)S(1)}, u32[]{:S(2)}, u32[]{:S(2)}) collective-permute-start(f32[1,4096]{1,0:T(1,128)S(1)} %add.76), channel_id=1, source_target_pairs={{0,8},{1,9},{2,10},{3,11},{4,12},{5,13},{6,14},{7,15},{8,0},{9,1},... | collective-permute-start | bytes 49160 | tf_op jit(solution)/shard_map/ppermute | solution.py:42
  216.4 3.4 %collective-permute-start.28 = (f32[1,4096]{1,0:T(1,128)S(1)}, f32[1,4096]{1,0:T(1,128)S(1)}, u32[]{:S(2)}, u32[]{:S(2)}) collective-permute-start(f32[1,4096]{1,0:T(1,128)S(1)} %add.77), channel_id=1, source_target_pairs={{0,16},{1,17},{2,18},{3,19},{4,20},{5,21},{6,22},{7,23},{8,24},{9,... | collective-permute-start | bytes 49160 | tf_op jit(solution)/shard_map/ppermute | solution.py:42
  219.8 3.1 %collective-permute-done.28 = f32[1,4096]{1,0:T(1,128)S(1)} collective-permute-done((f32[1,4096]{1,0:T(1,128)S(1)}, f32[1,4096]{1,0:T(1,128)S(1)}, u32[]{:S(2)}, u32[]{:S(2)}) %collective-permute-start.28) | collective-permute-done | bytes 16416 | tf_op jit(solution)/shard_map/ppermute | solution.py:42
  223.0 7.0 %collective-permute-start.29 = (f32[1,4096]{1,0:T(1,128)S(1)}, f32[1,4096]{1,0:T(1,128)S(1)}, u32[]{:S(2)}, u32[]{:S(2)}) collective-permute-start(f32[1,4096]{1,0:T(1,128)S(1)} %add.78), channel_id=1, source_target_pairs={{0,32},{1,33},{2,34},{3,35},{4,36},{5,37},{6,38},{7,39},{8,40},{9,... | collective-permute-start | bytes 49160 | tf_op jit(solution)/shard_map/ppermute | solution.py:42
  232.5 15.8 %collective-permute-start.30 = (f32[1,4096]{1,0:T(1,128)S(1)}, f32[1,4096]{1,0:T(1,128)S(1)}, u32[]{:S(2)}, u32[]{:S(2)}) collective-permute-start(f32[1,4096]{1,0:T(1,128)S(1)} %add.79), channel_id=1, source_target_pairs={{0,2},{1,3},{2,0},{3,1},{4,6},{5,7},{6,4},{7,5},{8,10},{9,11},{10,... | collective-permute-start | bytes 49160 | tf_op jit(solution)/shard_map/ppermute | solution.py:42
  253.1 3.6 %collective-permute-done.31 = f32[1,4096]{1,0:T(1,128)S(1)} collective-permute-done((f32[1,4096]{1,0:T(1,128)S(1)}, f32[1,4096]{1,0:T(1,128)S(1)}, u32[]{:S(2)}, u32[]{:S(2)}) %collective-permute-start.31) | collective-permute-done | bytes 16416 | tf_op jit(solution)/shard_map/ppermute | solution.py:42
  (104 shorter events, 64.2 us)
Async XLA Ops:
  1.6 4.4 %collective-permute-start = (bf16[64,512]{1,0:T(8,128)(2,1)S(1)}, bf16[64,512]{1,0:T(8,128)(2,1)S(1)}, u32[]{:S(2)}, u32[]{:S(2)}) collective-permute-start(bf16[64,512]{1,0:T(8,128)(2,1)S(1)} %broadcast_select_fusion.12), channel_id=1, source_target_pairs={{0,1},{1,0},{2,3},{3,2},{4,5},{5,4},{6,7},{7,6},{8,9},{9,8},{10,11... | collective-permute-start | bytes 196616 | tf_op jit(solution)/shard_map/ppermute | solution.py:42
  3.5 30.7 %collective-permute-start.5 = (bf16[128,4096]{1,0:T(8,128)(2,1)}, bf16[128,4096]{1,0:T(8,128)(2,1)}, u32[]{:S(2)}, u32[]{:S(2)}) collective-permute-start(bf16[128,4096]{1,0:T(8,128)(2,1)} %bitcast.23), channel_id=1, source_target_pairs={{0,1},{1,0},{2,3},{3,2},{4,5},{5,4},{6,7},{7,6},{8,9},{9,8},{10,11... | collective-permute-start | bytes 3145736 | tf_op jit(solution)/shard_map/ppermute | solution.py:42
  6.0 22.4 %collective-permute-start.1 = (bf16[128,512]{1,0:T(8,128)(2,1)S(1)}, bf16[128,512]{1,0:T(8,128)(2,1)S(1)}, u32[]{:S(2)}, u32[]{:S(2)}) collective-permute-start(bf16[128,512]{1,0:T(8,128)(2,1)S(1)} %pad_maximum_fusion.3), channel_id=1, source_target_pairs={{0,6},{1,7},{2,0},{3,1},{4,2},{5,3},{6,4},{7,5},{8,14},{9,15},{10,... | collective-permute-start | bytes 393224 | tf_op jit(solution)/shard_map/ppermute | solution.py:42
  14.0 14.6 %collective-permute-start.2 = (bf16[128,512]{1,0:T(8,128)(2,1)S(1)}, bf16[128,512]{1,0:T(8,128)(2,1)S(1)}, u32[]{:S(2)}, u32[]{:S(2)}) collective-permute-start(bf16[128,512]{1,0:T(8,128)(2,1)S(1)} %pad_maximum_fusion.3), channel_id=1, source_target_pairs={{0,4},{1,5},{2,6},{3,7},{4,0},{5,1},{6,2},{7,3},{8,12},{9,13},{10,... | collective-permute-start | bytes 393224 | tf_op jit(solution)/shard_map/ppermute | solution.py:42
  16.6 20.8 %collective-permute-start.4 = (f32[1,2048]{1,0:T(1,128)S(1)}, f32[1,2048]{1,0:T(1,128)S(1)}, u32[]{:S(2)}, u32[]{:S(2)}) collective-permute-start(f32[1,2048]{1,0:T(1,128)S(1)} %constant_dynamic-slice_fusion.1), channel_id=1, source_target_pairs={{0,64},{64,128},{128,192},{192,256},{256,320},{320,384},{384,448},... | collective-permute-start | bytes 24584 | tf_op jit(solution)/shard_map/ppermute | solution.py:81
  25.5 8.6 %collective-permute-start.3 = (bf16[128,512]{1,0:T(8,128)(2,1)S(1)}, bf16[128,512]{1,0:T(8,128)(2,1)S(1)}, u32[]{:S(2)}, u32[]{:S(2)}) collective-permute-start(bf16[128,512]{1,0:T(8,128)(2,1)S(1)} %pad_maximum_fusion.3), channel_id=1, source_target_pairs={{0,2},{1,3},{2,4},{3,5},{4,6},{5,7},{6,0},{7,1},{8,10},{9,11},{10,... | collective-permute-start | bytes 393224 | tf_op jit(solution)/shard_map/ppermute | solution.py:42
  37.4 14.7 %collective-permute-start.6 = (bf16[512,512]{1,0:T(8,128)(2,1)S(1)}, bf16[512,512]{1,0:T(8,128)(2,1)S(1)}, u32[]{:S(2)}, u32[]{:S(2)}) collective-permute-start(bf16[512,512]{1,0:T(8,128)(2,1)S(1)} %constant_dynamic-slice_fusion.2.refs_0_), channel_id=1, source_target_pairs={{0,8},{1,9},{2,10},{3,11},{4,12},{5,13},{6,14},{7,15},{8,16},{9,17... | collective-permute-start | bytes 1572872 | tf_op jit(solution)/shard_map/ppermute | solution.py:42
  40.1 14.6 %collective-permute-start.8 = (bf16[512,512]{1,0:T(8,128)(2,1)S(1)}, bf16[512,512]{1,0:T(8,128)(2,1)S(1)}, u32[]{:S(2)}, u32[]{:S(2)}) collective-permute-start(bf16[512,512]{1,0:T(8,128)(2,1)S(1)} %constant_dynamic-slice_fusion.2.refs_0_), channel_id=1, source_target_pairs={{0,56},{1,57},{2,58},{3,59},{4,60},{5,61},{6,62},{7,63},{8,0},{9,1... | collective-permute-start | bytes 1572872 | tf_op jit(solution)/shard_map/ppermute | solution.py:42
  43.4 14.5 %collective-permute-start.17 = (bf16[128,2048]{1,0:T(8,128)(2,1)S(1)}, bf16[128,2048]{1,0:T(8,128)(2,1)}, u32[]{:S(2)}, u32[]{:S(2)}) collective-permute-start(bf16[128,2048]{1,0:T(8,128)(2,1)S(1)} %constant_dynamic-slice_fusion), channel_id=1, source_target_pairs={{0,1},{1,0},{2,3},{3,2},{4,5},{5,4},{6,7},{7,6},{8,9},{9,8},{10,11... | collective-permute-start | bytes 1572872 | tf_op jit(solution)/shard_map/ppermute | solution.py:42
  45.7 41.4 %collective-permute-start.16 = (bf16[128,4096]{1,0:T(8,128)(2,1)S(1)}, bf16[128,4096]{1,0:T(8,128)(2,1)}, u32[]{:S(2)}, u32[]{:S(2)}) collective-permute-start(bf16[128,4096]{1,0:T(8,128)(2,1)S(1)} %bitcast.17), channel_id=1, source_target_pairs={{0,1},{1,0},{2,3},{3,2},{4,5},{5,4},{6,7},{7,6},{8,9},{9,8},{10,11... | collective-permute-start | bytes 3145736 | tf_op jit(solution)/shard_map/ppermute | solution.py:42
  48.1 28.4 %collective-permute-start.10 = (bf16[256,2048]{1,0:T(8,128)(2,1)}, bf16[256,2048]{1,0:T(8,128)(2,1)}, u32[]{:S(2)}, u32[]{:S(2)}) collective-permute-start(bf16[256,2048]{1,0:T(8,128)(2,1)} %fusion.6), channel_id=1, source_target_pairs={{0,4},{8,12},{16,20},{24,28},{32,36},{40,44},{48,52},{56,60},{1,69... | collective-permute-start | bytes 3145736 | tf_op jit(solution)/shard_map/ppermute | solution.py:60
  52.1 14.6 %collective-permute-start.7 = (bf16[512,512]{1,0:T(8,128)(2,1)S(1)}, bf16[512,512]{1,0:T(8,128)(2,1)S(1)}, u32[]{:S(2)}, u32[]{:S(2)}) collective-permute-start(bf16[512,512]{1,0:T(8,128)(2,1)S(1)} %collective-permute-done.6.refs_8_), channel_id=1, source_target_pairs={{0,8},{1,9},{2,10},{3,11},{4,12},{5,13},{6,14},{7,15},{8,16},{9,17... | collective-permute-start | bytes 1572872 | tf_op jit(solution)/shard_map/ppermute | solution.py:42
  54.7 14.4 %collective-permute-start.9 = (bf16[512,512]{1,0:T(8,128)(2,1)S(1)}, bf16[512,512]{1,0:T(8,128)(2,1)S(1)}, u32[]{:S(2)}, u32[]{:S(2)}) collective-permute-start(bf16[512,512]{1,0:T(8,128)(2,1)S(1)} %collective-permute-done.8.refs_1_), channel_id=1, source_target_pairs={{0,56},{1,57},{2,58},{3,59},{4,60},{5,61},{6,62},{7,63},{8,0},{9,1... | collective-permute-start | bytes 1572872 | tf_op jit(solution)/shard_map/ppermute | solution.py:42
  76.5 14.4 %collective-permute-start.11 = (bf16[512,512]{1,0:T(8,128)(2,1)S(1)}, bf16[512,512]{1,0:T(8,128)(2,1)S(1)}, u32[]{:S(2)}, u32[]{:S(2)}) collective-permute-start(bf16[512,512]{1,0:T(8,128)(2,1)S(1)} %collective-permute-done.7.refs_7_), channel_id=1, source_target_pairs={{0,8},{1,9},{2,10},{3,11},{4,12},{5,13},{6,14},{7,15},{8,16},{9,17... | collective-permute-start | bytes 1572872 | tf_op jit(solution)/shard_map/ppermute | solution.py:42
  79.1 14.4 %collective-permute-start.13 = (bf16[512,512]{1,0:T(8,128)(2,1)S(1)}, bf16[512,512]{1,0:T(8,128)(2,1)S(1)}, u32[]{:S(2)}, u32[]{:S(2)}) collective-permute-start(bf16[512,512]{1,0:T(8,128)(2,1)S(1)} %collective-permute-done.9.refs_2_), channel_id=1, source_target_pairs={{0,56},{1,57},{2,58},{3,59},{4,60},{5,61},{6,62},{7,63},{8,0},{9,1... | collective-permute-start | bytes 1572872 | tf_op jit(solution)/shard_map/ppermute | solution.py:42
  82.3 29.2 %collective-permute-start.15 = (bf16[256,2048]{1,0:T(8,128)(2,1)}, bf16[256,2048]{1,0:T(8,128)(2,1)S(1)}, u32[]{:S(2)}, u32[]{:S(2)}) collective-permute-start(bf16[256,2048]{1,0:T(8,128)(2,1)} %collective-permute-done.10), channel_id=1, source_target_pairs={{0,132},{8,140},{16,148},{24,156},{32,164},{40,172},{48,180},{56,1... | collective-permute-start | bytes 3145736 | tf_op jit(solution)/shard_map/ppermute | solution.py:60
  90.9 8.6 %collective-permute-start.12 = (bf16[256,512]{1,0:T(8,128)(2,1)S(1)}, bf16[256,512]{1,0:T(8,128)(2,1)S(1)}, u32[]{:S(2)}, u32[]{:S(2)}) collective-permute-start(bf16[256,512]{1,0:T(8,128)(2,1)S(1)} %slice.60), channel_id=1, source_target_pairs={{0,8},{1,9},{2,10},{3,11},{4,12},{5,13},{6,14},{7,15},{8,16},{9,17... | collective-permute-start | bytes 786440 | tf_op jit(solution)/shard_map/ppermute | solution.py:42
  93.5 8.7 %collective-permute-start.14 = (bf16[256,512]{1,0:T(8,128)(2,1)S(1)}, bf16[256,512]{1,0:T(8,128)(2,1)S(1)}, u32[]{:S(2)}, u32[]{:S(2)}) collective-permute-start(bf16[256,512]{1,0:T(8,128)(2,1)S(1)} %slice.61), channel_id=1, source_target_pairs={{0,56},{1,57},{2,58},{3,59},{4,60},{5,61},{6,62},{7,63},{8,0},{9,1... | collective-permute-start | bytes 786440 | tf_op jit(solution)/shard_map/ppermute | solution.py:42
  112.7 13.1 %collective-permute-start.18 = (bf16[256,512]{1,0:T(8,128)(2,1)S(1)}, bf16[256,512]{1,0:T(8,128)(2,1)S(1)}, u32[]{:S(2)}, u32[]{:S(2)}) collective-permute-start(bf16[256,512]{1,0:T(8,128)(2,1)S(1)} %project.2.own_ref), channel_id=1, source_target_pairs={{0,2},{1,3},{2,4},{3,5},{4,6},{5,7},{6,8},{7,9},{8,10},{9,11},{10,... | collective-permute-start | bytes 786440 | tf_op jit(solution)/shard_map/ppermute | solution.py:149
  115.9 21.9 %collective-permute-start.20 = (bf16[256,640]{1,0:T(8,128)(2,1)S(1)}, bf16[256,640]{1,0:T(8,128)(2,1)S(1)}, u32[]{:S(2)}, u32[]{:S(2)}) collective-permute-start(bf16[256,640]{1,0:T(8,128)(2,1)S(1)} %project.3), channel_id=1, source_target_pairs={{0,64},{64,128},{128,192},{192,256},{256,320},{320,384},{384,448},... | collective-permute-start | bytes 983048 | tf_op jit(solution)/shard_map/ppermute | solution.py:81
  132.8 12.4 %collective-permute-start.19 = (bf16[256,512]{1,0:T(8,128)(2,1)S(1)}, bf16[256,512]{1,0:T(8,128)(2,1)S(1)}, u32[]{:S(2)}, u32[]{:S(2)}) collective-permute-start(bf16[256,512]{1,0:T(8,128)(2,1)S(1)} %get-tuple-element.44), channel_id=1, source_target_pairs={{2,0},{3,1},{4,2},{5,3},{6,4},{7,5},{8,6},{9,7},{10,8},{11,9},{12,... | collective-permute-start | bytes 786440 | tf_op jit(solution)/shard_map/ppermute | solution.py:154
  147.3 4.6 %collective-permute-start.21 = (bf16[128,4096]{1,0:T(8,128)(2,1)S(1)}, bf16[128,4096]{1,0:T(8,128)(2,1)S(1)}, u32[]{:S(2)}, u32[]{:S(2)}) collective-permute-start(bf16[128,4096]{1,0:T(8,128)(2,1)S(1)} %partial_grad.3), channel_id=1, source_target_pairs={{0,1},{1,0},{2,3},{3,2},{4,5},{5,4},{6,7},{7,6},{8,9},{9,8},{10,11... | collective-permute-start | bytes 3145736 | tf_op jit(solution)/shard_map/ppermute | solution.py:42
  153.3 32.1 %collective-permute-start.24 = (bf16[128,4096]{1,0:T(8,128)(2,1)S(1)}, bf16[128,4096]{1,0:T(8,128)(2,1)S(1)}, u32[]{:S(2)}, u32[]{:S(2)}) collective-permute-start(bf16[128,4096]{1,0:T(8,128)(2,1)S(1)} %get-tuple-element.51), channel_id=1, source_target_pairs={{0,4},{8,12},{16,20},{24,28},{32,36},{40,44},{48,52},{56,60},{1,69... | collective-permute-start | bytes 3145736 | tf_op jit(solution)/shard_map/ppermute | solution.py:60
  155.9 38.3 %collective-permute-start.22 = (bf16[256,640]{1,0:T(8,128)(2,1)S(1)}, bf16[256,640]{1,0:T(8,128)(2,1)S(1)}, u32[]{:S(2)}, u32[]{:S(2)}) collective-permute-start(bf16[256,640]{1,0:T(8,128)(2,1)S(1)} %collective-permute-done.20.inv_ref.own_ref), channel_id=1, source_target_pairs={{0,2},{1,3},{2,4},{3,5},{4,6},{5,7},{6,8},{7,9},{8,10},{9,11},{10,... | collective-permute-start | bytes 983048 | tf_op jit(solution)/shard_map/ppermute | solution.py:149
  157.8 3.8 %collective-permute-start.25 = (f32[1,4096]{1,0:T(1,128)S(1)}, f32[1,4096]{1,0:T(1,128)S(1)}, u32[]{:S(2)}, u32[]{:S(2)}) collective-permute-start(f32[1,4096]{1,0:T(1,128)S(1)} %get-tuple-element.54), channel_id=1, source_target_pairs={{0,1},{1,0},{2,3},{3,2},{4,5},{5,4},{6,7},{7,6},{8,9},{9,8},{10,11... | collective-permute-start | bytes 49160 | tf_op jit(solution)/shard_map/ppermute | solution.py:42
  185.4 47.1 %collective-permute-start.26 = (bf16[128,4096]{1,0:T(8,128)(2,1)S(1)}, bf16[128,4096]{1,0:T(8,128)(2,1)S(1)}, u32[]{:S(2)}, u32[]{:S(2)}) collective-permute-start(bf16[128,4096]{1,0:T(8,128)(2,1)S(1)} %collective-permute-done.24), channel_id=1, source_target_pairs={{0,4},{8,12},{16,20},{24,28},{32,36},{40,44},{48,52},{56,60},{1,45... | collective-permute-start | bytes 3145736 | tf_op jit(solution)/shard_map/ppermute | solution.py:60
  201.1 47.2 %collective-permute-start.23 = (bf16[128,2048]{1,0:T(8,128)(2,1)S(1)}, bf16[128,2048]{1,0:T(8,128)(2,1)S(1)}, u32[]{:S(2)}, u32[]{:S(2)}) collective-permute-start(bf16[128,2048]{1,0:T(8,128)(2,1)S(1)} %broadcast_select_fusion.6), channel_id=1, source_target_pairs={{0,1},{1,0},{2,3},{3,2},{4,5},{5,4},{6,7},{7,6},{8,9},{9,8},{10,11... | collective-permute-start | bytes 1572872 | tf_op jit(solution)/shard_map/ppermute | solution.py:42
  203.0 13.3 %collective-permute-start.27 = (f32[1,4096]{1,0:T(1,128)S(1)}, f32[1,4096]{1,0:T(1,128)S(1)}, u32[]{:S(2)}, u32[]{:S(2)}) collective-permute-start(f32[1,4096]{1,0:T(1,128)S(1)} %add.76), channel_id=1, source_target_pairs={{0,8},{1,9},{2,10},{3,11},{4,12},{5,13},{6,14},{7,15},{8,0},{9,1},... | collective-permute-start | bytes 49160 | tf_op jit(solution)/shard_map/ppermute | solution.py:42
  216.4 6.5 %collective-permute-start.28 = (f32[1,4096]{1,0:T(1,128)S(1)}, f32[1,4096]{1,0:T(1,128)S(1)}, u32[]{:S(2)}, u32[]{:S(2)}) collective-permute-start(f32[1,4096]{1,0:T(1,128)S(1)} %add.77), channel_id=1, source_target_pairs={{0,16},{1,17},{2,18},{3,19},{4,20},{5,21},{6,22},{7,23},{8,24},{9,... | collective-permute-start | bytes 49160 | tf_op jit(solution)/shard_map/ppermute | solution.py:42
  223.0 9.5 %collective-permute-start.29 = (f32[1,4096]{1,0:T(1,128)S(1)}, f32[1,4096]{1,0:T(1,128)S(1)}, u32[]{:S(2)}, u32[]{:S(2)}) collective-permute-start(f32[1,4096]{1,0:T(1,128)S(1)} %add.78), channel_id=1, source_target_pairs={{0,32},{1,33},{2,34},{3,35},{4,36},{5,37},{6,38},{7,39},{8,40},{9,... | collective-permute-start | bytes 49160 | tf_op jit(solution)/shard_map/ppermute | solution.py:42
  232.5 17.5 %collective-permute-start.30 = (f32[1,4096]{1,0:T(1,128)S(1)}, f32[1,4096]{1,0:T(1,128)S(1)}, u32[]{:S(2)}, u32[]{:S(2)}) collective-permute-start(f32[1,4096]{1,0:T(1,128)S(1)} %add.79), channel_id=1, source_target_pairs={{0,2},{1,3},{2,0},{3,1},{4,6},{5,7},{6,4},{7,5},{8,10},{9,11},{10,... | collective-permute-start | bytes 49160 | tf_op jit(solution)/shard_map/ppermute | solution.py:42
  250.1 6.5 %collective-permute-start.31 = (f32[1,4096]{1,0:T(1,128)S(1)}, f32[1,4096]{1,0:T(1,128)S(1)}, u32[]{:S(2)}, u32[]{:S(2)}) collective-permute-start(f32[1,4096]{1,0:T(1,128)S(1)} %add.80), channel_id=1, source_target_pairs={{0,4},{1,5},{2,6},{3,7},{4,0},{5,1},{6,2},{7,3},{8,12},{9,13},{10,... | collective-permute-start | bytes 49160 | tf_op jit(solution)/shard_map/ppermute | solution.py:42
  (9 other events, 81.2 us)

commit v5 on v4

--- a/solution.py
+++ b/solution.py
@@ -60,18 +60,18 @@
     return lax.ppermute(value, ("section", "ctx"), grid_pairs(move))
 
 
-WAY = (2, -2)
-
-
-def halfway(value):
-    return over_grid(value, lambda x, z, core: (x, z + WAY[core]))
-
-
-def arrive(value, distance):
+UP, DOWN, SPLIT = (2, 2), (-2, -2), (2, -2)
+
+
+def halfway(value, way):
+    return over_grid(value, lambda x, z, core: (x, z + way[core]))
+
+
+def arrive(value, way, distance):
     def move(x, z, core):
-        z_hi = ((z - WAY[core]) % Z) // Z_LO
+        z_hi = ((z - way[core]) % Z) // Z_LO
         cross = (1 if z_hi == Z_HI - 1 else 0) if distance == 1 else (-1 if z_hi == 0 else 0)
-        return (x + cross, z + WAY[core])
+        return (x + cross, z + way[core])
 
     return over_grid(value, move)
 
@@ -95,21 +95,22 @@
     return jnp.concatenate(parts, axis=1)
 
 
-def gather_run(own_rows, core, z_lo):
+def gather_run(own_rows, core, z_lo, first):
     half = own_rows.shape[1] // 2
     columns = by_head(own_rows)
     low, high = columns[:, :half], columns[:, half:]
     keep = jnp.where(core == 0, low, high)
-    received = swap(jnp.where(core == 0, high, low))
+    received, first = lax.optimization_barrier((swap(jnp.where(core == 0, high, low)), first))
     chip = chip_rows(keep, received, core)
     rows = chip.shape[0]
     pieces = [chip]
     for step in range(1, Z_LO):
         pieces.append(over_ctx(chip, lambda y, z, c, step=step: (y, (z + step) % Z_LO, c)))
     back = pieces[::-1]
-    return lax.dynamic_slice_in_dim(
+    run = lax.dynamic_slice_in_dim(
         jnp.concatenate(back + back[:-1], axis=0), (Z_LO - 1 - z_lo) * rows, Z_LO * rows, 0
     )
+    return run, first
 
 
 def gather_weight(run, crossing):
@@ -119,19 +120,18 @@
     def down(piece):
         return over_ctx(piece, lambda y, z, c: ((y - 1) % Y, z, c))
 
-    crossing = halfway(crossing)
+    crossing = halfway(crossing, SPLIT)
     rising, falling = [up(run)], [down(run)]
     rising.append(up(rising[0]))
     falling.append(down(falling[0]))
     rising[1], falling[1], crossing = lax.optimization_barrier((rising[1], falling[1], crossing))
-    crossing = arrive(crossing, 1)
     rising.append(up(rising[1]))
     falling.append(down(falling[1]))
     middle = run.shape[0] // 2
     rising.append(up(rising[2][:middle]))
     falling.append(down(falling[2][middle:]))
-    rising[3], falling[3], crossing = lax.optimization_barrier((rising[3], falling[3], crossing))
-    return [run, *falling[:3], rising[3], falling[3], *rising[:3][::-1]], crossing
+    pieces = [run, *falling[:3], rising[3], falling[3], *rising[:3][::-1]]
+    return pieces, arrive(crossing, SPLIT, 1)
 
 
 def swap(value):
@@ -390,7 +390,9 @@
     )(where, own, after, dq, *pieces)
 
 
-def input_grad_kernel(own_ref, other_ref, x_ref, upper_ref, gain_ref, out_ref, gain_grad_ref, grad_ref):
+def input_grad_kernel(
+    own_ref, other_ref, x_ref, upper_ref, gain_ref, up_ref, down_ref, gain_grad_ref, grad_ref
+):
     features = x_ref.shape[1]
     width = 512
     blocks = [slice(at, at + width) for at in range(0, features, width)]
@@ -409,10 +411,12 @@
         inner += jnp.sum(product * gain, axis=-1, keepdims=True)
         grad_ref[:, cols] = grad * gain
     mean = inner * (1.0 / features)
-    for cols in blocks:
-        scaled = x_ref[:, cols].astype(jnp.float32) * inv_rms
-        out = inv_rms * (grad_ref[:, cols] - scaled * mean)
-        out_ref[:, cols] = (out + upper_ref[:, cols].astype(jnp.float32)).astype(jnp.bfloat16)
+    for first, ref in ((0, up_ref), (TOK // 2, down_ref)):
+        rows = slice(first, first + TOK // 2)
+        for cols in blocks:
+            scaled = x_ref[rows, cols].astype(jnp.float32) * inv_rms[rows]
+            out = inv_rms[rows] * (grad_ref[rows, cols] - scaled * mean[rows])
+            ref[:, cols] = (out + upper_ref[rows, cols].astype(jnp.float32)).astype(jnp.bfloat16)
 
 
 def input_grad(own, other, x, upper, gain_row):
@@ -420,9 +424,10 @@
     return pl.pallas_call(
         input_grad_kernel,
         in_specs=[WHOLE] * 5,
-        out_specs=[WHOLE, WHOLE],
+        out_specs=[WHOLE] * 3,
         out_shape=[
-            jax.ShapeDtypeStruct((TOK, features), jnp.bfloat16),
+            jax.ShapeDtypeStruct((TOK // 2, features), jnp.bfloat16),
+            jax.ShapeDtypeStruct((TOK // 2, features), jnp.bfloat16),
             jax.ShapeDtypeStruct((1, features), jnp.float32),
         ],
         scratch_shapes=[pltpu.VMEM((TOK, features), jnp.float32)],
@@ -450,11 +455,9 @@
 
     chip_x_fwd = chip_rows(section_in[0], swap(section_in[0]), core)
     crossing = columns_of(chip_x_fwd, core)
-    run = gather_run(kv_weight[0], core, z_lo)
     gain_here = direct(columns_of(gains, core), 1)
-    later_x, later_upper, run, gain_here, crossing = lax.optimization_barrier(
-        (x_back, upper_in, run, gain_here, crossing)
-    )
+    run, gain_here = gather_run(kv_weight[0], core, z_lo, gain_here)
+    later_x, later_upper, run, crossing = lax.optimization_barrier((x_back, upper_in, run, crossing))
     chip_x_back = chip_rows(x_back, swap(later_x), core)
     chip_back, _ = norm_forward(chip_x_back, gains)
     chip_fwd, inv_fwd = norm_forward(chip_x_fwd, gains)
@@ -470,33 +473,39 @@
     kv_here = direct(project(y_place, chip_fwd, pieces, norms, True), 1)
 
     dq, grad_before, grad_own = backward_attention(place, chip_back, chip_upper, before, kv_back)
-    after, kv_here = lax.optimization_barrier((to_chip_before(grad_before), kv_here))
+    after, kv_here, crossed = lax.optimization_barrier(
+        (to_chip_before(grad_before), kv_here, crossed)
+    )
 
     def partial(row, kind):
         return partial_grad(jnp.stack([row, core, y]), grad_own, after, dq, pieces, kind)
 
     away = swap(partial(1 - core, jnp.bfloat16))
     home = partial(core, jnp.float32)
-    grad_in, gain_grad = input_grad(home, away, x_back, upper_in, gains)
-    half_sent = halfway(grad_in)
-
-    kv_here, gain_here, _ = lax.optimization_barrier((kv_here, gain_here, grad_in))
-    out = forward_attention(place, crossed, gain_here, to_next_chip(kv_here), kv_here)
+    up, down, gain_grad = input_grad(home, away, x_back, upper_in, gains)
+    up_half, down_half = halfway(up, UP), halfway(down, DOWN)
+
+    kv_here, _ = lax.optimization_barrier((kv_here, up))
+    before_here = to_next_chip(kv_here)
+    gain_grad = gain_grad + swap(gain_grad)
+    for bit in (1, 2, 4):
+        gain_grad = gain_grad + over_ctx(gain_grad, lambda y, z, c: (y ^ bit, z, c))
+    up_half, down_half, gain_grad, crossed = lax.optimization_barrier(
+        (up_half, down_half, gain_grad, crossed)
+    )
+    up, down = arrive(up_half, UP, -1), arrive(down_half, DOWN, -1)
+    gain_grad = gain_grad + over_ctx(gain_grad, lambda y, z, c: (y, z ^ 1, c))
+    up, down, gain_grad = lax.optimization_barrier((up, down, gain_grad))
+    gain_grad = gain_grad + over_ctx(gain_grad, lambda y, z, c: (y, z ^ 2, c))
+    next_grad = jnp.concatenate([up, down], axis=0)
+
+    out = forward_attention(place, crossed, gain_here, before_here, kv_here)
     first, second = out[:TOK], out[TOK:]
     mine = jnp.where(core == 0, first, second)
     other = swap(jnp.where(core == 0, second, first))
     next_in = jnp.concatenate(
         [jnp.where(core == 0, mine, other), jnp.where(core == 0, other, mine)], axis=1
     )
-
-    gain_grad = gain_grad + swap(gain_grad)
-    half_sent, gain_grad = lax.optimization_barrier((half_sent, gain_grad))
-    next_grad = arrive(half_sent, -1)
-    for bit in (1, 2, 4):
-        gain_grad = gain_grad + over_ctx(gain_grad, lambda y, z, c: (y ^ bit, z, c))
-    next_grad, gain_grad = lax.optimization_barrier((next_grad, gain_grad))
-    for bit in (1, 2):
-        gain_grad = gain_grad + over_ctx(gain_grad, lambda y, z, c: (y, z ^ bit, c))
     return (next_in[None], next_grad[None], gain_grad)
 
 

time: 259 us -> 241 us (0.931)
  the two profiles are of different devices: /device:TPU:50 before, /device:TPU:1 now
where the time goes in v5:
time: 241 us; the launch traced here: 238 us
  starting transfers between devices  129 us (54%)
  waiting for transfers between devices  71.7 us (30%)
  Pallas kernels  21.9 us (9%)
  other arithmetic  11.5 us (5%)
  local copies, waits for them, and re-layouts  2.98 us (1%)
    ppermute x23, starting transfers between devices, over_ctx(): return lax.ppermute(value, 'ctx', ctx_pairs(move))  76.7 us
    ppermute x23, waiting for transfers between devices, over_ctx(): return lax.ppermute(value, 'ctx', ctx_pairs(move))  41.6 us
    ppermute x6, starting transfers between devices, over_grid(): return lax.ppermute(value, ('section', 'ctx'), grid_pairs(move))  34.2 us
    ppermute x2, waiting for transfers between devices, direct(): lax.ppermute(value, 'section', [(i, (i + distance) % peers) for i in rang...  21.8 us
    ppermute x2, starting transfers between devices, to_next_chip(): return lax.ppermute(value, 'ctx', pairs)  9.57 us
    ppermute x2, starting transfers between devices, direct(): lax.ppermute(value, 'section', [(i, (i + distance) % peers) for i in rang...  7.17 us
    pallas_call x1, Pallas kernels, backward_attention(): pl.pallas_call(backward_kernel, grid_spec=pltpu.PrefetchScalarGridSpec(nu...  7 us
    pallas_call x1, Pallas kernels, forward_attention(): pl.pallas_call(forward_kernel, grid_spec=pltpu.PrefetchScalarGridSpec(num...  6.91 us
  transfers between devices with their start and end apart: 34, of which 16 were waited for; matrix products, arithmetic and copies ran while one was open for 4% of the time, Pallas kernels for 8%

profile of v5, /device:TPU:1, one launch (start us, length us, event | category | flops | bytes accessed | tf_op | source)
XLA Modules:
  0.0 238.4 jit_solution(9648461169710198810)
XLA Ops:
  1.6 8.8 %collective-permute-start = (bf16[64,512]{1,0:T(8,128)(2,1)S(1)}, bf16[64,512]{1,0:T(8,128)(2,1)S(1)}, u32[]{:S(2)}, u32[]{:S(2)}) collective-permute-start(bf16[64,512]{1,0:T(8,128)(2,1)S(1)} %broadcast_select_fusion.12), channel_id=1, source_target_pairs={{0,1},{1,0},{2,3},{3,2},{4,5},{5,4},{6,7},{7,6},{8,9},{9,8},{10,11... | collective-permute-start | bytes 196616 | tf_op jit(solution)/shard_map/ppermute | solution.py:42
  11.1 5.3 %collective-permute-start.1 = (f32[1,2048]{1,0:T(1,128)S(1)}, f32[1,2048]{1,0:T(1,128)S(1)}, u32[]{:S(2)}, u32[]{:S(2)}) collective-permute-start(f32[1,2048]{1,0:T(1,128)S(1)} %constant_dynamic-slice_fusion.2), channel_id=1, source_target_pairs={{0,64},{64,128},{128,192},{192,256},{256,320},{320,384},{384,448},... | collective-permute-start | bytes 24584 | tf_op jit(solution)/shard_map/ppermute | solution.py:81
  16.4 5.1 %collective-permute-done.1.gain_ref = f32[1,2048]{1,0:T(1,128)S(1)} collective-permute-done((f32[1,2048]{1,0:T(1,128)S(1)}, f32[1,2048]{1,0:T(1,128)S(1)}, u32[]{:S(2)}, u32[]{:S(2)}) %collective-permute-start.1) | collective-permute-done | bytes 8224 | tf_op jit(solution)/shard_map/ppermute | solution.py:81
  21.6 3.0 %collective-permute-start.2 = (bf16[128,512]{1,0:T(8,128)(2,1)S(1)}, bf16[128,512]{1,0:T(8,128)(2,1)S(1)}, u32[]{:S(2)}, u32[]{:S(2)}) collective-permute-start(bf16[128,512]{1,0:T(8,128)(2,1)S(1)} %pad_maximum_fusion.3), channel_id=1, source_target_pairs={{0,6},{1,7},{2,0},{3,1},{4,2},{5,3},{6,4},{7,5},{8,14},{9,15},{10,... | collective-permute-start | bytes 393224 | tf_op jit(solution)/shard_map/ppermute | solution.py:42
  26.5 3.1 %collective-permute-start.5 = (bf16[128,4096]{1,0:T(8,128)(2,1)}, bf16[128,4096]{1,0:T(8,128)(2,1)}, u32[]{:S(2)}, u32[]{:S(2)}) collective-permute-start(bf16[128,4096]{1,0:T(8,128)(2,1)} %bitcast.24), channel_id=1, source_target_pairs={{0,1},{1,0},{2,3},{3,2},{4,5},{5,4},{6,7},{7,6},{8,9},{9,8},{10,11... | collective-permute-start | bytes 3145736 | tf_op jit(solution)/shard_map/ppermute | solution.py:42
  35.5 3.6 %collective-permute-done.4 = bf16[128,512]{1,0:T(8,128)(2,1)S(1)} collective-permute-done((bf16[128,512]{1,0:T(8,128)(2,1)S(1)}, bf16[128,512]{1,0:T(8,128)(2,1)S(1)}, u32[]{:S(2)}, u32[]{:S(2)}) %collective-permute-start.4) | collective-permute-done | bytes 131104 | tf_op jit(solution)/shard_map/ppermute | solution.py:42
  42.3 3.3 %collective-permute-start.9 = (bf16[512,512]{1,0:T(8,128)(2,1)S(1)}, bf16[512,512]{1,0:T(8,128)(2,1)S(1)}, u32[]{:S(2)}, u32[]{:S(2)}) collective-permute-start(bf16[512,512]{1,0:T(8,128)(2,1)S(1)} %constant_dynamic-slice_fusion.1.refs_0_), channel_id=1, source_target_pairs={{0,8},{1,9},{2,10},{3,11},{4,12},{5,13},{6,14},{7,15},{8,16},{9,17... | collective-permute-start | bytes 1572872 | tf_op jit(solution)/shard_map/ppermute | solution.py:42
  45.6 3.8 %collective-permute-start.8 = (bf16[512,512]{1,0:T(8,128)(2,1)S(1)}, bf16[512,512]{1,0:T(8,128)(2,1)S(1)}, u32[]{:S(2)}, u32[]{:S(2)}) collective-permute-start(bf16[512,512]{1,0:T(8,128)(2,1)S(1)} %constant_dynamic-slice_fusion.1.refs_0_), channel_id=1, source_target_pairs={{0,56},{1,57},{2,58},{3,59},{4,60},{5,61},{6,62},{7,63},{8,0},{9,1... | collective-permute-start | bytes 1572872 | tf_op jit(solution)/shard_map/ppermute | solution.py:42
  49.5 3.0 %collective-permute-start.7 = (bf16[128,2048]{1,0:T(8,128)(2,1)S(1)}, bf16[128,2048]{1,0:T(8,128)(2,1)}, u32[]{:S(2)}, u32[]{:S(2)}) collective-permute-start(bf16[128,2048]{1,0:T(8,128)(2,1)S(1)} %constant_dynamic-slice_fusion), channel_id=1, source_target_pairs={{0,1},{1,0},{2,3},{3,2},{4,5},{5,4},{6,7},{7,6},{8,9},{9,8},{10,11... | collective-permute-start | bytes 1572872 | tf_op jit(solution)/shard_map/ppermute | solution.py:42
  54.8 4.1 %collective-permute-start.12 = (bf16[256,2048]{1,0:T(8,128)(2,1)}, bf16[256,2048]{1,0:T(8,128)(2,1)}, u32[]{:S(2)}, u32[]{:S(2)}) collective-permute-start(bf16[256,2048]{1,0:T(8,128)(2,1)} %fusion.6), channel_id=1, source_target_pairs={{0,4},{8,12},{16,20},{24,28},{32,36},{40,44},{48,52},{56,60},{1,69... | collective-permute-start | bytes 3145736 | tf_op jit(solution)/shard_map/ppermute | solution.py:60
  61.8 4.6 %collective-permute-start.11 = (bf16[512,512]{1,0:T(8,128)(2,1)S(1)}, bf16[512,512]{1,0:T(8,128)(2,1)S(1)}, u32[]{:S(2)}, u32[]{:S(2)}) collective-permute-start(bf16[512,512]{1,0:T(8,128)(2,1)S(1)} %collective-permute-done.8.refs_1_), channel_id=1, source_target_pairs={{0,56},{1,57},{2,58},{3,59},{4,60},{5,61},{6,62},{7,63},{8,0},{9,1... | collective-permute-start | bytes 1572872 | tf_op jit(solution)/shard_map/ppermute | solution.py:42
  67.9 8.1 %collective-permute-done.10.refs_7_ = bf16[512,512]{1,0:T(8,128)(2,1)S(1)} collective-permute-done((bf16[512,512]{1,0:T(8,128)(2,1)S(1)}, bf16[512,512]{1,0:T(8,128)(2,1)S(1)}, u32[]{:S(2)}, u32[]{:S(2)}) %collective-permute-start.10) | collective-permute-done | bytes 524320 | tf_op jit(solution)/shard_map/ppermute | solution.py:42
  76.7 5.3 %collective-permute-done.12 = bf16[256,2048]{1,0:T(8,128)(2,1)} collective-permute-done((bf16[256,2048]{1,0:T(8,128)(2,1)}, bf16[256,2048]{1,0:T(8,128)(2,1)}, u32[]{:S(2)}, u32[]{:S(2)}) %collective-permute-start.12) | collective-permute-done | bytes 1048608 | tf_op jit(solution)/shard_map/ppermute | solution.py:60
  82.0 3.6 %collective-permute-start.13 = (bf16[512,512]{1,0:T(8,128)(2,1)S(1)}, bf16[512,512]{1,0:T(8,128)(2,1)S(1)}, u32[]{:S(2)}, u32[]{:S(2)}) collective-permute-start(bf16[512,512]{1,0:T(8,128)(2,1)S(1)} %collective-permute-done.11.refs_2_), channel_id=1, source_target_pairs={{0,56},{1,57},{2,58},{3,59},{4,60},{5,61},{6,62},{7,63},{8,0},{9,1... | collective-permute-start | bytes 1572872 | tf_op jit(solution)/shard_map/ppermute | solution.py:42
  87.5 4.9 %collective-permute-start.20 = (bf16[256,2048]{1,0:T(8,128)(2,1)}, bf16[256,2048]{1,0:T(8,128)(2,1)S(1)}, u32[]{:S(2)}, u32[]{:S(2)}) collective-permute-start(bf16[256,2048]{1,0:T(8,128)(2,1)} %collective-permute-done.12), channel_id=1, source_target_pairs={{0,132},{8,140},{16,148},{24,156},{32,164},{40,172},{48,180},{56,1... | collective-permute-start | bytes 3145736 | tf_op jit(solution)/shard_map/ppermute | solution.py:60
  94.4 4.7 %collective-permute-start.16 = (bf16[256,512]{1,0:T(8,128)(2,1)S(1)}, bf16[256,512]{1,0:T(8,128)(2,1)S(1)}, u32[]{:S(2)}, u32[]{:S(2)}) collective-permute-start(bf16[256,512]{1,0:T(8,128)(2,1)S(1)} %slice.61), channel_id=1, source_target_pairs={{0,56},{1,57},{2,58},{3,59},{4,60},{5,61},{6,62},{7,63},{8,0},{9,1... | collective-permute-start | bytes 786440 | tf_op jit(solution)/shard_map/ppermute | solution.py:42
  102.4 5.4 %collective-permute-done.15.refs_4_ = bf16[256,512]{1,0:T(8,128)(2,1)S(1)} collective-permute-done((bf16[256,512]{1,0:T(8,128)(2,1)S(1)}, bf16[256,512]{1,0:T(8,128)(2,1)S(1)}, u32[]{:S(2)}, u32[]{:S(2)}) %collective-permute-start.15) | collective-permute-done | bytes 262176 | tf_op jit(solution)/shard_map/ppermute | solution.py:42
  109.0 6.7 %collective-permute-start.17 = (bf16[256,512]{1,0:T(8,128)(2,1)S(1)}, bf16[256,512]{1,0:T(8,128)(2,1)S(1)}, u32[]{:S(2)}, u32[]{:S(2)}) collective-permute-start(bf16[256,512]{1,0:T(8,128)(2,1)S(1)} %project.2.own_ref), channel_id=1, source_target_pairs={{0,2},{1,3},{2,4},{3,5},{4,6},{5,7},{6,8},{7,9},{8,10},{9,11},{10,... | collective-permute-start | bytes 786440 | tf_op jit(solution)/shard_map/ppermute | solution.py:149
  119.0 3.1 %collective-permute-done.17.before_ref = bf16[256,512]{1,0:T(8,128)(2,1)S(1)} collective-permute-done((bf16[256,512]{1,0:T(8,128)(2,1)S(1)}, bf16[256,512]{1,0:T(8,128)(2,1)S(1)}, u32[]{:S(2)}, u32[]{:S(2)}) %collective-permute-start.17) | collective-permute-done | bytes 262176 | tf_op jit(solution)/shard_map/ppermute | solution.py:149
  122.1 7.0 %backward_attention.1 = (f32[256,2048]{1,0:T(8,128)S(1)}, bf16[256,512]{1,0:T(8,128)(2,1)S(1)}, f32[256,512]{1,0:T(8,128)S(1)}) custom-call(s32[1]{0:T(128)} %bitcast.index_ref, bf16[256,4096]{1,0:T(8,128)(2,1)S(1)} %get-tuple-element.36.normed_ref, bf16[256,2048]{1,0:T(8,128)(2,1)S(1)} %pad_maximum_fusion.2.upper_ref, ...), custom_call_target="tpu_custom_call" | custom-call | flops 1000 | bytes 1000 | tf_op jit(solution)/shard_map/backward_attention/pallas_call | solution.py:299
  130.4 16.6 %collective-permute-done.19.inv_ref.own_ref = bf16[256,640]{1,0:T(8,128)(2,1)S(1)} collective-permute-done((bf16[256,640]{1,0:T(8,128)(2,1)S(1)}, bf16[256,640]{1,0:T(8,128)(2,1)S(1)}, u32[]{:S(2)}, u32[]{:S(2)}) %collective-permute-start.19) | collective-permute-done | bytes 327712 | tf_op jit(solution)/shard_map/ppermute | solution.py:81
  149.1 3.6 %collective-permute-start.21 = (bf16[128,4096]{1,0:T(8,128)(2,1)S(1)}, bf16[128,4096]{1,0:T(8,128)(2,1)S(1)}, u32[]{:S(2)}, u32[]{:S(2)}) collective-permute-start(bf16[128,4096]{1,0:T(8,128)(2,1)S(1)} %partial_grad.3), channel_id=1, source_target_pairs={{0,1},{1,0},{2,3},{3,2},{4,5},{5,4},{6,7},{7,6},{8,9},{9,8},{10,11... | collective-permute-start | bytes 3145736 | tf_op jit(solution)/shard_map/ppermute | solution.py:42
  158.2 14.5 %collective-permute-start.22 = (bf16[64,4096]{1,0:T(8,128)(2,1)S(1)}, bf16[64,4096]{1,0:T(8,128)(2,1)S(1)}, u32[]{:S(2)}, u32[]{:S(2)}) collective-permute-start(bf16[64,4096]{1,0:T(8,128)(2,1)S(1)} %get-tuple-element.49), channel_id=1, source_target_pairs={{0,4},{8,12},{16,20},{24,28},{32,36},{40,44},{48,52},{56,60},{1,5}... | collective-permute-start | bytes 1572872 | tf_op jit(solution)/shard_map/ppermute | solution.py:60
  175.5 3.1 %collective-permute-start.24 = (f32[1,4096]{1,0:T(1,128)S(1)}, f32[1,4096]{1,0:T(1,128)S(1)}, u32[]{:S(2)}, u32[]{:S(2)}) collective-permute-start(f32[1,4096]{1,0:T(1,128)S(1)} %get-tuple-element.51), channel_id=1, source_target_pairs={{0,1},{1,0},{2,3},{3,2},{4,5},{5,4},{6,7},{7,6},{8,9},{9,8},{10,11... | collective-permute-start | bytes 49160 | tf_op jit(solution)/shard_map/ppermute | solution.py:42
  186.2 3.7 %collective-permute-done.26 = f32[1,4096]{1,0:T(1,128)S(1)} collective-permute-done((f32[1,4096]{1,0:T(1,128)S(1)}, f32[1,4096]{1,0:T(1,128)S(1)}, u32[]{:S(2)}, u32[]{:S(2)}) %collective-permute-start.26) | collective-permute-done | bytes 16416 | tf_op jit(solution)/shard_map/ppermute | solution.py:42
  191.9 6.4 %collective-permute-done.27 = f32[1,4096]{1,0:T(1,128)S(1)} collective-permute-done((f32[1,4096]{1,0:T(1,128)S(1)}, f32[1,4096]{1,0:T(1,128)S(1)}, u32[]{:S(2)}, u32[]{:S(2)}) %collective-permute-start.27) | collective-permute-done | bytes 16416 | tf_op jit(solution)/shard_map/ppermute | solution.py:42
  198.4 4.3 %collective-permute-start.30 = (bf16[64,4096]{1,0:T(8,128)(2,1)S(1)}, bf16[64,4096]{1,0:T(8,128)(2,1)S(1)}, u32[]{:S(2)}, u32[]{:S(2)}) collective-permute-start(bf16[64,4096]{1,0:T(8,128)(2,1)S(1)} %collective-permute-done.22), channel_id=1, source_target_pairs={{0,4},{8,12},{16,20},{24,28},{32,36},{40,44},{48,52},{56,60},{1,5}... | collective-permute-start | bytes 1572872 | tf_op jit(solution)/shard_map/ppermute | solution.py:60
  202.7 4.5 %collective-permute-start.31 = (bf16[64,4096]{1,0:T(8,128)(2,1)S(1)}, bf16[64,4096]{1,0:T(8,128)(2,1)S(1)}, u32[]{:S(2)}, u32[]{:S(2)}) collective-permute-start(bf16[64,4096]{1,0:T(8,128)(2,1)S(1)} %collective-permute-done.23), channel_id=1, source_target_pairs={{0,452},{8,460},{16,468},{24,476},{32,484},{40,492},{48,500},{56,5... | collective-permute-start | bytes 1572872 | tf_op jit(solution)/shard_map/ppermute | solution.py:60
  207.2 6.9 %forward_attention.1 = bf16[256,2048]{1,0:T(8,128)(2,1)S(1)} custom-call(s32[1]{0:T(128)} %bitcast.index_ref, bf16[256,2048]{1,0:T(8,128)(2,1)S(1)} %collective-permute-done.20.x_ref, bf16[256,640]{1,0:T(8,128)(2,1)S(1)} %collective-permute-done.19.inv_ref.own_ref, f32[1,2048]{1,0:T(1,128)S(1)} %collective-permute-done.1.gain_ref, ...), custom_call_target="tpu_custom_call" | custom-call | flops 1000 | bytes 1000 | tf_op jit(solution)/shard_map/forward_attention/pallas_call | solution.py:225
  214.1 5.8 %collective-permute-start.29 = (bf16[128,2048]{1,0:T(8,128)(2,1)S(1)}, bf16[128,2048]{1,0:T(8,128)(2,1)S(1)}, u32[]{:S(2)}, u32[]{:S(2)}) collective-permute-start(bf16[128,2048]{1,0:T(8,128)(2,1)S(1)} %broadcast_select_fusion.6), channel_id=1, source_target_pairs={{0,1},{1,0},{2,3},{3,2},{4,5},{5,4},{6,7},{7,6},{8,9},{9,8},{10,11... | collective-permute-start | bytes 1572872 | tf_op jit(solution)/shard_map/ppermute | solution.py:42
  220.0 6.3 %collective-permute-start.32 = (f32[1,4096]{1,0:T(1,128)S(1)}, f32[1,4096]{1,0:T(1,128)S(1)}, u32[]{:S(2)}, u32[]{:S(2)}) collective-permute-start(f32[1,4096]{1,0:T(1,128)S(1)} %add.79), channel_id=1, source_target_pairs={{0,2},{1,3},{2,0},{3,1},{4,6},{5,7},{6,4},{7,5},{8,10},{9,11},{10,... | collective-permute-start | bytes 49160 | tf_op jit(solution)/shard_map/ppermute | solution.py:42
  226.2 6.1 %collective-permute-done.32 = f32[1,4096]{1,0:T(1,128)S(1)} collective-permute-done((f32[1,4096]{1,0:T(1,128)S(1)}, f32[1,4096]{1,0:T(1,128)S(1)}, u32[]{:S(2)}, u32[]{:S(2)}) %collective-permute-start.32) | collective-permute-done | bytes 16416 | tf_op jit(solution)/shard_map/ppermute | solution.py:42
  (108 shorter events, 58.7 us)
Async XLA Ops:
  1.6 19.9 %collective-permute-start = (bf16[64,512]{1,0:T(8,128)(2,1)S(1)}, bf16[64,512]{1,0:T(8,128)(2,1)S(1)}, u32[]{:S(2)}, u32[]{:S(2)}) collective-permute-start(bf16[64,512]{1,0:T(8,128)(2,1)S(1)} %broadcast_select_fusion.12), channel_id=1, source_target_pairs={{0,1},{1,0},{2,3},{3,2},{4,5},{5,4},{6,7},{7,6},{8,9},{9,8},{10,11... | collective-permute-start | bytes 196616 | tf_op jit(solution)/shard_map/ppermute | solution.py:42
  11.1 10.4 %collective-permute-start.1 = (f32[1,2048]{1,0:T(1,128)S(1)}, f32[1,2048]{1,0:T(1,128)S(1)}, u32[]{:S(2)}, u32[]{:S(2)}) collective-permute-start(f32[1,2048]{1,0:T(1,128)S(1)} %constant_dynamic-slice_fusion.2), channel_id=1, source_target_pairs={{0,64},{64,128},{128,192},{192,256},{256,320},{320,384},{384,448},... | collective-permute-start | bytes 24584 | tf_op jit(solution)/shard_map/ppermute | solution.py:81
  21.6 11.4 %collective-permute-start.2 = (bf16[128,512]{1,0:T(8,128)(2,1)S(1)}, bf16[128,512]{1,0:T(8,128)(2,1)S(1)}, u32[]{:S(2)}, u32[]{:S(2)}) collective-permute-start(bf16[128,512]{1,0:T(8,128)(2,1)S(1)} %pad_maximum_fusion.3), channel_id=1, source_target_pairs={{0,6},{1,7},{2,0},{3,1},{4,2},{5,3},{6,4},{7,5},{8,14},{9,15},{10,... | collective-permute-start | bytes 393224 | tf_op jit(solution)/shard_map/ppermute | solution.py:42
  24.6 10.9 %collective-permute-start.3 = (bf16[128,512]{1,0:T(8,128)(2,1)S(1)}, bf16[128,512]{1,0:T(8,128)(2,1)S(1)}, u32[]{:S(2)}, u32[]{:S(2)}) collective-permute-start(bf16[128,512]{1,0:T(8,128)(2,1)S(1)} %pad_maximum_fusion.3), channel_id=1, source_target_pairs={{0,4},{1,5},{2,6},{3,7},{4,0},{5,1},{6,2},{7,3},{8,12},{9,13},{10,... | collective-permute-start | bytes 393224 | tf_op jit(solution)/shard_map/ppermute | solution.py:42
  26.5 12.7 %collective-permute-start.5 = (bf16[128,4096]{1,0:T(8,128)(2,1)}, bf16[128,4096]{1,0:T(8,128)(2,1)}, u32[]{:S(2)}, u32[]{:S(2)}) collective-permute-start(bf16[128,4096]{1,0:T(8,128)(2,1)} %bitcast.24), channel_id=1, source_target_pairs={{0,1},{1,0},{2,3},{3,2},{4,5},{5,4},{6,7},{7,6},{8,9},{9,8},{10,11... | collective-permute-start | bytes 3145736 | tf_op jit(solution)/shard_map/ppermute | solution.py:42
  30.3 8.8 %collective-permute-start.4 = (bf16[128,512]{1,0:T(8,128)(2,1)S(1)}, bf16[128,512]{1,0:T(8,128)(2,1)S(1)}, u32[]{:S(2)}, u32[]{:S(2)}) collective-permute-start(bf16[128,512]{1,0:T(8,128)(2,1)S(1)} %pad_maximum_fusion.3), channel_id=1, source_target_pairs={{0,2},{1,3},{2,4},{3,5},{4,6},{5,7},{6,0},{7,1},{8,10},{9,11},{10,... | collective-permute-start | bytes 393224 | tf_op jit(solution)/shard_map/ppermute | solution.py:42
  42.3 17.5 %collective-permute-start.9 = (bf16[512,512]{1,0:T(8,128)(2,1)S(1)}, bf16[512,512]{1,0:T(8,128)(2,1)S(1)}, u32[]{:S(2)}, u32[]{:S(2)}) collective-permute-start(bf16[512,512]{1,0:T(8,128)(2,1)S(1)} %constant_dynamic-slice_fusion.1.refs_0_), channel_id=1, source_target_pairs={{0,8},{1,9},{2,10},{3,11},{4,12},{5,13},{6,14},{7,15},{8,16},{9,17... | collective-permute-start | bytes 1572872 | tf_op jit(solution)/shard_map/ppermute | solution.py:42
  45.6 16.1 %collective-permute-start.8 = (bf16[512,512]{1,0:T(8,128)(2,1)S(1)}, bf16[512,512]{1,0:T(8,128)(2,1)S(1)}, u32[]{:S(2)}, u32[]{:S(2)}) collective-permute-start(bf16[512,512]{1,0:T(8,128)(2,1)S(1)} %constant_dynamic-slice_fusion.1.refs_0_), channel_id=1, source_target_pairs={{0,56},{1,57},{2,58},{3,59},{4,60},{5,61},{6,62},{7,63},{8,0},{9,1... | collective-permute-start | bytes 1572872 | tf_op jit(solution)/shard_map/ppermute | solution.py:42
  49.5 16.8 %collective-permute-start.7 = (bf16[128,2048]{1,0:T(8,128)(2,1)S(1)}, bf16[128,2048]{1,0:T(8,128)(2,1)}, u32[]{:S(2)}, u32[]{:S(2)}) collective-permute-start(bf16[128,2048]{1,0:T(8,128)(2,1)S(1)} %constant_dynamic-slice_fusion), channel_id=1, source_target_pairs={{0,1},{1,0},{2,3},{3,2},{4,5},{5,4},{6,7},{7,6},{8,9},{9,8},{10,11... | collective-permute-start | bytes 1572872 | tf_op jit(solution)/shard_map/ppermute | solution.py:42
  52.8 39.6 %collective-permute-start.6 = (bf16[128,4096]{1,0:T(8,128)(2,1)S(1)}, bf16[128,4096]{1,0:T(8,128)(2,1)}, u32[]{:S(2)}, u32[]{:S(2)}) collective-permute-start(bf16[128,4096]{1,0:T(8,128)(2,1)S(1)} %bitcast.18), channel_id=1, source_target_pairs={{0,1},{1,0},{2,3},{3,2},{4,5},{5,4},{6,7},{7,6},{8,9},{9,8},{10,11... | collective-permute-start | bytes 3145736 | tf_op jit(solution)/shard_map/ppermute | solution.py:42
  54.8 27.2 %collective-permute-start.12 = (bf16[256,2048]{1,0:T(8,128)(2,1)}, bf16[256,2048]{1,0:T(8,128)(2,1)}, u32[]{:S(2)}, u32[]{:S(2)}) collective-permute-start(bf16[256,2048]{1,0:T(8,128)(2,1)} %fusion.6), channel_id=1, source_target_pairs={{0,4},{8,12},{16,20},{24,28},{32,36},{40,44},{48,52},{56,60},{1,69... | collective-permute-start | bytes 3145736 | tf_op jit(solution)/shard_map/ppermute | solution.py:60
  59.8 16.1 %collective-permute-start.10 = (bf16[512,512]{1,0:T(8,128)(2,1)S(1)}, bf16[512,512]{1,0:T(8,128)(2,1)S(1)}, u32[]{:S(2)}, u32[]{:S(2)}) collective-permute-start(bf16[512,512]{1,0:T(8,128)(2,1)S(1)} %collective-permute-done.9.refs_8_), channel_id=1, source_target_pairs={{0,8},{1,9},{2,10},{3,11},{4,12},{5,13},{6,14},{7,15},{8,16},{9,17... | collective-permute-start | bytes 1572872 | tf_op jit(solution)/shard_map/ppermute | solution.py:42
  61.8 15.0 %collective-permute-start.11 = (bf16[512,512]{1,0:T(8,128)(2,1)S(1)}, bf16[512,512]{1,0:T(8,128)(2,1)S(1)}, u32[]{:S(2)}, u32[]{:S(2)}) collective-permute-start(bf16[512,512]{1,0:T(8,128)(2,1)S(1)} %collective-permute-done.8.refs_1_), channel_id=1, source_target_pairs={{0,56},{1,57},{2,58},{3,59},{4,60},{5,61},{6,62},{7,63},{8,0},{9,1... | collective-permute-start | bytes 1572872 | tf_op jit(solution)/shard_map/ppermute | solution.py:42
  82.0 12.4 %collective-permute-start.13 = (bf16[512,512]{1,0:T(8,128)(2,1)S(1)}, bf16[512,512]{1,0:T(8,128)(2,1)S(1)}, u32[]{:S(2)}, u32[]{:S(2)}) collective-permute-start(bf16[512,512]{1,0:T(8,128)(2,1)S(1)} %collective-permute-done.11.refs_2_), channel_id=1, source_target_pairs={{0,56},{1,57},{2,58},{3,59},{4,60},{5,61},{6,62},{7,63},{8,0},{9,1... | collective-permute-start | bytes 1572872 | tf_op jit(solution)/shard_map/ppermute | solution.py:42
  85.6 13.5 %collective-permute-start.14 = (bf16[512,512]{1,0:T(8,128)(2,1)S(1)}, bf16[512,512]{1,0:T(8,128)(2,1)S(1)}, u32[]{:S(2)}, u32[]{:S(2)}) collective-permute-start(bf16[512,512]{1,0:T(8,128)(2,1)S(1)} %collective-permute-done.10.refs_7_), channel_id=1, source_target_pairs={{0,8},{1,9},{2,10},{3,11},{4,12},{5,13},{6,14},{7,15},{8,16},{9,17... | collective-permute-start | bytes 1572872 | tf_op jit(solution)/shard_map/ppermute | solution.py:42
  87.5 42.9 %collective-permute-start.20 = (bf16[256,2048]{1,0:T(8,128)(2,1)}, bf16[256,2048]{1,0:T(8,128)(2,1)S(1)}, u32[]{:S(2)}, u32[]{:S(2)}) collective-permute-start(bf16[256,2048]{1,0:T(8,128)(2,1)} %collective-permute-done.12), channel_id=1, source_target_pairs={{0,132},{8,140},{16,148},{24,156},{32,164},{40,172},{48,180},{56,1... | collective-permute-start | bytes 3145736 | tf_op jit(solution)/shard_map/ppermute | solution.py:60
  94.4 8.0 %collective-permute-start.16 = (bf16[256,512]{1,0:T(8,128)(2,1)S(1)}, bf16[256,512]{1,0:T(8,128)(2,1)S(1)}, u32[]{:S(2)}, u32[]{:S(2)}) collective-permute-start(bf16[256,512]{1,0:T(8,128)(2,1)S(1)} %slice.61), channel_id=1, source_target_pairs={{0,56},{1,57},{2,58},{3,59},{4,60},{5,61},{6,62},{7,63},{8,0},{9,1... | collective-permute-start | bytes 786440 | tf_op jit(solution)/shard_map/ppermute | solution.py:42
  99.2 8.6 %collective-permute-start.15 = (bf16[256,512]{1,0:T(8,128)(2,1)S(1)}, bf16[256,512]{1,0:T(8,128)(2,1)S(1)}, u32[]{:S(2)}, u32[]{:S(2)}) collective-permute-start(bf16[256,512]{1,0:T(8,128)(2,1)S(1)} %slice.60), channel_id=1, source_target_pairs={{0,8},{1,9},{2,10},{3,11},{4,12},{5,13},{6,14},{7,15},{8,16},{9,17... | collective-permute-start | bytes 786440 | tf_op jit(solution)/shard_map/ppermute | solution.py:42
  109.0 13.0 %collective-permute-start.17 = (bf16[256,512]{1,0:T(8,128)(2,1)S(1)}, bf16[256,512]{1,0:T(8,128)(2,1)S(1)}, u32[]{:S(2)}, u32[]{:S(2)}) collective-permute-start(bf16[256,512]{1,0:T(8,128)(2,1)S(1)} %project.2.own_ref), channel_id=1, source_target_pairs={{0,2},{1,3},{2,4},{3,5},{4,6},{5,7},{6,8},{7,9},{8,10},{9,11},{10,... | collective-permute-start | bytes 786440 | tf_op jit(solution)/shard_map/ppermute | solution.py:149
  117.0 30.0 %collective-permute-start.19 = (bf16[256,640]{1,0:T(8,128)(2,1)S(1)}, bf16[256,640]{1,0:T(8,128)(2,1)S(1)}, u32[]{:S(2)}, u32[]{:S(2)}) collective-permute-start(bf16[256,640]{1,0:T(8,128)(2,1)S(1)} %project.3), channel_id=1, source_target_pairs={{0,64},{64,128},{128,192},{192,256},{256,320},{320,384},{384,448},... | collective-permute-start | bytes 983048 | tf_op jit(solution)/shard_map/ppermute | solution.py:81
  129.1 18.0 %collective-permute-start.18 = (bf16[256,512]{1,0:T(8,128)(2,1)S(1)}, bf16[256,512]{1,0:T(8,128)(2,1)S(1)}, u32[]{:S(2)}, u32[]{:S(2)}) collective-permute-start(bf16[256,512]{1,0:T(8,128)(2,1)S(1)} %get-tuple-element.44), channel_id=1, source_target_pairs={{2,0},{3,1},{4,2},{5,3},{6,4},{7,5},{8,6},{9,7},{10,8},{11,9},{12,... | collective-permute-start | bytes 786440 | tf_op jit(solution)/shard_map/ppermute | solution.py:154
  149.1 5.7 %collective-permute-start.21 = (bf16[128,4096]{1,0:T(8,128)(2,1)S(1)}, bf16[128,4096]{1,0:T(8,128)(2,1)S(1)}, u32[]{:S(2)}, u32[]{:S(2)}) collective-permute-start(bf16[128,4096]{1,0:T(8,128)(2,1)S(1)} %partial_grad.3), channel_id=1, source_target_pairs={{0,1},{1,0},{2,3},{3,2},{4,5},{5,4},{6,7},{7,6},{8,9},{9,8},{10,11... | collective-permute-start | bytes 3145736 | tf_op jit(solution)/shard_map/ppermute | solution.py:42
  156.3 42.1 %collective-permute-start.23 = (bf16[64,4096]{1,0:T(8,128)(2,1)S(1)}, bf16[64,4096]{1,0:T(8,128)(2,1)S(1)}, u32[]{:S(2)}, u32[]{:S(2)}) collective-permute-start(bf16[64,4096]{1,0:T(8,128)(2,1)S(1)} %get-tuple-element.50), channel_id=1, source_target_pairs={{0,68},{8,76},{16,84},{24,92},{32,100},{40,108},{48,116},{56,124},... | collective-permute-start | bytes 1572872 | tf_op jit(solution)/shard_map/ppermute | solution.py:60
  158.2 40.1 %collective-permute-start.22 = (bf16[64,4096]{1,0:T(8,128)(2,1)S(1)}, bf16[64,4096]{1,0:T(8,128)(2,1)S(1)}, u32[]{:S(2)}, u32[]{:S(2)}) collective-permute-start(bf16[64,4096]{1,0:T(8,128)(2,1)S(1)} %get-tuple-element.49), channel_id=1, source_target_pairs={{0,4},{8,12},{16,20},{24,28},{32,36},{40,44},{48,52},{56,60},{1,5}... | collective-permute-start | bytes 1572872 | tf_op jit(solution)/shard_map/ppermute | solution.py:60
  172.7 34.5 %collective-permute-start.28 = (bf16[256,640]{1,0:T(8,128)(2,1)S(1)}, bf16[256,640]{1,0:T(8,128)(2,1)S(1)}, u32[]{:S(2)}, u32[]{:S(2)}) collective-permute-start(bf16[256,640]{1,0:T(8,128)(2,1)S(1)} %collective-permute-done.19.inv_ref.own_ref), channel_id=1, source_target_pairs={{0,2},{1,3},{2,4},{3,5},{4,6},{5,7},{6,8},{7,9},{8,10},{9,11},{10,... | collective-permute-start | bytes 983048 | tf_op jit(solution)/shard_map/ppermute | solution.py:149
  184.2 5.7 %collective-permute-start.26 = (f32[1,4096]{1,0:T(1,128)S(1)}, f32[1,4096]{1,0:T(1,128)S(1)}, u32[]{:S(2)}, u32[]{:S(2)}) collective-permute-start(f32[1,4096]{1,0:T(1,128)S(1)} %add.77), channel_id=1, source_target_pairs={{0,16},{1,17},{2,18},{3,19},{4,20},{5,21},{6,22},{7,23},{8,24},{9,... | collective-permute-start | bytes 49160 | tf_op jit(solution)/shard_map/ppermute | solution.py:42
  189.9 8.4 %collective-permute-start.27 = (f32[1,4096]{1,0:T(1,128)S(1)}, f32[1,4096]{1,0:T(1,128)S(1)}, u32[]{:S(2)}, u32[]{:S(2)}) collective-permute-start(f32[1,4096]{1,0:T(1,128)S(1)} %add.78), channel_id=1, source_target_pairs={{0,32},{1,33},{2,34},{3,35},{4,36},{5,37},{6,38},{7,39},{8,40},{9,... | collective-permute-start | bytes 49160 | tf_op jit(solution)/shard_map/ppermute | solution.py:42
  198.4 34.1 %collective-permute-start.30 = (bf16[64,4096]{1,0:T(8,128)(2,1)S(1)}, bf16[64,4096]{1,0:T(8,128)(2,1)S(1)}, u32[]{:S(2)}, u32[]{:S(2)}) collective-permute-start(bf16[64,4096]{1,0:T(8,128)(2,1)S(1)} %collective-permute-done.22), channel_id=1, source_target_pairs={{0,4},{8,12},{16,20},{24,28},{32,36},{40,44},{48,52},{56,60},{1,5}... | collective-permute-start | bytes 1572872 | tf_op jit(solution)/shard_map/ppermute | solution.py:60
  202.7 29.8 %collective-permute-start.31 = (bf16[64,4096]{1,0:T(8,128)(2,1)S(1)}, bf16[64,4096]{1,0:T(8,128)(2,1)S(1)}, u32[]{:S(2)}, u32[]{:S(2)}) collective-permute-start(bf16[64,4096]{1,0:T(8,128)(2,1)S(1)} %collective-permute-done.23), channel_id=1, source_target_pairs={{0,452},{8,460},{16,468},{24,476},{32,484},{40,492},{48,500},{56,5... | collective-permute-start | bytes 1572872 | tf_op jit(solution)/shard_map/ppermute | solution.py:60
  214.1 20.2 %collective-permute-start.29 = (bf16[128,2048]{1,0:T(8,128)(2,1)S(1)}, bf16[128,2048]{1,0:T(8,128)(2,1)S(1)}, u32[]{:S(2)}, u32[]{:S(2)}) collective-permute-start(bf16[128,2048]{1,0:T(8,128)(2,1)S(1)} %broadcast_select_fusion.6), channel_id=1, source_target_pairs={{0,1},{1,0},{2,3},{3,2},{4,5},{5,4},{6,7},{7,6},{8,9},{9,8},{10,11... | collective-permute-start | bytes 1572872 | tf_op jit(solution)/shard_map/ppermute | solution.py:42
  220.0 12.4 %collective-permute-start.32 = (f32[1,4096]{1,0:T(1,128)S(1)}, f32[1,4096]{1,0:T(1,128)S(1)}, u32[]{:S(2)}, u32[]{:S(2)}) collective-permute-start(f32[1,4096]{1,0:T(1,128)S(1)} %add.79), channel_id=1, source_target_pairs={{0,2},{1,3},{2,0},{3,1},{4,6},{5,7},{6,4},{7,5},{8,10},{9,11},{10,... | collective-permute-start | bytes 49160 | tf_op jit(solution)/shard_map/ppermute | solution.py:42
  232.4 5.4 %collective-permute-start.33 = (f32[1,4096]{1,0:T(1,128)S(1)}, f32[1,4096]{1,0:T(1,128)S(1)}, u32[]{:S(2)}, u32[]{:S(2)}) collective-permute-start(f32[1,4096]{1,0:T(1,128)S(1)} %add.80), channel_id=1, source_target_pairs={{0,4},{1,5},{2,6},{3,7},{4,0},{5,1},{6,2},{7,3},{8,12},{9,13},{10,... | collective-permute-start | bytes 49160 | tf_op jit(solution)/shard_map/ppermute | solution.py:42
  (11 other events, 94.5 us)

commit v6 on v4

--- a/solution.py
+++ b/solution.py
@@ -74,11 +74,6 @@
         return (x + cross, z + WAY[core])
 
     return over_grid(value, move)
-
-
-def direct(value, distance):
-    peers = Z_HI * X
-    return lax.ppermute(value, "section", [(i, (i + distance) % peers) for i in range(peers)])
 
 
 def norm_forward(section_x, gain_row):
@@ -124,14 +119,13 @@
     rising.append(up(rising[0]))
     falling.append(down(falling[0]))
     rising[1], falling[1], crossing = lax.optimization_barrier((rising[1], falling[1], crossing))
-    crossing = arrive(crossing, 1)
     rising.append(up(rising[1]))
     falling.append(down(falling[1]))
     middle = run.shape[0] // 2
     rising.append(up(rising[2][:middle]))
     falling.append(down(falling[2][middle:]))
-    rising[3], falling[3], crossing = lax.optimization_barrier((rising[3], falling[3], crossing))
-    return [run, *falling[:3], rising[3], falling[3], *rising[:3][::-1]], crossing
+    pieces = [run, *falling[:3], rising[3], falling[3], *rising[:3][::-1]]
+    return pieces, arrive(crossing, 1), rising[0]
 
 
 def swap(value):
@@ -185,26 +179,35 @@
 PAIR = 2
 WIDE = GROUP * HD
 
+BESIDE = HALF // (2 * HEADS * HD) + 1
+
 BRIEF = pl.CostEstimate(flops=1000, bytes_accessed=1000, transcendentals=0)
 
 
-def forward_kernel(index_ref, x_ref, inv_ref, gain_ref, before_ref, own_ref, out_ref):
+def forward_kernel(index_ref, x_ref, beside_ref, before_ref, own_ref, out_ref):
     any_before = index_ref[0] >= CORES
+    beside = beside_ref[...].astype(jnp.float32)
+    beside = beside[:BESIDE] + beside[BESIDE : 2 * BESIDE] + beside[2 * BESIDE : 3 * BESIDE]
+    per_head = WIDE // beside.shape[1]
+    head = pl.program_id(0)
+    gain_rows = jnp.where(head == 0, beside[:per_head], beside[per_head : 2 * per_head])
+    gain = jnp.concatenate([gain_rows[i : i + 1] for i in range(per_head)], axis=1)
+    inv_row = beside[2 * per_head : 2 * per_head + 1, :CHIP_TOK]
+    inv_rms = jnp.broadcast_to(inv_row, (HD, CHIP_TOK)).T
     keys = jnp.concatenate([before_ref[:, :HD], own_ref[:, :HD]], axis=0)
     values = jnp.concatenate([before_ref[:, HD:], own_ref[:, HD:]], axis=0)
     values_t = values.astype(jnp.float32).T.astype(jnp.bfloat16)
     for tokens in range(CORES):
         span = slice(tokens * TOK, tokens * TOK + SPAN)
         rows = slice(tokens * TOK, (tokens + 1) * TOK)
-        terms = inv_ref[rows, :].astype(jnp.float32)
-        inv = terms[:, 0:1] + terms[:, 1:2] + terms[:, 2:3]
+        inv = inv_rms[rows]
         for pair in range(GROUP // PAIR):
             cols = [
                 slice(g * HD, (g + 1) * HD) for g in range(pair * PAIR, (pair + 1) * PAIR)
             ]
             x = [x_ref[rows, at].astype(jnp.float32) for at in cols]
             queries = jnp.concatenate(
-                [(part * inv * gain_ref[:, at]).astype(jnp.bfloat16) for part, at in zip(x, cols)],
+                [(part * inv * gain[:, at]).astype(jnp.bfloat16) for part, at in zip(x, cols)],
                 axis=0,
             )
             scores = masked_scores(keys[span], queries, tokens, any_before)
@@ -219,7 +222,7 @@
                 out_ref[rows, at] = out.astype(jnp.bfloat16)
 
 
-def forward_attention(index, crossed, gain, before, own):
+def forward_attention(index, crossed, before, own):
     heads = pl.BlockSpec((CHIP_TOK, WIDE), lambda h, index: (0, h))
     kv = pl.BlockSpec((CHIP_TOK, 2 * HD), lambda h, index: (0, h))
     return pl.pallas_call(
@@ -229,8 +232,7 @@
             grid=(HEADS,),
             in_specs=[
                 heads,
-                pl.BlockSpec((CHIP_TOK, HD), lambda h, index: (0, 2 * HEADS)),
-                pl.BlockSpec((1, WIDE), lambda h, index: (0, h)),
+                pl.BlockSpec((16, own.shape[1]), lambda h, index: (CHIP_TOK // 16, 0)),
                 kv,
                 kv,
             ],
@@ -240,7 +242,7 @@
         compiler_params=pltpu.CompilerParams(vmem_limit_bytes=20 * 2**20),
         cost_estimate=BRIEF,
         name="forward_attention",
-    )(index, crossed, own, gain, before, own)
+    )(index, crossed, own, before, own)
 
 
 def backward_kernel(
@@ -319,7 +321,7 @@
             jax.ShapeDtypeStruct(own.shape, jnp.float32),
         ],
         compiler_params=pltpu.CompilerParams(vmem_limit_bytes=24 * 2**20),
-        cost_estimate=BRIEF,
+        cost_estimate=pl.CostEstimate(flops=3*10**9, bytes_accessed=10**6, transcendentals=0),
         name="backward_attention",
     )(index, normed, upper, before, own)
 
@@ -341,9 +343,10 @@
         rows = piece.shape[0]
         part = normed_ref[:, pl.ds(pl.multiple_of(first, rows), rows)]
         total += jnp.dot(part, piece[...], preferred_element_type=jnp.float32)
-    out_ref[:, :width] = total.astype(out_ref.dtype)
-    if out_ref.shape[1] > width:
-        out_ref[:, width:] = beside_ref[...]
+    rows = total.shape[0]
+    out_ref[:rows, :] = total.astype(out_ref.dtype)
+    if out_ref.shape[0] > rows:
+        out_ref[rows:, :] = beside_ref[...]
 
 
 SCALARS = pl.BlockSpec(memory_space=pltpu.SMEM)
@@ -351,12 +354,12 @@
 
 
 def project(y, normed, pieces, beside, with_beside):
-    width = pieces[0].shape[1] + (beside.shape[1] if with_beside else 0)
+    rows = normed.shape[0] + (beside.shape[0] if with_beside else 0)
     return pl.pallas_call(
         project_kernel,
         in_specs=[SCALARS] + [WHOLE] * (2 + len(pieces)),
         out_specs=WHOLE,
-        out_shape=jax.ShapeDtypeStruct((normed.shape[0], width), jnp.bfloat16),
+        out_shape=jax.ShapeDtypeStruct((rows, pieces[0].shape[1]), jnp.bfloat16),
         compiler_params=pltpu.CompilerParams(vmem_limit_bytes=16 * 2**20),
         cost_estimate=BRIEF,
         name="project",
@@ -390,7 +393,9 @@
     )(where, own, after, dq, *pieces)
 
 
-def input_grad_kernel(own_ref, other_ref, x_ref, upper_ref, gain_ref, out_ref, gain_grad_ref, grad_ref):
+def input_grad_kernel(
+    own_ref, other_ref, x_ref, upper_ref, gain_ref, out_ref, gain_grad_ref, grad_ref
+):
     features = x_ref.shape[1]
     width = 512
     blocks = [slice(at, at + width) for at in range(0, features, width)]
@@ -420,7 +425,7 @@
     return pl.pallas_call(
         input_grad_kernel,
         in_specs=[WHOLE] * 5,
-        out_specs=[WHOLE, WHOLE],
+        out_specs=[WHOLE] * 2,
         out_shape=[
             jax.ShapeDtypeStruct((TOK, features), jnp.bfloat16),
             jax.ShapeDtypeStruct((1, features), jnp.float32),
@@ -438,8 +443,7 @@
         term = lax.reduce_precision(value, 8, 7)
         terms.append(term.astype(jnp.bfloat16))
         value = value - term
-    blank = jnp.zeros((value.shape[0], HD - len(terms)), jnp.bfloat16)
-    return jnp.concatenate(terms + [blank], axis=1)
+    return jnp.concatenate(terms, axis=0)
 
 
 def body(section_in, back_in, upstream, gains, kv_weight):
@@ -450,27 +454,33 @@
 
     chip_x_fwd = chip_rows(section_in[0], swap(section_in[0]), core)
     crossing = columns_of(chip_x_fwd, core)
-    run = gather_run(kv_weight[0], core, z_lo)
-    gain_here = direct(columns_of(gains, core), 1)
-    later_x, later_upper, run, gain_here, crossing = lax.optimization_barrier(
-        (x_back, upper_in, run, gain_here, crossing)
-    )
+    run, crossing = lax.optimization_barrier((gather_run(kv_weight[0], core, z_lo), crossing))
+    pieces, crossed, first_step = gather_weight(run, crossing)
+
+    later_x, later_upper, _ = lax.optimization_barrier((x_back, upper_in, first_step))
     chip_x_back = chip_rows(x_back, swap(later_x), core)
     chip_back, _ = norm_forward(chip_x_back, gains)
     chip_fwd, inv_fwd = norm_forward(chip_x_fwd, gains)
     chip_upper = chip_columns(later_upper, core)
 
-    pieces, crossed = gather_weight(run, crossing)
-    chip_back, chip_fwd, chip_upper, norms = lax.optimization_barrier(
-        (chip_back, chip_fwd, chip_upper, in_three(inv_fwd))
-    )
-
-    kv_back = project(y_place, chip_back, pieces, norms, False)
+    width = pieces[0].shape[1]
+    norms = jnp.pad(inv_fwd.reshape(1, CHIP_TOK), ((0, 0), (0, width - CHIP_TOK)))
+    beside = in_three(jnp.concatenate([columns_of(gains, core).reshape(-1, width), norms], axis=0))
+    beside = jnp.pad(beside, ((0, 16 - beside.shape[0]), (0, 0)))
+    chip_back, chip_fwd, chip_upper, beside = lax.optimization_barrier(
+        (chip_back, chip_fwd, chip_upper, beside)
+    )
+
+    kv_back = project(y_place, chip_back, pieces, beside, False)
+    kv_back, chip_fwd = lax.optimization_barrier((kv_back, chip_fwd))
     before = to_next_chip(kv_back)
-    kv_here = direct(project(y_place, chip_fwd, pieces, norms, True), 1)
+    kv_half = halfway(project(y_place, chip_fwd, pieces, beside, True))
 
     dq, grad_before, grad_own = backward_attention(place, chip_back, chip_upper, before, kv_back)
-    after, kv_here = lax.optimization_barrier((to_chip_before(grad_before), kv_here))
+    kv_half, grad_before = lax.optimization_barrier((kv_half, grad_before))
+    after, kv_here, crossed = lax.optimization_barrier(
+        (to_chip_before(grad_before), arrive(kv_half, 1), crossed)
+    )
 
     def partial(row, kind):
         return partial_grad(jnp.stack([row, core, y]), grad_own, after, dq, pieces, kind)
@@ -480,23 +490,24 @@
     grad_in, gain_grad = input_grad(home, away, x_back, upper_in, gains)
     half_sent = halfway(grad_in)
 
-    kv_here, gain_here, _ = lax.optimization_barrier((kv_here, gain_here, grad_in))
-    out = forward_attention(place, crossed, gain_here, to_next_chip(kv_here), kv_here)
+    kv_here, _ = lax.optimization_barrier((kv_here, grad_in))
+    before_here = to_next_chip(kv_here)
+    gain_grad = gain_grad + swap(gain_grad)
+    for bit in (1, 2, 4):
+        gain_grad = gain_grad + over_ctx(gain_grad, lambda y, z, c: (y ^ bit, z, c))
+    half_sent, gain_grad, crossed = lax.optimization_barrier((half_sent, gain_grad, crossed))
+    next_grad = arrive(half_sent, -1)
+    gain_grad = gain_grad + over_ctx(gain_grad, lambda y, z, c: (y, z ^ 1, c))
+    next_grad, gain_grad = lax.optimization_barrier((next_grad, gain_grad))
+    gain_grad = gain_grad + over_ctx(gain_grad, lambda y, z, c: (y, z ^ 2, c))
+
+    out = forward_attention(place, crossed, before_here, kv_here)
     first, second = out[:TOK], out[TOK:]
     mine = jnp.where(core == 0, first, second)
     other = swap(jnp.where(core == 0, second, first))
     next_in = jnp.concatenate(
         [jnp.where(core == 0, mine, other), jnp.where(core == 0, other, mine)], axis=1
     )
-
-    gain_grad = gain_grad + swap(gain_grad)
-    half_sent, gain_grad = lax.optimization_barrier((half_sent, gain_grad))
-    next_grad = arrive(half_sent, -1)
-    for bit in (1, 2, 4):
-        gain_grad = gain_grad + over_ctx(gain_grad, lambda y, z, c: (y ^ bit, z, c))
-    next_grad, gain_grad = lax.optimization_barrier((next_grad, gain_grad))
-    for bit in (1, 2):
-        gain_grad = gain_grad + over_ctx(gain_grad, lambda y, z, c: (y, z ^ bit, c))
     return (next_in[None], next_grad[None], gain_grad)
 
 

time: 259 us -> 221 us (0.85)
  the two profiles are of different devices: /device:TPU:50 before, /device:TPU:1 now
where the time goes in v6:
time: 221 us; the launch traced here: 218 us
  starting transfers between devices  132 us (60%)
  waiting for transfers between devices  52.7 us (24%)
  Pallas kernels  21.6 us (10%)
  other arithmetic  7.58 us (3%)
  local copies, waits for them, and re-layouts  3.36 us (2%)
    ppermute x23, starting transfers between devices, over_ctx(): return lax.ppermute(value, 'ctx', ctx_pairs(move))  92.7 us
    ppermute x23, waiting for transfers between devices, over_ctx(): return lax.ppermute(value, 'ctx', ctx_pairs(move))  40.7 us
    ppermute x6, starting transfers between devices, over_grid(): return lax.ppermute(value, ('section', 'ctx'), grid_pairs(move))  33.9 us
    ppermute x1, waiting for transfers between devices, to_chip_before(): return lax.ppermute(value, 'ctx', pairs)  10.7 us
    pallas_call x1, Pallas kernels, backward_attention(): pl.pallas_call(backward_kernel, grid_spec=pltpu.PrefetchScalarGridSpec(nu...  7 us
    pallas_call x1, Pallas kernels, forward_attention(): pl.pallas_call(forward_kernel, grid_spec=pltpu.PrefetchScalarGridSpec(num...  6.66 us
  transfers between devices with their start and end apart: 32, of which 15 were waited for; matrix products, arithmetic and copies ran while one was open for 3% of the time, Pallas kernels for 8%

profile of v6, /device:TPU:1, one launch (start us, length us, event | category | flops | bytes accessed | tf_op | source)
XLA Modules:
  0.0 218.3 jit_solution(8954732082167409775)
XLA Ops:
  1.6 8.8 %collective-permute-start = (bf16[64,512]{1,0:T(8,128)(2,1)S(1)}, bf16[64,512]{1,0:T(8,128)(2,1)S(1)}, u32[]{:S(2)}, u32[]{:S(2)}) collective-permute-start(bf16[64,512]{1,0:T(8,128)(2,1)S(1)} %broadcast_select_fusion.12), channel_id=1, source_target_pairs={{0,1},{1,0},{2,3},{3,2},{4,5},{5,4},{6,7},{7,6},{8,9},{9,8},{10,11... | collective-permute-start | bytes 196616 | tf_op jit(solution)/shard_map/ppermute | solution.py:42
  15.5 2.5 %collective-permute-start.4 = (bf16[128,4096]{1,0:T(8,128)(2,1)}, bf16[128,4096]{1,0:T(8,128)(2,1)S(1)}, u32[]{:S(2)}, u32[]{:S(2)}) collective-permute-start(bf16[128,4096]{1,0:T(8,128)(2,1)} %bitcast.23), channel_id=1, source_target_pairs={{0,1},{1,0},{2,3},{3,2},{4,5},{5,4},{6,7},{7,6},{8,9},{9,8},{10,11... | collective-permute-start | bytes 3145736 | tf_op jit(solution)/shard_map/ppermute | solution.py:42
  18.1 3.0 %collective-permute-start.3 = (bf16[128,512]{1,0:T(8,128)(2,1)S(1)}, bf16[128,512]{1,0:T(8,128)(2,1)S(1)}, u32[]{:S(2)}, u32[]{:S(2)}) collective-permute-start(bf16[128,512]{1,0:T(8,128)(2,1)S(1)} %pad_maximum_fusion.3), channel_id=1, source_target_pairs={{0,2},{1,3},{2,4},{3,5},{4,6},{5,7},{6,0},{7,1},{8,10},{9,11},{10,... | collective-permute-start | bytes 393224 | tf_op jit(solution)/shard_map/ppermute | solution.py:42
  21.2 2.6 %collective-permute-done.2 = bf16[128,512]{1,0:T(8,128)(2,1)S(1)} collective-permute-done((bf16[128,512]{1,0:T(8,128)(2,1)S(1)}, bf16[128,512]{1,0:T(8,128)(2,1)S(1)}, u32[]{:S(2)}, u32[]{:S(2)}) %collective-permute-start.2) | collective-permute-done | bytes 131104 | tf_op jit(solution)/shard_map/ppermute | solution.py:42
  23.8 3.5 %collective-permute-done.3 = bf16[128,512]{1,0:T(8,128)(2,1)S(1)} collective-permute-done((bf16[128,512]{1,0:T(8,128)(2,1)S(1)}, bf16[128,512]{1,0:T(8,128)(2,1)S(1)}, u32[]{:S(2)}, u32[]{:S(2)}) %collective-permute-start.3) | collective-permute-done | bytes 131104 | tf_op jit(solution)/shard_map/ppermute | solution.py:42
  29.0 2.9 %collective-permute-start.5 = (bf16[512,512]{1,0:T(8,128)(2,1)S(1)}, bf16[512,512]{1,0:T(8,128)(2,1)S(1)}, u32[]{:S(2)}, u32[]{:S(2)}) collective-permute-start(bf16[512,512]{1,0:T(8,128)(2,1)S(1)} %constant_dynamic-slice_fusion.1.refs_0_), channel_id=1, source_target_pairs={{0,8},{1,9},{2,10},{3,11},{4,12},{5,13},{6,14},{7,15},{8,16},{9,17... | collective-permute-start | bytes 1572872 | tf_op jit(solution)/shard_map/ppermute | solution.py:42
  31.9 3.8 %collective-permute-start.8 = (bf16[512,512]{1,0:T(8,128)(2,1)S(1)}, bf16[512,512]{1,0:T(8,128)(2,1)S(1)}, u32[]{:S(2)}, u32[]{:S(2)}) collective-permute-start(bf16[512,512]{1,0:T(8,128)(2,1)S(1)} %constant_dynamic-slice_fusion.1.refs_0_), channel_id=1, source_target_pairs={{0,56},{1,57},{2,58},{3,59},{4,60},{5,61},{6,62},{7,63},{8,0},{9,1... | collective-permute-start | bytes 1572872 | tf_op jit(solution)/shard_map/ppermute | solution.py:42
  35.7 7.1 %collective-permute-start.11 = (bf16[256,2048]{1,0:T(8,128)(2,1)}, bf16[256,2048]{1,0:T(8,128)(2,1)}, u32[]{:S(2)}, u32[]{:S(2)}) collective-permute-start(bf16[256,2048]{1,0:T(8,128)(2,1)} %fusion.6), channel_id=1, source_target_pairs={{0,4},{8,12},{16,20},{24,28},{32,36},{40,44},{48,52},{56,60},{1,69... | collective-permute-start | bytes 3145736 | tf_op jit(solution)/shard_map/ppermute | solution.py:60
  46.4 3.3 %collective-permute-start.7 = (bf16[128,2048]{1,0:T(8,128)(2,1)S(1)}, bf16[128,2048]{1,0:T(8,128)(2,1)S(1)}, u32[]{:S(2)}, u32[]{:S(2)}) collective-permute-start(bf16[128,2048]{1,0:T(8,128)(2,1)S(1)} %constant_dynamic-slice_fusion), channel_id=1, source_target_pairs={{0,1},{1,0},{2,3},{3,2},{4,5},{5,4},{6,7},{7,6},{8,9},{9,8},{10,11... | collective-permute-start | bytes 1572872 | tf_op jit(solution)/shard_map/ppermute | solution.py:42
  51.6 4.6 %collective-permute-start.10 = (bf16[512,512]{1,0:T(8,128)(2,1)S(1)}, bf16[512,512]{1,0:T(8,128)(2,1)S(1)}, u32[]{:S(2)}, u32[]{:S(2)}) collective-permute-start(bf16[512,512]{1,0:T(8,128)(2,1)S(1)} %collective-permute-done.8.refs_1_), channel_id=1, source_target_pairs={{0,56},{1,57},{2,58},{3,59},{4,60},{5,61},{6,62},{7,63},{8,0},{9,1... | collective-permute-start | bytes 1572872 | tf_op jit(solution)/shard_map/ppermute | solution.py:42
  58.2 2.5 %collective-permute-start.6 = (bf16[128,4096]{1,0:T(8,128)(2,1)S(1)}, bf16[128,4096]{1,0:T(8,128)(2,1)S(1)}, u32[]{:S(2)}, u32[]{:S(2)}) collective-permute-start(bf16[128,4096]{1,0:T(8,128)(2,1)S(1)} %bitcast.17), channel_id=1, source_target_pairs={{0,1},{1,0},{2,3},{3,2},{4,5},{5,4},{6,7},{7,6},{8,9},{9,8},{10,11... | collective-permute-start | bytes 3145736 | tf_op jit(solution)/shard_map/ppermute | solution.py:42
  60.8 6.4 %collective-permute-done.10.refs_2_ = bf16[512,512]{1,0:T(8,128)(2,1)S(1)} collective-permute-done((bf16[512,512]{1,0:T(8,128)(2,1)S(1)}, bf16[512,512]{1,0:T(8,128)(2,1)S(1)}, u32[]{:S(2)}, u32[]{:S(2)}) %collective-permute-start.10) | collective-permute-done | bytes 524320 | tf_op jit(solution)/shard_map/ppermute | solution.py:42
  67.2 5.3 %collective-permute-start.12 = (bf16[512,512]{1,0:T(8,128)(2,1)S(1)}, bf16[512,512]{1,0:T(8,128)(2,1)S(1)}, u32[]{:S(2)}, u32[]{:S(2)}) collective-permute-start(bf16[512,512]{1,0:T(8,128)(2,1)S(1)} %collective-permute-done.10.refs_2_), channel_id=1, source_target_pairs={{0,56},{1,57},{2,58},{3,59},{4,60},{5,61},{6,62},{7,63},{8,0},{9,1... | collective-permute-start | bytes 1572872 | tf_op jit(solution)/shard_map/ppermute | solution.py:42
  74.4 7.1 %collective-permute-start.20 = (bf16[256,2048]{1,0:T(8,128)(2,1)}, bf16[256,2048]{1,0:T(8,128)(2,1)S(1)}, u32[]{:S(2)}, u32[]{:S(2)}) collective-permute-start(bf16[256,2048]{1,0:T(8,128)(2,1)} %collective-permute-done.11), channel_id=1, source_target_pairs={{0,132},{8,140},{16,148},{24,156},{32,164},{40,172},{48,180},{56,1... | collective-permute-start | bytes 3145736 | tf_op jit(solution)/shard_map/ppermute | solution.py:60
  82.6 5.3 %collective-permute-start.15 = (bf16[256,512]{1,0:T(8,128)(2,1)S(1)}, bf16[256,512]{1,0:T(8,128)(2,1)S(1)}, u32[]{:S(2)}, u32[]{:S(2)}) collective-permute-start(bf16[256,512]{1,0:T(8,128)(2,1)S(1)} %slice.61), channel_id=1, source_target_pairs={{0,56},{1,57},{2,58},{3,59},{4,60},{5,61},{6,62},{7,63},{8,0},{9,1... | collective-permute-start | bytes 786440 | tf_op jit(solution)/shard_map/ppermute | solution.py:42
  91.9 5.5 %collective-permute-done.14.refs_4_ = bf16[256,512]{1,0:T(8,128)(2,1)S(1)} collective-permute-done((bf16[256,512]{1,0:T(8,128)(2,1)S(1)}, bf16[256,512]{1,0:T(8,128)(2,1)S(1)}, u32[]{:S(2)}, u32[]{:S(2)}) %collective-permute-start.14) | collective-permute-done | bytes 262176 | tf_op jit(solution)/shard_map/ppermute | solution.py:42
  98.7 2.4 %collective-permute-start.16 = (bf16[256,512]{1,0:T(8,128)(2,1)S(1)}, bf16[256,512]{1,0:T(8,128)(2,1)S(1)}, u32[]{:S(2)}, u32[]{:S(2)}) collective-permute-start(bf16[256,512]{1,0:T(8,128)(2,1)S(1)} %project.2.own_ref), channel_id=1, source_target_pairs={{0,2},{1,3},{2,4},{3,5},{4,6},{5,7},{6,8},{7,9},{8,10},{9,11},{10,... | collective-permute-start | bytes 786440 | tf_op jit(solution)/shard_map/ppermute | solution.py:143
  102.4 7.8 %collective-permute-start.17 = (bf16[272,512]{1,0:T(8,128)(2,1)S(1)}, bf16[272,512]{1,0:T(8,128)(2,1)S(1)}, u32[]{:S(2)}, u32[]{:S(2)}) collective-permute-start(bf16[272,512]{1,0:T(8,128)(2,1)S(1)} %project.3), channel_id=1, source_target_pairs={{0,4},{8,12},{16,20},{24,28},{32,36},{40,44},{48,52},{56,60},{1,69... | collective-permute-start | bytes 835592 | tf_op jit(solution)/shard_map/ppermute | solution.py:60
  111.5 7.0 %backward_attention.1 = (f32[256,2048]{1,0:T(8,128)S(1)}, bf16[256,512]{1,0:T(8,128)(2,1)S(1)}, f32[256,512]{1,0:T(8,128)S(1)}) custom-call(s32[1]{0:T(128)} %bitcast.index_ref, bf16[256,4096]{1,0:T(8,128)(2,1)S(1)} %get-tuple-element.35.normed_ref, bf16[256,2048]{1,0:T(8,128)(2,1)S(1)} %pad_maximum_fusion.2.upper_ref, ...), custom_call_target="tpu_custom_call" | custom-call | flops 3000000000 | bytes 1000000 | tf_op jit(solution)/shard_map/backward_attention/pallas_call | solution.py:301
  118.6 4.0 %collective-permute-start.19 = (bf16[272,512]{1,0:T(8,128)(2,1)S(1)}, bf16[272,512]{1,0:T(8,128)(2,1)S(1)}, u32[]{:S(2)}, u32[]{:S(2)}) collective-permute-start(bf16[272,512]{1,0:T(8,128)(2,1)S(1)} %collective-permute-done.17), channel_id=1, source_target_pairs={{0,132},{8,140},{16,148},{24,156},{32,164},{40,172},{48,180},{56,1... | collective-permute-start | bytes 835592 | tf_op jit(solution)/shard_map/ppermute | solution.py:60
  123.9 10.7 %collective-permute-done.18.after_ref = bf16[256,512]{1,0:T(8,128)(2,1)S(1)} collective-permute-done((bf16[256,512]{1,0:T(8,128)(2,1)S(1)}, bf16[256,512]{1,0:T(8,128)(2,1)S(1)}, u32[]{:S(2)}, u32[]{:S(2)}) %collective-permute-start.18) | collective-permute-done | bytes 262176 | tf_op jit(solution)/shard_map/ppermute | solution.py:148
  136.7 10.0 %collective-permute-start.21 = (bf16[128,4096]{1,0:T(8,128)(2,1)S(1)}, bf16[128,4096]{1,0:T(8,128)(2,1)S(1)}, u32[]{:S(2)}, u32[]{:S(2)}) collective-permute-start(bf16[128,4096]{1,0:T(8,128)(2,1)S(1)} %partial_grad.3), channel_id=1, source_target_pairs={{0,1},{1,0},{2,3},{3,2},{4,5},{5,4},{6,7},{7,6},{8,9},{9,8},{10,11... | collective-permute-start | bytes 3145736 | tf_op jit(solution)/shard_map/ppermute | solution.py:42
  153.4 4.2 %collective-permute-start.23 = (f32[1,4096]{1,0:T(1,128)S(1)}, f32[1,4096]{1,0:T(1,128)S(1)}, u32[]{:S(2)}, u32[]{:S(2)}) collective-permute-start(f32[1,4096]{1,0:T(1,128)S(1)} %get-tuple-element.52), channel_id=1, source_target_pairs={{0,1},{1,0},{2,3},{3,2},{4,5},{5,4},{6,7},{7,6},{8,9},{9,8},{10,11... | collective-permute-start | bytes 49160 | tf_op jit(solution)/shard_map/ppermute | solution.py:42
  158.4 2.7 %collective-permute-start.24 = (f32[1,4096]{1,0:T(1,128)S(1)}, f32[1,4096]{1,0:T(1,128)S(1)}, u32[]{:S(2)}, u32[]{:S(2)}) collective-permute-start(f32[1,4096]{1,0:T(1,128)S(1)} %add.73), channel_id=1, source_target_pairs={{0,8},{1,9},{2,10},{3,11},{4,12},{5,13},{6,14},{7,15},{8,0},{9,1},... | collective-permute-start | bytes 49160 | tf_op jit(solution)/shard_map/ppermute | solution.py:42
  163.2 5.8 %collective-permute-start.25 = (f32[1,4096]{1,0:T(1,128)S(1)}, f32[1,4096]{1,0:T(1,128)S(1)}, u32[]{:S(2)}, u32[]{:S(2)}) collective-permute-start(f32[1,4096]{1,0:T(1,128)S(1)} %add.74), channel_id=1, source_target_pairs={{0,16},{1,17},{2,18},{3,19},{4,20},{5,21},{6,22},{7,23},{8,24},{9,... | collective-permute-start | bytes 49160 | tf_op jit(solution)/shard_map/ppermute | solution.py:42
  170.5 5.7 %collective-permute-start.26 = (f32[1,4096]{1,0:T(1,128)S(1)}, f32[1,4096]{1,0:T(1,128)S(1)}, u32[]{:S(2)}, u32[]{:S(2)}) collective-permute-start(f32[1,4096]{1,0:T(1,128)S(1)} %add.75), channel_id=1, source_target_pairs={{0,32},{1,33},{2,34},{3,35},{4,36},{5,37},{6,38},{7,39},{8,40},{9,... | collective-permute-start | bytes 49160 | tf_op jit(solution)/shard_map/ppermute | solution.py:42
  176.2 2.7 %collective-permute-done.26 = f32[1,4096]{1,0:T(1,128)S(1)} collective-permute-done((f32[1,4096]{1,0:T(1,128)S(1)}, f32[1,4096]{1,0:T(1,128)S(1)}, u32[]{:S(2)}, u32[]{:S(2)}) %collective-permute-start.26) | collective-permute-done | bytes 16416 | tf_op jit(solution)/shard_map/ppermute | solution.py:42
  178.9 6.0 %collective-permute-start.29 = (bf16[128,4096]{1,0:T(8,128)(2,1)S(1)}, bf16[128,4096]{1,0:T(8,128)(2,1)S(1)}, u32[]{:S(2)}, u32[]{:S(2)}) collective-permute-start(bf16[128,4096]{1,0:T(8,128)(2,1)S(1)} %collective-permute-done.22), channel_id=1, source_target_pairs={{0,4},{8,12},{16,20},{24,28},{32,36},{40,44},{48,52},{56,60},{1,45... | collective-permute-start | bytes 3145736 | tf_op jit(solution)/shard_map/ppermute | solution.py:60
  184.9 6.7 %forward_attention.1 = bf16[256,2048]{1,0:T(8,128)(2,1)S(1)} custom-call(s32[1]{0:T(128)} %bitcast.index_ref, bf16[256,2048]{1,0:T(8,128)(2,1)S(1)} %collective-permute-done.20.x_ref, bf16[272,512]{1,0:T(8,128)(2,1)S(1)} %collective-permute-done.19.beside_ref.own_ref, bf16[272,512]{1,0:T(8,128)(2,1)S(1)} %collective-permute-done.27.before_ref, ...), custom_call_target="tpu_custom_call" | custom-call | flops 1000 | bytes 1000 | tf_op jit(solution)/shard_map/forward_attention/pallas_call | solution.py:228
  191.6 2.9 %collective-permute-start.28 = (bf16[128,2048]{1,0:T(8,128)(2,1)S(1)}, bf16[128,2048]{1,0:T(8,128)(2,1)S(1)}, u32[]{:S(2)}, u32[]{:S(2)}) collective-permute-start(bf16[128,2048]{1,0:T(8,128)(2,1)S(1)} %broadcast_select_fusion.6), channel_id=1, source_target_pairs={{0,1},{1,0},{2,3},{3,2},{4,5},{5,4},{6,7},{7,6},{8,9},{9,8},{10,11... | collective-permute-start | bytes 1572872 | tf_op jit(solution)/shard_map/ppermute | solution.py:42
  194.5 7.4 %collective-permute-start.30 = (f32[1,4096]{1,0:T(1,128)S(1)}, f32[1,4096]{1,0:T(1,128)S(1)}, u32[]{:S(2)}, u32[]{:S(2)}) collective-permute-start(f32[1,4096]{1,0:T(1,128)S(1)} %add.76), channel_id=1, source_target_pairs={{0,2},{1,3},{2,0},{3,1},{4,6},{5,7},{6,4},{7,5},{8,10},{9,11},{10,... | collective-permute-start | bytes 49160 | tf_op jit(solution)/shard_map/ppermute | solution.py:42
  201.9 9.2 %collective-permute-done.30 = f32[1,4096]{1,0:T(1,128)S(1)} collective-permute-done((f32[1,4096]{1,0:T(1,128)S(1)}, f32[1,4096]{1,0:T(1,128)S(1)}, u32[]{:S(2)}, u32[]{:S(2)}) %collective-permute-start.30) | collective-permute-done | bytes 16416 | tf_op jit(solution)/shard_map/ppermute | solution.py:42
  (97 shorter events, 47.5 us)
Async XLA Ops:
  1.6 9.7 %collective-permute-start = (bf16[64,512]{1,0:T(8,128)(2,1)S(1)}, bf16[64,512]{1,0:T(8,128)(2,1)S(1)}, u32[]{:S(2)}, u32[]{:S(2)}) collective-permute-start(bf16[64,512]{1,0:T(8,128)(2,1)S(1)} %broadcast_select_fusion.12), channel_id=1, source_target_pairs={{0,1},{1,0},{2,3},{3,2},{4,5},{5,4},{6,7},{7,6},{8,9},{9,8},{10,11... | collective-permute-start | bytes 196616 | tf_op jit(solution)/shard_map/ppermute | solution.py:42
  11.4 9.8 %collective-permute-start.1 = (bf16[128,512]{1,0:T(8,128)(2,1)S(1)}, bf16[128,512]{1,0:T(8,128)(2,1)S(1)}, u32[]{:S(2)}, u32[]{:S(2)}) collective-permute-start(bf16[128,512]{1,0:T(8,128)(2,1)S(1)} %pad_maximum_fusion.3), channel_id=1, source_target_pairs={{0,6},{1,7},{2,0},{3,1},{4,2},{5,3},{6,4},{7,5},{8,14},{9,15},{10,... | collective-permute-start | bytes 393224 | tf_op jit(solution)/shard_map/ppermute | solution.py:42
  13.6 10.2 %collective-permute-start.2 = (bf16[128,512]{1,0:T(8,128)(2,1)S(1)}, bf16[128,512]{1,0:T(8,128)(2,1)S(1)}, u32[]{:S(2)}, u32[]{:S(2)}) collective-permute-start(bf16[128,512]{1,0:T(8,128)(2,1)S(1)} %pad_maximum_fusion.3), channel_id=1, source_target_pairs={{0,4},{1,5},{2,6},{3,7},{4,0},{5,1},{6,2},{7,3},{8,12},{9,13},{10,... | collective-permute-start | bytes 393224 | tf_op jit(solution)/shard_map/ppermute | solution.py:42
  15.5 11.9 %collective-permute-start.4 = (bf16[128,4096]{1,0:T(8,128)(2,1)}, bf16[128,4096]{1,0:T(8,128)(2,1)S(1)}, u32[]{:S(2)}, u32[]{:S(2)}) collective-permute-start(bf16[128,4096]{1,0:T(8,128)(2,1)} %bitcast.23), channel_id=1, source_target_pairs={{0,1},{1,0},{2,3},{3,2},{4,5},{5,4},{6,7},{7,6},{8,9},{9,8},{10,11... | collective-permute-start | bytes 3145736 | tf_op jit(solution)/shard_map/ppermute | solution.py:42
  18.1 9.2 %collective-permute-start.3 = (bf16[128,512]{1,0:T(8,128)(2,1)S(1)}, bf16[128,512]{1,0:T(8,128)(2,1)S(1)}, u32[]{:S(2)}, u32[]{:S(2)}) collective-permute-start(bf16[128,512]{1,0:T(8,128)(2,1)S(1)} %pad_maximum_fusion.3), channel_id=1, source_target_pairs={{0,2},{1,3},{2,4},{3,5},{4,6},{5,7},{6,0},{7,1},{8,10},{9,11},{10,... | collective-permute-start | bytes 393224 | tf_op jit(solution)/shard_map/ppermute | solution.py:42
  29.0 16.3 %collective-permute-start.5 = (bf16[512,512]{1,0:T(8,128)(2,1)S(1)}, bf16[512,512]{1,0:T(8,128)(2,1)S(1)}, u32[]{:S(2)}, u32[]{:S(2)}) collective-permute-start(bf16[512,512]{1,0:T(8,128)(2,1)S(1)} %constant_dynamic-slice_fusion.1.refs_0_), channel_id=1, source_target_pairs={{0,8},{1,9},{2,10},{3,11},{4,12},{5,13},{6,14},{7,15},{8,16},{9,17... | collective-permute-start | bytes 1572872 | tf_op jit(solution)/shard_map/ppermute | solution.py:42
  31.9 19.7 %collective-permute-start.8 = (bf16[512,512]{1,0:T(8,128)(2,1)S(1)}, bf16[512,512]{1,0:T(8,128)(2,1)S(1)}, u32[]{:S(2)}, u32[]{:S(2)}) collective-permute-start(bf16[512,512]{1,0:T(8,128)(2,1)S(1)} %constant_dynamic-slice_fusion.1.refs_0_), channel_id=1, source_target_pairs={{0,56},{1,57},{2,58},{3,59},{4,60},{5,61},{6,62},{7,63},{8,0},{9,1... | collective-permute-start | bytes 1572872 | tf_op jit(solution)/shard_map/ppermute | solution.py:42
  35.7 31.5 %collective-permute-start.11 = (bf16[256,2048]{1,0:T(8,128)(2,1)}, bf16[256,2048]{1,0:T(8,128)(2,1)}, u32[]{:S(2)}, u32[]{:S(2)}) collective-permute-start(bf16[256,2048]{1,0:T(8,128)(2,1)} %fusion.6), channel_id=1, source_target_pairs={{0,4},{8,12},{16,20},{24,28},{32,36},{40,44},{48,52},{56,60},{1,69... | collective-permute-start | bytes 3145736 | tf_op jit(solution)/shard_map/ppermute | solution.py:60
  46.4 35.1 %collective-permute-start.7 = (bf16[128,2048]{1,0:T(8,128)(2,1)S(1)}, bf16[128,2048]{1,0:T(8,128)(2,1)S(1)}, u32[]{:S(2)}, u32[]{:S(2)}) collective-permute-start(bf16[128,2048]{1,0:T(8,128)(2,1)S(1)} %constant_dynamic-slice_fusion), channel_id=1, source_target_pairs={{0,1},{1,0},{2,3},{3,2},{4,5},{5,4},{6,7},{7,6},{8,9},{9,8},{10,11... | collective-permute-start | bytes 1572872 | tf_op jit(solution)/shard_map/ppermute | solution.py:42
  49.7 17.5 %collective-permute-start.9 = (bf16[512,512]{1,0:T(8,128)(2,1)S(1)}, bf16[512,512]{1,0:T(8,128)(2,1)S(1)}, u32[]{:S(2)}, u32[]{:S(2)}) collective-permute-start(bf16[512,512]{1,0:T(8,128)(2,1)S(1)} %collective-permute-done.5.refs_8_), channel_id=1, source_target_pairs={{0,8},{1,9},{2,10},{3,11},{4,12},{5,13},{6,14},{7,15},{8,16},{9,17... | collective-permute-start | bytes 1572872 | tf_op jit(solution)/shard_map/ppermute | solution.py:42
  51.6 15.6 %collective-permute-start.10 = (bf16[512,512]{1,0:T(8,128)(2,1)S(1)}, bf16[512,512]{1,0:T(8,128)(2,1)S(1)}, u32[]{:S(2)}, u32[]{:S(2)}) collective-permute-start(bf16[512,512]{1,0:T(8,128)(2,1)S(1)} %collective-permute-done.8.refs_1_), channel_id=1, source_target_pairs={{0,56},{1,57},{2,58},{3,59},{4,60},{5,61},{6,62},{7,63},{8,0},{9,1... | collective-permute-start | bytes 1572872 | tf_op jit(solution)/shard_map/ppermute | solution.py:42
  58.2 29.7 %collective-permute-start.6 = (bf16[128,4096]{1,0:T(8,128)(2,1)S(1)}, bf16[128,4096]{1,0:T(8,128)(2,1)S(1)}, u32[]{:S(2)}, u32[]{:S(2)}) collective-permute-start(bf16[128,4096]{1,0:T(8,128)(2,1)S(1)} %bitcast.17), channel_id=1, source_target_pairs={{0,1},{1,0},{2,3},{3,2},{4,5},{5,4},{6,7},{7,6},{8,9},{9,8},{10,11... | collective-permute-start | bytes 3145736 | tf_op jit(solution)/shard_map/ppermute | solution.py:42
  67.2 15.4 %collective-permute-start.12 = (bf16[512,512]{1,0:T(8,128)(2,1)S(1)}, bf16[512,512]{1,0:T(8,128)(2,1)S(1)}, u32[]{:S(2)}, u32[]{:S(2)}) collective-permute-start(bf16[512,512]{1,0:T(8,128)(2,1)S(1)} %collective-permute-done.10.refs_2_), channel_id=1, source_target_pairs={{0,56},{1,57},{2,58},{3,59},{4,60},{5,61},{6,62},{7,63},{8,0},{9,1... | collective-permute-start | bytes 1572872 | tf_op jit(solution)/shard_map/ppermute | solution.py:42
  72.5 16.1 %collective-permute-start.13 = (bf16[512,512]{1,0:T(8,128)(2,1)S(1)}, bf16[512,512]{1,0:T(8,128)(2,1)S(1)}, u32[]{:S(2)}, u32[]{:S(2)}) collective-permute-start(bf16[512,512]{1,0:T(8,128)(2,1)S(1)} %collective-permute-done.9.refs_7_), channel_id=1, source_target_pairs={{0,8},{1,9},{2,10},{3,11},{4,12},{5,13},{6,14},{7,15},{8,16},{9,17... | collective-permute-start | bytes 1572872 | tf_op jit(solution)/shard_map/ppermute | solution.py:42
  74.4 49.5 %collective-permute-start.20 = (bf16[256,2048]{1,0:T(8,128)(2,1)}, bf16[256,2048]{1,0:T(8,128)(2,1)S(1)}, u32[]{:S(2)}, u32[]{:S(2)}) collective-permute-start(bf16[256,2048]{1,0:T(8,128)(2,1)} %collective-permute-done.11), channel_id=1, source_target_pairs={{0,132},{8,140},{16,148},{24,156},{32,164},{40,172},{48,180},{56,1... | collective-permute-start | bytes 3145736 | tf_op jit(solution)/shard_map/ppermute | solution.py:60
  82.6 9.3 %collective-permute-start.15 = (bf16[256,512]{1,0:T(8,128)(2,1)S(1)}, bf16[256,512]{1,0:T(8,128)(2,1)S(1)}, u32[]{:S(2)}, u32[]{:S(2)}) collective-permute-start(bf16[256,512]{1,0:T(8,128)(2,1)S(1)} %slice.61), channel_id=1, source_target_pairs={{0,56},{1,57},{2,58},{3,59},{4,60},{5,61},{6,62},{7,63},{8,0},{9,1... | collective-permute-start | bytes 786440 | tf_op jit(solution)/shard_map/ppermute | solution.py:42
  88.7 8.8 %collective-permute-start.14 = (bf16[256,512]{1,0:T(8,128)(2,1)S(1)}, bf16[256,512]{1,0:T(8,128)(2,1)S(1)}, u32[]{:S(2)}, u32[]{:S(2)}) collective-permute-start(bf16[256,512]{1,0:T(8,128)(2,1)S(1)} %slice.60), channel_id=1, source_target_pairs={{0,8},{1,9},{2,10},{3,11},{4,12},{5,13},{6,14},{7,15},{8,16},{9,17... | collective-permute-start | bytes 786440 | tf_op jit(solution)/shard_map/ppermute | solution.py:42
  98.7 12.9 %collective-permute-start.16 = (bf16[256,512]{1,0:T(8,128)(2,1)S(1)}, bf16[256,512]{1,0:T(8,128)(2,1)S(1)}, u32[]{:S(2)}, u32[]{:S(2)}) collective-permute-start(bf16[256,512]{1,0:T(8,128)(2,1)S(1)} %project.2.own_ref), channel_id=1, source_target_pairs={{0,2},{1,3},{2,4},{3,5},{4,6},{5,7},{6,8},{7,9},{8,10},{9,11},{10,... | collective-permute-start | bytes 786440 | tf_op jit(solution)/shard_map/ppermute | solution.py:143
  102.4 16.2 %collective-permute-start.17 = (bf16[272,512]{1,0:T(8,128)(2,1)S(1)}, bf16[272,512]{1,0:T(8,128)(2,1)S(1)}, u32[]{:S(2)}, u32[]{:S(2)}) collective-permute-start(bf16[272,512]{1,0:T(8,128)(2,1)S(1)} %project.3), channel_id=1, source_target_pairs={{0,4},{8,12},{16,20},{24,28},{32,36},{40,44},{48,52},{56,60},{1,69... | collective-permute-start | bytes 835592 | tf_op jit(solution)/shard_map/ppermute | solution.py:60
  118.6 16.1 %collective-permute-start.19 = (bf16[272,512]{1,0:T(8,128)(2,1)S(1)}, bf16[272,512]{1,0:T(8,128)(2,1)S(1)}, u32[]{:S(2)}, u32[]{:S(2)}) collective-permute-start(bf16[272,512]{1,0:T(8,128)(2,1)S(1)} %collective-permute-done.17), channel_id=1, source_target_pairs={{0,132},{8,140},{16,148},{24,156},{32,164},{40,172},{48,180},{56,1... | collective-permute-start | bytes 835592 | tf_op jit(solution)/shard_map/ppermute | solution.py:60
  122.6 12.1 %collective-permute-start.18 = (bf16[256,512]{1,0:T(8,128)(2,1)S(1)}, bf16[256,512]{1,0:T(8,128)(2,1)S(1)}, u32[]{:S(2)}, u32[]{:S(2)}) collective-permute-start(bf16[256,512]{1,0:T(8,128)(2,1)S(1)} %get-tuple-element.46), channel_id=1, source_target_pairs={{2,0},{3,1},{4,2},{5,3},{6,4},{7,5},{8,6},{9,7},{10,8},{11,9},{12,... | collective-permute-start | bytes 786440 | tf_op jit(solution)/shard_map/ppermute | solution.py:148
  136.7 12.1 %collective-permute-start.21 = (bf16[128,4096]{1,0:T(8,128)(2,1)S(1)}, bf16[128,4096]{1,0:T(8,128)(2,1)S(1)}, u32[]{:S(2)}, u32[]{:S(2)}) collective-permute-start(bf16[128,4096]{1,0:T(8,128)(2,1)S(1)} %partial_grad.3), channel_id=1, source_target_pairs={{0,1},{1,0},{2,3},{3,2},{4,5},{5,4},{6,7},{7,6},{8,9},{9,8},{10,11... | collective-permute-start | bytes 3145736 | tf_op jit(solution)/shard_map/ppermute | solution.py:42
  150.2 28.7 %collective-permute-start.22 = (bf16[128,4096]{1,0:T(8,128)(2,1)S(1)}, bf16[128,4096]{1,0:T(8,128)(2,1)S(1)}, u32[]{:S(2)}, u32[]{:S(2)}) collective-permute-start(bf16[128,4096]{1,0:T(8,128)(2,1)S(1)} %get-tuple-element.51), channel_id=1, source_target_pairs={{0,4},{8,12},{16,20},{24,28},{32,36},{40,44},{48,52},{56,60},{1,69... | collective-permute-start | bytes 3145736 | tf_op jit(solution)/shard_map/ppermute | solution.py:60
  152.1 32.8 %collective-permute-start.27 = (bf16[272,512]{1,0:T(8,128)(2,1)S(1)}, bf16[272,512]{1,0:T(8,128)(2,1)S(1)}, u32[]{:S(2)}, u32[]{:S(2)}) collective-permute-start(bf16[272,512]{1,0:T(8,128)(2,1)S(1)} %collective-permute-done.19.beside_ref.own_ref), channel_id=1, source_target_pairs={{0,2},{1,3},{2,4},{3,5},{4,6},{5,7},{6,8},{7,9},{8,10},{9,11},{10,... | collective-permute-start | bytes 835592 | tf_op jit(solution)/shard_map/ppermute | solution.py:143
  153.4 5.0 %collective-permute-start.23 = (f32[1,4096]{1,0:T(1,128)S(1)}, f32[1,4096]{1,0:T(1,128)S(1)}, u32[]{:S(2)}, u32[]{:S(2)}) collective-permute-start(f32[1,4096]{1,0:T(1,128)S(1)} %get-tuple-element.52), channel_id=1, source_target_pairs={{0,1},{1,0},{2,3},{3,2},{4,5},{5,4},{6,7},{7,6},{8,9},{9,8},{10,11... | collective-permute-start | bytes 49160 | tf_op jit(solution)/shard_map/ppermute | solution.py:42
  158.4 4.8 %collective-permute-start.24 = (f32[1,4096]{1,0:T(1,128)S(1)}, f32[1,4096]{1,0:T(1,128)S(1)}, u32[]{:S(2)}, u32[]{:S(2)}) collective-permute-start(f32[1,4096]{1,0:T(1,128)S(1)} %add.73), channel_id=1, source_target_pairs={{0,8},{1,9},{2,10},{3,11},{4,12},{5,13},{6,14},{7,15},{8,0},{9,1},... | collective-permute-start | bytes 49160 | tf_op jit(solution)/shard_map/ppermute | solution.py:42
  163.2 7.2 %collective-permute-start.25 = (f32[1,4096]{1,0:T(1,128)S(1)}, f32[1,4096]{1,0:T(1,128)S(1)}, u32[]{:S(2)}, u32[]{:S(2)}) collective-permute-start(f32[1,4096]{1,0:T(1,128)S(1)} %add.74), channel_id=1, source_target_pairs={{0,16},{1,17},{2,18},{3,19},{4,20},{5,21},{6,22},{7,23},{8,24},{9,... | collective-permute-start | bytes 49160 | tf_op jit(solution)/shard_map/ppermute | solution.py:42
  170.5 8.4 %collective-permute-start.26 = (f32[1,4096]{1,0:T(1,128)S(1)}, f32[1,4096]{1,0:T(1,128)S(1)}, u32[]{:S(2)}, u32[]{:S(2)}) collective-permute-start(f32[1,4096]{1,0:T(1,128)S(1)} %add.75), channel_id=1, source_target_pairs={{0,32},{1,33},{2,34},{3,35},{4,36},{5,37},{6,38},{7,39},{8,40},{9,... | collective-permute-start | bytes 49160 | tf_op jit(solution)/shard_map/ppermute | solution.py:42
  178.9 32.4 %collective-permute-start.29 = (bf16[128,4096]{1,0:T(8,128)(2,1)S(1)}, bf16[128,4096]{1,0:T(8,128)(2,1)S(1)}, u32[]{:S(2)}, u32[]{:S(2)}) collective-permute-start(bf16[128,4096]{1,0:T(8,128)(2,1)S(1)} %collective-permute-done.22), channel_id=1, source_target_pairs={{0,4},{8,12},{16,20},{24,28},{32,36},{40,44},{48,52},{56,60},{1,45... | collective-permute-start | bytes 3145736 | tf_op jit(solution)/shard_map/ppermute | solution.py:60
  191.6 19.6 %collective-permute-start.28 = (bf16[128,2048]{1,0:T(8,128)(2,1)S(1)}, bf16[128,2048]{1,0:T(8,128)(2,1)S(1)}, u32[]{:S(2)}, u32[]{:S(2)}) collective-permute-start(bf16[128,2048]{1,0:T(8,128)(2,1)S(1)} %broadcast_select_fusion.6), channel_id=1, source_target_pairs={{0,1},{1,0},{2,3},{3,2},{4,5},{5,4},{6,7},{7,6},{8,9},{9,8},{10,11... | collective-permute-start | bytes 1572872 | tf_op jit(solution)/shard_map/ppermute | solution.py:42
  194.5 16.6 %collective-permute-start.30 = (f32[1,4096]{1,0:T(1,128)S(1)}, f32[1,4096]{1,0:T(1,128)S(1)}, u32[]{:S(2)}, u32[]{:S(2)}) collective-permute-start(f32[1,4096]{1,0:T(1,128)S(1)} %add.76), channel_id=1, source_target_pairs={{0,2},{1,3},{2,0},{3,1},{4,6},{5,7},{6,4},{7,5},{8,10},{9,11},{10,... | collective-permute-start | bytes 49160 | tf_op jit(solution)/shard_map/ppermute | solution.py:42
  211.3 5.4 %collective-permute-start.31 = (f32[1,4096]{1,0:T(1,128)S(1)}, f32[1,4096]{1,0:T(1,128)S(1)}, u32[]{:S(2)}, u32[]{:S(2)}) collective-permute-start(f32[1,4096]{1,0:T(1,128)S(1)} %add.77), channel_id=1, source_target_pairs={{0,4},{1,5},{2,6},{3,7},{4,0},{5,1},{6,2},{7,3},{8,12},{9,13},{10,... | collective-permute-start | bytes 49160 | tf_op jit(solution)/shard_map/ppermute | solution.py:42
  (8 other events, 120.7 us)

commit v7 on v6

--- a/solution.py
+++ b/solution.py
@@ -125,7 +125,7 @@
     rising.append(up(rising[2][:middle]))
     falling.append(down(falling[2][middle:]))
     pieces = [run, *falling[:3], rising[3], falling[3], *rising[:3][::-1]]
-    return pieces, arrive(crossing, 1), rising[0]
+    return pieces, arrive(crossing, 1), falling[0]
 
 
 def swap(value):
@@ -477,16 +477,17 @@
     kv_half = halfway(project(y_place, chip_fwd, pieces, beside, True))
 
     dq, grad_before, grad_own = backward_attention(place, chip_back, chip_upper, before, kv_back)
-    kv_half, grad_before = lax.optimization_barrier((kv_half, grad_before))
-    after, kv_here, crossed = lax.optimization_barrier(
-        (to_chip_before(grad_before), arrive(kv_half, 1), crossed)
-    )
+    kv_half, after, crossed = lax.optimization_barrier(
+        (kv_half, to_chip_before(grad_before), crossed)
+    )
+    kv_here = arrive(kv_half, 1)
 
     def partial(row, kind):
         return partial_grad(jnp.stack([row, core, y]), grad_own, after, dq, pieces, kind)
 
     away = swap(partial(1 - core, jnp.bfloat16))
     home = partial(core, jnp.float32)
+    away, home, kv_here = lax.optimization_barrier((away, home, kv_here))
     grad_in, gain_grad = input_grad(home, away, x_back, upper_in, gains)
     half_sent = halfway(grad_in)
 

time: 221 us -> 226 us (1.023)
  the two profiles are of different devices: /device:TPU:1 before, /device:TPU:8 now
where the time goes in v7:
time: 226 us; the launch traced here: 225 us
  starting transfers between devices  101 us (45%)
  waiting for transfers between devices  90.4 us (40%)
  Pallas kernels  21.6 us (10%)
  other arithmetic  7.58 us (3%)
  local copies, waits for them, and re-layouts  3.36 us (1%)
    ppermute x23, starting transfers between devices, over_ctx(): return lax.ppermute(value, 'ctx', ctx_pairs(move))  65.8 us
    ppermute x23, waiting for transfers between devices, over_ctx(): return lax.ppermute(value, 'ctx', ctx_pairs(move))  63.7 us
    ppermute x6, starting transfers between devices, over_grid(): return lax.ppermute(value, ('section', 'ctx'), grid_pairs(move))  18.9 us
    ppermute x6, waiting for transfers between devices, over_grid(): return lax.ppermute(value, ('section', 'ctx'), grid_pairs(move))  15 us
    ppermute x2, starting transfers between devices, to_next_chip(): return lax.ppermute(value, 'ctx', pairs)  9.93 us
    ppermute x2, waiting for transfers between devices, to_next_chip(): return lax.ppermute(value, 'ctx', pairs)  7.96 us
    pallas_call x1, Pallas kernels, backward_attention(): pl.pallas_call(backward_kernel, grid_spec=pltpu.PrefetchScalarGridSpec(nu...  6.99 us
    pallas_call x1, Pallas kernels, forward_attention(): pl.pallas_call(forward_kernel, grid_spec=pltpu.PrefetchScalarGridSpec(num...  6.65 us
  transfers between devices with their start and end apart: 32, of which 18 were waited for; matrix products, arithmetic and copies ran while one was open for 3% of the time, Pallas kernels for 8%

profile of v7, /device:TPU:8, one launch (start us, length us, event | category | flops | bytes accessed | tf_op | source)
XLA Modules:
  0.0 225.0 jit_solution(5587125511730374957)
XLA Ops:
  4.8 7.9 %collective-permute-start.1 = (bf16[128,512]{1,0:T(8,128)(2,1)S(1)}, bf16[128,512]{1,0:T(8,128)(2,1)S(1)}, u32[]{:S(2)}, u32[]{:S(2)}) collective-permute-start(bf16[128,512]{1,0:T(8,128)(2,1)S(1)} %pad_maximum_fusion.3), channel_id=1, source_target_pairs={{0,6},{1,7},{2,0},{3,1},{4,2},{5,3},{6,4},{7,5},{8,14},{9,15},{10,... | collective-permute-start | bytes 393224 | tf_op jit(solution)/shard_map/ppermute | solution.py:42
  19.1 3.0 %collective-permute-done.2 = bf16[128,512]{1,0:T(8,128)(2,1)S(1)} collective-permute-done((bf16[128,512]{1,0:T(8,128)(2,1)S(1)}, bf16[128,512]{1,0:T(8,128)(2,1)S(1)}, u32[]{:S(2)}, u32[]{:S(2)}) %collective-permute-start.2) | collective-permute-done | bytes 131104 | tf_op jit(solution)/shard_map/ppermute | solution.py:42
  22.2 4.1 %collective-permute-done.3 = bf16[128,512]{1,0:T(8,128)(2,1)S(1)} collective-permute-done((bf16[128,512]{1,0:T(8,128)(2,1)S(1)}, bf16[128,512]{1,0:T(8,128)(2,1)S(1)}, u32[]{:S(2)}, u32[]{:S(2)}) %collective-permute-start.3) | collective-permute-done | bytes 131104 | tf_op jit(solution)/shard_map/ppermute | solution.py:42
  27.9 2.7 %collective-permute-start.5 = (bf16[512,512]{1,0:T(8,128)(2,1)S(1)}, bf16[512,512]{1,0:T(8,128)(2,1)S(1)}, u32[]{:S(2)}, u32[]{:S(2)}) collective-permute-start(bf16[512,512]{1,0:T(8,128)(2,1)S(1)} %constant_dynamic-slice_fusion.1.refs_0_), channel_id=1, source_target_pairs={{0,56},{1,57},{2,58},{3,59},{4,60},{5,61},{6,62},{7,63},{8,0},{9,1... | collective-permute-start | bytes 1572872 | tf_op jit(solution)/shard_map/ppermute | solution.py:42
  30.6 3.3 %collective-permute-start.8 = (bf16[512,512]{1,0:T(8,128)(2,1)S(1)}, bf16[512,512]{1,0:T(8,128)(2,1)S(1)}, u32[]{:S(2)}, u32[]{:S(2)}) collective-permute-start(bf16[512,512]{1,0:T(8,128)(2,1)S(1)} %constant_dynamic-slice_fusion.1.refs_0_), channel_id=1, source_target_pairs={{0,8},{1,9},{2,10},{3,11},{4,12},{5,13},{6,14},{7,15},{8,16},{9,17... | collective-permute-start | bytes 1572872 | tf_op jit(solution)/shard_map/ppermute | solution.py:42
  33.9 3.3 %collective-permute-start.11 = (bf16[256,2048]{1,0:T(8,128)(2,1)}, bf16[256,2048]{1,0:T(8,128)(2,1)}, u32[]{:S(2)}, u32[]{:S(2)}) collective-permute-start(bf16[256,2048]{1,0:T(8,128)(2,1)} %fusion.6), channel_id=1, source_target_pairs={{0,4},{8,12},{16,20},{24,28},{32,36},{40,44},{48,52},{56,60},{1,69... | collective-permute-start | bytes 3145736 | tf_op jit(solution)/shard_map/ppermute | solution.py:60
  37.2 6.2 %collective-permute-done.5.refs_1_ = bf16[512,512]{1,0:T(8,128)(2,1)S(1)} collective-permute-done((bf16[512,512]{1,0:T(8,128)(2,1)S(1)}, bf16[512,512]{1,0:T(8,128)(2,1)S(1)}, u32[]{:S(2)}, u32[]{:S(2)}) %collective-permute-start.5) | collective-permute-done | bytes 524320 | tf_op jit(solution)/shard_map/ppermute | solution.py:42
  46.4 3.3 %collective-permute-start.10 = (bf16[512,512]{1,0:T(8,128)(2,1)S(1)}, bf16[512,512]{1,0:T(8,128)(2,1)S(1)}, u32[]{:S(2)}, u32[]{:S(2)}) collective-permute-start(bf16[512,512]{1,0:T(8,128)(2,1)S(1)} %collective-permute-done.5.refs_1_), channel_id=1, source_target_pairs={{0,56},{1,57},{2,58},{3,59},{4,60},{5,61},{6,62},{7,63},{8,0},{9,1... | collective-permute-start | bytes 1572872 | tf_op jit(solution)/shard_map/ppermute | solution.py:42
  49.8 2.5 %collective-permute-start.9 = (bf16[512,512]{1,0:T(8,128)(2,1)S(1)}, bf16[512,512]{1,0:T(8,128)(2,1)S(1)}, u32[]{:S(2)}, u32[]{:S(2)}) collective-permute-start(bf16[512,512]{1,0:T(8,128)(2,1)S(1)} %collective-permute-done.8.refs_8_), channel_id=1, source_target_pairs={{0,8},{1,9},{2,10},{3,11},{4,12},{5,13},{6,14},{7,15},{8,16},{9,17... | collective-permute-start | bytes 1572872 | tf_op jit(solution)/shard_map/ppermute | solution.py:42
  56.3 11.4 %collective-permute-done.9.refs_7_ = bf16[512,512]{1,0:T(8,128)(2,1)S(1)} collective-permute-done((bf16[512,512]{1,0:T(8,128)(2,1)S(1)}, bf16[512,512]{1,0:T(8,128)(2,1)S(1)}, u32[]{:S(2)}, u32[]{:S(2)}) %collective-permute-start.9) | collective-permute-done | bytes 524320 | tf_op jit(solution)/shard_map/ppermute | solution.py:42
  67.7 4.8 %collective-permute-start.12 = (bf16[512,512]{1,0:T(8,128)(2,1)S(1)}, bf16[512,512]{1,0:T(8,128)(2,1)S(1)}, u32[]{:S(2)}, u32[]{:S(2)}) collective-permute-start(bf16[512,512]{1,0:T(8,128)(2,1)S(1)} %collective-permute-done.10.refs_2_), channel_id=1, source_target_pairs={{0,56},{1,57},{2,58},{3,59},{4,60},{5,61},{6,62},{7,63},{8,0},{9,1... | collective-permute-start | bytes 1572872 | tf_op jit(solution)/shard_map/ppermute | solution.py:42
  74.5 4.3 %collective-permute-start.19 = (bf16[256,2048]{1,0:T(8,128)(2,1)}, bf16[256,2048]{1,0:T(8,128)(2,1)S(1)}, u32[]{:S(2)}, u32[]{:S(2)}) collective-permute-start(bf16[256,2048]{1,0:T(8,128)(2,1)} %collective-permute-done.11), channel_id=1, source_target_pairs={{0,132},{8,140},{16,148},{24,156},{32,164},{40,172},{48,180},{56,1... | collective-permute-start | bytes 3145736 | tf_op jit(solution)/shard_map/ppermute | solution.py:60
  79.1 4.1 %collective-permute-done.12.refs_3_ = bf16[512,512]{1,0:T(8,128)(2,1)S(1)} collective-permute-done((bf16[512,512]{1,0:T(8,128)(2,1)S(1)}, bf16[512,512]{1,0:T(8,128)(2,1)S(1)}, u32[]{:S(2)}, u32[]{:S(2)}) %collective-permute-start.12) | collective-permute-done | bytes 524320 | tf_op jit(solution)/shard_map/ppermute | solution.py:42
  83.3 4.4 %collective-permute-start.15 = (bf16[256,512]{1,0:T(8,128)(2,1)S(1)}, bf16[256,512]{1,0:T(8,128)(2,1)S(1)}, u32[]{:S(2)}, u32[]{:S(2)}) collective-permute-start(bf16[256,512]{1,0:T(8,128)(2,1)S(1)} %slice.61), channel_id=1, source_target_pairs={{0,56},{1,57},{2,58},{3,59},{4,60},{5,61},{6,62},{7,63},{8,0},{9,1... | collective-permute-start | bytes 786440 | tf_op jit(solution)/shard_map/ppermute | solution.py:42
  92.1 4.8 %collective-permute-done.14.refs_4_ = bf16[256,512]{1,0:T(8,128)(2,1)S(1)} collective-permute-done((bf16[256,512]{1,0:T(8,128)(2,1)S(1)}, bf16[256,512]{1,0:T(8,128)(2,1)S(1)}, u32[]{:S(2)}, u32[]{:S(2)}) %collective-permute-start.14) | collective-permute-done | bytes 262176 | tf_op jit(solution)/shard_map/ppermute | solution.py:42
  101.5 5.0 %collective-permute-start.17 = (bf16[272,512]{1,0:T(8,128)(2,1)S(1)}, bf16[272,512]{1,0:T(8,128)(2,1)S(1)}, u32[]{:S(2)}, u32[]{:S(2)}) collective-permute-start(bf16[272,512]{1,0:T(8,128)(2,1)S(1)} %project.3), channel_id=1, source_target_pairs={{0,4},{8,12},{16,20},{24,28},{32,36},{40,44},{48,52},{56,60},{1,69... | collective-permute-start | bytes 835592 | tf_op jit(solution)/shard_map/ppermute | solution.py:60
  106.5 8.0 %collective-permute-done.16.before_ref = bf16[256,512]{1,0:T(8,128)(2,1)S(1)} collective-permute-done((bf16[256,512]{1,0:T(8,128)(2,1)S(1)}, bf16[256,512]{1,0:T(8,128)(2,1)S(1)}, u32[]{:S(2)}, u32[]{:S(2)}) %collective-permute-start.16) | collective-permute-done | bytes 262176 | tf_op jit(solution)/shard_map/ppermute | solution.py:143
  114.4 7.0 %backward_attention.1 = (f32[256,2048]{1,0:T(8,128)S(1)}, bf16[256,512]{1,0:T(8,128)(2,1)S(1)}, f32[256,512]{1,0:T(8,128)S(1)}) custom-call(s32[1]{0:T(128)} %bitcast.index_ref, bf16[256,4096]{1,0:T(8,128)(2,1)S(1)} %get-tuple-element.36.normed_ref, bf16[256,2048]{1,0:T(8,128)(2,1)S(1)} %pad_maximum_fusion.2.upper_ref, ...), custom_call_target="tpu_custom_call" | custom-call | flops 3000000000 | bytes 1000000 | tf_op jit(solution)/shard_map/backward_attention/pallas_call | solution.py:301
  121.4 6.0 %collective-permute-start.18 = (bf16[256,512]{1,0:T(8,128)(2,1)S(1)}, bf16[256,512]{1,0:T(8,128)(2,1)S(1)}, u32[]{:S(2)}, u32[]{:S(2)}) collective-permute-start(bf16[256,512]{1,0:T(8,128)(2,1)S(1)} %get-tuple-element.46), channel_id=1, source_target_pairs={{2,0},{3,1},{4,2},{5,3},{6,4},{7,5},{8,6},{9,7},{10,8},{11,9},{12,... | collective-permute-start | bytes 786440 | tf_op jit(solution)/shard_map/ppermute | solution.py:148
  127.6 3.8 %collective-permute-done.18.after_ref = bf16[256,512]{1,0:T(8,128)(2,1)S(1)} collective-permute-done((bf16[256,512]{1,0:T(8,128)(2,1)S(1)}, bf16[256,512]{1,0:T(8,128)(2,1)S(1)}, u32[]{:S(2)}, u32[]{:S(2)}) %collective-permute-start.18) | collective-permute-done | bytes 262176 | tf_op jit(solution)/shard_map/ppermute | solution.py:148
  135.3 2.5 %collective-permute-start.21 = (bf16[272,512]{1,0:T(8,128)(2,1)S(1)}, bf16[272,512]{1,0:T(8,128)(2,1)S(1)}, u32[]{:S(2)}, u32[]{:S(2)}) collective-permute-start(bf16[272,512]{1,0:T(8,128)(2,1)S(1)} %collective-permute-done.17), channel_id=1, source_target_pairs={{0,132},{8,140},{16,148},{24,156},{32,164},{40,172},{48,180},{56,1... | collective-permute-start | bytes 835592 | tf_op jit(solution)/shard_map/ppermute | solution.py:60
  139.9 10.7 %collective-permute-done.21.beside_ref.own_ref = bf16[272,512]{1,0:T(8,128)(2,1)S(1)} collective-permute-done((bf16[272,512]{1,0:T(8,128)(2,1)S(1)}, bf16[272,512]{1,0:T(8,128)(2,1)S(1)}, u32[]{:S(2)}, u32[]{:S(2)}) %collective-permute-start.21) | collective-permute-done | bytes 278560 | tf_op jit(solution)/shard_map/ppermute | solution.py:60
  154.0 7.8 %collective-permute-start.27 = (bf16[272,512]{1,0:T(8,128)(2,1)S(1)}, bf16[272,512]{1,0:T(8,128)(2,1)S(1)}, u32[]{:S(2)}, u32[]{:S(2)}) collective-permute-start(bf16[272,512]{1,0:T(8,128)(2,1)S(1)} %collective-permute-done.21.beside_ref.own_ref), channel_id=1, source_target_pairs={{0,2},{1,3},{2,4},{3,5},{4,6},{5,7},{6,8},{7,9},{8,10},{9,11},{10,... | collective-permute-start | bytes 835592 | tf_op jit(solution)/shard_map/ppermute | solution.py:143
  166.8 3.7 %collective-permute-done.24 = f32[1,4096]{1,0:T(1,128)S(1)} collective-permute-done((f32[1,4096]{1,0:T(1,128)S(1)}, f32[1,4096]{1,0:T(1,128)S(1)}, u32[]{:S(2)}, u32[]{:S(2)}) %collective-permute-start.24) | collective-permute-done | bytes 16416 | tf_op jit(solution)/shard_map/ppermute | solution.py:42
  172.5 4.6 %collective-permute-done.25 = f32[1,4096]{1,0:T(1,128)S(1)} collective-permute-done((f32[1,4096]{1,0:T(1,128)S(1)}, f32[1,4096]{1,0:T(1,128)S(1)}, u32[]{:S(2)}, u32[]{:S(2)}) %collective-permute-start.25) | collective-permute-done | bytes 16416 | tf_op jit(solution)/shard_map/ppermute | solution.py:42
  177.1 4.7 %collective-permute-start.26 = (f32[1,4096]{1,0:T(1,128)S(1)}, f32[1,4096]{1,0:T(1,128)S(1)}, u32[]{:S(2)}, u32[]{:S(2)}) collective-permute-start(f32[1,4096]{1,0:T(1,128)S(1)} %add.75), channel_id=1, source_target_pairs={{0,32},{1,33},{2,34},{3,35},{4,36},{5,37},{6,38},{7,39},{8,40},{9,... | collective-permute-start | bytes 49160 | tf_op jit(solution)/shard_map/ppermute | solution.py:42
  181.8 4.8 %collective-permute-done.26 = f32[1,4096]{1,0:T(1,128)S(1)} collective-permute-done((f32[1,4096]{1,0:T(1,128)S(1)}, f32[1,4096]{1,0:T(1,128)S(1)}, u32[]{:S(2)}, u32[]{:S(2)}) %collective-permute-start.26) | collective-permute-done | bytes 16416 | tf_op jit(solution)/shard_map/ppermute | solution.py:42
  188.6 6.7 %forward_attention.1 = bf16[256,2048]{1,0:T(8,128)(2,1)S(1)} custom-call(s32[1]{0:T(128)} %bitcast.index_ref, bf16[256,2048]{1,0:T(8,128)(2,1)S(1)} %collective-permute-done.19.x_ref, bf16[272,512]{1,0:T(8,128)(2,1)S(1)} %collective-permute-done.21.beside_ref.own_ref, bf16[272,512]{1,0:T(8,128)(2,1)S(1)} %collective-permute-done.27.before_ref, ...), custom_call_target="tpu_custom_call" | custom-call | flops 1000 | bytes 1000 | tf_op jit(solution)/shard_map/forward_attention/pallas_call | solution.py:228
  197.2 4.6 %collective-permute-start.30 = (f32[1,4096]{1,0:T(1,128)S(1)}, f32[1,4096]{1,0:T(1,128)S(1)}, u32[]{:S(2)}, u32[]{:S(2)}) collective-permute-start(f32[1,4096]{1,0:T(1,128)S(1)} %add.76), channel_id=1, source_target_pairs={{0,2},{1,3},{2,0},{3,1},{4,6},{5,7},{6,4},{7,5},{8,10},{9,11},{10,... | collective-permute-start | bytes 49160 | tf_op jit(solution)/shard_map/ppermute | solution.py:42
  201.8 10.6 %collective-permute-done.30 = f32[1,4096]{1,0:T(1,128)S(1)} collective-permute-done((f32[1,4096]{1,0:T(1,128)S(1)}, f32[1,4096]{1,0:T(1,128)S(1)}, u32[]{:S(2)}, u32[]{:S(2)}) %collective-permute-start.30) | collective-permute-done | bytes 16416 | tf_op jit(solution)/shard_map/ppermute | solution.py:42
  212.6 4.3 %collective-permute-done.29 = bf16[128,4096]{1,0:T(8,128)(2,1)S(1)} collective-permute-done((bf16[128,4096]{1,0:T(8,128)(2,1)S(1)}, bf16[128,4096]{1,0:T(8,128)(2,1)S(1)}, u32[]{:S(2)}, u32[]{:S(2)}) %collective-permute-start.29) | collective-permute-done | bytes 1048608 | tf_op jit(solution)/shard_map/ppermute | solution.py:60
  219.9 3.5 %collective-permute-done.31 = f32[1,4096]{1,0:T(1,128)S(1)} collective-permute-done((f32[1,4096]{1,0:T(1,128)S(1)}, f32[1,4096]{1,0:T(1,128)S(1)}, u32[]{:S(2)}, u32[]{:S(2)}) %collective-permute-start.31) | collective-permute-done | bytes 16416 | tf_op jit(solution)/shard_map/ppermute | solution.py:42
  (97 shorter events, 55.2 us)
Async XLA Ops:
  1.6 3.1 %collective-permute-start = (bf16[64,512]{1,0:T(8,128)(2,1)S(1)}, bf16[64,512]{1,0:T(8,128)(2,1)S(1)}, u32[]{:S(2)}, u32[]{:S(2)}) collective-permute-start(bf16[64,512]{1,0:T(8,128)(2,1)S(1)} %broadcast_select_fusion.12), channel_id=1, source_target_pairs={{0,1},{1,0},{2,3},{3,2},{4,5},{5,4},{6,7},{7,6},{8,9},{9,8},{10,11... | collective-permute-start | bytes 196616 | tf_op jit(solution)/shard_map/ppermute | solution.py:42
  4.8 14.3 %collective-permute-start.1 = (bf16[128,512]{1,0:T(8,128)(2,1)S(1)}, bf16[128,512]{1,0:T(8,128)(2,1)S(1)}, u32[]{:S(2)}, u32[]{:S(2)}) collective-permute-start(bf16[128,512]{1,0:T(8,128)(2,1)S(1)} %pad_maximum_fusion.3), channel_id=1, source_target_pairs={{0,6},{1,7},{2,0},{3,1},{4,2},{5,3},{6,4},{7,5},{8,14},{9,15},{10,... | collective-permute-start | bytes 393224 | tf_op jit(solution)/shard_map/ppermute | solution.py:42
  12.7 9.4 %collective-permute-start.2 = (bf16[128,512]{1,0:T(8,128)(2,1)S(1)}, bf16[128,512]{1,0:T(8,128)(2,1)S(1)}, u32[]{:S(2)}, u32[]{:S(2)}) collective-permute-start(bf16[128,512]{1,0:T(8,128)(2,1)S(1)} %pad_maximum_fusion.3), channel_id=1, source_target_pairs={{0,4},{1,5},{2,6},{3,7},{4,0},{5,1},{6,2},{7,3},{8,12},{9,13},{10,... | collective-permute-start | bytes 393224 | tf_op jit(solution)/shard_map/ppermute | solution.py:42
  14.7 11.7 %collective-permute-start.4 = (bf16[128,4096]{1,0:T(8,128)(2,1)}, bf16[128,4096]{1,0:T(8,128)(2,1)S(1)}, u32[]{:S(2)}, u32[]{:S(2)}) collective-permute-start(bf16[128,4096]{1,0:T(8,128)(2,1)} %bitcast.23), channel_id=1, source_target_pairs={{0,1},{1,0},{2,3},{3,2},{4,5},{5,4},{6,7},{7,6},{8,9},{9,8},{10,11... | collective-permute-start | bytes 3145736 | tf_op jit(solution)/shard_map/ppermute | solution.py:42
  16.6 9.6 %collective-permute-start.3 = (bf16[128,512]{1,0:T(8,128)(2,1)S(1)}, bf16[128,512]{1,0:T(8,128)(2,1)S(1)}, u32[]{:S(2)}, u32[]{:S(2)}) collective-permute-start(bf16[128,512]{1,0:T(8,128)(2,1)S(1)} %pad_maximum_fusion.3), channel_id=1, source_target_pairs={{0,2},{1,3},{2,4},{3,5},{4,6},{5,7},{6,0},{7,1},{8,10},{9,11},{10,... | collective-permute-start | bytes 393224 | tf_op jit(solution)/shard_map/ppermute | solution.py:42
  27.9 15.6 %collective-permute-start.5 = (bf16[512,512]{1,0:T(8,128)(2,1)S(1)}, bf16[512,512]{1,0:T(8,128)(2,1)S(1)}, u32[]{:S(2)}, u32[]{:S(2)}) collective-permute-start(bf16[512,512]{1,0:T(8,128)(2,1)S(1)} %constant_dynamic-slice_fusion.1.refs_0_), channel_id=1, source_target_pairs={{0,56},{1,57},{2,58},{3,59},{4,60},{5,61},{6,62},{7,63},{8,0},{9,1... | collective-permute-start | bytes 1572872 | tf_op jit(solution)/shard_map/ppermute | solution.py:42
  30.6 19.2 %collective-permute-start.8 = (bf16[512,512]{1,0:T(8,128)(2,1)S(1)}, bf16[512,512]{1,0:T(8,128)(2,1)S(1)}, u32[]{:S(2)}, u32[]{:S(2)}) collective-permute-start(bf16[512,512]{1,0:T(8,128)(2,1)S(1)} %constant_dynamic-slice_fusion.1.refs_0_), channel_id=1, source_target_pairs={{0,8},{1,9},{2,10},{3,11},{4,12},{5,13},{6,14},{7,15},{8,16},{9,17... | collective-permute-start | bytes 1572872 | tf_op jit(solution)/shard_map/ppermute | solution.py:42
  33.9 33.9 %collective-permute-start.11 = (bf16[256,2048]{1,0:T(8,128)(2,1)}, bf16[256,2048]{1,0:T(8,128)(2,1)}, u32[]{:S(2)}, u32[]{:S(2)}) collective-permute-start(bf16[256,2048]{1,0:T(8,128)(2,1)} %fusion.6), channel_id=1, source_target_pairs={{0,4},{8,12},{16,20},{24,28},{32,36},{40,44},{48,52},{56,60},{1,69... | collective-permute-start | bytes 3145736 | tf_op jit(solution)/shard_map/ppermute | solution.py:60
  44.5 34.3 %collective-permute-start.7 = (bf16[128,2048]{1,0:T(8,128)(2,1)S(1)}, bf16[128,2048]{1,0:T(8,128)(2,1)S(1)}, u32[]{:S(2)}, u32[]{:S(2)}) collective-permute-start(bf16[128,2048]{1,0:T(8,128)(2,1)S(1)} %constant_dynamic-slice_fusion), channel_id=1, source_target_pairs={{0,1},{1,0},{2,3},{3,2},{4,5},{5,4},{6,7},{7,6},{8,9},{9,8},{10,11... | collective-permute-start | bytes 1572872 | tf_op jit(solution)/shard_map/ppermute | solution.py:42
  46.4 21.3 %collective-permute-start.10 = (bf16[512,512]{1,0:T(8,128)(2,1)S(1)}, bf16[512,512]{1,0:T(8,128)(2,1)S(1)}, u32[]{:S(2)}, u32[]{:S(2)}) collective-permute-start(bf16[512,512]{1,0:T(8,128)(2,1)S(1)} %collective-permute-done.5.refs_1_), channel_id=1, source_target_pairs={{0,56},{1,57},{2,58},{3,59},{4,60},{5,61},{6,62},{7,63},{8,0},{9,1... | collective-permute-start | bytes 1572872 | tf_op jit(solution)/shard_map/ppermute | solution.py:42
  49.8 17.9 %collective-permute-start.9 = (bf16[512,512]{1,0:T(8,128)(2,1)S(1)}, bf16[512,512]{1,0:T(8,128)(2,1)S(1)}, u32[]{:S(2)}, u32[]{:S(2)}) collective-permute-start(bf16[512,512]{1,0:T(8,128)(2,1)S(1)} %collective-permute-done.8.refs_8_), channel_id=1, source_target_pairs={{0,8},{1,9},{2,10},{3,11},{4,12},{5,13},{6,14},{7,15},{8,16},{9,17... | collective-permute-start | bytes 1572872 | tf_op jit(solution)/shard_map/ppermute | solution.py:42
  54.4 33.4 %collective-permute-start.6 = (bf16[128,4096]{1,0:T(8,128)(2,1)S(1)}, bf16[128,4096]{1,0:T(8,128)(2,1)S(1)}, u32[]{:S(2)}, u32[]{:S(2)}) collective-permute-start(bf16[128,4096]{1,0:T(8,128)(2,1)S(1)} %bitcast.17), channel_id=1, source_target_pairs={{0,1},{1,0},{2,3},{3,2},{4,5},{5,4},{6,7},{7,6},{8,9},{9,8},{10,11... | collective-permute-start | bytes 3145736 | tf_op jit(solution)/shard_map/ppermute | solution.py:42
  67.7 15.6 %collective-permute-start.12 = (bf16[512,512]{1,0:T(8,128)(2,1)S(1)}, bf16[512,512]{1,0:T(8,128)(2,1)S(1)}, u32[]{:S(2)}, u32[]{:S(2)}) collective-permute-start(bf16[512,512]{1,0:T(8,128)(2,1)S(1)} %collective-permute-done.10.refs_2_), channel_id=1, source_target_pairs={{0,56},{1,57},{2,58},{3,59},{4,60},{5,61},{6,62},{7,63},{8,0},{9,1... | collective-permute-start | bytes 1572872 | tf_op jit(solution)/shard_map/ppermute | solution.py:42
  72.6 15.8 %collective-permute-start.13 = (bf16[512,512]{1,0:T(8,128)(2,1)S(1)}, bf16[512,512]{1,0:T(8,128)(2,1)S(1)}, u32[]{:S(2)}, u32[]{:S(2)}) collective-permute-start(bf16[512,512]{1,0:T(8,128)(2,1)S(1)} %collective-permute-done.9.refs_7_), channel_id=1, source_target_pairs={{0,8},{1,9},{2,10},{3,11},{4,12},{5,13},{6,14},{7,15},{8,16},{9,17... | collective-permute-start | bytes 1572872 | tf_op jit(solution)/shard_map/ppermute | solution.py:42
  74.5 53.1 %collective-permute-start.19 = (bf16[256,2048]{1,0:T(8,128)(2,1)}, bf16[256,2048]{1,0:T(8,128)(2,1)S(1)}, u32[]{:S(2)}, u32[]{:S(2)}) collective-permute-start(bf16[256,2048]{1,0:T(8,128)(2,1)} %collective-permute-done.11), channel_id=1, source_target_pairs={{0,132},{8,140},{16,148},{24,156},{32,164},{40,172},{48,180},{56,1... | collective-permute-start | bytes 3145736 | tf_op jit(solution)/shard_map/ppermute | solution.py:60
  83.3 8.8 %collective-permute-start.15 = (bf16[256,512]{1,0:T(8,128)(2,1)S(1)}, bf16[256,512]{1,0:T(8,128)(2,1)S(1)}, u32[]{:S(2)}, u32[]{:S(2)}) collective-permute-start(bf16[256,512]{1,0:T(8,128)(2,1)S(1)} %slice.61), channel_id=1, source_target_pairs={{0,56},{1,57},{2,58},{3,59},{4,60},{5,61},{6,62},{7,63},{8,0},{9,1... | collective-permute-start | bytes 786440 | tf_op jit(solution)/shard_map/ppermute | solution.py:42
  88.4 8.5 %collective-permute-start.14 = (bf16[256,512]{1,0:T(8,128)(2,1)S(1)}, bf16[256,512]{1,0:T(8,128)(2,1)S(1)}, u32[]{:S(2)}, u32[]{:S(2)}) collective-permute-start(bf16[256,512]{1,0:T(8,128)(2,1)S(1)} %slice.60), channel_id=1, source_target_pairs={{0,8},{1,9},{2,10},{3,11},{4,12},{5,13},{6,14},{7,15},{8,16},{9,17... | collective-permute-start | bytes 786440 | tf_op jit(solution)/shard_map/ppermute | solution.py:42
  98.1 16.3 %collective-permute-start.16 = (bf16[256,512]{1,0:T(8,128)(2,1)S(1)}, bf16[256,512]{1,0:T(8,128)(2,1)S(1)}, u32[]{:S(2)}, u32[]{:S(2)}) collective-permute-start(bf16[256,512]{1,0:T(8,128)(2,1)S(1)} %project.2.own_ref), channel_id=1, source_target_pairs={{0,2},{1,3},{2,4},{3,5},{4,6},{5,7},{6,8},{7,9},{8,10},{9,11},{10,... | collective-permute-start | bytes 786440 | tf_op jit(solution)/shard_map/ppermute | solution.py:143
  101.5 26.0 %collective-permute-start.17 = (bf16[272,512]{1,0:T(8,128)(2,1)S(1)}, bf16[272,512]{1,0:T(8,128)(2,1)S(1)}, u32[]{:S(2)}, u32[]{:S(2)}) collective-permute-start(bf16[272,512]{1,0:T(8,128)(2,1)S(1)} %project.3), channel_id=1, source_target_pairs={{0,4},{8,12},{16,20},{24,28},{32,36},{40,44},{48,52},{56,60},{1,69... | collective-permute-start | bytes 835592 | tf_op jit(solution)/shard_map/ppermute | solution.py:60
  121.4 9.9 %collective-permute-start.18 = (bf16[256,512]{1,0:T(8,128)(2,1)S(1)}, bf16[256,512]{1,0:T(8,128)(2,1)S(1)}, u32[]{:S(2)}, u32[]{:S(2)}) collective-permute-start(bf16[256,512]{1,0:T(8,128)(2,1)S(1)} %get-tuple-element.46), channel_id=1, source_target_pairs={{2,0},{3,1},{4,2},{5,3},{6,4},{7,5},{8,6},{9,7},{10,8},{11,9},{12,... | collective-permute-start | bytes 786440 | tf_op jit(solution)/shard_map/ppermute | solution.py:148
  133.4 17.3 %collective-permute-start.20 = (bf16[128,4096]{1,0:T(8,128)(2,1)S(1)}, bf16[128,4096]{1,0:T(8,128)(2,1)S(1)}, u32[]{:S(2)}, u32[]{:S(2)}) collective-permute-start(bf16[128,4096]{1,0:T(8,128)(2,1)S(1)} %partial_grad.2), channel_id=1, source_target_pairs={{0,1},{1,0},{2,3},{3,2},{4,5},{5,4},{6,7},{7,6},{8,9},{9,8},{10,11... | collective-permute-start | bytes 3145736 | tf_op jit(solution)/shard_map/ppermute | solution.py:42
  135.3 15.3 %collective-permute-start.21 = (bf16[272,512]{1,0:T(8,128)(2,1)S(1)}, bf16[272,512]{1,0:T(8,128)(2,1)S(1)}, u32[]{:S(2)}, u32[]{:S(2)}) collective-permute-start(bf16[272,512]{1,0:T(8,128)(2,1)S(1)} %collective-permute-done.17), channel_id=1, source_target_pairs={{0,132},{8,140},{16,148},{24,156},{32,164},{40,172},{48,180},{56,1... | collective-permute-start | bytes 835592 | tf_op jit(solution)/shard_map/ppermute | solution.py:60
  152.0 34.6 %collective-permute-start.22 = (bf16[128,4096]{1,0:T(8,128)(2,1)S(1)}, bf16[128,4096]{1,0:T(8,128)(2,1)S(1)}, u32[]{:S(2)}, u32[]{:S(2)}) collective-permute-start(bf16[128,4096]{1,0:T(8,128)(2,1)S(1)} %get-tuple-element.53), channel_id=1, source_target_pairs={{0,4},{8,12},{16,20},{24,28},{32,36},{40,44},{48,52},{56,60},{1,69... | collective-permute-start | bytes 3145736 | tf_op jit(solution)/shard_map/ppermute | solution.py:60
  154.0 34.6 %collective-permute-start.27 = (bf16[272,512]{1,0:T(8,128)(2,1)S(1)}, bf16[272,512]{1,0:T(8,128)(2,1)S(1)}, u32[]{:S(2)}, u32[]{:S(2)}) collective-permute-start(bf16[272,512]{1,0:T(8,128)(2,1)S(1)} %collective-permute-done.21.beside_ref.own_ref), channel_id=1, source_target_pairs={{0,2},{1,3},{2,4},{3,5},{4,6},{5,7},{6,8},{7,9},{8,10},{9,11},{10,... | collective-permute-start | bytes 835592 | tf_op jit(solution)/shard_map/ppermute | solution.py:143
  161.8 3.1 %collective-permute-start.23 = (f32[1,4096]{1,0:T(1,128)S(1)}, f32[1,4096]{1,0:T(1,128)S(1)}, u32[]{:S(2)}, u32[]{:S(2)}) collective-permute-start(f32[1,4096]{1,0:T(1,128)S(1)} %get-tuple-element.54), channel_id=1, source_target_pairs={{0,1},{1,0},{2,3},{3,2},{4,5},{5,4},{6,7},{7,6},{8,9},{9,8},{10,11... | collective-permute-start | bytes 49160 | tf_op jit(solution)/shard_map/ppermute | solution.py:42
  164.9 5.6 %collective-permute-start.24 = (f32[1,4096]{1,0:T(1,128)S(1)}, f32[1,4096]{1,0:T(1,128)S(1)}, u32[]{:S(2)}, u32[]{:S(2)}) collective-permute-start(f32[1,4096]{1,0:T(1,128)S(1)} %add.73), channel_id=1, source_target_pairs={{0,8},{1,9},{2,10},{3,11},{4,12},{5,13},{6,14},{7,15},{8,0},{9,1},... | collective-permute-start | bytes 49160 | tf_op jit(solution)/shard_map/ppermute | solution.py:42
  170.5 6.5 %collective-permute-start.25 = (f32[1,4096]{1,0:T(1,128)S(1)}, f32[1,4096]{1,0:T(1,128)S(1)}, u32[]{:S(2)}, u32[]{:S(2)}) collective-permute-start(f32[1,4096]{1,0:T(1,128)S(1)} %add.74), channel_id=1, source_target_pairs={{0,16},{1,17},{2,18},{3,19},{4,20},{5,21},{6,22},{7,23},{8,24},{9,... | collective-permute-start | bytes 49160 | tf_op jit(solution)/shard_map/ppermute | solution.py:42
  177.1 9.5 %collective-permute-start.26 = (f32[1,4096]{1,0:T(1,128)S(1)}, f32[1,4096]{1,0:T(1,128)S(1)}, u32[]{:S(2)}, u32[]{:S(2)}) collective-permute-start(f32[1,4096]{1,0:T(1,128)S(1)} %add.75), channel_id=1, source_target_pairs={{0,32},{1,33},{2,34},{3,35},{4,36},{5,37},{6,38},{7,39},{8,40},{9,... | collective-permute-start | bytes 49160 | tf_op jit(solution)/shard_map/ppermute | solution.py:42
  186.7 30.2 %collective-permute-start.29 = (bf16[128,4096]{1,0:T(8,128)(2,1)S(1)}, bf16[128,4096]{1,0:T(8,128)(2,1)S(1)}, u32[]{:S(2)}, u32[]{:S(2)}) collective-permute-start(bf16[128,4096]{1,0:T(8,128)(2,1)S(1)} %collective-permute-done.22), channel_id=1, source_target_pairs={{0,4},{8,12},{16,20},{24,28},{32,36},{40,44},{48,52},{56,60},{1,45... | collective-permute-start | bytes 3145736 | tf_op jit(solution)/shard_map/ppermute | solution.py:60
  195.3 17.2 %collective-permute-start.28 = (bf16[128,2048]{1,0:T(8,128)(2,1)S(1)}, bf16[128,2048]{1,0:T(8,128)(2,1)S(1)}, u32[]{:S(2)}, u32[]{:S(2)}) collective-permute-start(bf16[128,2048]{1,0:T(8,128)(2,1)S(1)} %broadcast_select_fusion.6), channel_id=1, source_target_pairs={{0,1},{1,0},{2,3},{3,2},{4,5},{5,4},{6,7},{7,6},{8,9},{9,8},{10,11... | collective-permute-start | bytes 1572872 | tf_op jit(solution)/shard_map/ppermute | solution.py:42
  197.2 15.2 %collective-permute-start.30 = (f32[1,4096]{1,0:T(1,128)S(1)}, f32[1,4096]{1,0:T(1,128)S(1)}, u32[]{:S(2)}, u32[]{:S(2)}) collective-permute-start(f32[1,4096]{1,0:T(1,128)S(1)} %add.76), channel_id=1, source_target_pairs={{0,2},{1,3},{2,0},{3,1},{4,6},{5,7},{6,4},{7,5},{8,10},{9,11},{10,... | collective-permute-start | bytes 49160 | tf_op jit(solution)/shard_map/ppermute | solution.py:42
  216.9 6.5 %collective-permute-start.31 = (f32[1,4096]{1,0:T(1,128)S(1)}, f32[1,4096]{1,0:T(1,128)S(1)}, u32[]{:S(2)}, u32[]{:S(2)}) collective-permute-start(f32[1,4096]{1,0:T(1,128)S(1)} %add.77), channel_id=1, source_target_pairs={{0,4},{1,5},{2,6},{3,7},{4,0},{5,1},{6,2},{7,3},{8,12},{9,13},{10,... | collective-permute-start | bytes 49160 | tf_op jit(solution)/shard_map/ppermute | solution.py:42
  (8 other events, 115.0 us)

commit v8 on v7

--- a/solution.py
+++ b/solution.py
@@ -125,7 +125,7 @@
     rising.append(up(rising[2][:middle]))
     falling.append(down(falling[2][middle:]))
     pieces = [run, *falling[:3], rising[3], falling[3], *rising[:3][::-1]]
-    return pieces, arrive(crossing, 1), falling[0]
+    return pieces, arrive(crossing, 1), rising[0]
 
 
 def swap(value):
@@ -321,7 +321,7 @@
             jax.ShapeDtypeStruct(own.shape, jnp.float32),
         ],
         compiler_params=pltpu.CompilerParams(vmem_limit_bytes=24 * 2**20),
-        cost_estimate=pl.CostEstimate(flops=3*10**9, bytes_accessed=10**6, transcendentals=0),
+        cost_estimate=BRIEF,
         name="backward_attention",
     )(index, normed, upper, before, own)
 
@@ -480,24 +480,24 @@
     kv_half, after, crossed = lax.optimization_barrier(
         (kv_half, to_chip_before(grad_before), crossed)
     )
-    kv_here = arrive(kv_half, 1)
 
     def partial(row, kind):
         return partial_grad(jnp.stack([row, core, y]), grad_own, after, dq, pieces, kind)
 
     away = swap(partial(1 - core, jnp.bfloat16))
     home = partial(core, jnp.float32)
-    away, home, kv_here = lax.optimization_barrier((away, home, kv_here))
     grad_in, gain_grad = input_grad(home, away, x_back, upper_in, gains)
     half_sent = halfway(grad_in)
 
-    kv_here, _ = lax.optimization_barrier((kv_here, grad_in))
+    kv_half, _ = lax.optimization_barrier((kv_half, grad_in))
+    kv_here = arrive(kv_half, 1)
     before_here = to_next_chip(kv_here)
     gain_grad = gain_grad + swap(gain_grad)
-    for bit in (1, 2, 4):
+    for bit in (1, 2):
         gain_grad = gain_grad + over_ctx(gain_grad, lambda y, z, c: (y ^ bit, z, c))
     half_sent, gain_grad, crossed = lax.optimization_barrier((half_sent, gain_grad, crossed))
     next_grad = arrive(half_sent, -1)
+    gain_grad = gain_grad + over_ctx(gain_grad, lambda y, z, c: (y ^ 4, z, c))
     gain_grad = gain_grad + over_ctx(gain_grad, lambda y, z, c: (y, z ^ 1, c))
     next_grad, gain_grad = lax.optimization_barrier((next_grad, gain_grad))
     gain_grad = gain_grad + over_ctx(gain_grad, lambda y, z, c: (y, z ^ 2, c))

time: 226 us -> 235 us (1.040)
  the two profiles are of different devices: /device:TPU:8 before, /device:TPU:1 now
where the time goes in v8:
time: 235 us; the launch traced here: 233 us
  starting transfers between devices  139 us (59%)
  waiting for transfers between devices  60.3 us (26%)
  Pallas kernels  21.6 us (9%)
  other arithmetic  7.58 us (3%)
  local copies, waits for them, and re-layouts  3.36 us (1%)
    ppermute x23, starting transfers between devices, over_ctx(): return lax.ppermute(value, 'ctx', ctx_pairs(move))  86.8 us
    ppermute x23, waiting for transfers between devices, over_ctx(): return lax.ppermute(value, 'ctx', ctx_pairs(move))  32.7 us
    ppermute x6, starting transfers between devices, over_grid(): return lax.ppermute(value, ('section', 'ctx'), grid_pairs(move))  29.9 us
    ppermute x2, starting transfers between devices, to_next_chip(): return lax.ppermute(value, 'ctx', pairs)  20.7 us
    ppermute x6, waiting for transfers between devices, over_grid(): return lax.ppermute(value, ('section', 'ctx'), grid_pairs(move))  17.3 us
    ppermute x1, waiting for transfers between devices, to_chip_before(): return lax.ppermute(value, 'ctx', pairs)  9 us
    pallas_call x1, Pallas kernels, backward_attention(): pl.pallas_call(backward_kernel, grid_spec=pltpu.PrefetchScalarGridSpec(nu...  7 us
    pallas_call x1, Pallas kernels, forward_attention(): pl.pallas_call(forward_kernel, grid_spec=pltpu.PrefetchScalarGridSpec(num...  6.65 us
  transfers between devices with their start and end apart: 32, of which 16 were waited for; matrix products, arithmetic and copies ran while one was open for 3% of the time, Pallas kernels for 8%

profile of v8, /device:TPU:1, one launch (start us, length us, event | category | flops | bytes accessed | tf_op | source)
XLA Modules:
  0.0 233.0 jit_solution(2791805310140052140)
XLA Ops:
  1.6 8.8 %collective-permute-start = (bf16[64,512]{1,0:T(8,128)(2,1)S(1)}, bf16[64,512]{1,0:T(8,128)(2,1)S(1)}, u32[]{:S(2)}, u32[]{:S(2)}) collective-permute-start(bf16[64,512]{1,0:T(8,128)(2,1)S(1)} %broadcast_select_fusion.12), channel_id=1, source_target_pairs={{0,1},{1,0},{2,3},{3,2},{4,5},{5,4},{6,7},{7,6},{8,9},{9,8},{10,11... | collective-permute-start | bytes 196616 | tf_op jit(solution)/shard_map/ppermute | solution.py:42
  15.5 2.5 %collective-permute-start.4 = (bf16[128,4096]{1,0:T(8,128)(2,1)}, bf16[128,4096]{1,0:T(8,128)(2,1)S(1)}, u32[]{:S(2)}, u32[]{:S(2)}) collective-permute-start(bf16[128,4096]{1,0:T(8,128)(2,1)} %bitcast.23), channel_id=1, source_target_pairs={{0,1},{1,0},{2,3},{3,2},{4,5},{5,4},{6,7},{7,6},{8,9},{9,8},{10,11... | collective-permute-start | bytes 3145736 | tf_op jit(solution)/shard_map/ppermute | solution.py:42
  18.1 3.0 %collective-permute-start.3 = (bf16[128,512]{1,0:T(8,128)(2,1)S(1)}, bf16[128,512]{1,0:T(8,128)(2,1)S(1)}, u32[]{:S(2)}, u32[]{:S(2)}) collective-permute-start(bf16[128,512]{1,0:T(8,128)(2,1)S(1)} %pad_maximum_fusion.3), channel_id=1, source_target_pairs={{0,2},{1,3},{2,4},{3,5},{4,6},{5,7},{6,0},{7,1},{8,10},{9,11},{10,... | collective-permute-start | bytes 393224 | tf_op jit(solution)/shard_map/ppermute | solution.py:42
  21.2 2.6 %collective-permute-done.2 = bf16[128,512]{1,0:T(8,128)(2,1)S(1)} collective-permute-done((bf16[128,512]{1,0:T(8,128)(2,1)S(1)}, bf16[128,512]{1,0:T(8,128)(2,1)S(1)}, u32[]{:S(2)}, u32[]{:S(2)}) %collective-permute-start.2) | collective-permute-done | bytes 131104 | tf_op jit(solution)/shard_map/ppermute | solution.py:42
  23.8 3.5 %collective-permute-done.3 = bf16[128,512]{1,0:T(8,128)(2,1)S(1)} collective-permute-done((bf16[128,512]{1,0:T(8,128)(2,1)S(1)}, bf16[128,512]{1,0:T(8,128)(2,1)S(1)}, u32[]{:S(2)}, u32[]{:S(2)}) %collective-permute-start.3) | collective-permute-done | bytes 131104 | tf_op jit(solution)/shard_map/ppermute | solution.py:42
  29.0 2.9 %collective-permute-start.5 = (bf16[512,512]{1,0:T(8,128)(2,1)S(1)}, bf16[512,512]{1,0:T(8,128)(2,1)S(1)}, u32[]{:S(2)}, u32[]{:S(2)}) collective-permute-start(bf16[512,512]{1,0:T(8,128)(2,1)S(1)} %constant_dynamic-slice_fusion.1.refs_0_), channel_id=1, source_target_pairs={{0,8},{1,9},{2,10},{3,11},{4,12},{5,13},{6,14},{7,15},{8,16},{9,17... | collective-permute-start | bytes 1572872 | tf_op jit(solution)/shard_map/ppermute | solution.py:42
  31.9 3.8 %collective-permute-start.8 = (bf16[512,512]{1,0:T(8,128)(2,1)S(1)}, bf16[512,512]{1,0:T(8,128)(2,1)S(1)}, u32[]{:S(2)}, u32[]{:S(2)}) collective-permute-start(bf16[512,512]{1,0:T(8,128)(2,1)S(1)} %constant_dynamic-slice_fusion.1.refs_0_), channel_id=1, source_target_pairs={{0,56},{1,57},{2,58},{3,59},{4,60},{5,61},{6,62},{7,63},{8,0},{9,1... | collective-permute-start | bytes 1572872 | tf_op jit(solution)/shard_map/ppermute | solution.py:42
  35.7 7.1 %collective-permute-start.11 = (bf16[256,2048]{1,0:T(8,128)(2,1)}, bf16[256,2048]{1,0:T(8,128)(2,1)}, u32[]{:S(2)}, u32[]{:S(2)}) collective-permute-start(bf16[256,2048]{1,0:T(8,128)(2,1)} %fusion.6), channel_id=1, source_target_pairs={{0,4},{8,12},{16,20},{24,28},{32,36},{40,44},{48,52},{56,60},{1,69... | collective-permute-start | bytes 3145736 | tf_op jit(solution)/shard_map/ppermute | solution.py:60
  46.4 3.3 %collective-permute-start.7 = (bf16[128,2048]{1,0:T(8,128)(2,1)S(1)}, bf16[128,2048]{1,0:T(8,128)(2,1)S(1)}, u32[]{:S(2)}, u32[]{:S(2)}) collective-permute-start(bf16[128,2048]{1,0:T(8,128)(2,1)S(1)} %constant_dynamic-slice_fusion), channel_id=1, source_target_pairs={{0,1},{1,0},{2,3},{3,2},{4,5},{5,4},{6,7},{7,6},{8,9},{9,8},{10,11... | collective-permute-start | bytes 1572872 | tf_op jit(solution)/shard_map/ppermute | solution.py:42
  51.6 4.6 %collective-permute-start.10 = (bf16[512,512]{1,0:T(8,128)(2,1)S(1)}, bf16[512,512]{1,0:T(8,128)(2,1)S(1)}, u32[]{:S(2)}, u32[]{:S(2)}) collective-permute-start(bf16[512,512]{1,0:T(8,128)(2,1)S(1)} %collective-permute-done.8.refs_1_), channel_id=1, source_target_pairs={{0,56},{1,57},{2,58},{3,59},{4,60},{5,61},{6,62},{7,63},{8,0},{9,1... | collective-permute-start | bytes 1572872 | tf_op jit(solution)/shard_map/ppermute | solution.py:42
  60.8 6.4 %collective-permute-done.10.refs_2_ = bf16[512,512]{1,0:T(8,128)(2,1)S(1)} collective-permute-done((bf16[512,512]{1,0:T(8,128)(2,1)S(1)}, bf16[512,512]{1,0:T(8,128)(2,1)S(1)}, u32[]{:S(2)}, u32[]{:S(2)}) %collective-permute-start.10) | collective-permute-done | bytes 524320 | tf_op jit(solution)/shard_map/ppermute | solution.py:42
  67.2 5.3 %collective-permute-start.12 = (bf16[512,512]{1,0:T(8,128)(2,1)S(1)}, bf16[512,512]{1,0:T(8,128)(2,1)S(1)}, u32[]{:S(2)}, u32[]{:S(2)}) collective-permute-start(bf16[512,512]{1,0:T(8,128)(2,1)S(1)} %collective-permute-done.10.refs_2_), channel_id=1, source_target_pairs={{0,56},{1,57},{2,58},{3,59},{4,60},{5,61},{6,62},{7,63},{8,0},{9,1... | collective-permute-start | bytes 1572872 | tf_op jit(solution)/shard_map/ppermute | solution.py:42
  74.4 7.1 %collective-permute-start.19 = (bf16[256,2048]{1,0:T(8,128)(2,1)}, bf16[256,2048]{1,0:T(8,128)(2,1)S(1)}, u32[]{:S(2)}, u32[]{:S(2)}) collective-permute-start(bf16[256,2048]{1,0:T(8,128)(2,1)} %collective-permute-done.11), channel_id=1, source_target_pairs={{0,132},{8,140},{16,148},{24,156},{32,164},{40,172},{48,180},{56,1... | collective-permute-start | bytes 3145736 | tf_op jit(solution)/shard_map/ppermute | solution.py:60
  82.6 5.3 %collective-permute-start.15 = (bf16[256,512]{1,0:T(8,128)(2,1)S(1)}, bf16[256,512]{1,0:T(8,128)(2,1)S(1)}, u32[]{:S(2)}, u32[]{:S(2)}) collective-permute-start(bf16[256,512]{1,0:T(8,128)(2,1)S(1)} %slice.61), channel_id=1, source_target_pairs={{0,56},{1,57},{2,58},{3,59},{4,60},{5,61},{6,62},{7,63},{8,0},{9,1... | collective-permute-start | bytes 786440 | tf_op jit(solution)/shard_map/ppermute | solution.py:42
  91.9 5.5 %collective-permute-done.14.refs_4_ = bf16[256,512]{1,0:T(8,128)(2,1)S(1)} collective-permute-done((bf16[256,512]{1,0:T(8,128)(2,1)S(1)}, bf16[256,512]{1,0:T(8,128)(2,1)S(1)}, u32[]{:S(2)}, u32[]{:S(2)}) %collective-permute-start.14) | collective-permute-done | bytes 262176 | tf_op jit(solution)/shard_map/ppermute | solution.py:42
  102.4 7.8 %collective-permute-start.17 = (bf16[272,512]{1,0:T(8,128)(2,1)S(1)}, bf16[272,512]{1,0:T(8,128)(2,1)S(1)}, u32[]{:S(2)}, u32[]{:S(2)}) collective-permute-start(bf16[272,512]{1,0:T(8,128)(2,1)S(1)} %project.3), channel_id=1, source_target_pairs={{0,4},{8,12},{16,20},{24,28},{32,36},{40,44},{48,52},{56,60},{1,69... | collective-permute-start | bytes 835592 | tf_op jit(solution)/shard_map/ppermute | solution.py:60
  111.5 7.0 %backward_attention.1 = (f32[256,2048]{1,0:T(8,128)S(1)}, bf16[256,512]{1,0:T(8,128)(2,1)S(1)}, f32[256,512]{1,0:T(8,128)S(1)}) custom-call(s32[1]{0:T(128)} %bitcast.index_ref, bf16[256,4096]{1,0:T(8,128)(2,1)S(1)} %get-tuple-element.33.normed_ref, bf16[256,2048]{1,0:T(8,128)(2,1)S(1)} %pad_maximum_fusion.2.upper_ref, ...), custom_call_target="tpu_custom_call" | custom-call | flops 1000 | bytes 1000 | tf_op jit(solution)/shard_map/backward_attention/pallas_call | solution.py:301
  119.9 9.0 %collective-permute-done.18.after_ref = bf16[256,512]{1,0:T(8,128)(2,1)S(1)} collective-permute-done((bf16[256,512]{1,0:T(8,128)(2,1)S(1)}, bf16[256,512]{1,0:T(8,128)(2,1)S(1)}, u32[]{:S(2)}, u32[]{:S(2)}) %collective-permute-start.18) | collective-permute-done | bytes 262176 | tf_op jit(solution)/shard_map/ppermute | solution.py:148
  131.0 3.1 %collective-permute-start.20 = (bf16[128,4096]{1,0:T(8,128)(2,1)S(1)}, bf16[128,4096]{1,0:T(8,128)(2,1)S(1)}, u32[]{:S(2)}, u32[]{:S(2)}) collective-permute-start(bf16[128,4096]{1,0:T(8,128)(2,1)S(1)} %partial_grad.3), channel_id=1, source_target_pairs={{0,1},{1,0},{2,3},{3,2},{4,5},{5,4},{6,7},{7,6},{8,9},{9,8},{10,11... | collective-permute-start | bytes 3145736 | tf_op jit(solution)/shard_map/ppermute | solution.py:42
  137.6 3.0 %collective-permute-start.21 = (bf16[128,4096]{1,0:T(8,128)(2,1)S(1)}, bf16[128,4096]{1,0:T(8,128)(2,1)S(1)}, u32[]{:S(2)}, u32[]{:S(2)}) collective-permute-start(bf16[128,4096]{1,0:T(8,128)(2,1)S(1)} %get-tuple-element.47), channel_id=1, source_target_pairs={{0,4},{8,12},{16,20},{24,28},{32,36},{40,44},{48,52},{56,60},{1,69... | collective-permute-start | bytes 3145736 | tf_op jit(solution)/shard_map/ppermute | solution.py:60
  140.6 2.7 %collective-permute-start.25 = (bf16[272,512]{1,0:T(8,128)(2,1)S(1)}, bf16[272,512]{1,0:T(8,128)(2,1)S(1)}, u32[]{:S(2)}, u32[]{:S(2)}) collective-permute-start(bf16[272,512]{1,0:T(8,128)(2,1)S(1)} %collective-permute-done.17), channel_id=1, source_target_pairs={{0,132},{8,140},{16,148},{24,156},{32,164},{40,172},{48,180},{56,1... | collective-permute-start | bytes 835592 | tf_op jit(solution)/shard_map/ppermute | solution.py:60
  143.3 17.2 %collective-permute-done.25.beside_ref.own_ref = bf16[272,512]{1,0:T(8,128)(2,1)S(1)} collective-permute-done((bf16[272,512]{1,0:T(8,128)(2,1)S(1)}, bf16[272,512]{1,0:T(8,128)(2,1)S(1)}, u32[]{:S(2)}, u32[]{:S(2)}) %collective-permute-start.25) | collective-permute-done | bytes 278560 | tf_op jit(solution)/shard_map/ppermute | solution.py:60
  160.5 18.3 %collective-permute-start.26 = (bf16[272,512]{1,0:T(8,128)(2,1)S(1)}, bf16[272,512]{1,0:T(8,128)(2,1)S(1)}, u32[]{:S(2)}, u32[]{:S(2)}) collective-permute-start(bf16[272,512]{1,0:T(8,128)(2,1)S(1)} %collective-permute-done.25.beside_ref.own_ref), channel_id=1, source_target_pairs={{0,2},{1,3},{2,4},{3,5},{4,6},{5,7},{6,8},{7,9},{8,10},{9,11},{10,... | collective-permute-start | bytes 835592 | tf_op jit(solution)/shard_map/ppermute | solution.py:143
  178.8 4.2 %collective-permute-start.22 = (f32[1,4096]{1,0:T(1,128)S(1)}, f32[1,4096]{1,0:T(1,128)S(1)}, u32[]{:S(2)}, u32[]{:S(2)}) collective-permute-start(f32[1,4096]{1,0:T(1,128)S(1)} %get-tuple-element.48), channel_id=1, source_target_pairs={{0,1},{1,0},{2,3},{3,2},{4,5},{5,4},{6,7},{7,6},{8,9},{9,8},{10,11... | collective-permute-start | bytes 49160 | tf_op jit(solution)/shard_map/ppermute | solution.py:42
  183.8 3.6 %collective-permute-start.23 = (f32[1,4096]{1,0:T(1,128)S(1)}, f32[1,4096]{1,0:T(1,128)S(1)}, u32[]{:S(2)}, u32[]{:S(2)}) collective-permute-start(f32[1,4096]{1,0:T(1,128)S(1)} %add.73), channel_id=1, source_target_pairs={{0,8},{1,9},{2,10},{3,11},{4,12},{5,13},{6,14},{7,15},{8,0},{9,1},... | collective-permute-start | bytes 49160 | tf_op jit(solution)/shard_map/ppermute | solution.py:42
  188.5 7.1 %collective-permute-start.24 = (f32[1,4096]{1,0:T(1,128)S(1)}, f32[1,4096]{1,0:T(1,128)S(1)}, u32[]{:S(2)}, u32[]{:S(2)}) collective-permute-start(f32[1,4096]{1,0:T(1,128)S(1)} %add.74), channel_id=1, source_target_pairs={{0,16},{1,17},{2,18},{3,19},{4,20},{5,21},{6,22},{7,23},{8,24},{9,... | collective-permute-start | bytes 49160 | tf_op jit(solution)/shard_map/ppermute | solution.py:42
  199.0 6.7 %forward_attention.1 = bf16[256,2048]{1,0:T(8,128)(2,1)S(1)} custom-call(s32[1]{0:T(128)} %bitcast.index_ref, bf16[256,2048]{1,0:T(8,128)(2,1)S(1)} %collective-permute-done.19.x_ref, bf16[272,512]{1,0:T(8,128)(2,1)S(1)} %collective-permute-done.25.beside_ref.own_ref, bf16[272,512]{1,0:T(8,128)(2,1)S(1)} %collective-permute-done.26.before_ref, ...), custom_call_target="tpu_custom_call" | custom-call | flops 1000 | bytes 1000 | tf_op jit(solution)/shard_map/forward_attention/pallas_call | solution.py:228
  205.8 3.7 %collective-permute-start.27 = (bf16[128,2048]{1,0:T(8,128)(2,1)S(1)}, bf16[128,2048]{1,0:T(8,128)(2,1)S(1)}, u32[]{:S(2)}, u32[]{:S(2)}) collective-permute-start(bf16[128,2048]{1,0:T(8,128)(2,1)S(1)} %broadcast_select_fusion.6), channel_id=1, source_target_pairs={{0,1},{1,0},{2,3},{3,2},{4,5},{5,4},{6,7},{7,6},{8,9},{9,8},{10,11... | collective-permute-start | bytes 1572872 | tf_op jit(solution)/shard_map/ppermute | solution.py:42
  209.5 6.2 %collective-permute-start.29 = (f32[1,4096]{1,0:T(1,128)S(1)}, f32[1,4096]{1,0:T(1,128)S(1)}, u32[]{:S(2)}, u32[]{:S(2)}) collective-permute-start(f32[1,4096]{1,0:T(1,128)S(1)} %add.75), channel_id=1, source_target_pairs={{0,32},{1,33},{2,34},{3,35},{4,36},{5,37},{6,38},{7,39},{8,40},{9,... | collective-permute-start | bytes 49160 | tf_op jit(solution)/shard_map/ppermute | solution.py:42
  217.9 5.0 %collective-permute-start.30 = (f32[1,4096]{1,0:T(1,128)S(1)}, f32[1,4096]{1,0:T(1,128)S(1)}, u32[]{:S(2)}, u32[]{:S(2)}) collective-permute-start(f32[1,4096]{1,0:T(1,128)S(1)} %add.76), channel_id=1, source_target_pairs={{0,2},{1,3},{2,0},{3,1},{4,6},{5,7},{6,4},{7,5},{8,10},{9,11},{10,... | collective-permute-start | bytes 49160 | tf_op jit(solution)/shard_map/ppermute | solution.py:42
  222.9 2.9 %collective-permute-done.30 = f32[1,4096]{1,0:T(1,128)S(1)} collective-permute-done((f32[1,4096]{1,0:T(1,128)S(1)}, f32[1,4096]{1,0:T(1,128)S(1)}, u32[]{:S(2)}, u32[]{:S(2)}) %collective-permute-start.30) | collective-permute-done | bytes 16416 | tf_op jit(solution)/shard_map/ppermute | solution.py:42
  228.9 2.5 %collective-permute-done.31 = f32[1,4096]{1,0:T(1,128)S(1)} collective-permute-done((f32[1,4096]{1,0:T(1,128)S(1)}, f32[1,4096]{1,0:T(1,128)S(1)}, u32[]{:S(2)}, u32[]{:S(2)}) %collective-permute-start.31) | collective-permute-done | bytes 16416 | tf_op jit(solution)/shard_map/ppermute | solution.py:42
  (97 shorter events, 49.9 us)
Async XLA Ops:
  1.6 9.7 %collective-permute-start = (bf16[64,512]{1,0:T(8,128)(2,1)S(1)}, bf16[64,512]{1,0:T(8,128)(2,1)S(1)}, u32[]{:S(2)}, u32[]{:S(2)}) collective-permute-start(bf16[64,512]{1,0:T(8,128)(2,1)S(1)} %broadcast_select_fusion.12), channel_id=1, source_target_pairs={{0,1},{1,0},{2,3},{3,2},{4,5},{5,4},{6,7},{7,6},{8,9},{9,8},{10,11... | collective-permute-start | bytes 196616 | tf_op jit(solution)/shard_map/ppermute | solution.py:42
  11.4 9.8 %collective-permute-start.1 = (bf16[128,512]{1,0:T(8,128)(2,1)S(1)}, bf16[128,512]{1,0:T(8,128)(2,1)S(1)}, u32[]{:S(2)}, u32[]{:S(2)}) collective-permute-start(bf16[128,512]{1,0:T(8,128)(2,1)S(1)} %pad_maximum_fusion.3), channel_id=1, source_target_pairs={{0,6},{1,7},{2,0},{3,1},{4,2},{5,3},{6,4},{7,5},{8,14},{9,15},{10,... | collective-permute-start | bytes 393224 | tf_op jit(solution)/shard_map/ppermute | solution.py:42
  13.6 10.2 %collective-permute-start.2 = (bf16[128,512]{1,0:T(8,128)(2,1)S(1)}, bf16[128,512]{1,0:T(8,128)(2,1)S(1)}, u32[]{:S(2)}, u32[]{:S(2)}) collective-permute-start(bf16[128,512]{1,0:T(8,128)(2,1)S(1)} %pad_maximum_fusion.3), channel_id=1, source_target_pairs={{0,4},{1,5},{2,6},{3,7},{4,0},{5,1},{6,2},{7,3},{8,12},{9,13},{10,... | collective-permute-start | bytes 393224 | tf_op jit(solution)/shard_map/ppermute | solution.py:42
  15.5 11.9 %collective-permute-start.4 = (bf16[128,4096]{1,0:T(8,128)(2,1)}, bf16[128,4096]{1,0:T(8,128)(2,1)S(1)}, u32[]{:S(2)}, u32[]{:S(2)}) collective-permute-start(bf16[128,4096]{1,0:T(8,128)(2,1)} %bitcast.23), channel_id=1, source_target_pairs={{0,1},{1,0},{2,3},{3,2},{4,5},{5,4},{6,7},{7,6},{8,9},{9,8},{10,11... | collective-permute-start | bytes 3145736 | tf_op jit(solution)/shard_map/ppermute | solution.py:42
  18.1 9.2 %collective-permute-start.3 = (bf16[128,512]{1,0:T(8,128)(2,1)S(1)}, bf16[128,512]{1,0:T(8,128)(2,1)S(1)}, u32[]{:S(2)}, u32[]{:S(2)}) collective-permute-start(bf16[128,512]{1,0:T(8,128)(2,1)S(1)} %pad_maximum_fusion.3), channel_id=1, source_target_pairs={{0,2},{1,3},{2,4},{3,5},{4,6},{5,7},{6,0},{7,1},{8,10},{9,11},{10,... | collective-permute-start | bytes 393224 | tf_op jit(solution)/shard_map/ppermute | solution.py:42
  29.0 16.3 %collective-permute-start.5 = (bf16[512,512]{1,0:T(8,128)(2,1)S(1)}, bf16[512,512]{1,0:T(8,128)(2,1)S(1)}, u32[]{:S(2)}, u32[]{:S(2)}) collective-permute-start(bf16[512,512]{1,0:T(8,128)(2,1)S(1)} %constant_dynamic-slice_fusion.1.refs_0_), channel_id=1, source_target_pairs={{0,8},{1,9},{2,10},{3,11},{4,12},{5,13},{6,14},{7,15},{8,16},{9,17... | collective-permute-start | bytes 1572872 | tf_op jit(solution)/shard_map/ppermute | solution.py:42
  31.9 19.7 %collective-permute-start.8 = (bf16[512,512]{1,0:T(8,128)(2,1)S(1)}, bf16[512,512]{1,0:T(8,128)(2,1)S(1)}, u32[]{:S(2)}, u32[]{:S(2)}) collective-permute-start(bf16[512,512]{1,0:T(8,128)(2,1)S(1)} %constant_dynamic-slice_fusion.1.refs_0_), channel_id=1, source_target_pairs={{0,56},{1,57},{2,58},{3,59},{4,60},{5,61},{6,62},{7,63},{8,0},{9,1... | collective-permute-start | bytes 1572872 | tf_op jit(solution)/shard_map/ppermute | solution.py:42
  35.7 31.5 %collective-permute-start.11 = (bf16[256,2048]{1,0:T(8,128)(2,1)}, bf16[256,2048]{1,0:T(8,128)(2,1)}, u32[]{:S(2)}, u32[]{:S(2)}) collective-permute-start(bf16[256,2048]{1,0:T(8,128)(2,1)} %fusion.6), channel_id=1, source_target_pairs={{0,4},{8,12},{16,20},{24,28},{32,36},{40,44},{48,52},{56,60},{1,69... | collective-permute-start | bytes 3145736 | tf_op jit(solution)/shard_map/ppermute | solution.py:60
  46.4 35.1 %collective-permute-start.7 = (bf16[128,2048]{1,0:T(8,128)(2,1)S(1)}, bf16[128,2048]{1,0:T(8,128)(2,1)S(1)}, u32[]{:S(2)}, u32[]{:S(2)}) collective-permute-start(bf16[128,2048]{1,0:T(8,128)(2,1)S(1)} %constant_dynamic-slice_fusion), channel_id=1, source_target_pairs={{0,1},{1,0},{2,3},{3,2},{4,5},{5,4},{6,7},{7,6},{8,9},{9,8},{10,11... | collective-permute-start | bytes 1572872 | tf_op jit(solution)/shard_map/ppermute | solution.py:42
  49.7 17.5 %collective-permute-start.9 = (bf16[512,512]{1,0:T(8,128)(2,1)S(1)}, bf16[512,512]{1,0:T(8,128)(2,1)S(1)}, u32[]{:S(2)}, u32[]{:S(2)}) collective-permute-start(bf16[512,512]{1,0:T(8,128)(2,1)S(1)} %collective-permute-done.5.refs_8_), channel_id=1, source_target_pairs={{0,8},{1,9},{2,10},{3,11},{4,12},{5,13},{6,14},{7,15},{8,16},{9,17... | collective-permute-start | bytes 1572872 | tf_op jit(solution)/shard_map/ppermute | solution.py:42
  51.6 15.6 %collective-permute-start.10 = (bf16[512,512]{1,0:T(8,128)(2,1)S(1)}, bf16[512,512]{1,0:T(8,128)(2,1)S(1)}, u32[]{:S(2)}, u32[]{:S(2)}) collective-permute-start(bf16[512,512]{1,0:T(8,128)(2,1)S(1)} %collective-permute-done.8.refs_1_), channel_id=1, source_target_pairs={{0,56},{1,57},{2,58},{3,59},{4,60},{5,61},{6,62},{7,63},{8,0},{9,1... | collective-permute-start | bytes 1572872 | tf_op jit(solution)/shard_map/ppermute | solution.py:42
  58.2 29.7 %collective-permute-start.6 = (bf16[128,4096]{1,0:T(8,128)(2,1)S(1)}, bf16[128,4096]{1,0:T(8,128)(2,1)S(1)}, u32[]{:S(2)}, u32[]{:S(2)}) collective-permute-start(bf16[128,4096]{1,0:T(8,128)(2,1)S(1)} %bitcast.17), channel_id=1, source_target_pairs={{0,1},{1,0},{2,3},{3,2},{4,5},{5,4},{6,7},{7,6},{8,9},{9,8},{10,11... | collective-permute-start | bytes 3145736 | tf_op jit(solution)/shard_map/ppermute | solution.py:42
  67.2 15.4 %collective-permute-start.12 = (bf16[512,512]{1,0:T(8,128)(2,1)S(1)}, bf16[512,512]{1,0:T(8,128)(2,1)S(1)}, u32[]{:S(2)}, u32[]{:S(2)}) collective-permute-start(bf16[512,512]{1,0:T(8,128)(2,1)S(1)} %collective-permute-done.10.refs_2_), channel_id=1, source_target_pairs={{0,56},{1,57},{2,58},{3,59},{4,60},{5,61},{6,62},{7,63},{8,0},{9,1... | collective-permute-start | bytes 1572872 | tf_op jit(solution)/shard_map/ppermute | solution.py:42
  72.5 16.1 %collective-permute-start.13 = (bf16[512,512]{1,0:T(8,128)(2,1)S(1)}, bf16[512,512]{1,0:T(8,128)(2,1)S(1)}, u32[]{:S(2)}, u32[]{:S(2)}) collective-permute-start(bf16[512,512]{1,0:T(8,128)(2,1)S(1)} %collective-permute-done.9.refs_7_), channel_id=1, source_target_pairs={{0,8},{1,9},{2,10},{3,11},{4,12},{5,13},{6,14},{7,15},{8,16},{9,17... | collective-permute-start | bytes 1572872 | tf_op jit(solution)/shard_map/ppermute | solution.py:42
  74.4 45.5 %collective-permute-start.19 = (bf16[256,2048]{1,0:T(8,128)(2,1)}, bf16[256,2048]{1,0:T(8,128)(2,1)S(1)}, u32[]{:S(2)}, u32[]{:S(2)}) collective-permute-start(bf16[256,2048]{1,0:T(8,128)(2,1)} %collective-permute-done.11), channel_id=1, source_target_pairs={{0,132},{8,140},{16,148},{24,156},{32,164},{40,172},{48,180},{56,1... | collective-permute-start | bytes 3145736 | tf_op jit(solution)/shard_map/ppermute | solution.py:60
  82.6 9.3 %collective-permute-start.15 = (bf16[256,512]{1,0:T(8,128)(2,1)S(1)}, bf16[256,512]{1,0:T(8,128)(2,1)S(1)}, u32[]{:S(2)}, u32[]{:S(2)}) collective-permute-start(bf16[256,512]{1,0:T(8,128)(2,1)S(1)} %slice.61), channel_id=1, source_target_pairs={{0,56},{1,57},{2,58},{3,59},{4,60},{5,61},{6,62},{7,63},{8,0},{9,1... | collective-permute-start | bytes 786440 | tf_op jit(solution)/shard_map/ppermute | solution.py:42
  88.7 8.8 %collective-permute-start.14 = (bf16[256,512]{1,0:T(8,128)(2,1)S(1)}, bf16[256,512]{1,0:T(8,128)(2,1)S(1)}, u32[]{:S(2)}, u32[]{:S(2)}) collective-permute-start(bf16[256,512]{1,0:T(8,128)(2,1)S(1)} %slice.60), channel_id=1, source_target_pairs={{0,8},{1,9},{2,10},{3,11},{4,12},{5,13},{6,14},{7,15},{8,16},{9,17... | collective-permute-start | bytes 786440 | tf_op jit(solution)/shard_map/ppermute | solution.py:42
  98.7 12.9 %collective-permute-start.16 = (bf16[256,512]{1,0:T(8,128)(2,1)S(1)}, bf16[256,512]{1,0:T(8,128)(2,1)S(1)}, u32[]{:S(2)}, u32[]{:S(2)}) collective-permute-start(bf16[256,512]{1,0:T(8,128)(2,1)S(1)} %project.2.own_ref), channel_id=1, source_target_pairs={{0,2},{1,3},{2,4},{3,5},{4,6},{5,7},{6,8},{7,9},{8,10},{9,11},{10,... | collective-permute-start | bytes 786440 | tf_op jit(solution)/shard_map/ppermute | solution.py:143
  102.4 17.6 %collective-permute-start.17 = (bf16[272,512]{1,0:T(8,128)(2,1)S(1)}, bf16[272,512]{1,0:T(8,128)(2,1)S(1)}, u32[]{:S(2)}, u32[]{:S(2)}) collective-permute-start(bf16[272,512]{1,0:T(8,128)(2,1)S(1)} %project.3), channel_id=1, source_target_pairs={{0,4},{8,12},{16,20},{24,28},{32,36},{40,44},{48,52},{56,60},{1,69... | collective-permute-start | bytes 835592 | tf_op jit(solution)/shard_map/ppermute | solution.py:60
  118.6 10.4 %collective-permute-start.18 = (bf16[256,512]{1,0:T(8,128)(2,1)S(1)}, bf16[256,512]{1,0:T(8,128)(2,1)S(1)}, u32[]{:S(2)}, u32[]{:S(2)}) collective-permute-start(bf16[256,512]{1,0:T(8,128)(2,1)S(1)} %get-tuple-element.43), channel_id=1, source_target_pairs={{2,0},{3,1},{4,2},{5,3},{6,4},{7,5},{8,6},{9,7},{10,8},{11,9},{12,... | collective-permute-start | bytes 786440 | tf_op jit(solution)/shard_map/ppermute | solution.py:148
  131.0 5.2 %collective-permute-start.20 = (bf16[128,4096]{1,0:T(8,128)(2,1)S(1)}, bf16[128,4096]{1,0:T(8,128)(2,1)S(1)}, u32[]{:S(2)}, u32[]{:S(2)}) collective-permute-start(bf16[128,4096]{1,0:T(8,128)(2,1)S(1)} %partial_grad.3), channel_id=1, source_target_pairs={{0,1},{1,0},{2,3},{3,2},{4,5},{5,4},{6,7},{7,6},{8,9},{9,8},{10,11... | collective-permute-start | bytes 3145736 | tf_op jit(solution)/shard_map/ppermute | solution.py:42
  137.6 59.2 %collective-permute-start.21 = (bf16[128,4096]{1,0:T(8,128)(2,1)S(1)}, bf16[128,4096]{1,0:T(8,128)(2,1)S(1)}, u32[]{:S(2)}, u32[]{:S(2)}) collective-permute-start(bf16[128,4096]{1,0:T(8,128)(2,1)S(1)} %get-tuple-element.47), channel_id=1, source_target_pairs={{0,4},{8,12},{16,20},{24,28},{32,36},{40,44},{48,52},{56,60},{1,69... | collective-permute-start | bytes 3145736 | tf_op jit(solution)/shard_map/ppermute | solution.py:60
  140.6 20.0 %collective-permute-start.25 = (bf16[272,512]{1,0:T(8,128)(2,1)S(1)}, bf16[272,512]{1,0:T(8,128)(2,1)S(1)}, u32[]{:S(2)}, u32[]{:S(2)}) collective-permute-start(bf16[272,512]{1,0:T(8,128)(2,1)S(1)} %collective-permute-done.17), channel_id=1, source_target_pairs={{0,132},{8,140},{16,148},{24,156},{32,164},{40,172},{48,180},{56,1... | collective-permute-start | bytes 835592 | tf_op jit(solution)/shard_map/ppermute | solution.py:60
  160.5 38.5 %collective-permute-start.26 = (bf16[272,512]{1,0:T(8,128)(2,1)S(1)}, bf16[272,512]{1,0:T(8,128)(2,1)S(1)}, u32[]{:S(2)}, u32[]{:S(2)}) collective-permute-start(bf16[272,512]{1,0:T(8,128)(2,1)S(1)} %collective-permute-done.25.beside_ref.own_ref), channel_id=1, source_target_pairs={{0,2},{1,3},{2,4},{3,5},{4,6},{5,7},{6,8},{7,9},{8,10},{9,11},{10,... | collective-permute-start | bytes 835592 | tf_op jit(solution)/shard_map/ppermute | solution.py:143
  178.8 5.0 %collective-permute-start.22 = (f32[1,4096]{1,0:T(1,128)S(1)}, f32[1,4096]{1,0:T(1,128)S(1)}, u32[]{:S(2)}, u32[]{:S(2)}) collective-permute-start(f32[1,4096]{1,0:T(1,128)S(1)} %get-tuple-element.48), channel_id=1, source_target_pairs={{0,1},{1,0},{2,3},{3,2},{4,5},{5,4},{6,7},{7,6},{8,9},{9,8},{10,11... | collective-permute-start | bytes 49160 | tf_op jit(solution)/shard_map/ppermute | solution.py:42
  183.8 4.7 %collective-permute-start.23 = (f32[1,4096]{1,0:T(1,128)S(1)}, f32[1,4096]{1,0:T(1,128)S(1)}, u32[]{:S(2)}, u32[]{:S(2)}) collective-permute-start(f32[1,4096]{1,0:T(1,128)S(1)} %add.73), channel_id=1, source_target_pairs={{0,8},{1,9},{2,10},{3,11},{4,12},{5,13},{6,14},{7,15},{8,0},{9,1},... | collective-permute-start | bytes 49160 | tf_op jit(solution)/shard_map/ppermute | solution.py:42
  188.5 8.3 %collective-permute-start.24 = (f32[1,4096]{1,0:T(1,128)S(1)}, f32[1,4096]{1,0:T(1,128)S(1)}, u32[]{:S(2)}, u32[]{:S(2)}) collective-permute-start(f32[1,4096]{1,0:T(1,128)S(1)} %add.74), channel_id=1, source_target_pairs={{0,16},{1,17},{2,18},{3,19},{4,20},{5,21},{6,22},{7,23},{8,24},{9,... | collective-permute-start | bytes 49160 | tf_op jit(solution)/shard_map/ppermute | solution.py:42
  196.8 29.1 %collective-permute-start.28 = (bf16[128,4096]{1,0:T(8,128)(2,1)S(1)}, bf16[128,4096]{1,0:T(8,128)(2,1)S(1)}, u32[]{:S(2)}, u32[]{:S(2)}) collective-permute-start(bf16[128,4096]{1,0:T(8,128)(2,1)S(1)} %collective-permute-done.21), channel_id=1, source_target_pairs={{0,4},{8,12},{16,20},{24,28},{32,36},{40,44},{48,52},{56,60},{1,45... | collective-permute-start | bytes 3145736 | tf_op jit(solution)/shard_map/ppermute | solution.py:60
  205.8 20.0 %collective-permute-start.27 = (bf16[128,2048]{1,0:T(8,128)(2,1)S(1)}, bf16[128,2048]{1,0:T(8,128)(2,1)S(1)}, u32[]{:S(2)}, u32[]{:S(2)}) collective-permute-start(bf16[128,2048]{1,0:T(8,128)(2,1)S(1)} %broadcast_select_fusion.6), channel_id=1, source_target_pairs={{0,1},{1,0},{2,3},{3,2},{4,5},{5,4},{6,7},{7,6},{8,9},{9,8},{10,11... | collective-permute-start | bytes 1572872 | tf_op jit(solution)/shard_map/ppermute | solution.py:42
  209.5 8.4 %collective-permute-start.29 = (f32[1,4096]{1,0:T(1,128)S(1)}, f32[1,4096]{1,0:T(1,128)S(1)}, u32[]{:S(2)}, u32[]{:S(2)}) collective-permute-start(f32[1,4096]{1,0:T(1,128)S(1)} %add.75), channel_id=1, source_target_pairs={{0,32},{1,33},{2,34},{3,35},{4,36},{5,37},{6,38},{7,39},{8,40},{9,... | collective-permute-start | bytes 49160 | tf_op jit(solution)/shard_map/ppermute | solution.py:42
  217.9 7.9 %collective-permute-start.30 = (f32[1,4096]{1,0:T(1,128)S(1)}, f32[1,4096]{1,0:T(1,128)S(1)}, u32[]{:S(2)}, u32[]{:S(2)}) collective-permute-start(f32[1,4096]{1,0:T(1,128)S(1)} %add.76), channel_id=1, source_target_pairs={{0,2},{1,3},{2,0},{3,1},{4,6},{5,7},{6,4},{7,5},{8,10},{9,11},{10,... | collective-permute-start | bytes 49160 | tf_op jit(solution)/shard_map/ppermute | solution.py:42
  225.9 5.5 %collective-permute-start.31 = (f32[1,4096]{1,0:T(1,128)S(1)}, f32[1,4096]{1,0:T(1,128)S(1)}, u32[]{:S(2)}, u32[]{:S(2)}) collective-permute-start(f32[1,4096]{1,0:T(1,128)S(1)} %add.77), channel_id=1, source_target_pairs={{0,4},{1,5},{2,6},{3,7},{4,0},{5,1},{6,2},{7,3},{8,12},{9,13},{10,... | collective-permute-start | bytes 49160 | tf_op jit(solution)/shard_map/ppermute | solution.py:42
  (8 other events, 120.7 us)
